TPU v7x, 32 devices: a whole 2x2x4 slice. The times are simulated.
32 devices in a mesh: hist: 16 (over z, y, core), col: 2 (over x).
Axes of the slice: x: 2, y: 2, z: 4, core: 2. Of those that a mesh axis runs over, the one named last changes fastest.
Arguments:
- lesser: float32 [16, 128, 16, 128], P('col', None, 'hist'), may hold values from -0.1875 to 0.1875
- advanced: float32 [16, 128, 16, 128], P('col', None, 'hist'), may hold values from -0.1875 to 0.1875
- first_row: float32 [128, 16, 128], P(None, 'col'), may hold values from -4 to 4
- greater_rows: float32 [4, 128, 16, 128], P(None, None, 'col'), may hold values from -4 to 4
- hamiltonian: float32 [128, 128], replicated, may hold values from -0.5 to 0.5
- coupling: float32 [128, 128], replicated, may hold values from 0.3 to 1
- cutoff: int32 [16], P('hist'), may hold values from 1 to 16, as said below
- step_index: int32 [1], replicated, may hold values from 4 to 11
Outputs:
- final_row: float32 [128, 16, 128], P(None, 'col')
Inputs may be any that keep to these rules, and one draw needn't show every extreme that they name: Some second time has cutoff 16.
All inputs are finite; a program needn't handle non-finite values.
Results may differ from a plain program's by a relative error of at most 0.0001.
Values sent between devices are 32-bit elements; how exact they have to be, the bound alone decides.
No kernel may reach another device: no remote copies, remote signals or barrier semaphores. Data moves between devices by JAX's collectives and lax.ppermute only.
A program may use at most 64 MiB of HBM per device.

v0:
```python
import jax
import jax.numpy as jnp
from jax import lax
from jax.sharding import PartitionSpec as P

STEPS = 4


STEP_SIZE = 0.2
PRECISE = lax.Precision.HIGHEST


def on_device(lesser, advanced, first_row, greater_rows, hamiltonian, coupling, cutoff, step_index):
    rows_dev = lesser.shape[0]
    orbitals = lesser.shape[1]
    cols_dev = lesser.shape[2]
    col_pos = lax.axis_index("col")
    row_times = col_pos * rows_dev + jnp.arange(rows_dev, dtype=jnp.int32)
    inside = (row_times[:, None] < cutoff[None, :]).astype(jnp.float32)
    adv_flat = (advanced * inside[:, None, :, None]).reshape(
        rows_dev * orbitals, cols_dev * orbitals
    )
    hist_flat = lesser.reshape(rows_dev * orbitals, cols_dev * orbitals)
    propagator = jnp.eye(orbitals, dtype=jnp.float32) - STEP_SIZE * hamiltonian
    strength = (coupling * coupling)[:, None, :]
    current = first_row
    for section in range(STEPS):
        greater = greater_rows[section]
        sigma_less = -strength * current * current * greater
        sigma_ret = -strength * greater * greater * current - sigma_less
        active = (row_times < step_index[0] + section).astype(jnp.float32)
        ret_flat = (sigma_ret * active[None, :, None]).reshape(orbitals, rows_dev * orbitals)
        less_flat = sigma_less.reshape(orbitals, rows_dev * orbitals)
        memory = jnp.dot(ret_flat, hist_flat, precision=PRECISE, preferred_element_type=jnp.float32)
        memory = memory + jnp.dot(
            less_flat, adv_flat, precision=PRECISE, preferred_element_type=jnp.float32
        )
        slab_rows = lax.psum_scatter(
            memory.reshape(
                orbitals // lax.axis_size("col") * lax.axis_size("col"), cols_dev, orbitals
            ),
            "col",
            scatter_dimension=0,
            tiled=True,
        )
        spread = lax.all_gather(slab_rows, "hist", axis=1, tiled=True)
        memory_block = lax.all_to_all(spread, "col", split_axis=1, concat_axis=0, tiled=True)
        moved = jnp.einsum("ik,ksj->isj", propagator, current, precision=PRECISE)
        current = moved - STEP_SIZE * memory_block
    return current


def solution(mesh):
    in_specs = (
        P("col", None, "hist", None),
        P("col", None, "hist", None),
        P(None, "col", None),
        P(None, None, "col", None),
        P(),
        P(),
        P("hist"),
        P(),
    )
    out_specs = P(None, "col", None)
    return jax.shard_map(
        on_device, mesh=mesh, in_specs=in_specs, out_specs=out_specs, check_vma=False
    )
```

profile of v0, /device:TPU:0, one launch (start us, length us, event | category | flops | bytes accessed | tf_op | source)
XLA Modules:
  0.0 211.1 jit_solution(4326922517885189734)
XLA Ops:
  6.5 2.7 %fusion.33 = (f32[1,128,8,128]{3,2,1,0:T(8,128)S(1)}, f32[1,128,8,128]{3,2,1,0:T(8,128)}, f32[1,128,8,128]{3,2,1,0:T(8,128)S(1)}, f32[1,128,8,128]{3,2,1,0:T(8,128)}) fusion(f32[4,128,8,128]{3,2,1,0:T(8,128)} %param.11), kind=kLoop, calls=%fused_computation.60 | loop fusion | bytes 4194304 | tf_op jit(solution)/shard_map/slice | solution.py:28
  9.4 0.2 copy.79
  9.6 0.2 copy.102
  11.2 0.2 fusion.7
  11.4 1.0 fusion.34
  12.4 0.4 broadcast_multiply_fusion
  12.9 1.6 fusion.3
  14.5 12.7 %reduce-scatter.5.cloned.1.call-done = f32[64,1,128]{2,0,1:T(8,128)} async-done(((f32[128,1,128]{2,0,1:T(8,128)}), f32[64,1,128]{2,0,1:T(8,128)}) %reduce-scatter.5.cloned.1.call-update) | async-done | bytes 32784 | tf_op jit(solution)/shard_map/reduce_scatter | solution.py:38
  27.2 24.5 %all_gather.12 = f32[64,16,128]{2,0,1:T(8,128)} all-gather(f32[64,1,128]{2,0,1:T(8,128)} %reduce-scatter.5.cloned.1.call-done), channel_id=1, replica_groups=mesh['hist'=16,'col'=2] {'hist'}, dimensions={1}, use_global_device_ids=true | all-gather | bytes 557056 | tf_op jit(solution)/shard_map/all_gather | solution.py:46
  51.8 3.5 %all-to-all-start = ((f32[64,16,128]{2,0,1:T(8,128)}), f32[64,16,128]{2,0,1:T(8,128)S(1)}, u32[]{:S(2)}, u32[]{:S(2)}) async-start(f32[64,16,128]{2,0,1:T(8,128)} %all_gather.12), calls=%async_computation.1 | async-start | bytes 1048576 | tf_op jit(solution)/shard_map/all_to_all | solution.py:47
  55.3 0.2 copy.103
  55.6 0.6 fusion.27
  56.2 7.9 %all-to-all-done = f32[64,16,128]{2,0,1:T(8,128)S(1)} async-done(((f32[64,16,128]{2,0,1:T(8,128)}), f32[64,16,128]{2,0,1:T(8,128)S(1)}, u32[]{:S(2)}, u32[]{:S(2)}) %all-to-all-start) | async-done | bytes 524320 | tf_op jit(solution)/shard_map/all_to_all | solution.py:47
  64.0 0.3 fusion.23
  64.4 0.2 copy.87
  64.9 1.0 fusion.35
  65.9 1.6 fusion.2
  67.6 6.1 %reduce-scatter.7.cloned.1.call-done = f32[64,1,128]{2,0,1:T(8,128)} async-done(((f32[128,1,128]{2,0,1:T(8,128)}), f32[64,1,128]{2,0,1:T(8,128)}) %reduce-scatter.7.cloned.1.call-update) | async-done | bytes 32784 | tf_op jit(solution)/shard_map/reduce_scatter | solution.py:38
  73.7 24.4 %all_gather.13 = f32[64,16,128]{2,0,1:T(8,128)} all-gather(f32[64,1,128]{2,0,1:T(8,128)} %reduce-scatter.7.cloned.1.call-done), channel_id=1, replica_groups=mesh['hist'=16,'col'=2] {'hist'}, dimensions={1}, use_global_device_ids=true | all-gather | bytes 557056 | tf_op jit(solution)/shard_map/all_gather | solution.py:46
  98.1 3.5 %all-to-all-start.1 = ((f32[64,16,128]{2,0,1:T(8,128)}), f32[64,16,128]{2,0,1:T(8,128)S(1)}, u32[]{:S(2)}, u32[]{:S(2)}) async-start(f32[64,16,128]{2,0,1:T(8,128)} %all_gather.13), calls=%async_computation.3 | async-start | bytes 1048576 | tf_op jit(solution)/shard_map/all_to_all | solution.py:47
  101.7 0.2 copy.104
  101.9 0.6 fusion.26
  102.5 7.8 %all-to-all-done.1 = f32[64,16,128]{2,0,1:T(8,128)S(1)} async-done(((f32[64,16,128]{2,0,1:T(8,128)}), f32[64,16,128]{2,0,1:T(8,128)S(1)}, u32[]{:S(2)}, u32[]{:S(2)}) %all-to-all-start.1) | async-done | bytes 524320 | tf_op jit(solution)/shard_map/all_to_all | solution.py:47
  110.4 0.3 fusion.22
  110.8 1.0 copy.91
  111.8 1.1 fusion.15
  112.9 0.2 fusion.14
  113.1 1.0 fusion.36
  114.1 1.6 fusion.1
  115.8 6.1 %reduce-scatter.9.cloned.1.call-done = f32[64,1,128]{2,0,1:T(8,128)} async-done(((f32[128,1,128]{2,0,1:T(8,128)}), f32[64,1,128]{2,0,1:T(8,128)}) %reduce-scatter.9.cloned.1.call-update) | async-done | bytes 32784 | tf_op jit(solution)/shard_map/reduce_scatter | solution.py:38
  121.9 24.4 %all_gather.14 = f32[64,16,128]{2,0,1:T(8,128)} all-gather(f32[64,1,128]{2,0,1:T(8,128)} %reduce-scatter.9.cloned.1.call-done), channel_id=1, replica_groups=mesh['hist'=16,'col'=2] {'hist'}, dimensions={1}, use_global_device_ids=true | all-gather | bytes 557056 | tf_op jit(solution)/shard_map/all_gather | solution.py:46
  146.3 3.5 %all-to-all-start.2 = ((f32[64,16,128]{2,0,1:T(8,128)}), f32[64,16,128]{2,0,1:T(8,128)S(1)}, u32[]{:S(2)}, u32[]{:S(2)}) async-start(f32[64,16,128]{2,0,1:T(8,128)} %all_gather.14), calls=%async_computation.5 | async-start | bytes 1048576 | tf_op jit(solution)/shard_map/all_to_all | solution.py:47
  149.8 0.2 reduce-scatter.11.cloned.1.call-start
  150.0 0.2 copy.105
  150.3 0.6 fusion.25
  150.9 7.7 %all-to-all-done.2 = f32[64,16,128]{2,0,1:T(8,128)S(1)} async-done(((f32[64,16,128]{2,0,1:T(8,128)}), f32[64,16,128]{2,0,1:T(8,128)S(1)}, u32[]{:S(2)}, u32[]{:S(2)}) %all-to-all-start.2) | async-done | bytes 524320 | tf_op jit(solution)/shard_map/all_to_all | solution.py:47
  158.5 0.3 fusion.21
  158.9 0.2 copy.95
  159.2 0.2 fusion.19
  159.3 1.0 fusion.37
  160.3 1.6 fusion
  162.0 6.1 %reduce-scatter.11.cloned.1.call-done = f32[64,1,128]{2,0,1:T(8,128)} async-done(((f32[128,1,128]{2,0,1:T(8,128)}), f32[64,1,128]{2,0,1:T(8,128)}) %reduce-scatter.11.cloned.1.call-update) | async-done | bytes 32784 | tf_op jit(solution)/shard_map/reduce_scatter | solution.py:38
  168.1 23.1 %all_gather.15 = f32[64,16,128]{2,0,1:T(8,128)S(1)} all-gather(f32[64,1,128]{2,0,1:T(8,128)} %reduce-scatter.11.cloned.1.call-done), channel_id=1, replica_groups=mesh['hist'=16,'col'=2] {'hist'}, dimensions={1}, use_global_device_ids=true | all-gather | bytes 557056 | tf_op jit(solution)/shard_map/all_gather | solution.py:46
  191.2 11.2 %all_to_all.16 = f32[64,16,128]{2,0,1:T(8,128)S(1)} all-to-all(f32[64,16,128]{2,0,1:T(8,128)S(1)} %all_gather.15), channel_id=1, replica_groups=mesh['hist'=16,'col'=2] {'col'}, dimensions={1} | all-to-all | bytes 1048576 | tf_op jit(solution)/shard_map/all_to_all | solution.py:47
  202.3 0.3 fusion.20
  202.7 0.2 copy.99
  202.9 0.6 convolution_subtract_fusion
  203.5 1.1 copy.100
  (31 shorter events, 0.7 us)
Async XLA Ops:
  6.5 4.8 %copy-start = (f32[8,128,1,128]{3,2,1,0:T(1,128)S(1)}, f32[8,128,1,128]{3,2,1,0:T(1,128)}, u32[]{:S(2)}) copy-start(f32[8,128,1,128]{3,2,1,0:T(1,128)} %param.8) | copy-start | bytes 1572868
  6.5 20.7 %reduce-scatter.5.cloned.1.call-start = ((), (), s32[]{:S(2)}) async-start(), calls=%async_computation.8 | async-start | bytes 98304 | tf_op jit(solution)/shard_map/reduce_scatter | solution.py:38
  6.5 2.7 %copy-start.6 = (f32[128,128]{1,0:T(8,128)S(1)}, f32[128,128]{1,0:T(8,128)}, u32[]{:S(2)}) copy-start(f32[128,128]{1,0:T(8,128)} %param.13) | copy-start | bytes 196612
  6.5 2.8 %copy-start.4 = (f32[128,8,128]{2,1,0:T(8,128)S(1)}, f32[128,8,128]{2,1,0:T(8,128)}, u32[]{:S(2)}) copy-start(f32[128,8,128]{2,1,0:T(8,128)} %param.10) | copy-start | bytes 1572868
  9.6 2.8 %copy-start.5 = (f32[8,128,1,128]{3,2,1,0:T(1,128)S(1)}, f32[8,128,1,128]{3,2,1,0:T(1,128)}, u32[]{:S(2)}) copy-start(f32[8,128,1,128]{3,2,1,0:T(1,128)} %param.9) | copy-start | bytes 1572868
  12.8 42.7 %copy-start.3 = (f32[128,128]{1,0:T(8,128)S(1)}, f32[128,128]{1,0:T(8,128)}, u32[]{:S(2)}) copy-start(f32[128,128]{1,0:T(8,128)} %param.12) | copy-start | bytes 196612
  51.8 12.2 %all-to-all-start = ((f32[64,16,128]{2,0,1:T(8,128)}), f32[64,16,128]{2,0,1:T(8,128)S(1)}, u32[]{:S(2)}, u32[]{:S(2)}) async-start(f32[64,16,128]{2,0,1:T(8,128)} %all_gather.12), calls=%async_computation.1 | async-start | bytes 1048576 | tf_op jit(solution)/shard_map/all_to_all | solution.py:47
  55.3 18.4 %reduce-scatter.7.cloned.1.call-start = ((), (), s32[]{:S(2)}) async-start(), calls=%async_computation.9 | async-start | bytes 98304 | tf_op jit(solution)/shard_map/reduce_scatter | solution.py:38
  64.9 36.8 %copy-start.2 = (f32[1,128,8,128]{3,2,1,0:T(8,128)S(1)}, f32[1,128,8,128]{3,2,1,0:T(8,128)}, u32[]{:S(2)}) copy-start(f32[1,128,8,128]{3,2,1,0:T(8,128)} %get-tuple-element.10) | copy-start | bytes 1572868
  98.1 12.2 %all-to-all-start.1 = ((f32[64,16,128]{2,0,1:T(8,128)}), f32[64,16,128]{2,0,1:T(8,128)S(1)}, u32[]{:S(2)}, u32[]{:S(2)}) async-start(f32[64,16,128]{2,0,1:T(8,128)} %all_gather.13), calls=%async_computation.3 | async-start | bytes 1048576 | tf_op jit(solution)/shard_map/all_to_all | solution.py:47
  101.6 20.2 %reduce-scatter.9.cloned.1.call-start = ((), (), s32[]{:S(2)}) async-start(), calls=%async_computation.10 | async-start | bytes 98304 | tf_op jit(solution)/shard_map/reduce_scatter | solution.py:38
  113.1 36.9 %copy-start.1 = (f32[1,128,8,128]{3,2,1,0:T(8,128)S(1)}, f32[1,128,8,128]{3,2,1,0:T(8,128)}, u32[]{:S(2)}) copy-start(f32[1,128,8,128]{3,2,1,0:T(8,128)} %get-tuple-element.12) | copy-start | bytes 1572868
  146.3 12.2 %all-to-all-start.2 = ((f32[64,16,128]{2,0,1:T(8,128)}), f32[64,16,128]{2,0,1:T(8,128)S(1)}, u32[]{:S(2)}, u32[]{:S(2)}) async-start(f32[64,16,128]{2,0,1:T(8,128)} %all_gather.14), calls=%async_computation.5 | async-start | bytes 1048576 | tf_op jit(solution)/shard_map/all_to_all | solution.py:47
  149.8 18.3 %reduce-scatter.11.cloned.1.call-start = ((), (), s32[]{:S(2)}) async-start(), calls=%async_computation.11 | async-start | bytes 98304 | tf_op jit(solution)/shard_map/reduce_scatter | solution.py:38
Sparse Core Ops, SparseCore 0:
  14.6 12.5 reduce-scatter.4
  67.7 5.9 reduce-scatter.6
  115.9 5.9 reduce-scatter.8
  162.1 5.9 reduce-scatter.10
where the time goes:
time: 212 us; the launch traced here: 211 us
  blocking collectives  108 us (51%)
  waiting for transfers between devices  54.5 us (26%)
  between operations  14.8 us (7%)
  matrix products  12.9 us (6%)
  starting transfers between devices  10.8 us (5%)
  local copies, waits for them, and re-layouts  6.84 us (3%)
  other arithmetic  3.74 us (2%)
    all_gather x4, blocking collectives, on_device(): spread = lax.all_gather(slab_rows, 'hist', axis=1, tiled=True)  96.5 us
    reduce_scatter x4, waiting for transfers between devices, on_device(): lax.psum_scatter(memory.reshape(orbitals // lax.axis_size('col') * lax.ax...  31 us
    all_to_all x3, waiting for transfers between devices, on_device(): lax.all_to_all(spread, 'col', split_axis=1, concat_axis=0, tiled=True)  23.4 us
    all_to_all x1, blocking collectives, on_device(): lax.all_to_all(spread, 'col', split_axis=1, concat_axis=0, tiled=True)  11.2 us
    all_to_all x3, starting transfers between devices, on_device(): lax.all_to_all(spread, 'col', split_axis=1, concat_axis=0, tiled=True)  10.5 us
    dot_general x4, matrix products, on_device(): jnp.dot(less_flat, adv_flat, precision=PRECISE, preferred_element_type=jn...  6.52 us
  transfers between devices with their start and end apart: 7, of which 7 were waited for; matrix products, arithmetic and copies ran while one was open for 1% of the time, Pallas kernels for 0%

commit v1 on v0

v1 whole, which is shorter than its diff:
```python
import functools

import jax
import jax.numpy as jnp
from jax import lax
from jax.experimental import pallas as pl
from jax.experimental.pallas import tpu as pltpu
from jax.sharding import PartitionSpec as P

STEP_SIZE = 0.2
BF16 = jnp.bfloat16
F32 = jnp.float32


def split(x):
    high = x.astype(BF16)
    return high, (x - high.astype(F32)).astype(BF16)


def times_wide(high, low, wide):
    n = wide.shape[-1] // 2
    first = jnp.dot(high, wide, preferred_element_type=F32)
    second = jnp.dot(low, wide[:, :n], preferred_element_type=F32)
    return first[:, :n] + first[:, n:] + second


def advance(section, rows_dev, n, owner, own_row, cur, g_ref, coup_ref, ham_ref, active_ref, wide_ref, part_ref, high_ref, low_ref):
    coup = coup_ref[...]
    strength = coup * coup
    for s in range(rows_dev):
        x = cur[s]
        g = g_ref[pl.ds(s, n, stride=rows_dev), :]
        active = active_ref[pl.ds(section * rows_dev + s, 1), :]
        u = strength * x * g
        less = -(u * x)
        ret = (u * x - u * g) * active
        for where, value in ((s, ret), (rows_dev + s, less)):
            high, low = split(value)
            high_ref[:, where * n : (where + 1) * n] = high
            low_ref[:, where * n : (where + 1) * n] = low
    total = times_wide(high_ref[...], low_ref[...], wide_ref[...])
    h_high, h_low = split(ham_ref[...])
    row = cur[own_row] * owner
    row_wide = jnp.concatenate(split(row), axis=1)
    part_ref[...] = total + times_wide(h_high, h_low, row_wide)


def places(rows_dev):
    hist_pos, col_pos = lax.axis_index("hist"), lax.axis_index("col")
    own_row = lax.rem(hist_pos, rows_dev)
    owner = jnp.where(lax.div(hist_pos, rows_dev) == col_pos, 1.0, 0.0).astype(F32)
    return own_row, owner, col_pos


def first_kernel(rows_dev, n, steps, step_ref, cutoff_ref, lesser_ref, adv_ref, first_ref, g_ref, coup_ref, ham_ref,
                 cur_ref, wide_ref, active_ref, part_ref, high_ref, low_ref):
    own_row, owner, col_pos = places(rows_dev)
    cutoff, start = cutoff_ref[0], step_ref[0]
    for s in range(rows_dev):
        time = col_pos * rows_dev + s
        cur_ref[s] = first_ref[pl.ds(s, n, stride=rows_dev), :]
        for q in range(steps):
            active_ref[q * rows_dev + s : q * rows_dev + s + 1, :] = jnp.full(
                (1, n), jnp.where(time < start + q, 1.0, 0.0).astype(F32)
            )
        inside = jnp.where(time < cutoff, 1.0, 0.0).astype(F32)
        for where, value in (
            (s, lesser_ref[s * n : (s + 1) * n, :]),
            (rows_dev + s, adv_ref[s * n : (s + 1) * n, :] * inside),
        ):
            high, low = split(value)
            wide_ref[where * n : (where + 1) * n, :n] = high
            wide_ref[where * n : (where + 1) * n, n:] = low
    advance(0, rows_dev, n, owner, own_row, cur_ref, g_ref, coup_ref, ham_ref, active_ref, wide_ref, part_ref, high_ref, low_ref)


def next_kernel(section, rows_dev, n, order, prev_ref, g_ref, coup_ref, ham_ref, active_ref, wide_ref, *rest):
    pieces, (cur_ref, part_ref, high_ref, low_ref) = rest[:rows_dev], rest[rows_dev:]
    own_row, owner, _ = places(rows_dev)
    for k, piece in enumerate(pieces):
        s = order(own_row, k)
        cur_ref[s] = prev_ref[s] - STEP_SIZE * piece[...]
    advance(section, rows_dev, n, owner, own_row, cur_ref, g_ref, coup_ref, ham_ref, active_ref, wide_ref, part_ref, high_ref, low_ref)


def last_kernel(rows_dev, n, order, prev_ref, *rest):
    pieces, (out_ref,) = rest[:rows_dev], rest[rows_dev:]
    own_row, _, _ = places(rows_dev)
    for k, piece in enumerate(pieces):
        s = order(own_row, k)
        out_ref[pl.ds(s, n, stride=rows_dev), :] = prev_ref[s] - STEP_SIZE * piece[...]


def call(kernel, outs, scratch, smem, vmem, name):
    return pl.pallas_call(
        kernel,
        out_shape=outs,
        in_specs=[pl.BlockSpec(memory_space=pltpu.SMEM)] * smem + [pl.BlockSpec(memory_space=pltpu.VMEM)] * vmem,
        out_specs=jax.tree.map(lambda _: pl.BlockSpec(memory_space=pltpu.VMEM), outs),
        scratch_shapes=scratch,
        name=name,
    )


def exchange_pairs(hist, rows_dev, part):
    def at(h, c):
        return h * 2 + c

    def moved(x, pairs):
        return lax.ppermute(x, ("hist", "col"), pairs)

    def flip(x, bits):
        return moved(x, [(at(h, c), at(h ^ bits, c)) for h in range(hist) for c in range(2)])

    total = part + moved(part, [(at(h, c), at(h, 1 - c)) for h in range(hist) for c in range(2)])
    other = flip(total, rows_dev)
    reads_own = lax.axis_index("hist") // rows_dev == lax.axis_index("col")
    own = jnp.where(reads_own, total, other)
    pieces = [own] + [None] * (rows_dev - 1)
    for bits in range(2, rows_dev, 2):
        pieces[bits] = flip(own, bits)
    for bits in range(0, rows_dev, 2):
        pieces[bits + 1] = flip(pieces[bits], 1)
    return pieces


def exchange_any(rows_dev, part):
    total = lax.psum(part, "col")
    rows = lax.all_gather(total, "hist", axis=0)
    block = lax.dynamic_slice_in_dim(rows, lax.axis_index("col") * rows_dev, rows_dev, axis=0)
    return [block[s] for s in range(rows_dev)]


def on_device(hist, cols, lesser, advanced, first_row, greater_rows, hamiltonian, coupling, cutoff, step_index):
    rows_dev, n, cols_dev, _ = lesser.shape
    steps = greater_rows.shape[0]
    assert cols_dev == 1 and hist == cols * rows_dev
    flat = (rows_dev * n, n)
    pairs = cols == 2 and hist & (hist - 1) == 0 and rows_dev >= 2
    if pairs:
        exchange = functools.partial(exchange_pairs, hist, rows_dev)
        order = lambda own_row, k: jnp.bitwise_xor(own_row, k)
    else:
        exchange = functools.partial(exchange_any, rows_dev)
        order = lambda own_row, k: k
    shape = jax.ShapeDtypeStruct
    cur_shape, part_shape = shape((rows_dev, n, n), F32), shape((n, n), F32)
    scratch = [pltpu.VMEM((n, 2 * rows_dev * n), BF16)] * 2
    current, wide, active, part = call(
        functools.partial(first_kernel, rows_dev, n, steps),
        (cur_shape, shape((2 * rows_dev * n, 2 * n), BF16), shape((steps * rows_dev, n), F32), part_shape),
        scratch, 2, 6, "first_step",
    )(step_index, cutoff, lesser.reshape(flat), advanced.reshape(flat), first_row.reshape(flat),
      greater_rows[0].reshape(flat), coupling, hamiltonian)
    for section in range(1, steps):
        pieces = exchange(part)
        current, part = call(
            functools.partial(next_kernel, section, rows_dev, n, order),
            (cur_shape, part_shape), scratch, 0, 6 + rows_dev, "next_step",
        )(current, greater_rows[section].reshape(flat), coupling, hamiltonian, active, wide, *pieces)
    pieces = exchange(part)
    final = call(
        functools.partial(last_kernel, rows_dev, n, order), shape(flat, F32), [], 0, 1 + rows_dev, "last_step",
    )(current, *pieces)
    return final.reshape(first_row.shape)


def solution(mesh):
    in_specs = (
        P("col", None, "hist", None),
        P("col", None, "hist", None),
        P(None, "col", None),
        P(None, None, "col", None),
        P(),
        P(),
        P("hist"),
        P(),
    )
    return jax.shard_map(
        functools.partial(on_device, mesh.shape["hist"], mesh.shape["col"]),
        mesh=mesh, in_specs=in_specs, out_specs=P(None, "col", None), check_vma=False,
    )
```

time: 212 us -> 98.9 us (0.47)
  the two profiles are of different devices: /device:TPU:0 before, /device:TPU:25 now
where the time goes in v1:
time: 98.9 us; the launch traced here: 97.9 us
  starting transfers between devices  42.3 us (43%)
  waiting for transfers between devices  30.7 us (31%)
  Pallas kernels  14.6 us (15%)
  local copies, waits for them, and re-layouts  5.29 us (5%)
  other arithmetic  3.44 us (3%)
  between operations  1.65 us (2%)
    ppermute x36, starting transfers between devices, moved(): return lax.ppermute(x, ('hist', 'col'), pairs)  42.3 us
    ppermute x36, waiting for transfers between devices, moved(): return lax.ppermute(x, ('hist', 'col'), pairs)  30.7 us
    pallas_call x3, Pallas kernels, on_device(): call(functools.partial(next_kernel, section, rows_dev, n, order), (cur_sh...  9.1 us
    add x4, other arithmetic, exchange_pairs(): part + moved(part, [(at(h, c), at(h, 1 - c)) for h in range(hist) for c i...  3.41 us
    pallas_call x1, Pallas kernels, on_device(): call(functools.partial(first_kernel, rows_dev, n, steps), (cur_shape, sha...  3.34 us
    another operation x1, local copies, waits for them, and re-layouts, on_device(): greater_rows[section].reshape(flat)  2.88 us
    unnamed x64, local copies, waits for them, and re-layouts  2.4 us
    pallas_call x1, Pallas kernels, on_device(): call(functools.partial(last_kernel, rows_dev, n, order), shape(flat, F32)...  2.17 us
  transfers between devices with their start and end apart: 36, of which 14 were waited for; matrix products, arithmetic and copies ran while one was open for 0% of the time, Pallas kernels for 0%

profile of v1, /device:TPU:25, one launch (start us, length us, event | category | flops | bytes accessed | tf_op | source)
XLA Modules:
  0.0 97.9 jit_solution(7628040446166389160)
XLA Ops:
  1.3 2.9 %slice_bitcast_fusion = (f32[1024,128]{1,0:T(8,128)}, f32[1024,128]{1,0:T(8,128)}, f32[1024,128]{1,0:T(8,128)}, f32[1024,128]{1,0:T(8,128)}) fusion(f32[4,128,8,128]{3,2,1,0:T(8,128)} %param.11), kind=kLoop, calls=%fused_computation | loop fusion | bytes 4194304 | tf_op jit(solution)/shard_map/reshape;squeeze | solution.py:160
  4.2 3.3 %first_step.1 = (f32[8,128,128]{2,1,0:T(8,128)}, bf16[2048,256]{1,0:T(8,128)(2,1)}, f32[32,128]{1,0:T(8,128)}, f32[128,128]{1,0:T(8,128)}) custom-call(s32[1]{0:T(128)S(6)} %copy.10.step_ref, s32[1]{0:T(128)S(6)} %copy.9.cutoff_ref, f32[1024,128]{1,0:T(8,128)} %bitcast.12, f32[1024,128]{1,0:T(8,128)} %bitcast.13, f32[1024,128]{1,0:T(8,128)} %bitcast.14, ...), custom_call_target="tpu_custom_call" | custom-call | tf_op jit(solution)/shard_map/first_step/pallas_call | solution.py:149
  7.5 1.2 %collective-permute-start = (f32[128,128]{1,0:T(8,128)}, f32[128,128]{1,0:T(8,128)S(1)}, u32[]{:S(2)}, u32[]{:S(2)}) collective-permute-start(f32[128,128]{1,0:T(8,128)} %get-tuple-element.18), channel_id=1, source_target_pairs={{0,1},{1,0},{2,3},{3,2},{4,5},{5,4},{6,7},{7,6},{8,9},{9,8},{10,11... | collective-permute-start | bytes 196616 | tf_op jit(solution)/shard_map/ppermute | solution.py:110
  8.7 2.1 %collective-permute-done = f32[128,128]{1,0:T(8,128)S(1)} collective-permute-done((f32[128,128]{1,0:T(8,128)}, f32[128,128]{1,0:T(8,128)S(1)}, u32[]{:S(2)}, u32[]{:S(2)}) %collective-permute-start) | collective-permute-done | bytes 65568 | tf_op jit(solution)/shard_map/ppermute | solution.py:110
  10.8 0.9 add.13
  11.8 4.5 %collective-permute-done.1 = f32[128,128]{1,0:T(8,128)S(1)} collective-permute-done((f32[128,128]{1,0:T(8,128)S(1)}, f32[128,128]{1,0:T(8,128)S(1)}, u32[]{:S(2)}, u32[]{:S(2)}) %collective-permute-start.1) | collective-permute-done | bytes 65568 | tf_op jit(solution)/shard_map/ppermute | solution.py:110
  16.4 0.7 collective-permute-start.7
  17.0 1.8 %collective-permute-start.5 = (f32[128,128]{1,0:T(8,128)S(1)}, f32[128,128]{1,0:T(8,128)S(1)}, u32[]{:S(2)}, u32[]{:S(2)}) collective-permute-start(f32[128,128]{1,0:T(8,128)S(1)} %broadcast_select_fusion.3.rest_0_), channel_id=1, source_target_pairs={{0,8},{1,9},{2,10},{3,11},{4,12},{5,13},{6,14},{7,15},{8,0},{9,1},... | collective-permute-start | bytes 196616 | tf_op jit(solution)/shard_map/ppermute | solution.py:110
  19.1 3.8 %collective-permute-start.2 = (f32[128,128]{1,0:T(8,128)S(1)}, f32[128,128]{1,0:T(8,128)S(1)}, u32[]{:S(2)}, u32[]{:S(2)}) collective-permute-start(f32[128,128]{1,0:T(8,128)S(1)} %broadcast_select_fusion.3.rest_0_), channel_id=1, source_target_pairs={{0,2},{1,3},{2,0},{3,1},{4,6},{5,7},{6,4},{7,5},{8,10},{9,11},{10,... | collective-permute-start | bytes 196616 | tf_op jit(solution)/shard_map/ppermute | solution.py:110
  22.9 1.7 %collective-permute-start.8 = (f32[128,128]{1,0:T(8,128)S(1)}, f32[128,128]{1,0:T(8,128)S(1)}, u32[]{:S(2)}, u32[]{:S(2)}) collective-permute-start(f32[128,128]{1,0:T(8,128)S(1)} %collective-permute-done.7.rest_6_), channel_id=1, source_target_pairs={{0,2},{1,3},{2,0},{3,1},{4,6},{5,7},{6,4},{7,5},{8,10},{9,11},{10,... | collective-permute-start | bytes 196616 | tf_op jit(solution)/shard_map/ppermute | solution.py:110
  24.6 0.8 collective-permute-start.6
  25.4 1.3 %collective-permute-start.4 = (f32[128,128]{1,0:T(8,128)S(1)}, f32[128,128]{1,0:T(8,128)S(1)}, u32[]{:S(2)}, u32[]{:S(2)}) collective-permute-start(f32[128,128]{1,0:T(8,128)S(1)} %collective-permute-done.3.rest_2_), channel_id=1, source_target_pairs={{0,2},{1,3},{2,0},{3,1},{4,6},{5,7},{6,4},{7,5},{8,10},{9,11},{10,... | collective-permute-start | bytes 196616 | tf_op jit(solution)/shard_map/ppermute | solution.py:110
  26.7 0.9 collective-permute-done.4.rest_3_
  28.2 3.0 %next_step.3 = (f32[8,128,128]{2,1,0:T(8,128)}, f32[128,128]{1,0:T(8,128)}) custom-call(f32[8,128,128]{2,1,0:T(8,128)} %get-tuple-element.15.prev_ref, f32[1024,128]{1,0:T(8,128)} %get-tuple-element.26.g_ref, f32[128,128]{1,0:T(8,128)} %coup_ref.7, f32[128,128]{1,0:T(8,128)} %ham_ref.7, f32[32,128]{1,0:T(8,128)} %get-tuple-element.16.active_ref, ...), custom_call_target="tpu_custom_call" | custom-call | tf_op jit(solution)/shard_map/next_step/pallas_call | solution.py:157
  31.2 1.2 %collective-permute-start.9 = (f32[128,128]{1,0:T(8,128)}, f32[128,128]{1,0:T(8,128)S(1)}, u32[]{:S(2)}, u32[]{:S(2)}) collective-permute-start(f32[128,128]{1,0:T(8,128)} %get-tuple-element.20), channel_id=1, source_target_pairs={{0,1},{1,0},{2,3},{3,2},{4,5},{5,4},{6,7},{7,6},{8,9},{9,8},{10,11... | collective-permute-start | bytes 196616 | tf_op jit(solution)/shard_map/ppermute | solution.py:110
  32.5 2.1 %collective-permute-done.9 = f32[128,128]{1,0:T(8,128)S(1)} collective-permute-done((f32[128,128]{1,0:T(8,128)}, f32[128,128]{1,0:T(8,128)S(1)}, u32[]{:S(2)}, u32[]{:S(2)}) %collective-permute-start.9) | collective-permute-done | bytes 65568 | tf_op jit(solution)/shard_map/ppermute | solution.py:110
  34.6 0.9 add.14
  35.5 4.7 %collective-permute-done.10 = f32[128,128]{1,0:T(8,128)S(1)} collective-permute-done((f32[128,128]{1,0:T(8,128)S(1)}, f32[128,128]{1,0:T(8,128)S(1)}, u32[]{:S(2)}, u32[]{:S(2)}) %collective-permute-start.10) | collective-permute-done | bytes 65568 | tf_op jit(solution)/shard_map/ppermute | solution.py:110
  40.3 1.4 %collective-permute-start.14 = (f32[128,128]{1,0:T(8,128)S(1)}, f32[128,128]{1,0:T(8,128)S(1)}, u32[]{:S(2)}, u32[]{:S(2)}) collective-permute-start(f32[128,128]{1,0:T(8,128)S(1)} %broadcast_select_fusion.2.rest_0_), channel_id=1, source_target_pairs={{0,8},{1,9},{2,10},{3,11},{4,12},{5,13},{6,14},{7,15},{8,0},{9,1},... | collective-permute-start | bytes 196616 | tf_op jit(solution)/shard_map/ppermute | solution.py:110
  41.7 1.2 %collective-permute-start.12 = (f32[128,128]{1,0:T(8,128)S(1)}, f32[128,128]{1,0:T(8,128)S(1)}, u32[]{:S(2)}, u32[]{:S(2)}) collective-permute-start(f32[128,128]{1,0:T(8,128)S(1)} %broadcast_select_fusion.2.rest_0_), channel_id=1, source_target_pairs={{0,4},{1,5},{2,6},{3,7},{4,0},{5,1},{6,2},{7,3},{8,12},{9,13},{10,... | collective-permute-start | bytes 196616 | tf_op jit(solution)/shard_map/ppermute | solution.py:110
  42.9 3.2 %collective-permute-start.11 = (f32[128,128]{1,0:T(8,128)S(1)}, f32[128,128]{1,0:T(8,128)S(1)}, u32[]{:S(2)}, u32[]{:S(2)}) collective-permute-start(f32[128,128]{1,0:T(8,128)S(1)} %broadcast_select_fusion.2.rest_0_), channel_id=1, source_target_pairs={{0,2},{1,3},{2,0},{3,1},{4,6},{5,7},{6,4},{7,5},{8,10},{9,11},{10,... | collective-permute-start | bytes 196616 | tf_op jit(solution)/shard_map/ppermute | solution.py:110
  46.1 1.7 %collective-permute-start.17 = (f32[128,128]{1,0:T(8,128)S(1)}, f32[128,128]{1,0:T(8,128)S(1)}, u32[]{:S(2)}, u32[]{:S(2)}) collective-permute-start(f32[128,128]{1,0:T(8,128)S(1)} %collective-permute-done.16.rest_6_), channel_id=1, source_target_pairs={{0,2},{1,3},{2,0},{3,1},{4,6},{5,7},{6,4},{7,5},{8,10},{9,11},{10,... | collective-permute-start | bytes 196616 | tf_op jit(solution)/shard_map/ppermute | solution.py:110
  47.9 1.0 %collective-permute-start.13 = (f32[128,128]{1,0:T(8,128)S(1)}, f32[128,128]{1,0:T(8,128)S(1)}, u32[]{:S(2)}, u32[]{:S(2)}) collective-permute-start(f32[128,128]{1,0:T(8,128)S(1)} %collective-permute-done.12.rest_2_), channel_id=1, source_target_pairs={{0,2},{1,3},{2,0},{3,1},{4,6},{5,7},{6,4},{7,5},{8,10},{9,11},{10,... | collective-permute-start | bytes 196616 | tf_op jit(solution)/shard_map/ppermute | solution.py:110
  49.1 0.7 collective-permute-done.13.rest_3_
  50.4 3.0 %next_step.4 = (f32[8,128,128]{2,1,0:T(8,128)}, f32[128,128]{1,0:T(8,128)}) custom-call(f32[8,128,128]{2,1,0:T(8,128)} %get-tuple-element.19.prev_ref, f32[1024,128]{1,0:T(8,128)} %get-tuple-element.28.g_ref, f32[128,128]{1,0:T(8,128)} %coup_ref.7, f32[128,128]{1,0:T(8,128)} %ham_ref.7, f32[32,128]{1,0:T(8,128)} %get-tuple-element.16.active_ref, ...), custom_call_target="tpu_custom_call" | custom-call | tf_op jit(solution)/shard_map/next_step/pallas_call | solution.py:157
  53.4 1.2 %collective-permute-start.18 = (f32[128,128]{1,0:T(8,128)}, f32[128,128]{1,0:T(8,128)S(1)}, u32[]{:S(2)}, u32[]{:S(2)}) collective-permute-start(f32[128,128]{1,0:T(8,128)} %get-tuple-element.22), channel_id=1, source_target_pairs={{0,1},{1,0},{2,3},{3,2},{4,5},{5,4},{6,7},{7,6},{8,9},{9,8},{10,11... | collective-permute-start | bytes 196616 | tf_op jit(solution)/shard_map/ppermute | solution.py:110
  54.6 2.1 %collective-permute-done.18 = f32[128,128]{1,0:T(8,128)S(1)} collective-permute-done((f32[128,128]{1,0:T(8,128)}, f32[128,128]{1,0:T(8,128)S(1)}, u32[]{:S(2)}, u32[]{:S(2)}) %collective-permute-start.18) | collective-permute-done | bytes 65568 | tf_op jit(solution)/shard_map/ppermute | solution.py:110
  56.7 0.9 add.15
  57.7 4.7 %collective-permute-done.19 = f32[128,128]{1,0:T(8,128)S(1)} collective-permute-done((f32[128,128]{1,0:T(8,128)S(1)}, f32[128,128]{1,0:T(8,128)S(1)}, u32[]{:S(2)}, u32[]{:S(2)}) %collective-permute-start.19) | collective-permute-done | bytes 65568 | tf_op jit(solution)/shard_map/ppermute | solution.py:110
  62.4 0.9 collective-permute-start.25
  63.3 1.6 %collective-permute-start.23 = (f32[128,128]{1,0:T(8,128)S(1)}, f32[128,128]{1,0:T(8,128)S(1)}, u32[]{:S(2)}, u32[]{:S(2)}) collective-permute-start(f32[128,128]{1,0:T(8,128)S(1)} %broadcast_select_fusion.1.rest_0_), channel_id=1, source_target_pairs={{0,8},{1,9},{2,10},{3,11},{4,12},{5,13},{6,14},{7,15},{8,0},{9,1},... | collective-permute-start | bytes 196616 | tf_op jit(solution)/shard_map/ppermute | solution.py:110
  65.1 3.2 %collective-permute-start.20 = (f32[128,128]{1,0:T(8,128)S(1)}, f32[128,128]{1,0:T(8,128)S(1)}, u32[]{:S(2)}, u32[]{:S(2)}) collective-permute-start(f32[128,128]{1,0:T(8,128)S(1)} %broadcast_select_fusion.1.rest_0_), channel_id=1, source_target_pairs={{0,2},{1,3},{2,0},{3,1},{4,6},{5,7},{6,4},{7,5},{8,10},{9,11},{10,... | collective-permute-start | bytes 196616 | tf_op jit(solution)/shard_map/ppermute | solution.py:110
  68.3 1.7 %collective-permute-start.26 = (f32[128,128]{1,0:T(8,128)S(1)}, f32[128,128]{1,0:T(8,128)S(1)}, u32[]{:S(2)}, u32[]{:S(2)}) collective-permute-start(f32[128,128]{1,0:T(8,128)S(1)} %collective-permute-done.25.rest_6_), channel_id=1, source_target_pairs={{0,2},{1,3},{2,0},{3,1},{4,6},{5,7},{6,4},{7,5},{8,10},{9,11},{10,... | collective-permute-start | bytes 196616 | tf_op jit(solution)/shard_map/ppermute | solution.py:110
  70.0 0.8 collective-permute-start.24
  70.7 1.3 %collective-permute-start.22 = (f32[128,128]{1,0:T(8,128)S(1)}, f32[128,128]{1,0:T(8,128)S(1)}, u32[]{:S(2)}, u32[]{:S(2)}) collective-permute-start(f32[128,128]{1,0:T(8,128)S(1)} %collective-permute-done.21.rest_2_), channel_id=1, source_target_pairs={{0,2},{1,3},{2,0},{3,1},{4,6},{5,7},{6,4},{7,5},{8,10},{9,11},{10,... | collective-permute-start | bytes 196616 | tf_op jit(solution)/shard_map/ppermute | solution.py:110
  72.1 0.9 collective-permute-done.22.rest_3_
  73.6 3.0 %next_step.5 = (f32[8,128,128]{2,1,0:T(8,128)}, f32[128,128]{1,0:T(8,128)}) custom-call(f32[8,128,128]{2,1,0:T(8,128)} %get-tuple-element.21.prev_ref, f32[1024,128]{1,0:T(8,128)} %get-tuple-element.25.g_ref, f32[128,128]{1,0:T(8,128)} %coup_ref.7, f32[128,128]{1,0:T(8,128)} %ham_ref.7, f32[32,128]{1,0:T(8,128)} %get-tuple-element.16.active_ref, ...), custom_call_target="tpu_custom_call" | custom-call | tf_op jit(solution)/shard_map/next_step/pallas_call | solution.py:157
  76.6 1.2 %collective-permute-start.27 = (f32[128,128]{1,0:T(8,128)}, f32[128,128]{1,0:T(8,128)S(1)}, u32[]{:S(2)}, u32[]{:S(2)}) collective-permute-start(f32[128,128]{1,0:T(8,128)} %get-tuple-element.24), channel_id=1, source_target_pairs={{0,1},{1,0},{2,3},{3,2},{4,5},{5,4},{6,7},{7,6},{8,9},{9,8},{10,11... | collective-permute-start | bytes 196616 | tf_op jit(solution)/shard_map/ppermute | solution.py:110
  77.8 2.1 %collective-permute-done.27 = f32[128,128]{1,0:T(8,128)S(1)} collective-permute-done((f32[128,128]{1,0:T(8,128)}, f32[128,128]{1,0:T(8,128)S(1)}, u32[]{:S(2)}, u32[]{:S(2)}) %collective-permute-start.27) | collective-permute-done | bytes 65568 | tf_op jit(solution)/shard_map/ppermute | solution.py:110
  79.9 0.9 add.16
  80.9 4.7 %collective-permute-done.28 = f32[128,128]{1,0:T(8,128)S(1)} collective-permute-done((f32[128,128]{1,0:T(8,128)S(1)}, f32[128,128]{1,0:T(8,128)S(1)}, u32[]{:S(2)}, u32[]{:S(2)}) %collective-permute-start.28) | collective-permute-done | bytes 65568 | tf_op jit(solution)/shard_map/ppermute | solution.py:110
  85.7 1.4 %collective-permute-start.32 = (f32[128,128]{1,0:T(8,128)S(1)}, f32[128,128]{1,0:T(8,128)S(1)}, u32[]{:S(2)}, u32[]{:S(2)}) collective-permute-start(f32[128,128]{1,0:T(8,128)S(1)} %broadcast_select_fusion.rest_0_), channel_id=1, source_target_pairs={{0,8},{1,9},{2,10},{3,11},{4,12},{5,13},{6,14},{7,15},{8,0},{9,1},... | collective-permute-start | bytes 196616 | tf_op jit(solution)/shard_map/ppermute | solution.py:110
  87.1 1.2 %collective-permute-start.30 = (f32[128,128]{1,0:T(8,128)S(1)}, f32[128,128]{1,0:T(8,128)S(1)}, u32[]{:S(2)}, u32[]{:S(2)}) collective-permute-start(f32[128,128]{1,0:T(8,128)S(1)} %broadcast_select_fusion.rest_0_), channel_id=1, source_target_pairs={{0,4},{1,5},{2,6},{3,7},{4,0},{5,1},{6,2},{7,3},{8,12},{9,13},{10,... | collective-permute-start | bytes 196616 | tf_op jit(solution)/shard_map/ppermute | solution.py:110
  88.3 3.2 %collective-permute-start.29 = (f32[128,128]{1,0:T(8,128)S(1)}, f32[128,128]{1,0:T(8,128)S(1)}, u32[]{:S(2)}, u32[]{:S(2)}) collective-permute-start(f32[128,128]{1,0:T(8,128)S(1)} %broadcast_select_fusion.rest_0_), channel_id=1, source_target_pairs={{0,2},{1,3},{2,0},{3,1},{4,6},{5,7},{6,4},{7,5},{8,10},{9,11},{10,... | collective-permute-start | bytes 196616 | tf_op jit(solution)/shard_map/ppermute | solution.py:110
  91.5 1.7 %collective-permute-start.35 = (f32[128,128]{1,0:T(8,128)S(1)}, f32[128,128]{1,0:T(8,128)S(1)}, u32[]{:S(2)}, u32[]{:S(2)}) collective-permute-start(f32[128,128]{1,0:T(8,128)S(1)} %collective-permute-done.34.rest_6_), channel_id=1, source_target_pairs={{0,2},{1,3},{2,0},{3,1},{4,6},{5,7},{6,4},{7,5},{8,10},{9,11},{10,... | collective-permute-start | bytes 196616 | tf_op jit(solution)/shard_map/ppermute | solution.py:110
  93.2 1.0 %collective-permute-start.31 = (f32[128,128]{1,0:T(8,128)S(1)}, f32[128,128]{1,0:T(8,128)S(1)}, u32[]{:S(2)}, u32[]{:S(2)}) collective-permute-start(f32[128,128]{1,0:T(8,128)S(1)} %collective-permute-done.30.rest_2_), channel_id=1, source_target_pairs={{0,2},{1,3},{2,0},{3,1},{4,6},{5,7},{6,4},{7,5},{8,10},{9,11},{10,... | collective-permute-start | bytes 196616 | tf_op jit(solution)/shard_map/ppermute | solution.py:110
  94.4 0.7 collective-permute-done.31.rest_3_
  95.8 2.2 %last_step.1 = f32[1024,128]{1,0:T(8,128)} custom-call(f32[8,128,128]{2,1,0:T(8,128)} %get-tuple-element.23.prev_ref, f32[128,128]{1,0:T(8,128)} %copy-done.3, f32[128,128]{1,0:T(8,128)} %copy-done.20, f32[128,128]{1,0:T(8,128)} %copy-done.18, f32[128,128]{1,0:T(8,128)} %copy-done.31, f32[128,128]{1,0:T(8,128)} %copy-done.15, f32[128,128]{1,0:T(8,128)} %copy-done.28, ...), custom_call_target="tpu_custom_call" | custom-call | tf_op jit(solution)/shard_map/last_step/pallas_call | solution.py:162
  (102 shorter events, 3.9 us)
Async XLA Ops:
  7.5 3.3 %collective-permute-start = (f32[128,128]{1,0:T(8,128)}, f32[128,128]{1,0:T(8,128)S(1)}, u32[]{:S(2)}, u32[]{:S(2)}) collective-permute-start(f32[128,128]{1,0:T(8,128)} %get-tuple-element.18), channel_id=1, source_target_pairs={{0,1},{1,0},{2,3},{3,2},{4,5},{5,4},{6,7},{7,6},{8,9},{9,8},{10,11... | collective-permute-start | bytes 196616 | tf_op jit(solution)/shard_map/ppermute | solution.py:110
  11.7 4.7 %collective-permute-start.1 = (f32[128,128]{1,0:T(8,128)S(1)}, f32[128,128]{1,0:T(8,128)S(1)}, u32[]{:S(2)}, u32[]{:S(2)}) collective-permute-start(f32[128,128]{1,0:T(8,128)S(1)} %add.13), channel_id=1, source_target_pairs={{0,16},{1,17},{2,18},{3,19},{4,20},{5,21},{6,22},{7,23},{8,24},{9,... | collective-permute-start | bytes 196616 | tf_op jit(solution)/shard_map/ppermute | solution.py:110
  16.4 11.2 %copy-start.1 = (f32[128,128]{1,0:T(8,128)}, f32[128,128]{1,0:T(8,128)S(1)}, u32[]{:S(2)}) copy-start(f32[128,128]{1,0:T(8,128)S(1)} %broadcast_select_fusion.3.rest_0_) | copy-start | bytes 196612
  16.4 6.5 %collective-permute-start.7 = (f32[128,128]{1,0:T(8,128)S(1)}, f32[128,128]{1,0:T(8,128)S(1)}, u32[]{:S(2)}, u32[]{:S(2)}) collective-permute-start(f32[128,128]{1,0:T(8,128)S(1)} %broadcast_select_fusion.3.rest_0_), channel_id=1, source_target_pairs={{0,12},{1,13},{2,14},{3,15},{4,8},{5,9},{6,10},{7,11},{8,4},{9,5},... | collective-permute-start | bytes 196616 | tf_op jit(solution)/shard_map/ppermute | solution.py:110
  17.0 7.5 %collective-permute-start.5 = (f32[128,128]{1,0:T(8,128)S(1)}, f32[128,128]{1,0:T(8,128)S(1)}, u32[]{:S(2)}, u32[]{:S(2)}) collective-permute-start(f32[128,128]{1,0:T(8,128)S(1)} %broadcast_select_fusion.3.rest_0_), channel_id=1, source_target_pairs={{0,8},{1,9},{2,10},{3,11},{4,12},{5,13},{6,14},{7,15},{8,0},{9,1},... | collective-permute-start | bytes 196616 | tf_op jit(solution)/shard_map/ppermute | solution.py:110
  18.9 6.5 %collective-permute-start.3 = (f32[128,128]{1,0:T(8,128)S(1)}, f32[128,128]{1,0:T(8,128)S(1)}, u32[]{:S(2)}, u32[]{:S(2)}) collective-permute-start(f32[128,128]{1,0:T(8,128)S(1)} %broadcast_select_fusion.3.rest_0_), channel_id=1, source_target_pairs={{0,4},{1,5},{2,6},{3,7},{4,0},{5,1},{6,2},{7,3},{8,12},{9,13},{10,... | collective-permute-start | bytes 196616 | tf_op jit(solution)/shard_map/ppermute | solution.py:110
  19.1 7.6 %collective-permute-start.2 = (f32[128,128]{1,0:T(8,128)S(1)}, f32[128,128]{1,0:T(8,128)S(1)}, u32[]{:S(2)}, u32[]{:S(2)}) collective-permute-start(f32[128,128]{1,0:T(8,128)S(1)} %broadcast_select_fusion.3.rest_0_), channel_id=1, source_target_pairs={{0,2},{1,3},{2,0},{3,1},{4,6},{5,7},{6,4},{7,5},{8,10},{9,11},{10,... | collective-permute-start | bytes 196616 | tf_op jit(solution)/shard_map/ppermute | solution.py:110
  22.9 4.7 %copy-start.5 = (f32[128,128]{1,0:T(8,128)}, f32[128,128]{1,0:T(8,128)S(1)}, u32[]{:S(2)}) copy-start(f32[128,128]{1,0:T(8,128)S(1)} %collective-permute-done.7.rest_6_) | copy-start | bytes 196612
  22.9 3.8 %collective-permute-start.8 = (f32[128,128]{1,0:T(8,128)S(1)}, f32[128,128]{1,0:T(8,128)S(1)}, u32[]{:S(2)}, u32[]{:S(2)}) collective-permute-start(f32[128,128]{1,0:T(8,128)S(1)} %collective-permute-done.7.rest_6_), channel_id=1, source_target_pairs={{0,2},{1,3},{2,0},{3,1},{4,6},{5,7},{6,4},{7,5},{8,10},{9,11},{10,... | collective-permute-start | bytes 196616 | tf_op jit(solution)/shard_map/ppermute | solution.py:110
  24.6 3.0 %copy-start.8 = (f32[128,128]{1,0:T(8,128)}, f32[128,128]{1,0:T(8,128)S(1)}, u32[]{:S(2)}) copy-start(f32[128,128]{1,0:T(8,128)S(1)} %collective-permute-done.5.rest_4_) | copy-start | bytes 196612
  24.6 2.1 %collective-permute-start.6 = (f32[128,128]{1,0:T(8,128)S(1)}, f32[128,128]{1,0:T(8,128)S(1)}, u32[]{:S(2)}, u32[]{:S(2)}) collective-permute-start(f32[128,128]{1,0:T(8,128)S(1)} %collective-permute-done.5.rest_4_), channel_id=1, source_target_pairs={{0,2},{1,3},{2,0},{3,1},{4,6},{5,7},{6,4},{7,5},{8,10},{9,11},{10,... | collective-permute-start | bytes 196616 | tf_op jit(solution)/shard_map/ppermute | solution.py:110
  25.4 2.2 %copy-start.12 = (f32[128,128]{1,0:T(8,128)}, f32[128,128]{1,0:T(8,128)S(1)}, u32[]{:S(2)}) copy-start(f32[128,128]{1,0:T(8,128)S(1)} %collective-permute-done.3.rest_2_) | copy-start | bytes 196612
  25.4 2.2 %collective-permute-start.4 = (f32[128,128]{1,0:T(8,128)S(1)}, f32[128,128]{1,0:T(8,128)S(1)}, u32[]{:S(2)}, u32[]{:S(2)}) collective-permute-start(f32[128,128]{1,0:T(8,128)S(1)} %collective-permute-done.3.rest_2_), channel_id=1, source_target_pairs={{0,2},{1,3},{2,0},{3,1},{4,6},{5,7},{6,4},{7,5},{8,10},{9,11},{10,... | collective-permute-start | bytes 196616 | tf_op jit(solution)/shard_map/ppermute | solution.py:110
  31.2 3.3 %collective-permute-start.9 = (f32[128,128]{1,0:T(8,128)}, f32[128,128]{1,0:T(8,128)S(1)}, u32[]{:S(2)}, u32[]{:S(2)}) collective-permute-start(f32[128,128]{1,0:T(8,128)} %get-tuple-element.20), channel_id=1, source_target_pairs={{0,1},{1,0},{2,3},{3,2},{4,5},{5,4},{6,7},{7,6},{8,9},{9,8},{10,11... | collective-permute-start | bytes 196616 | tf_op jit(solution)/shard_map/ppermute | solution.py:110
  35.4 4.8 %collective-permute-start.10 = (f32[128,128]{1,0:T(8,128)S(1)}, f32[128,128]{1,0:T(8,128)S(1)}, u32[]{:S(2)}, u32[]{:S(2)}) collective-permute-start(f32[128,128]{1,0:T(8,128)S(1)} %add.14), channel_id=1, source_target_pairs={{0,16},{1,17},{2,18},{3,19},{4,20},{5,21},{6,22},{7,23},{8,24},{9,... | collective-permute-start | bytes 196616 | tf_op jit(solution)/shard_map/ppermute | solution.py:110
  40.2 9.6 %copy-start.2 = (f32[128,128]{1,0:T(8,128)}, f32[128,128]{1,0:T(8,128)S(1)}, u32[]{:S(2)}) copy-start(f32[128,128]{1,0:T(8,128)S(1)} %broadcast_select_fusion.2.rest_0_) | copy-start | bytes 196612
  40.2 5.9 %collective-permute-start.16 = (f32[128,128]{1,0:T(8,128)S(1)}, f32[128,128]{1,0:T(8,128)S(1)}, u32[]{:S(2)}, u32[]{:S(2)}) collective-permute-start(f32[128,128]{1,0:T(8,128)S(1)} %broadcast_select_fusion.2.rest_0_), channel_id=1, source_target_pairs={{0,12},{1,13},{2,14},{3,15},{4,8},{5,9},{6,10},{7,11},{8,4},{9,5},... | collective-permute-start | bytes 196616 | tf_op jit(solution)/shard_map/ppermute | solution.py:110
  40.3 7.5 %collective-permute-start.14 = (f32[128,128]{1,0:T(8,128)S(1)}, f32[128,128]{1,0:T(8,128)S(1)}, u32[]{:S(2)}, u32[]{:S(2)}) collective-permute-start(f32[128,128]{1,0:T(8,128)S(1)} %broadcast_select_fusion.2.rest_0_), channel_id=1, source_target_pairs={{0,8},{1,9},{2,10},{3,11},{4,12},{5,13},{6,14},{7,15},{8,0},{9,1},... | collective-permute-start | bytes 196616 | tf_op jit(solution)/shard_map/ppermute | solution.py:110
  41.7 6.2 %collective-permute-start.12 = (f32[128,128]{1,0:T(8,128)S(1)}, f32[128,128]{1,0:T(8,128)S(1)}, u32[]{:S(2)}, u32[]{:S(2)}) collective-permute-start(f32[128,128]{1,0:T(8,128)S(1)} %broadcast_select_fusion.2.rest_0_), channel_id=1, source_target_pairs={{0,4},{1,5},{2,6},{3,7},{4,0},{5,1},{6,2},{7,3},{8,12},{9,13},{10,... | collective-permute-start | bytes 196616 | tf_op jit(solution)/shard_map/ppermute | solution.py:110
  42.9 5.9 %collective-permute-start.11 = (f32[128,128]{1,0:T(8,128)S(1)}, f32[128,128]{1,0:T(8,128)S(1)}, u32[]{:S(2)}, u32[]{:S(2)}) collective-permute-start(f32[128,128]{1,0:T(8,128)S(1)} %broadcast_select_fusion.2.rest_0_), channel_id=1, source_target_pairs={{0,2},{1,3},{2,0},{3,1},{4,6},{5,7},{6,4},{7,5},{8,10},{9,11},{10,... | collective-permute-start | bytes 196616 | tf_op jit(solution)/shard_map/ppermute | solution.py:110
  46.1 3.7 %copy-start.6 = (f32[128,128]{1,0:T(8,128)}, f32[128,128]{1,0:T(8,128)S(1)}, u32[]{:S(2)}) copy-start(f32[128,128]{1,0:T(8,128)S(1)} %collective-permute-done.16.rest_6_) | copy-start | bytes 196612
  46.1 2.8 %collective-permute-start.17 = (f32[128,128]{1,0:T(8,128)S(1)}, f32[128,128]{1,0:T(8,128)S(1)}, u32[]{:S(2)}, u32[]{:S(2)}) collective-permute-start(f32[128,128]{1,0:T(8,128)S(1)} %collective-permute-done.16.rest_6_), channel_id=1, source_target_pairs={{0,2},{1,3},{2,0},{3,1},{4,6},{5,7},{6,4},{7,5},{8,10},{9,11},{10,... | collective-permute-start | bytes 196616 | tf_op jit(solution)/shard_map/ppermute | solution.py:110
  47.8 1.3 %collective-permute-start.15 = (f32[128,128]{1,0:T(8,128)S(1)}, f32[128,128]{1,0:T(8,128)S(1)}, u32[]{:S(2)}, u32[]{:S(2)}) collective-permute-start(f32[128,128]{1,0:T(8,128)S(1)} %collective-permute-done.14.rest_4_), channel_id=1, source_target_pairs={{0,2},{1,3},{2,0},{3,1},{4,6},{5,7},{6,4},{7,5},{8,10},{9,11},{10,... | collective-permute-start | bytes 196616 | tf_op jit(solution)/shard_map/ppermute | solution.py:110
  47.9 1.9 %collective-permute-start.13 = (f32[128,128]{1,0:T(8,128)S(1)}, f32[128,128]{1,0:T(8,128)S(1)}, u32[]{:S(2)}, u32[]{:S(2)}) collective-permute-start(f32[128,128]{1,0:T(8,128)S(1)} %collective-permute-done.12.rest_2_), channel_id=1, source_target_pairs={{0,2},{1,3},{2,0},{3,1},{4,6},{5,7},{6,4},{7,5},{8,10},{9,11},{10,... | collective-permute-start | bytes 196616 | tf_op jit(solution)/shard_map/ppermute | solution.py:110
  53.4 3.3 %collective-permute-start.18 = (f32[128,128]{1,0:T(8,128)}, f32[128,128]{1,0:T(8,128)S(1)}, u32[]{:S(2)}, u32[]{:S(2)}) collective-permute-start(f32[128,128]{1,0:T(8,128)} %get-tuple-element.22), channel_id=1, source_target_pairs={{0,1},{1,0},{2,3},{3,2},{4,5},{5,4},{6,7},{7,6},{8,9},{9,8},{10,11... | collective-permute-start | bytes 196616 | tf_op jit(solution)/shard_map/ppermute | solution.py:110
  57.6 4.8 %collective-permute-start.19 = (f32[128,128]{1,0:T(8,128)S(1)}, f32[128,128]{1,0:T(8,128)S(1)}, u32[]{:S(2)}, u32[]{:S(2)}) collective-permute-start(f32[128,128]{1,0:T(8,128)S(1)} %add.15), channel_id=1, source_target_pairs={{0,16},{1,17},{2,18},{3,19},{4,20},{5,21},{6,22},{7,23},{8,24},{9,... | collective-permute-start | bytes 196616 | tf_op jit(solution)/shard_map/ppermute | solution.py:110
  62.4 10.6 %copy-start = (f32[128,128]{1,0:T(8,128)}, f32[128,128]{1,0:T(8,128)S(1)}, u32[]{:S(2)}) copy-start(f32[128,128]{1,0:T(8,128)S(1)} %broadcast_select_fusion.1.rest_0_) | copy-start | bytes 196612
  62.4 5.9 %collective-permute-start.25 = (f32[128,128]{1,0:T(8,128)S(1)}, f32[128,128]{1,0:T(8,128)S(1)}, u32[]{:S(2)}, u32[]{:S(2)}) collective-permute-start(f32[128,128]{1,0:T(8,128)S(1)} %broadcast_select_fusion.1.rest_0_), channel_id=1, source_target_pairs={{0,12},{1,13},{2,14},{3,15},{4,8},{5,9},{6,10},{7,11},{8,4},{9,5},... | collective-permute-start | bytes 196616 | tf_op jit(solution)/shard_map/ppermute | solution.py:110
  63.3 6.6 %collective-permute-start.23 = (f32[128,128]{1,0:T(8,128)S(1)}, f32[128,128]{1,0:T(8,128)S(1)}, u32[]{:S(2)}, u32[]{:S(2)}) collective-permute-start(f32[128,128]{1,0:T(8,128)S(1)} %broadcast_select_fusion.1.rest_0_), channel_id=1, source_target_pairs={{0,8},{1,9},{2,10},{3,11},{4,12},{5,13},{6,14},{7,15},{8,0},{9,1},... | collective-permute-start | bytes 196616 | tf_op jit(solution)/shard_map/ppermute | solution.py:110
  64.9 5.8 %collective-permute-start.21 = (f32[128,128]{1,0:T(8,128)S(1)}, f32[128,128]{1,0:T(8,128)S(1)}, u32[]{:S(2)}, u32[]{:S(2)}) collective-permute-start(f32[128,128]{1,0:T(8,128)S(1)} %broadcast_select_fusion.1.rest_0_), channel_id=1, source_target_pairs={{0,4},{1,5},{2,6},{3,7},{4,0},{5,1},{6,2},{7,3},{8,12},{9,13},{10,... | collective-permute-start | bytes 196616 | tf_op jit(solution)/shard_map/ppermute | solution.py:110
  65.1 6.9 %collective-permute-start.20 = (f32[128,128]{1,0:T(8,128)S(1)}, f32[128,128]{1,0:T(8,128)S(1)}, u32[]{:S(2)}, u32[]{:S(2)}) collective-permute-start(f32[128,128]{1,0:T(8,128)S(1)} %broadcast_select_fusion.1.rest_0_), channel_id=1, source_target_pairs={{0,2},{1,3},{2,0},{3,1},{4,6},{5,7},{6,4},{7,5},{8,10},{9,11},{10,... | collective-permute-start | bytes 196616 | tf_op jit(solution)/shard_map/ppermute | solution.py:110
  68.3 4.7 %copy-start.4 = (f32[128,128]{1,0:T(8,128)}, f32[128,128]{1,0:T(8,128)S(1)}, u32[]{:S(2)}) copy-start(f32[128,128]{1,0:T(8,128)S(1)} %collective-permute-done.25.rest_6_) | copy-start | bytes 196612
  68.3 3.8 %collective-permute-start.26 = (f32[128,128]{1,0:T(8,128)S(1)}, f32[128,128]{1,0:T(8,128)S(1)}, u32[]{:S(2)}, u32[]{:S(2)}) collective-permute-start(f32[128,128]{1,0:T(8,128)S(1)} %collective-permute-done.25.rest_6_), channel_id=1, source_target_pairs={{0,2},{1,3},{2,0},{3,1},{4,6},{5,7},{6,4},{7,5},{8,10},{9,11},{10,... | collective-permute-start | bytes 196616 | tf_op jit(solution)/shard_map/ppermute | solution.py:110
  70.0 3.0 %copy-start.7 = (f32[128,128]{1,0:T(8,128)}, f32[128,128]{1,0:T(8,128)S(1)}, u32[]{:S(2)}) copy-start(f32[128,128]{1,0:T(8,128)S(1)} %collective-permute-done.23.rest_4_) | copy-start | bytes 196612
  70.0 2.1 %collective-permute-start.24 = (f32[128,128]{1,0:T(8,128)S(1)}, f32[128,128]{1,0:T(8,128)S(1)}, u32[]{:S(2)}, u32[]{:S(2)}) collective-permute-start(f32[128,128]{1,0:T(8,128)S(1)} %collective-permute-done.23.rest_4_), channel_id=1, source_target_pairs={{0,2},{1,3},{2,0},{3,1},{4,6},{5,7},{6,4},{7,5},{8,10},{9,11},{10,... | collective-permute-start | bytes 196616 | tf_op jit(solution)/shard_map/ppermute | solution.py:110
  70.7 2.2 %copy-start.10 = (f32[128,128]{1,0:T(8,128)}, f32[128,128]{1,0:T(8,128)S(1)}, u32[]{:S(2)}) copy-start(f32[128,128]{1,0:T(8,128)S(1)} %collective-permute-done.21.rest_2_) | copy-start | bytes 196612
  70.7 2.2 %collective-permute-start.22 = (f32[128,128]{1,0:T(8,128)S(1)}, f32[128,128]{1,0:T(8,128)S(1)}, u32[]{:S(2)}, u32[]{:S(2)}) collective-permute-start(f32[128,128]{1,0:T(8,128)S(1)} %collective-permute-done.21.rest_2_), channel_id=1, source_target_pairs={{0,2},{1,3},{2,0},{3,1},{4,6},{5,7},{6,4},{7,5},{8,10},{9,11},{10,... | collective-permute-start | bytes 196616 | tf_op jit(solution)/shard_map/ppermute | solution.py:110
  76.6 3.3 %collective-permute-start.27 = (f32[128,128]{1,0:T(8,128)}, f32[128,128]{1,0:T(8,128)S(1)}, u32[]{:S(2)}, u32[]{:S(2)}) collective-permute-start(f32[128,128]{1,0:T(8,128)} %get-tuple-element.24), channel_id=1, source_target_pairs={{0,1},{1,0},{2,3},{3,2},{4,5},{5,4},{6,7},{7,6},{8,9},{9,8},{10,11... | collective-permute-start | bytes 196616 | tf_op jit(solution)/shard_map/ppermute | solution.py:110
  80.8 4.8 %collective-permute-start.28 = (f32[128,128]{1,0:T(8,128)S(1)}, f32[128,128]{1,0:T(8,128)S(1)}, u32[]{:S(2)}, u32[]{:S(2)}) collective-permute-start(f32[128,128]{1,0:T(8,128)S(1)} %add.16), channel_id=1, source_target_pairs={{0,16},{1,17},{2,18},{3,19},{4,20},{5,21},{6,22},{7,23},{8,24},{9,... | collective-permute-start | bytes 196616 | tf_op jit(solution)/shard_map/ppermute | solution.py:110
  85.6 9.6 %copy-start.3 = (f32[128,128]{1,0:T(8,128)}, f32[128,128]{1,0:T(8,128)S(1)}, u32[]{:S(2)}) copy-start(f32[128,128]{1,0:T(8,128)S(1)} %broadcast_select_fusion.rest_0_) | copy-start | bytes 196612
  85.6 5.9 %collective-permute-start.34 = (f32[128,128]{1,0:T(8,128)S(1)}, f32[128,128]{1,0:T(8,128)S(1)}, u32[]{:S(2)}, u32[]{:S(2)}) collective-permute-start(f32[128,128]{1,0:T(8,128)S(1)} %broadcast_select_fusion.rest_0_), channel_id=1, source_target_pairs={{0,12},{1,13},{2,14},{3,15},{4,8},{5,9},{6,10},{7,11},{8,4},{9,5},... | collective-permute-start | bytes 196616 | tf_op jit(solution)/shard_map/ppermute | solution.py:110
  85.7 7.5 %collective-permute-start.32 = (f32[128,128]{1,0:T(8,128)S(1)}, f32[128,128]{1,0:T(8,128)S(1)}, u32[]{:S(2)}, u32[]{:S(2)}) collective-permute-start(f32[128,128]{1,0:T(8,128)S(1)} %broadcast_select_fusion.rest_0_), channel_id=1, source_target_pairs={{0,8},{1,9},{2,10},{3,11},{4,12},{5,13},{6,14},{7,15},{8,0},{9,1},... | collective-permute-start | bytes 196616 | tf_op jit(solution)/shard_map/ppermute | solution.py:110
  87.1 6.2 %collective-permute-start.30 = (f32[128,128]{1,0:T(8,128)S(1)}, f32[128,128]{1,0:T(8,128)S(1)}, u32[]{:S(2)}, u32[]{:S(2)}) collective-permute-start(f32[128,128]{1,0:T(8,128)S(1)} %broadcast_select_fusion.rest_0_), channel_id=1, source_target_pairs={{0,4},{1,5},{2,6},{3,7},{4,0},{5,1},{6,2},{7,3},{8,12},{9,13},{10,... | collective-permute-start | bytes 196616 | tf_op jit(solution)/shard_map/ppermute | solution.py:110
  88.3 5.9 %collective-permute-start.29 = (f32[128,128]{1,0:T(8,128)S(1)}, f32[128,128]{1,0:T(8,128)S(1)}, u32[]{:S(2)}, u32[]{:S(2)}) collective-permute-start(f32[128,128]{1,0:T(8,128)S(1)} %broadcast_select_fusion.rest_0_), channel_id=1, source_target_pairs={{0,2},{1,3},{2,0},{3,1},{4,6},{5,7},{6,4},{7,5},{8,10},{9,11},{10,... | collective-permute-start | bytes 196616 | tf_op jit(solution)/shard_map/ppermute | solution.py:110
  91.5 3.7 %copy-start.11 = (f32[128,128]{1,0:T(8,128)}, f32[128,128]{1,0:T(8,128)S(1)}, u32[]{:S(2)}) copy-start(f32[128,128]{1,0:T(8,128)S(1)} %collective-permute-done.34.rest_6_) | copy-start | bytes 196612
  91.5 2.8 %collective-permute-start.35 = (f32[128,128]{1,0:T(8,128)S(1)}, f32[128,128]{1,0:T(8,128)S(1)}, u32[]{:S(2)}, u32[]{:S(2)}) collective-permute-start(f32[128,128]{1,0:T(8,128)S(1)} %collective-permute-done.34.rest_6_), channel_id=1, source_target_pairs={{0,2},{1,3},{2,0},{3,1},{4,6},{5,7},{6,4},{7,5},{8,10},{9,11},{10,... | collective-permute-start | bytes 196616 | tf_op jit(solution)/shard_map/ppermute | solution.py:110
  93.2 1.3 %collective-permute-start.33 = (f32[128,128]{1,0:T(8,128)S(1)}, f32[128,128]{1,0:T(8,128)S(1)}, u32[]{:S(2)}, u32[]{:S(2)}) collective-permute-start(f32[128,128]{1,0:T(8,128)S(1)} %collective-permute-done.32.rest_4_), channel_id=1, source_target_pairs={{0,2},{1,3},{2,0},{3,1},{4,6},{5,7},{6,4},{7,5},{8,10},{9,11},{10,... | collective-permute-start | bytes 196616 | tf_op jit(solution)/shard_map/ppermute | solution.py:110
  93.2 1.9 %collective-permute-start.31 = (f32[128,128]{1,0:T(8,128)S(1)}, f32[128,128]{1,0:T(8,128)S(1)}, u32[]{:S(2)}, u32[]{:S(2)}) collective-permute-start(f32[128,128]{1,0:T(8,128)S(1)} %collective-permute-done.30.rest_2_), channel_id=1, source_target_pairs={{0,2},{1,3},{2,0},{3,1},{4,6},{5,7},{6,4},{7,5},{8,10},{9,11},{10,... | collective-permute-start | bytes 196616 | tf_op jit(solution)/shard_map/ppermute | solution.py:110
  (20 other events, 21.0 us)

commit v2 on v1

--- a/solution.py
+++ b/solution.py
@@ -10,6 +10,7 @@
 STEP_SIZE = 0.2
 BF16 = jnp.bfloat16
 F32 = jnp.float32
+VMEM_BYTES = 12 * 2**20
 
 
 def split(x):
@@ -29,7 +30,7 @@
     strength = coup * coup
     for s in range(rows_dev):
         x = cur[s]
-        g = g_ref[pl.ds(s, n, stride=rows_dev), :]
+        g = g_ref[pl.ds(section * rows_dev * n + s, n, stride=rows_dev), :]
         active = active_ref[pl.ds(section * rows_dev + s, 1), :]
         u = strength * x * g
         less = -(u * x)
@@ -98,6 +99,7 @@
         in_specs=[pl.BlockSpec(memory_space=pltpu.SMEM)] * smem + [pl.BlockSpec(memory_space=pltpu.VMEM)] * vmem,
         out_specs=jax.tree.map(lambda _: pl.BlockSpec(memory_space=pltpu.VMEM), outs),
         scratch_shapes=scratch,
+        compiler_params=pltpu.CompilerParams(vmem_limit_bytes=VMEM_BYTES),
         name=name,
     )
 
@@ -145,19 +147,20 @@
         order = lambda own_row, k: k
     shape = jax.ShapeDtypeStruct
     cur_shape, part_shape = shape((rows_dev, n, n), F32), shape((n, n), F32)
+    greater = greater_rows.reshape(steps * rows_dev * n, n)
     scratch = [pltpu.VMEM((n, 2 * rows_dev * n), BF16)] * 2
     current, wide, active, part = call(
         functools.partial(first_kernel, rows_dev, n, steps),
         (cur_shape, shape((2 * rows_dev * n, 2 * n), BF16), shape((steps * rows_dev, n), F32), part_shape),
         scratch, 2, 6, "first_step",
     )(step_index, cutoff, lesser.reshape(flat), advanced.reshape(flat), first_row.reshape(flat),
-      greater_rows[0].reshape(flat), coupling, hamiltonian)
+      greater, coupling, hamiltonian)
     for section in range(1, steps):
         pieces = exchange(part)
         current, part = call(
             functools.partial(next_kernel, section, rows_dev, n, order),
             (cur_shape, part_shape), scratch, 0, 6 + rows_dev, "next_step",
-        )(current, greater_rows[section].reshape(flat), coupling, hamiltonian, active, wide, *pieces)
+        )(current, greater, coupling, hamiltonian, active, wide, *pieces)
     pieces = exchange(part)
     final = call(
         functools.partial(last_kernel, rows_dev, n, order), shape(flat, F32), [], 0, 1 + rows_dev, "last_step",

time: 98.9 us -> 87.3 us (0.88)
  Pallas kernels: 14.6 us -> 4.16 us
  other arithmetic: 3.44 us -> 0.08 us
  local copies, waits for them, and re-layouts: 5.29 us -> 8.22 us
    pallas_call x3, Pallas kernels: 9.1 us -> 2.23 us  [on_device(): call(functools.partial(next_kernel, section, rows_dev, n, order), (cur_sh...]
    unnamed x64 -> x22, local copies, waits for them, and re-layouts: 2.4 us -> 8.22 us
    add x4, other arithmetic: 3.41 us -> 0.04 us  [exchange_pairs(): part + moved(part, [(at(h, c), at(h, 1 - c)) for h in range(hist) for c i...]
    another operation x1 -> x0, local copies, waits for them, and re-layouts: 2.88 us -> none  [on_device(): greater_rows[section].reshape(flat)]
    pallas_call x1, Pallas kernels: 3.34 us -> 0.95 us  [on_device(): call(functools.partial(first_kernel, rows_dev, n, steps), (cur_shape, sha...]
    pallas_call x1, Pallas kernels: 2.17 us -> 0.98 us  [on_device(): call(functools.partial(last_kernel, rows_dev, n, order), shape(flat, F32)...]
where the time goes in v2:
time: 87.3 us; the launch traced here: 86.3 us
  starting transfers between devices  42.5 us (49%)
  waiting for transfers between devices  29.9 us (34%)
  local copies, waits for them, and re-layouts  8.22 us (9%)
  Pallas kernels  4.16 us (5%)
  between operations  1.46 us (2%)
    ppermute x36, starting transfers between devices, moved(): return lax.ppermute(x, ('hist', 'col'), pairs)  42.5 us
    ppermute x36, waiting for transfers between devices, moved(): return lax.ppermute(x, ('hist', 'col'), pairs)  29.9 us
    unnamed x22, local copies, waits for them, and re-layouts  8.22 us
    pallas_call x3, Pallas kernels, on_device(): call(functools.partial(next_kernel, section, rows_dev, n, order), (cur_sh...  2.23 us
  transfers between devices with their start and end apart: 36, of which 14 were waited for; matrix products, arithmetic and copies ran while one was open for 0% of the time, Pallas kernels for 0%

profile of v2, /device:TPU:25, one launch (start us, length us, event | category | flops | bytes accessed | tf_op | source)
XLA Modules:
  0.0 86.3 jit_solution(6536767793855213357)
XLA Ops:
  1.3 1.6 %copy-done = f32[4,128,8,128]{3,2,1,0:T(8,128)S(1)} copy-done((f32[4,128,8,128]{3,2,1,0:T(8,128)S(1)}, f32[4,128,8,128]{3,2,1,0:T(8,128)}, u32[]{:S(2)}) %copy-start) | copy-done | bytes 2097176
  2.9 0.8 copy-done.2
  3.7 0.8 copy-done.4
  4.6 1.0 %copy-done.8 = f32[8,128,1,128]{3,2,1,0:T(1,128)S(1)} copy-done((f32[8,128,1,128]{3,2,1,0:T(1,128)S(1)}, f32[8,128,1,128]{3,2,1,0:T(1,128)}, u32[]{:S(2)}) %copy-start.8) | copy-done | bytes 524312
  5.6 1.0 %copy-done.9 = f32[8,128,1,128]{3,2,1,0:T(1,128)S(1)} copy-done((f32[8,128,1,128]{3,2,1,0:T(1,128)S(1)}, f32[8,128,1,128]{3,2,1,0:T(1,128)}, u32[]{:S(2)}) %copy-start.9) | copy-done | bytes 524312
  6.7 1.0 %copy-done.10 = f32[128,8,128]{2,1,0:T(8,128)S(1)} copy-done((f32[128,8,128]{2,1,0:T(8,128)S(1)}, f32[128,8,128]{2,1,0:T(8,128)}, u32[]{:S(2)}) %copy-start.10) | copy-done | bytes 524312
  7.7 0.9 %first_step.1 = (f32[8,128,128]{2,1,0:T(8,128)S(1)}, bf16[2048,256]{1,0:T(8,128)(2,1)S(1)}, f32[32,128]{1,0:T(8,128)S(1)}, f32[128,128]{1,0:T(8,128)S(1)}) custom-call(s32[1]{0:T(128)S(6)} %copy.10.step_ref, s32[1]{0:T(128)S(6)} %copy.9.cutoff_ref, f32[1024,128]{1,0:T(8,128)S(1)} %bitcast.9, f32[1024,128]{1,0:T(8,128)S(1)} %bitcast.10, ...), custom_call_target="tpu_custom_call" | custom-call | tf_op jit(solution)/shard_map/first_step/pallas_call | solution.py:152
  8.7 0.8 copy-done.6
  9.5 1.2 %collective-permute-start = (f32[128,128]{1,0:T(8,128)S(1)}, f32[128,128]{1,0:T(8,128)S(1)}, u32[]{:S(2)}, u32[]{:S(2)}) collective-permute-start(f32[128,128]{1,0:T(8,128)S(1)} %get-tuple-element.18), channel_id=1, source_target_pairs={{0,1},{1,0},{2,3},{3,2},{4,5},{5,4},{6,7},{7,6},{8,9},{9,8},{10,11... | collective-permute-start | bytes 196616 | tf_op jit(solution)/shard_map/ppermute | solution.py:112
  10.7 1.9 %collective-permute-done = f32[128,128]{1,0:T(8,128)S(1)} collective-permute-done((f32[128,128]{1,0:T(8,128)S(1)}, f32[128,128]{1,0:T(8,128)S(1)}, u32[]{:S(2)}, u32[]{:S(2)}) %collective-permute-start) | collective-permute-done | bytes 65568 | tf_op jit(solution)/shard_map/ppermute | solution.py:112
  12.7 4.5 %collective-permute-done.1 = f32[128,128]{1,0:T(8,128)S(1)} collective-permute-done((f32[128,128]{1,0:T(8,128)S(1)}, f32[128,128]{1,0:T(8,128)S(1)}, u32[]{:S(2)}, u32[]{:S(2)}) %collective-permute-start.1) | collective-permute-done | bytes 65568 | tf_op jit(solution)/shard_map/ppermute | solution.py:112
  17.9 1.8 %collective-permute-start.5 = (f32[128,128]{1,0:T(8,128)S(1)}, f32[128,128]{1,0:T(8,128)S(1)}, u32[]{:S(2)}, u32[]{:S(2)}) collective-permute-start(f32[128,128]{1,0:T(8,128)S(1)} %broadcast_select_fusion.3.rest_0_), channel_id=1, source_target_pairs={{0,8},{1,9},{2,10},{3,11},{4,12},{5,13},{6,14},{7,15},{8,0},{9,1},... | collective-permute-start | bytes 196616 | tf_op jit(solution)/shard_map/ppermute | solution.py:112
  20.0 3.8 %collective-permute-start.2 = (f32[128,128]{1,0:T(8,128)S(1)}, f32[128,128]{1,0:T(8,128)S(1)}, u32[]{:S(2)}, u32[]{:S(2)}) collective-permute-start(f32[128,128]{1,0:T(8,128)S(1)} %broadcast_select_fusion.3.rest_0_), channel_id=1, source_target_pairs={{0,2},{1,3},{2,0},{3,1},{4,6},{5,7},{6,4},{7,5},{8,10},{9,11},{10,... | collective-permute-start | bytes 196616 | tf_op jit(solution)/shard_map/ppermute | solution.py:112
  23.8 1.7 %collective-permute-start.8 = (f32[128,128]{1,0:T(8,128)S(1)}, f32[128,128]{1,0:T(8,128)S(1)}, u32[]{:S(2)}, u32[]{:S(2)}) collective-permute-start(f32[128,128]{1,0:T(8,128)S(1)} %collective-permute-done.7.rest_6_), channel_id=1, source_target_pairs={{0,2},{1,3},{2,0},{3,1},{4,6},{5,7},{6,4},{7,5},{8,10},{9,11},{10,... | collective-permute-start | bytes 196616 | tf_op jit(solution)/shard_map/ppermute | solution.py:112
  25.5 0.8 collective-permute-start.6
  26.2 1.3 %collective-permute-start.4 = (f32[128,128]{1,0:T(8,128)S(1)}, f32[128,128]{1,0:T(8,128)S(1)}, u32[]{:S(2)}, u32[]{:S(2)}) collective-permute-start(f32[128,128]{1,0:T(8,128)S(1)} %collective-permute-done.3.rest_2_), channel_id=1, source_target_pairs={{0,2},{1,3},{2,0},{3,1},{4,6},{5,7},{6,4},{7,5},{8,10},{9,11},{10,... | collective-permute-start | bytes 196616 | tf_op jit(solution)/shard_map/ppermute | solution.py:112
  27.6 0.9 %collective-permute-done.4.rest_3_ = f32[128,128]{1,0:T(8,128)S(1)} collective-permute-done((f32[128,128]{1,0:T(8,128)S(1)}, f32[128,128]{1,0:T(8,128)S(1)}, u32[]{:S(2)}, u32[]{:S(2)}) %collective-permute-start.4) | collective-permute-done | bytes 65568 | tf_op jit(solution)/shard_map/ppermute | solution.py:112
  28.5 1.0 %copy-done.7 = f32[8,128,128]{2,1,0:T(8,128)S(1)} copy-done((f32[8,128,128]{2,1,0:T(8,128)S(1)}, f32[8,128,128]{2,1,0:T(8,128)}, u32[]{:S(2)}) %copy-start.7) | copy-done | bytes 524312
  29.5 0.7 next_step.3
  30.3 1.3 %collective-permute-start.9 = (f32[128,128]{1,0:T(8,128)S(1)}, f32[128,128]{1,0:T(8,128)S(1)}, u32[]{:S(2)}, u32[]{:S(2)}) collective-permute-start(f32[128,128]{1,0:T(8,128)S(1)} %get-tuple-element.20), channel_id=1, source_target_pairs={{0,1},{1,0},{2,3},{3,2},{4,5},{5,4},{6,7},{7,6},{8,9},{9,8},{10,11... | collective-permute-start | bytes 196616 | tf_op jit(solution)/shard_map/ppermute | solution.py:112
  31.5 1.9 %collective-permute-done.9 = f32[128,128]{1,0:T(8,128)S(1)} collective-permute-done((f32[128,128]{1,0:T(8,128)S(1)}, f32[128,128]{1,0:T(8,128)S(1)}, u32[]{:S(2)}, u32[]{:S(2)}) %collective-permute-start.9) | collective-permute-done | bytes 65568 | tf_op jit(solution)/shard_map/ppermute | solution.py:112
  33.5 4.7 %collective-permute-done.10 = f32[128,128]{1,0:T(8,128)S(1)} collective-permute-done((f32[128,128]{1,0:T(8,128)S(1)}, f32[128,128]{1,0:T(8,128)S(1)}, u32[]{:S(2)}, u32[]{:S(2)}) %collective-permute-start.10) | collective-permute-done | bytes 65568 | tf_op jit(solution)/shard_map/ppermute | solution.py:112
  38.3 1.4 %collective-permute-start.14 = (f32[128,128]{1,0:T(8,128)S(1)}, f32[128,128]{1,0:T(8,128)S(1)}, u32[]{:S(2)}, u32[]{:S(2)}) collective-permute-start(f32[128,128]{1,0:T(8,128)S(1)} %broadcast_select_fusion.2.rest_0_), channel_id=1, source_target_pairs={{0,8},{1,9},{2,10},{3,11},{4,12},{5,13},{6,14},{7,15},{8,0},{9,1},... | collective-permute-start | bytes 196616 | tf_op jit(solution)/shard_map/ppermute | solution.py:112
  39.7 1.2 %collective-permute-start.12 = (f32[128,128]{1,0:T(8,128)S(1)}, f32[128,128]{1,0:T(8,128)S(1)}, u32[]{:S(2)}, u32[]{:S(2)}) collective-permute-start(f32[128,128]{1,0:T(8,128)S(1)} %broadcast_select_fusion.2.rest_0_), channel_id=1, source_target_pairs={{0,4},{1,5},{2,6},{3,7},{4,0},{5,1},{6,2},{7,3},{8,12},{9,13},{10,... | collective-permute-start | bytes 196616 | tf_op jit(solution)/shard_map/ppermute | solution.py:112
  41.0 3.2 %collective-permute-start.11 = (f32[128,128]{1,0:T(8,128)S(1)}, f32[128,128]{1,0:T(8,128)S(1)}, u32[]{:S(2)}, u32[]{:S(2)}) collective-permute-start(f32[128,128]{1,0:T(8,128)S(1)} %broadcast_select_fusion.2.rest_0_), channel_id=1, source_target_pairs={{0,2},{1,3},{2,0},{3,1},{4,6},{5,7},{6,4},{7,5},{8,10},{9,11},{10,... | collective-permute-start | bytes 196616 | tf_op jit(solution)/shard_map/ppermute | solution.py:112
  44.1 1.7 %collective-permute-start.17 = (f32[128,128]{1,0:T(8,128)S(1)}, f32[128,128]{1,0:T(8,128)S(1)}, u32[]{:S(2)}, u32[]{:S(2)}) collective-permute-start(f32[128,128]{1,0:T(8,128)S(1)} %collective-permute-done.16.rest_6_), channel_id=1, source_target_pairs={{0,2},{1,3},{2,0},{3,1},{4,6},{5,7},{6,4},{7,5},{8,10},{9,11},{10,... | collective-permute-start | bytes 196616 | tf_op jit(solution)/shard_map/ppermute | solution.py:112
  45.8 1.1 %collective-permute-start.13 = (f32[128,128]{1,0:T(8,128)S(1)}, f32[128,128]{1,0:T(8,128)S(1)}, u32[]{:S(2)}, u32[]{:S(2)}) collective-permute-start(f32[128,128]{1,0:T(8,128)S(1)} %collective-permute-done.12.rest_2_), channel_id=1, source_target_pairs={{0,2},{1,3},{2,0},{3,1},{4,6},{5,7},{6,4},{7,5},{8,10},{9,11},{10,... | collective-permute-start | bytes 196616 | tf_op jit(solution)/shard_map/ppermute | solution.py:112
  47.8 0.7 next_step.4
  48.5 1.3 %collective-permute-start.18 = (f32[128,128]{1,0:T(8,128)S(1)}, f32[128,128]{1,0:T(8,128)S(1)}, u32[]{:S(2)}, u32[]{:S(2)}) collective-permute-start(f32[128,128]{1,0:T(8,128)S(1)} %get-tuple-element.22), channel_id=1, source_target_pairs={{0,1},{1,0},{2,3},{3,2},{4,5},{5,4},{6,7},{7,6},{8,9},{9,8},{10,11... | collective-permute-start | bytes 196616 | tf_op jit(solution)/shard_map/ppermute | solution.py:112
  49.8 1.9 %collective-permute-done.18 = f32[128,128]{1,0:T(8,128)S(1)} collective-permute-done((f32[128,128]{1,0:T(8,128)S(1)}, f32[128,128]{1,0:T(8,128)S(1)}, u32[]{:S(2)}, u32[]{:S(2)}) %collective-permute-start.18) | collective-permute-done | bytes 65568 | tf_op jit(solution)/shard_map/ppermute | solution.py:112
  51.8 4.7 %collective-permute-done.19 = f32[128,128]{1,0:T(8,128)S(1)} collective-permute-done((f32[128,128]{1,0:T(8,128)S(1)}, f32[128,128]{1,0:T(8,128)S(1)}, u32[]{:S(2)}, u32[]{:S(2)}) %collective-permute-start.19) | collective-permute-done | bytes 65568 | tf_op jit(solution)/shard_map/ppermute | solution.py:112
  56.5 0.9 %collective-permute-start.25 = (f32[128,128]{1,0:T(8,128)S(1)}, f32[128,128]{1,0:T(8,128)S(1)}, u32[]{:S(2)}, u32[]{:S(2)}) collective-permute-start(f32[128,128]{1,0:T(8,128)S(1)} %broadcast_select_fusion.1.rest_0_), channel_id=1, source_target_pairs={{0,12},{1,13},{2,14},{3,15},{4,8},{5,9},{6,10},{7,11},{8,4},{9,5},... | collective-permute-start | bytes 196616 | tf_op jit(solution)/shard_map/ppermute | solution.py:112
  57.5 1.6 %collective-permute-start.23 = (f32[128,128]{1,0:T(8,128)S(1)}, f32[128,128]{1,0:T(8,128)S(1)}, u32[]{:S(2)}, u32[]{:S(2)}) collective-permute-start(f32[128,128]{1,0:T(8,128)S(1)} %broadcast_select_fusion.1.rest_0_), channel_id=1, source_target_pairs={{0,8},{1,9},{2,10},{3,11},{4,12},{5,13},{6,14},{7,15},{8,0},{9,1},... | collective-permute-start | bytes 196616 | tf_op jit(solution)/shard_map/ppermute | solution.py:112
  59.2 3.2 %collective-permute-start.20 = (f32[128,128]{1,0:T(8,128)S(1)}, f32[128,128]{1,0:T(8,128)S(1)}, u32[]{:S(2)}, u32[]{:S(2)}) collective-permute-start(f32[128,128]{1,0:T(8,128)S(1)} %broadcast_select_fusion.1.rest_0_), channel_id=1, source_target_pairs={{0,2},{1,3},{2,0},{3,1},{4,6},{5,7},{6,4},{7,5},{8,10},{9,11},{10,... | collective-permute-start | bytes 196616 | tf_op jit(solution)/shard_map/ppermute | solution.py:112
  62.4 1.7 %collective-permute-start.26 = (f32[128,128]{1,0:T(8,128)S(1)}, f32[128,128]{1,0:T(8,128)S(1)}, u32[]{:S(2)}, u32[]{:S(2)}) collective-permute-start(f32[128,128]{1,0:T(8,128)S(1)} %collective-permute-done.25.rest_6_), channel_id=1, source_target_pairs={{0,2},{1,3},{2,0},{3,1},{4,6},{5,7},{6,4},{7,5},{8,10},{9,11},{10,... | collective-permute-start | bytes 196616 | tf_op jit(solution)/shard_map/ppermute | solution.py:112
  64.1 0.8 collective-permute-start.24
  64.9 1.3 %collective-permute-start.22 = (f32[128,128]{1,0:T(8,128)S(1)}, f32[128,128]{1,0:T(8,128)S(1)}, u32[]{:S(2)}, u32[]{:S(2)}) collective-permute-start(f32[128,128]{1,0:T(8,128)S(1)} %collective-permute-done.21.rest_2_), channel_id=1, source_target_pairs={{0,2},{1,3},{2,0},{3,1},{4,6},{5,7},{6,4},{7,5},{8,10},{9,11},{10,... | collective-permute-start | bytes 196616 | tf_op jit(solution)/shard_map/ppermute | solution.py:112
  66.2 0.9 %collective-permute-done.22.rest_3_ = f32[128,128]{1,0:T(8,128)S(1)} collective-permute-done((f32[128,128]{1,0:T(8,128)S(1)}, f32[128,128]{1,0:T(8,128)S(1)}, u32[]{:S(2)}, u32[]{:S(2)}) %collective-permute-start.22) | collective-permute-done | bytes 65568 | tf_op jit(solution)/shard_map/ppermute | solution.py:112
  67.1 0.7 next_step.5
  67.8 1.3 %collective-permute-start.27 = (f32[128,128]{1,0:T(8,128)S(1)}, f32[128,128]{1,0:T(8,128)S(1)}, u32[]{:S(2)}, u32[]{:S(2)}) collective-permute-start(f32[128,128]{1,0:T(8,128)S(1)} %get-tuple-element.24), channel_id=1, source_target_pairs={{0,1},{1,0},{2,3},{3,2},{4,5},{5,4},{6,7},{7,6},{8,9},{9,8},{10,11... | collective-permute-start | bytes 196616 | tf_op jit(solution)/shard_map/ppermute | solution.py:112
  69.1 1.9 %collective-permute-done.27 = f32[128,128]{1,0:T(8,128)S(1)} collective-permute-done((f32[128,128]{1,0:T(8,128)S(1)}, f32[128,128]{1,0:T(8,128)S(1)}, u32[]{:S(2)}, u32[]{:S(2)}) %collective-permute-start.27) | collective-permute-done | bytes 65568 | tf_op jit(solution)/shard_map/ppermute | solution.py:112
  71.1 4.7 %collective-permute-done.28 = f32[128,128]{1,0:T(8,128)S(1)} collective-permute-done((f32[128,128]{1,0:T(8,128)S(1)}, f32[128,128]{1,0:T(8,128)S(1)}, u32[]{:S(2)}, u32[]{:S(2)}) %collective-permute-start.28) | collective-permute-done | bytes 65568 | tf_op jit(solution)/shard_map/ppermute | solution.py:112
  75.9 1.4 %collective-permute-start.32 = (f32[128,128]{1,0:T(8,128)S(1)}, f32[128,128]{1,0:T(8,128)S(1)}, u32[]{:S(2)}, u32[]{:S(2)}) collective-permute-start(f32[128,128]{1,0:T(8,128)S(1)} %broadcast_select_fusion.rest_0_), channel_id=1, source_target_pairs={{0,8},{1,9},{2,10},{3,11},{4,12},{5,13},{6,14},{7,15},{8,0},{9,1},... | collective-permute-start | bytes 196616 | tf_op jit(solution)/shard_map/ppermute | solution.py:112
  77.3 1.2 %collective-permute-start.30 = (f32[128,128]{1,0:T(8,128)S(1)}, f32[128,128]{1,0:T(8,128)S(1)}, u32[]{:S(2)}, u32[]{:S(2)}) collective-permute-start(f32[128,128]{1,0:T(8,128)S(1)} %broadcast_select_fusion.rest_0_), channel_id=1, source_target_pairs={{0,4},{1,5},{2,6},{3,7},{4,0},{5,1},{6,2},{7,3},{8,12},{9,13},{10,... | collective-permute-start | bytes 196616 | tf_op jit(solution)/shard_map/ppermute | solution.py:112
  78.5 3.2 %collective-permute-start.29 = (f32[128,128]{1,0:T(8,128)S(1)}, f32[128,128]{1,0:T(8,128)S(1)}, u32[]{:S(2)}, u32[]{:S(2)}) collective-permute-start(f32[128,128]{1,0:T(8,128)S(1)} %broadcast_select_fusion.rest_0_), channel_id=1, source_target_pairs={{0,2},{1,3},{2,0},{3,1},{4,6},{5,7},{6,4},{7,5},{8,10},{9,11},{10,... | collective-permute-start | bytes 196616 | tf_op jit(solution)/shard_map/ppermute | solution.py:112
  81.7 1.7 %collective-permute-start.35 = (f32[128,128]{1,0:T(8,128)S(1)}, f32[128,128]{1,0:T(8,128)S(1)}, u32[]{:S(2)}, u32[]{:S(2)}) collective-permute-start(f32[128,128]{1,0:T(8,128)S(1)} %collective-permute-done.34.rest_6_), channel_id=1, source_target_pairs={{0,2},{1,3},{2,0},{3,1},{4,6},{5,7},{6,4},{7,5},{8,10},{9,11},{10,... | collective-permute-start | bytes 196616 | tf_op jit(solution)/shard_map/ppermute | solution.py:112
  83.4 1.1 %collective-permute-start.31 = (f32[128,128]{1,0:T(8,128)S(1)}, f32[128,128]{1,0:T(8,128)S(1)}, u32[]{:S(2)}, u32[]{:S(2)}) collective-permute-start(f32[128,128]{1,0:T(8,128)S(1)} %collective-permute-done.30.rest_2_), channel_id=1, source_target_pairs={{0,2},{1,3},{2,0},{3,1},{4,6},{5,7},{6,4},{7,5},{8,10},{9,11},{10,... | collective-permute-start | bytes 196616 | tf_op jit(solution)/shard_map/ppermute | solution.py:112
  85.4 1.0 %last_step.1 = f32[1024,128]{1,0:T(8,128)} custom-call(f32[8,128,128]{2,1,0:T(8,128)S(1)} %get-tuple-element.23.prev_ref, f32[128,128]{1,0:T(8,128)S(1)} %broadcast_select_fusion.rest_0_, f32[128,128]{1,0:T(8,128)S(1)} %collective-permute-done.29.rest_1_, f32[128,128]{1,0:T(8,128)S(1)} %collective-permute-done.30.rest_2_, ...), custom_call_target="tpu_custom_call" | custom-call | tf_op jit(solution)/shard_map/last_step/pallas_call | solution.py:165
  (59 shorter events, 3.6 us)
Async XLA Ops:
  1.3 1.6 %copy-start = (f32[4,128,8,128]{3,2,1,0:T(8,128)S(1)}, f32[4,128,8,128]{3,2,1,0:T(8,128)}, u32[]{:S(2)}) copy-start(f32[4,128,8,128]{3,2,1,0:T(8,128)} %param.11) | copy-start | bytes 6291460
  2.9 0.8 copy-start.2
  3.7 0.8 copy-start.4
  4.6 1.0 %copy-start.8 = (f32[8,128,1,128]{3,2,1,0:T(1,128)S(1)}, f32[8,128,1,128]{3,2,1,0:T(1,128)}, u32[]{:S(2)}) copy-start(f32[8,128,1,128]{3,2,1,0:T(1,128)} %param.8) | copy-start | bytes 1572868
  5.6 1.0 %copy-start.9 = (f32[8,128,1,128]{3,2,1,0:T(1,128)S(1)}, f32[8,128,1,128]{3,2,1,0:T(1,128)}, u32[]{:S(2)}) copy-start(f32[8,128,1,128]{3,2,1,0:T(1,128)} %param.9) | copy-start | bytes 1572868
  6.7 1.0 %copy-start.10 = (f32[128,8,128]{2,1,0:T(8,128)S(1)}, f32[128,8,128]{2,1,0:T(8,128)}, u32[]{:S(2)}) copy-start(f32[128,8,128]{2,1,0:T(8,128)} %param.10) | copy-start | bytes 1572868
  7.7 20.8 %copy-start.1 = (f32[4,128,8,128]{3,2,1,0:T(8,128)S(1)}, f32[4,128,8,128]{3,2,1,0:T(8,128)}, u32[]{:S(2)}) copy-start(f32[4,128,8,128]{3,2,1,0:T(8,128)} %param.11) | copy-start | bytes 6291460
  7.7 20.8 %copy-start.3 = (f32[128,128]{1,0:T(8,128)S(1)}, f32[128,128]{1,0:T(8,128)}, u32[]{:S(2)}) copy-start(f32[128,128]{1,0:T(8,128)} %coup_ref.7) | copy-start | bytes 196612
  7.7 20.8 %copy-start.5 = (f32[128,128]{1,0:T(8,128)S(1)}, f32[128,128]{1,0:T(8,128)}, u32[]{:S(2)}) copy-start(f32[128,128]{1,0:T(8,128)} %ham_ref.7) | copy-start | bytes 196612
  8.7 0.8 copy-start.6
  9.5 3.1 %collective-permute-start = (f32[128,128]{1,0:T(8,128)S(1)}, f32[128,128]{1,0:T(8,128)S(1)}, u32[]{:S(2)}, u32[]{:S(2)}) collective-permute-start(f32[128,128]{1,0:T(8,128)S(1)} %get-tuple-element.18), channel_id=1, source_target_pairs={{0,1},{1,0},{2,3},{3,2},{4,5},{5,4},{6,7},{7,6},{8,9},{9,8},{10,11... | collective-permute-start | bytes 196616 | tf_op jit(solution)/shard_map/ppermute | solution.py:112
  12.6 4.7 %collective-permute-start.1 = (f32[128,128]{1,0:T(8,128)S(1)}, f32[128,128]{1,0:T(8,128)S(1)}, u32[]{:S(2)}, u32[]{:S(2)}) collective-permute-start(f32[128,128]{1,0:T(8,128)S(1)} %add.13), channel_id=1, source_target_pairs={{0,16},{1,17},{2,18},{3,19},{4,20},{5,21},{6,22},{7,23},{8,24},{9,... | collective-permute-start | bytes 196616 | tf_op jit(solution)/shard_map/ppermute | solution.py:112
  17.3 6.5 %collective-permute-start.7 = (f32[128,128]{1,0:T(8,128)S(1)}, f32[128,128]{1,0:T(8,128)S(1)}, u32[]{:S(2)}, u32[]{:S(2)}) collective-permute-start(f32[128,128]{1,0:T(8,128)S(1)} %broadcast_select_fusion.3.rest_0_), channel_id=1, source_target_pairs={{0,12},{1,13},{2,14},{3,15},{4,8},{5,9},{6,10},{7,11},{8,4},{9,5},... | collective-permute-start | bytes 196616 | tf_op jit(solution)/shard_map/ppermute | solution.py:112
  17.9 7.5 %collective-permute-start.5 = (f32[128,128]{1,0:T(8,128)S(1)}, f32[128,128]{1,0:T(8,128)S(1)}, u32[]{:S(2)}, u32[]{:S(2)}) collective-permute-start(f32[128,128]{1,0:T(8,128)S(1)} %broadcast_select_fusion.3.rest_0_), channel_id=1, source_target_pairs={{0,8},{1,9},{2,10},{3,11},{4,12},{5,13},{6,14},{7,15},{8,0},{9,1},... | collective-permute-start | bytes 196616 | tf_op jit(solution)/shard_map/ppermute | solution.py:112
  19.8 6.5 %collective-permute-start.3 = (f32[128,128]{1,0:T(8,128)S(1)}, f32[128,128]{1,0:T(8,128)S(1)}, u32[]{:S(2)}, u32[]{:S(2)}) collective-permute-start(f32[128,128]{1,0:T(8,128)S(1)} %broadcast_select_fusion.3.rest_0_), channel_id=1, source_target_pairs={{0,4},{1,5},{2,6},{3,7},{4,0},{5,1},{6,2},{7,3},{8,12},{9,13},{10,... | collective-permute-start | bytes 196616 | tf_op jit(solution)/shard_map/ppermute | solution.py:112
  20.0 7.6 %collective-permute-start.2 = (f32[128,128]{1,0:T(8,128)S(1)}, f32[128,128]{1,0:T(8,128)S(1)}, u32[]{:S(2)}, u32[]{:S(2)}) collective-permute-start(f32[128,128]{1,0:T(8,128)S(1)} %broadcast_select_fusion.3.rest_0_), channel_id=1, source_target_pairs={{0,2},{1,3},{2,0},{3,1},{4,6},{5,7},{6,4},{7,5},{8,10},{9,11},{10,... | collective-permute-start | bytes 196616 | tf_op jit(solution)/shard_map/ppermute | solution.py:112
  23.8 3.8 %collective-permute-start.8 = (f32[128,128]{1,0:T(8,128)S(1)}, f32[128,128]{1,0:T(8,128)S(1)}, u32[]{:S(2)}, u32[]{:S(2)}) collective-permute-start(f32[128,128]{1,0:T(8,128)S(1)} %collective-permute-done.7.rest_6_), channel_id=1, source_target_pairs={{0,2},{1,3},{2,0},{3,1},{4,6},{5,7},{6,4},{7,5},{8,10},{9,11},{10,... | collective-permute-start | bytes 196616 | tf_op jit(solution)/shard_map/ppermute | solution.py:112
  25.5 2.1 %collective-permute-start.6 = (f32[128,128]{1,0:T(8,128)S(1)}, f32[128,128]{1,0:T(8,128)S(1)}, u32[]{:S(2)}, u32[]{:S(2)}) collective-permute-start(f32[128,128]{1,0:T(8,128)S(1)} %collective-permute-done.5.rest_4_), channel_id=1, source_target_pairs={{0,2},{1,3},{2,0},{3,1},{4,6},{5,7},{6,4},{7,5},{8,10},{9,11},{10,... | collective-permute-start | bytes 196616 | tf_op jit(solution)/shard_map/ppermute | solution.py:112
  26.2 2.2 %collective-permute-start.4 = (f32[128,128]{1,0:T(8,128)S(1)}, f32[128,128]{1,0:T(8,128)S(1)}, u32[]{:S(2)}, u32[]{:S(2)}) collective-permute-start(f32[128,128]{1,0:T(8,128)S(1)} %collective-permute-done.3.rest_2_), channel_id=1, source_target_pairs={{0,2},{1,3},{2,0},{3,1},{4,6},{5,7},{6,4},{7,5},{8,10},{9,11},{10,... | collective-permute-start | bytes 196616 | tf_op jit(solution)/shard_map/ppermute | solution.py:112
  28.5 1.0 %copy-start.7 = (f32[8,128,128]{2,1,0:T(8,128)S(1)}, f32[8,128,128]{2,1,0:T(8,128)}, u32[]{:S(2)}) copy-start(f32[8,128,128]{2,1,0:T(8,128)} %copy-done.6) | copy-start | bytes 1572868
  30.3 3.2 %collective-permute-start.9 = (f32[128,128]{1,0:T(8,128)S(1)}, f32[128,128]{1,0:T(8,128)S(1)}, u32[]{:S(2)}, u32[]{:S(2)}) collective-permute-start(f32[128,128]{1,0:T(8,128)S(1)} %get-tuple-element.20), channel_id=1, source_target_pairs={{0,1},{1,0},{2,3},{3,2},{4,5},{5,4},{6,7},{7,6},{8,9},{9,8},{10,11... | collective-permute-start | bytes 196616 | tf_op jit(solution)/shard_map/ppermute | solution.py:112
  33.5 4.8 %collective-permute-start.10 = (f32[128,128]{1,0:T(8,128)S(1)}, f32[128,128]{1,0:T(8,128)S(1)}, u32[]{:S(2)}, u32[]{:S(2)}) collective-permute-start(f32[128,128]{1,0:T(8,128)S(1)} %add.14), channel_id=1, source_target_pairs={{0,16},{1,17},{2,18},{3,19},{4,20},{5,21},{6,22},{7,23},{8,24},{9,... | collective-permute-start | bytes 196616 | tf_op jit(solution)/shard_map/ppermute | solution.py:112
  38.2 5.9 %collective-permute-start.16 = (f32[128,128]{1,0:T(8,128)S(1)}, f32[128,128]{1,0:T(8,128)S(1)}, u32[]{:S(2)}, u32[]{:S(2)}) collective-permute-start(f32[128,128]{1,0:T(8,128)S(1)} %broadcast_select_fusion.2.rest_0_), channel_id=1, source_target_pairs={{0,12},{1,13},{2,14},{3,15},{4,8},{5,9},{6,10},{7,11},{8,4},{9,5},... | collective-permute-start | bytes 196616 | tf_op jit(solution)/shard_map/ppermute | solution.py:112
  38.3 7.5 %collective-permute-start.14 = (f32[128,128]{1,0:T(8,128)S(1)}, f32[128,128]{1,0:T(8,128)S(1)}, u32[]{:S(2)}, u32[]{:S(2)}) collective-permute-start(f32[128,128]{1,0:T(8,128)S(1)} %broadcast_select_fusion.2.rest_0_), channel_id=1, source_target_pairs={{0,8},{1,9},{2,10},{3,11},{4,12},{5,13},{6,14},{7,15},{8,0},{9,1},... | collective-permute-start | bytes 196616 | tf_op jit(solution)/shard_map/ppermute | solution.py:112
  39.7 6.1 %collective-permute-start.12 = (f32[128,128]{1,0:T(8,128)S(1)}, f32[128,128]{1,0:T(8,128)S(1)}, u32[]{:S(2)}, u32[]{:S(2)}) collective-permute-start(f32[128,128]{1,0:T(8,128)S(1)} %broadcast_select_fusion.2.rest_0_), channel_id=1, source_target_pairs={{0,4},{1,5},{2,6},{3,7},{4,0},{5,1},{6,2},{7,3},{8,12},{9,13},{10,... | collective-permute-start | bytes 196616 | tf_op jit(solution)/shard_map/ppermute | solution.py:112
  41.0 5.9 %collective-permute-start.11 = (f32[128,128]{1,0:T(8,128)S(1)}, f32[128,128]{1,0:T(8,128)S(1)}, u32[]{:S(2)}, u32[]{:S(2)}) collective-permute-start(f32[128,128]{1,0:T(8,128)S(1)} %broadcast_select_fusion.2.rest_0_), channel_id=1, source_target_pairs={{0,2},{1,3},{2,0},{3,1},{4,6},{5,7},{6,4},{7,5},{8,10},{9,11},{10,... | collective-permute-start | bytes 196616 | tf_op jit(solution)/shard_map/ppermute | solution.py:112
  44.1 2.8 %collective-permute-start.17 = (f32[128,128]{1,0:T(8,128)S(1)}, f32[128,128]{1,0:T(8,128)S(1)}, u32[]{:S(2)}, u32[]{:S(2)}) collective-permute-start(f32[128,128]{1,0:T(8,128)S(1)} %collective-permute-done.16.rest_6_), channel_id=1, source_target_pairs={{0,2},{1,3},{2,0},{3,1},{4,6},{5,7},{6,4},{7,5},{8,10},{9,11},{10,... | collective-permute-start | bytes 196616 | tf_op jit(solution)/shard_map/ppermute | solution.py:112
  45.8 1.3 %collective-permute-start.15 = (f32[128,128]{1,0:T(8,128)S(1)}, f32[128,128]{1,0:T(8,128)S(1)}, u32[]{:S(2)}, u32[]{:S(2)}) collective-permute-start(f32[128,128]{1,0:T(8,128)S(1)} %collective-permute-done.14.rest_4_), channel_id=1, source_target_pairs={{0,2},{1,3},{2,0},{3,1},{4,6},{5,7},{6,4},{7,5},{8,10},{9,11},{10,... | collective-permute-start | bytes 196616 | tf_op jit(solution)/shard_map/ppermute | solution.py:112
  45.8 2.0 %collective-permute-start.13 = (f32[128,128]{1,0:T(8,128)S(1)}, f32[128,128]{1,0:T(8,128)S(1)}, u32[]{:S(2)}, u32[]{:S(2)}) collective-permute-start(f32[128,128]{1,0:T(8,128)S(1)} %collective-permute-done.12.rest_2_), channel_id=1, source_target_pairs={{0,2},{1,3},{2,0},{3,1},{4,6},{5,7},{6,4},{7,5},{8,10},{9,11},{10,... | collective-permute-start | bytes 196616 | tf_op jit(solution)/shard_map/ppermute | solution.py:112
  48.5 3.2 %collective-permute-start.18 = (f32[128,128]{1,0:T(8,128)S(1)}, f32[128,128]{1,0:T(8,128)S(1)}, u32[]{:S(2)}, u32[]{:S(2)}) collective-permute-start(f32[128,128]{1,0:T(8,128)S(1)} %get-tuple-element.22), channel_id=1, source_target_pairs={{0,1},{1,0},{2,3},{3,2},{4,5},{5,4},{6,7},{7,6},{8,9},{9,8},{10,11... | collective-permute-start | bytes 196616 | tf_op jit(solution)/shard_map/ppermute | solution.py:112
  51.7 4.8 %collective-permute-start.19 = (f32[128,128]{1,0:T(8,128)S(1)}, f32[128,128]{1,0:T(8,128)S(1)}, u32[]{:S(2)}, u32[]{:S(2)}) collective-permute-start(f32[128,128]{1,0:T(8,128)S(1)} %add.15), channel_id=1, source_target_pairs={{0,16},{1,17},{2,18},{3,19},{4,20},{5,21},{6,22},{7,23},{8,24},{9,... | collective-permute-start | bytes 196616 | tf_op jit(solution)/shard_map/ppermute | solution.py:112
  56.5 5.9 %collective-permute-start.25 = (f32[128,128]{1,0:T(8,128)S(1)}, f32[128,128]{1,0:T(8,128)S(1)}, u32[]{:S(2)}, u32[]{:S(2)}) collective-permute-start(f32[128,128]{1,0:T(8,128)S(1)} %broadcast_select_fusion.1.rest_0_), channel_id=1, source_target_pairs={{0,12},{1,13},{2,14},{3,15},{4,8},{5,9},{6,10},{7,11},{8,4},{9,5},... | collective-permute-start | bytes 196616 | tf_op jit(solution)/shard_map/ppermute | solution.py:112
  57.5 6.6 %collective-permute-start.23 = (f32[128,128]{1,0:T(8,128)S(1)}, f32[128,128]{1,0:T(8,128)S(1)}, u32[]{:S(2)}, u32[]{:S(2)}) collective-permute-start(f32[128,128]{1,0:T(8,128)S(1)} %broadcast_select_fusion.1.rest_0_), channel_id=1, source_target_pairs={{0,8},{1,9},{2,10},{3,11},{4,12},{5,13},{6,14},{7,15},{8,0},{9,1},... | collective-permute-start | bytes 196616 | tf_op jit(solution)/shard_map/ppermute | solution.py:112
  59.0 5.8 %collective-permute-start.21 = (f32[128,128]{1,0:T(8,128)S(1)}, f32[128,128]{1,0:T(8,128)S(1)}, u32[]{:S(2)}, u32[]{:S(2)}) collective-permute-start(f32[128,128]{1,0:T(8,128)S(1)} %broadcast_select_fusion.1.rest_0_), channel_id=1, source_target_pairs={{0,4},{1,5},{2,6},{3,7},{4,0},{5,1},{6,2},{7,3},{8,12},{9,13},{10,... | collective-permute-start | bytes 196616 | tf_op jit(solution)/shard_map/ppermute | solution.py:112
  59.2 6.9 %collective-permute-start.20 = (f32[128,128]{1,0:T(8,128)S(1)}, f32[128,128]{1,0:T(8,128)S(1)}, u32[]{:S(2)}, u32[]{:S(2)}) collective-permute-start(f32[128,128]{1,0:T(8,128)S(1)} %broadcast_select_fusion.1.rest_0_), channel_id=1, source_target_pairs={{0,2},{1,3},{2,0},{3,1},{4,6},{5,7},{6,4},{7,5},{8,10},{9,11},{10,... | collective-permute-start | bytes 196616 | tf_op jit(solution)/shard_map/ppermute | solution.py:112
  62.4 3.8 %collective-permute-start.26 = (f32[128,128]{1,0:T(8,128)S(1)}, f32[128,128]{1,0:T(8,128)S(1)}, u32[]{:S(2)}, u32[]{:S(2)}) collective-permute-start(f32[128,128]{1,0:T(8,128)S(1)} %collective-permute-done.25.rest_6_), channel_id=1, source_target_pairs={{0,2},{1,3},{2,0},{3,1},{4,6},{5,7},{6,4},{7,5},{8,10},{9,11},{10,... | collective-permute-start | bytes 196616 | tf_op jit(solution)/shard_map/ppermute | solution.py:112
  64.1 2.1 %collective-permute-start.24 = (f32[128,128]{1,0:T(8,128)S(1)}, f32[128,128]{1,0:T(8,128)S(1)}, u32[]{:S(2)}, u32[]{:S(2)}) collective-permute-start(f32[128,128]{1,0:T(8,128)S(1)} %collective-permute-done.23.rest_4_), channel_id=1, source_target_pairs={{0,2},{1,3},{2,0},{3,1},{4,6},{5,7},{6,4},{7,5},{8,10},{9,11},{10,... | collective-permute-start | bytes 196616 | tf_op jit(solution)/shard_map/ppermute | solution.py:112
  64.9 2.2 %collective-permute-start.22 = (f32[128,128]{1,0:T(8,128)S(1)}, f32[128,128]{1,0:T(8,128)S(1)}, u32[]{:S(2)}, u32[]{:S(2)}) collective-permute-start(f32[128,128]{1,0:T(8,128)S(1)} %collective-permute-done.21.rest_2_), channel_id=1, source_target_pairs={{0,2},{1,3},{2,0},{3,1},{4,6},{5,7},{6,4},{7,5},{8,10},{9,11},{10,... | collective-permute-start | bytes 196616 | tf_op jit(solution)/shard_map/ppermute | solution.py:112
  67.8 3.2 %collective-permute-start.27 = (f32[128,128]{1,0:T(8,128)S(1)}, f32[128,128]{1,0:T(8,128)S(1)}, u32[]{:S(2)}, u32[]{:S(2)}) collective-permute-start(f32[128,128]{1,0:T(8,128)S(1)} %get-tuple-element.24), channel_id=1, source_target_pairs={{0,1},{1,0},{2,3},{3,2},{4,5},{5,4},{6,7},{7,6},{8,9},{9,8},{10,11... | collective-permute-start | bytes 196616 | tf_op jit(solution)/shard_map/ppermute | solution.py:112
  71.0 4.8 %collective-permute-start.28 = (f32[128,128]{1,0:T(8,128)S(1)}, f32[128,128]{1,0:T(8,128)S(1)}, u32[]{:S(2)}, u32[]{:S(2)}) collective-permute-start(f32[128,128]{1,0:T(8,128)S(1)} %add.16), channel_id=1, source_target_pairs={{0,16},{1,17},{2,18},{3,19},{4,20},{5,21},{6,22},{7,23},{8,24},{9,... | collective-permute-start | bytes 196616 | tf_op jit(solution)/shard_map/ppermute | solution.py:112
  75.8 5.9 %collective-permute-start.34 = (f32[128,128]{1,0:T(8,128)S(1)}, f32[128,128]{1,0:T(8,128)S(1)}, u32[]{:S(2)}, u32[]{:S(2)}) collective-permute-start(f32[128,128]{1,0:T(8,128)S(1)} %broadcast_select_fusion.rest_0_), channel_id=1, source_target_pairs={{0,12},{1,13},{2,14},{3,15},{4,8},{5,9},{6,10},{7,11},{8,4},{9,5},... | collective-permute-start | bytes 196616 | tf_op jit(solution)/shard_map/ppermute | solution.py:112
  75.9 7.5 %collective-permute-start.32 = (f32[128,128]{1,0:T(8,128)S(1)}, f32[128,128]{1,0:T(8,128)S(1)}, u32[]{:S(2)}, u32[]{:S(2)}) collective-permute-start(f32[128,128]{1,0:T(8,128)S(1)} %broadcast_select_fusion.rest_0_), channel_id=1, source_target_pairs={{0,8},{1,9},{2,10},{3,11},{4,12},{5,13},{6,14},{7,15},{8,0},{9,1},... | collective-permute-start | bytes 196616 | tf_op jit(solution)/shard_map/ppermute | solution.py:112
  77.3 6.1 %collective-permute-start.30 = (f32[128,128]{1,0:T(8,128)S(1)}, f32[128,128]{1,0:T(8,128)S(1)}, u32[]{:S(2)}, u32[]{:S(2)}) collective-permute-start(f32[128,128]{1,0:T(8,128)S(1)} %broadcast_select_fusion.rest_0_), channel_id=1, source_target_pairs={{0,4},{1,5},{2,6},{3,7},{4,0},{5,1},{6,2},{7,3},{8,12},{9,13},{10,... | collective-permute-start | bytes 196616 | tf_op jit(solution)/shard_map/ppermute | solution.py:112
  78.5 5.9 %collective-permute-start.29 = (f32[128,128]{1,0:T(8,128)S(1)}, f32[128,128]{1,0:T(8,128)S(1)}, u32[]{:S(2)}, u32[]{:S(2)}) collective-permute-start(f32[128,128]{1,0:T(8,128)S(1)} %broadcast_select_fusion.rest_0_), channel_id=1, source_target_pairs={{0,2},{1,3},{2,0},{3,1},{4,6},{5,7},{6,4},{7,5},{8,10},{9,11},{10,... | collective-permute-start | bytes 196616 | tf_op jit(solution)/shard_map/ppermute | solution.py:112
  81.7 2.8 %collective-permute-start.35 = (f32[128,128]{1,0:T(8,128)S(1)}, f32[128,128]{1,0:T(8,128)S(1)}, u32[]{:S(2)}, u32[]{:S(2)}) collective-permute-start(f32[128,128]{1,0:T(8,128)S(1)} %collective-permute-done.34.rest_6_), channel_id=1, source_target_pairs={{0,2},{1,3},{2,0},{3,1},{4,6},{5,7},{6,4},{7,5},{8,10},{9,11},{10,... | collective-permute-start | bytes 196616 | tf_op jit(solution)/shard_map/ppermute | solution.py:112
  83.4 1.3 %collective-permute-start.33 = (f32[128,128]{1,0:T(8,128)S(1)}, f32[128,128]{1,0:T(8,128)S(1)}, u32[]{:S(2)}, u32[]{:S(2)}) collective-permute-start(f32[128,128]{1,0:T(8,128)S(1)} %collective-permute-done.32.rest_4_), channel_id=1, source_target_pairs={{0,2},{1,3},{2,0},{3,1},{4,6},{5,7},{6,4},{7,5},{8,10},{9,11},{10,... | collective-permute-start | bytes 196616 | tf_op jit(solution)/shard_map/ppermute | solution.py:112
  83.4 2.0 %collective-permute-start.31 = (f32[128,128]{1,0:T(8,128)S(1)}, f32[128,128]{1,0:T(8,128)S(1)}, u32[]{:S(2)}, u32[]{:S(2)}) collective-permute-start(f32[128,128]{1,0:T(8,128)S(1)} %collective-permute-done.30.rest_2_), channel_id=1, source_target_pairs={{0,2},{1,3},{2,0},{3,1},{4,6},{5,7},{6,4},{7,5},{8,10},{9,11},{10,... | collective-permute-start | bytes 196616 | tf_op jit(solution)/shard_map/ppermute | solution.py:112

commit v3 on v2

v3 whole, which is shorter than its diff:
```python
import functools

import jax
import jax.numpy as jnp
from jax import lax
from jax.experimental import pallas as pl
from jax.experimental.pallas import tpu as pltpu
from jax.sharding import PartitionSpec as P

STEP_SIZE = 0.2
BF16 = jnp.bfloat16
F32 = jnp.float32
VMEM_BYTES = 12 * 2**20
PARTS = 4


def split(x):
    high = x.astype(BF16)
    return high, (x - high.astype(F32)).astype(BF16)


def times_wide(high, low, wide):
    n = wide.shape[-1] // 2
    first = jnp.dot(high, wide, preferred_element_type=F32)
    second = jnp.dot(low, wide[:, :n], preferred_element_type=F32)
    return first[:, :n] + first[:, n:] + second


def advance(section, rows_dev, n, owner, own_row, cur, g_ref, active_ref, strength_ref, ham_ref, wide_ref, part_ref, high_ref, low_ref):
    strength = strength_ref[...]
    for s in range(rows_dev):
        x = cur[s]
        g = g_ref[pl.ds(s, n, stride=rows_dev), :]
        active = active_ref[pl.ds(section * rows_dev + s, 1), :]
        u = strength * x * g
        less = -(u * x)
        ret = (u * x - u * g) * active
        for where, value in ((s, ret), (rows_dev + s, less)):
            high, low = split(value)
            high_ref[:, where * n : (where + 1) * n] = high
            low_ref[:, where * n : (where + 1) * n] = low
    total = times_wide(high_ref[...], low_ref[...], wide_ref[...])
    row = cur[own_row] * owner
    row_wide = jnp.concatenate(split(row), axis=1)
    part_ref[...] = total + times_wide(ham_ref[:, :n], ham_ref[:, n:], row_wide)


def places(rows_dev):
    hist_pos, col_pos = lax.axis_index("hist"), lax.axis_index("col")
    own_row = lax.rem(hist_pos, rows_dev)
    owner = jnp.where(lax.div(hist_pos, rows_dev) == col_pos, 1.0, 0.0).astype(F32)
    return own_row, owner, col_pos


def first_kernel(rows_dev, n, steps, step_hbm, cutoff_hbm, lesser_hbm, adv_hbm, first_hbm, g_hbm, coup_hbm, ham_hbm,
                 cur_ref, wide_ref, active_ref, strength_ref, ham_ref, part_ref,
                 high_ref, low_ref, step_ref, cutoff_ref, coup_ref, h_ref, first_ref, g_ref, table_ref, sems):
    sources = [(step_hbm, step_ref), (cutoff_hbm, cutoff_ref), (coup_hbm, coup_ref), (ham_hbm, h_ref)]
    half = rows_dev * n // PARTS
    for part in range(PARTS):
        rows = pl.ds(part * half, half)
        sources += [(first_hbm.at[rows], first_ref.at[rows]), (g_hbm.at[rows], g_ref.at[rows])]
    for table, source in enumerate((lesser_hbm, adv_hbm)):
        for part in range(PARTS):
            rows = pl.ds(part * half, half)
            sources.append((source.at[rows], table_ref.at[pl.ds(table * rows_dev * n + part * half, half)]))
    copies = [pltpu.make_async_copy(a, b, sems.at[k]) for k, (a, b) in enumerate(sources)]
    for copy in copies:
        copy.start()
    own_row, owner, col_pos = places(rows_dev)
    for copy in copies[:4]:
        copy.wait()
    cutoff, start = cutoff_ref[0], step_ref[0]
    coup = coup_ref[...]
    strength_ref[...] = coup * coup
    ham_ref[...] = jnp.concatenate(split(h_ref[...]), axis=1)
    for q in range(steps):
        for s in range(rows_dev):
            active_ref[q * rows_dev + s : q * rows_dev + s + 1, :] = jnp.full(
                (1, n), jnp.where(col_pos * rows_dev + s < start + q, 1.0, 0.0).astype(F32)
            )
    for copy in copies[4 : 4 + 2 * PARTS]:
        copy.wait()
    for s in range(rows_dev):
        cur_ref[s] = first_ref[pl.ds(s, n, stride=rows_dev), :]
    for table in range(2):
        for part in range(PARTS):
            copies[4 + (2 + table) * PARTS + part].wait()
            for s in range(part * rows_dev // PARTS, (part + 1) * rows_dev // PARTS):
                inside = jnp.where(col_pos * rows_dev + s < cutoff, 1.0, 0.0).astype(F32)
                where = (table * rows_dev + s) * n
                value = table_ref[where : where + n, :]
                wide_ref[where : where + n, :] = jnp.concatenate(split(value * inside if table else value), axis=1)
    advance(0, rows_dev, n, owner, own_row, cur_ref, g_ref, active_ref, strength_ref, ham_ref, wide_ref, part_ref, high_ref, low_ref)


def next_kernel(section, rows_dev, n, order, prev_ref, greater_ref, active_ref, strength_ref, ham_ref, wide_ref, *rest):
    pieces, (cur_ref, part_ref, high_ref, low_ref) = rest[:rows_dev], rest[rows_dev:]
    own_row, owner, _ = places(rows_dev)
    for k, piece in enumerate(pieces):
        s = order(own_row, k)
        cur_ref[s] = prev_ref[s] - STEP_SIZE * piece[...]
    g_ref = greater_ref.at[pl.ds(section * rows_dev * n, rows_dev * n)]
    advance(section, rows_dev, n, owner, own_row, cur_ref, g_ref, active_ref, strength_ref, ham_ref, wide_ref, part_ref, high_ref, low_ref)


def last_kernel(rows_dev, n, order, prev_ref, *rest):
    pieces, (out_hbm, out_ref, sems) = rest[:rows_dev], rest[rows_dev:]
    own_row, _, _ = places(rows_dev)
    size = n // PARTS
    copies = []
    for part in range(PARTS):
        rows = pl.ds(part * size, size)
        for k, piece in enumerate(pieces):
            s = order(own_row, k)
            out_ref[pl.ds(part * size * rows_dev + s, size, stride=rows_dev), :] = prev_ref[s, rows, :] - STEP_SIZE * piece[rows, :]
        flat = pl.ds(part * size * rows_dev, size * rows_dev)
        copies.append(pltpu.make_async_copy(out_ref.at[flat], out_hbm.at[flat], sems.at[part]))
        copies[-1].start()
    for copy in copies:
        copy.wait()


def call(kernel, ins, outs, scratch, name):
    return pl.pallas_call(
        kernel,
        out_shape=[shape for shape, _ in outs],
        in_specs=[pl.BlockSpec(memory_space=space) for space in ins],
        out_specs=[pl.BlockSpec(memory_space=space) for _, space in outs],
        scratch_shapes=scratch,
        compiler_params=pltpu.CompilerParams(vmem_limit_bytes=VMEM_BYTES),
        name=name,
    )


def exchange_pairs(hist, rows_dev, part):
    def at(h, c):
        return h * 2 + c

    def moved(x, pairs):
        return lax.ppermute(x, ("hist", "col"), pairs)

    def flip(x, bits):
        return moved(x, [(at(h, c), at(h ^ bits, c)) for h in range(hist) for c in range(2)])

    def block(h):
        return h // rows_dev

    cycle = [(at(h, 1 - block(h)), at(h, block(h))) for h in range(hist)]
    cycle += [(at(h, block(h)), at(h ^ rows_dev, block(h))) for h in range(hist)]
    across = [(at(h, 1 - block(h)), at(h ^ rows_dev, block(h))) for h in range(hist)]
    across += [(at(h, block(h)), at(h, block(h))) for h in range(hist)]
    own = moved(part, cycle) + moved(part, across)
    pieces = [own] + [None] * (rows_dev - 1)
    for bits in range(2, rows_dev, 2):
        pieces[bits] = flip(own, bits)
    for bits in range(0, rows_dev, 2):
        pieces[bits + 1] = flip(pieces[bits], 1)
    return pieces


def exchange_any(rows_dev, part):
    total = lax.psum(part, "col")
    rows = lax.all_gather(total, "hist", axis=0)
    block = lax.dynamic_slice_in_dim(rows, lax.axis_index("col") * rows_dev, rows_dev, axis=0)
    return [block[s] for s in range(rows_dev)]


def on_device(hist, cols, lesser, advanced, first_row, greater_rows, hamiltonian, coupling, cutoff, step_index):
    rows_dev, n, cols_dev, _ = lesser.shape
    steps = greater_rows.shape[0]
    assert cols_dev == 1 and hist == cols * rows_dev
    flat = (rows_dev * n, n)
    pairs = cols == 2 and hist & (hist - 1) == 0 and rows_dev >= 2
    if pairs:
        exchange = functools.partial(exchange_pairs, hist, rows_dev)
        order = lambda own_row, k: jnp.bitwise_xor(own_row, k)
    else:
        exchange = functools.partial(exchange_any, rows_dev)
        order = lambda own_row, k: k
    shape = jax.ShapeDtypeStruct
    cur_shape, part_shape = shape((rows_dev, n, n), F32), shape((n, n), F32)
    greater = greater_rows.reshape(steps * rows_dev * n, n)
    shape, vmem, hbm = jax.ShapeDtypeStruct, pltpu.VMEM, pltpu.HBM
    cur = (shape((rows_dev, n, n), F32), vmem)
    part_out = (shape((n, n), F32), vmem)
    parts = [vmem((n, 2 * rows_dev * n), BF16)] * 2
    current, wide, active, strength, ham, part = call(
        functools.partial(first_kernel, rows_dev, n, steps),
        [hbm] * 8,
        [cur, (shape((2 * rows_dev * n, 2 * n), BF16), vmem), (shape((steps * rows_dev, n), F32), vmem),
         (shape((n, n), F32), vmem), (shape((n, 2 * n), BF16), vmem), part_out],
        parts + [pltpu.SMEM((1,), jnp.int32)] * 2 + [vmem((n, n), F32)] * 2 + [vmem(flat, F32)] * 2
        + [vmem((2 * rows_dev * n, n), F32), pltpu.SemaphoreType.DMA((4 + 4 * PARTS,))],
        "first_step",
    )(*[x if x.ndim == 1 else pltpu.with_memory_space_constraint(x, hbm) for x in (
        step_index, cutoff, lesser.reshape(flat), advanced.reshape(flat), first_row.reshape(flat), greater, coupling, hamiltonian
    )])
    for section in range(1, steps):
        pieces = exchange(part)
        current, part = call(
            functools.partial(next_kernel, section, rows_dev, n, order),
            [vmem] * (6 + rows_dev), [cur, part_out], parts, "next_step",
        )(current, greater, active, strength, ham, wide, *pieces)
    pieces = exchange(part)
    final = call(
        functools.partial(last_kernel, rows_dev, n, order),
        [vmem] * (1 + rows_dev), [(shape(flat, F32), hbm)], [vmem(flat, F32), pltpu.SemaphoreType.DMA((PARTS,))], "last_step",
    )(current, *pieces)[0]
    return final.reshape(first_row.shape)


def solution(mesh):
    in_specs = (
        P("col", None, "hist", None),
        P("col", None, "hist", None),
        P(None, "col", None),
        P(None, None, "col", None),
        P(),
        P(),
        P("hist"),
        P(),
    )
    return jax.shard_map(
        functools.partial(on_device, mesh.shape["hist"], mesh.shape["col"]),
        mesh=mesh, in_specs=in_specs, out_specs=P(None, "col", None), check_vma=False,
    )
```

time: 87.3 us -> 79.5 us (0.911)
  local copies, waits for them, and re-layouts: 8.22 us -> 0.01 us
  waiting for transfers between devices: 29.9 us -> 27.8 us
  Pallas kernels: 4.16 us -> 5.66 us
  starting transfers between devices: 42.5 us -> 43.5 us
    unnamed x22 -> x2, local copies, waits for them, and re-layouts: 8.22 us -> 0.01 us
    ppermute x36, waiting for transfers between devices: 29.9 us -> 27.8 us  [moved(): return lax.ppermute(x, ('hist', 'col'), pairs)]
    pallas_call x5, Pallas kernels: 4.16 us -> 5.66 us  [the longest x1 2.55 us: on_device(): call(functools.partial(first_kernel, rows_dev, n, steps), [hbm] * 8, [cur...]
    ppermute x36, starting transfers between devices: 42.5 us -> 43.5 us  [moved(): return lax.ppermute(x, ('hist', 'col'), pairs)]
  transfers between devices with their start and end apart: 36 -> 36, of which waited for: 14 -> 13; matrix products, arithmetic and copies ran while one was open for 0% -> 0% of each run, Pallas kernels for 0% -> 0%
where the time goes in v3:
time: 79.5 us; the launch traced here: 78.6 us
  starting transfers between devices  43.5 us (55%)
  waiting for transfers between devices  27.8 us (35%)
  Pallas kernels  5.66 us (7%)
  between operations  1.62 us (2%)
    ppermute x36, starting transfers between devices, moved(): return lax.ppermute(x, ('hist', 'col'), pairs)  43.5 us
    ppermute x36, waiting for transfers between devices, moved(): return lax.ppermute(x, ('hist', 'col'), pairs)  27.8 us
    pallas_call x1, Pallas kernels, on_device(): call(functools.partial(first_kernel, rows_dev, n, steps), [hbm] * 8, [cur...  2.55 us
    pallas_call x3, Pallas kernels, on_device(): call(functools.partial(next_kernel, section, rows_dev, n, order), [vmem]...  2.23 us
  transfers between devices with their start and end apart: 36, of which 13 were waited for; matrix products, arithmetic and copies ran while one was open for 0% of the time, Pallas kernels for 0%

profile of v3, /device:TPU:25, one launch (start us, length us, event | category | flops | bytes accessed | tf_op | source)
XLA Modules:
  0.0 78.6 jit_solution(6350159364384487399)
XLA Ops:
  1.4 2.6 %first_step.1 = (f32[8,128,128]{2,1,0:T(8,128)S(1)}, bf16[2048,256]{1,0:T(8,128)(2,1)S(1)}, f32[32,128]{1,0:T(8,128)S(1)}, f32[128,128]{1,0:T(8,128)S(1)}, bf16[...) custom-call(s32[1]{0:T(128)S(6)} %copy.10.step_hbm, s32[1]{0:T(128)S(6)} %copy.9.cutoff_hbm, f32[1024,128]{1,0:T(8,128)} %bitcast.9, ...), custom_call_target="tpu_custom_call" | custom-call | tf_op jit(solution)/shard_map/first_step/pallas_call | solution.py:188
  4.0 2.9 %collective-permute-start.1 = (f32[128,128]{1,0:T(8,128)S(1)}, f32[128,128]{1,0:T(8,128)S(1)}, u32[]{:S(2)}, u32[]{:S(2)}) collective-permute-start(f32[128,128]{1,0:T(8,128)S(1)} %get-tuple-element.22), channel_id=1, source_target_pairs={{1,16},{3,18},{5,20},{7,22},{9,24},{11,26},{13,28},{15,30},{16,1},... | collective-permute-start | bytes 196616 | tf_op jit(solution)/shard_map/ppermute | solution.py:141
  6.9 0.1 collective-permute-start
  7.0 5.7 %collective-permute-done.1 = f32[128,128]{1,0:T(8,128)S(1)} collective-permute-done((f32[128,128]{1,0:T(8,128)S(1)}, f32[128,128]{1,0:T(8,128)S(1)}, u32[]{:S(2)}, u32[]{:S(2)}) %collective-permute-start.1) | collective-permute-done | bytes 65568 | tf_op jit(solution)/shard_map/ppermute | solution.py:141
  12.7 0.1 collective-permute-start.7
  12.8 2.4 %collective-permute-start.5 = (f32[128,128]{1,0:T(8,128)S(1)}, f32[128,128]{1,0:T(8,128)S(1)}, u32[]{:S(2)}, u32[]{:S(2)}) collective-permute-start(f32[128,128]{1,0:T(8,128)S(1)} %add.12.rest_0_), channel_id=1, source_target_pairs={{0,8},{1,9},{2,10},{3,11},{4,12},{5,13},{6,14},{7,15},{8,0},{9,1},... | collective-permute-start | bytes 196616 | tf_op jit(solution)/shard_map/ppermute | solution.py:141
  15.2 0.2 collective-permute-start.3
  15.4 1.9 %collective-permute-start.2 = (f32[128,128]{1,0:T(8,128)S(1)}, f32[128,128]{1,0:T(8,128)S(1)}, u32[]{:S(2)}, u32[]{:S(2)}) collective-permute-start(f32[128,128]{1,0:T(8,128)S(1)} %add.12.rest_0_), channel_id=1, source_target_pairs={{0,2},{1,3},{2,0},{3,1},{4,6},{5,7},{6,4},{7,5},{8,10},{9,11},{10,... | collective-permute-start | bytes 196616 | tf_op jit(solution)/shard_map/ppermute | solution.py:141
  17.2 1.7 %collective-permute-start.8 = (f32[128,128]{1,0:T(8,128)S(1)}, f32[128,128]{1,0:T(8,128)S(1)}, u32[]{:S(2)}, u32[]{:S(2)}) collective-permute-start(f32[128,128]{1,0:T(8,128)S(1)} %collective-permute-done.7.rest_6_), channel_id=1, source_target_pairs={{0,2},{1,3},{2,0},{3,1},{4,6},{5,7},{6,4},{7,5},{8,10},{9,11},{10,... | collective-permute-start | bytes 196616 | tf_op jit(solution)/shard_map/ppermute | solution.py:141
  19.0 0.7 collective-permute-start.6
  19.7 1.3 %collective-permute-start.4 = (f32[128,128]{1,0:T(8,128)S(1)}, f32[128,128]{1,0:T(8,128)S(1)}, u32[]{:S(2)}, u32[]{:S(2)}) collective-permute-start(f32[128,128]{1,0:T(8,128)S(1)} %collective-permute-done.3.rest_2_), channel_id=1, source_target_pairs={{0,2},{1,3},{2,0},{3,1},{4,6},{5,7},{6,4},{7,5},{8,10},{9,11},{10,... | collective-permute-start | bytes 196616 | tf_op jit(solution)/shard_map/ppermute | solution.py:141
  21.0 0.9 %collective-permute-done.4.rest_3_ = f32[128,128]{1,0:T(8,128)S(1)} collective-permute-done((f32[128,128]{1,0:T(8,128)S(1)}, f32[128,128]{1,0:T(8,128)S(1)}, u32[]{:S(2)}, u32[]{:S(2)}) %collective-permute-start.4) | collective-permute-done | bytes 65568 | tf_op jit(solution)/shard_map/ppermute | solution.py:141
  21.9 0.7 next_step.3
  22.7 4.2 %collective-permute-start.10 = (f32[128,128]{1,0:T(8,128)S(1)}, f32[128,128]{1,0:T(8,128)S(1)}, u32[]{:S(2)}, u32[]{:S(2)}) collective-permute-start(f32[128,128]{1,0:T(8,128)S(1)} %get-tuple-element.24), channel_id=1, source_target_pairs={{1,16},{3,18},{5,20},{7,22},{9,24},{11,26},{13,28},{15,30},{16,1},... | collective-permute-start | bytes 196616 | tf_op jit(solution)/shard_map/ppermute | solution.py:141
  26.9 4.7 %collective-permute-done.10 = f32[128,128]{1,0:T(8,128)S(1)} collective-permute-done((f32[128,128]{1,0:T(8,128)S(1)}, f32[128,128]{1,0:T(8,128)S(1)}, u32[]{:S(2)}, u32[]{:S(2)}) %collective-permute-start.10) | collective-permute-done | bytes 65568 | tf_op jit(solution)/shard_map/ppermute | solution.py:141
  31.6 1.3 %collective-permute-done.9 = f32[128,128]{1,0:T(8,128)S(1)} collective-permute-done((f32[128,128]{1,0:T(8,128)S(1)}, f32[128,128]{1,0:T(8,128)S(1)}, u32[]{:S(2)}, u32[]{:S(2)}) %collective-permute-start.9) | collective-permute-done | bytes 65568 | tf_op jit(solution)/shard_map/ppermute | solution.py:141
  32.9 0.1 collective-permute-start.16
  33.0 1.0 %collective-permute-start.14 = (f32[128,128]{1,0:T(8,128)S(1)}, f32[128,128]{1,0:T(8,128)S(1)}, u32[]{:S(2)}, u32[]{:S(2)}) collective-permute-start(f32[128,128]{1,0:T(8,128)S(1)} %add.13.rest_0_), channel_id=1, source_target_pairs={{0,8},{1,9},{2,10},{3,11},{4,12},{5,13},{6,14},{7,15},{8,0},{9,1},... | collective-permute-start | bytes 196616 | tf_op jit(solution)/shard_map/ppermute | solution.py:141
  34.0 1.6 %collective-permute-start.12 = (f32[128,128]{1,0:T(8,128)S(1)}, f32[128,128]{1,0:T(8,128)S(1)}, u32[]{:S(2)}, u32[]{:S(2)}) collective-permute-start(f32[128,128]{1,0:T(8,128)S(1)} %add.13.rest_0_), channel_id=1, source_target_pairs={{0,4},{1,5},{2,6},{3,7},{4,0},{5,1},{6,2},{7,3},{8,12},{9,13},{10,... | collective-permute-start | bytes 196616 | tf_op jit(solution)/shard_map/ppermute | solution.py:141
  35.6 1.4 %collective-permute-start.11 = (f32[128,128]{1,0:T(8,128)S(1)}, f32[128,128]{1,0:T(8,128)S(1)}, u32[]{:S(2)}, u32[]{:S(2)}) collective-permute-start(f32[128,128]{1,0:T(8,128)S(1)} %add.13.rest_0_), channel_id=1, source_target_pairs={{0,2},{1,3},{2,0},{3,1},{4,6},{5,7},{6,4},{7,5},{8,10},{9,11},{10,... | collective-permute-start | bytes 196616 | tf_op jit(solution)/shard_map/ppermute | solution.py:141
  37.1 2.0 %collective-permute-start.17 = (f32[128,128]{1,0:T(8,128)S(1)}, f32[128,128]{1,0:T(8,128)S(1)}, u32[]{:S(2)}, u32[]{:S(2)}) collective-permute-start(f32[128,128]{1,0:T(8,128)S(1)} %collective-permute-done.16.rest_6_), channel_id=1, source_target_pairs={{0,2},{1,3},{2,0},{3,1},{4,6},{5,7},{6,4},{7,5},{8,10},{9,11},{10,... | collective-permute-start | bytes 196616 | tf_op jit(solution)/shard_map/ppermute | solution.py:141
  39.1 0.7 collective-permute-start.13
  39.8 0.2 collective-permute-done.17.rest_7_
  40.0 0.4 collective-permute-done.15.rest_5_
  40.4 0.3 collective-permute-done.13.rest_3_
  40.7 0.7 next_step.4
  41.5 2.1 %collective-permute-start.19 = (f32[128,128]{1,0:T(8,128)S(1)}, f32[128,128]{1,0:T(8,128)S(1)}, u32[]{:S(2)}, u32[]{:S(2)}) collective-permute-start(f32[128,128]{1,0:T(8,128)S(1)} %get-tuple-element.26), channel_id=1, source_target_pairs={{1,16},{3,18},{5,20},{7,22},{9,24},{11,26},{13,28},{15,30},{16,1},... | collective-permute-start | bytes 196616 | tf_op jit(solution)/shard_map/ppermute | solution.py:141
  43.6 6.5 %collective-permute-done.19 = f32[128,128]{1,0:T(8,128)S(1)} collective-permute-done((f32[128,128]{1,0:T(8,128)S(1)}, f32[128,128]{1,0:T(8,128)S(1)}, u32[]{:S(2)}, u32[]{:S(2)}) %collective-permute-start.19) | collective-permute-done | bytes 65568 | tf_op jit(solution)/shard_map/ppermute | solution.py:141
  50.2 0.1 collective-permute-start.25
  50.3 2.6 %collective-permute-start.23 = (f32[128,128]{1,0:T(8,128)S(1)}, f32[128,128]{1,0:T(8,128)S(1)}, u32[]{:S(2)}, u32[]{:S(2)}) collective-permute-start(f32[128,128]{1,0:T(8,128)S(1)} %add.14.rest_0_), channel_id=1, source_target_pairs={{0,8},{1,9},{2,10},{3,11},{4,12},{5,13},{6,14},{7,15},{8,0},{9,1},... | collective-permute-start | bytes 196616 | tf_op jit(solution)/shard_map/ppermute | solution.py:141
  52.9 1.4 %collective-permute-start.20 = (f32[128,128]{1,0:T(8,128)S(1)}, f32[128,128]{1,0:T(8,128)S(1)}, u32[]{:S(2)}, u32[]{:S(2)}) collective-permute-start(f32[128,128]{1,0:T(8,128)S(1)} %add.14.rest_0_), channel_id=1, source_target_pairs={{0,2},{1,3},{2,0},{3,1},{4,6},{5,7},{6,4},{7,5},{8,10},{9,11},{10,... | collective-permute-start | bytes 196616 | tf_op jit(solution)/shard_map/ppermute | solution.py:141
  54.3 2.2 %collective-permute-start.26 = (f32[128,128]{1,0:T(8,128)S(1)}, f32[128,128]{1,0:T(8,128)S(1)}, u32[]{:S(2)}, u32[]{:S(2)}) collective-permute-start(f32[128,128]{1,0:T(8,128)S(1)} %collective-permute-done.25.rest_6_), channel_id=1, source_target_pairs={{0,2},{1,3},{2,0},{3,1},{4,6},{5,7},{6,4},{7,5},{8,10},{9,11},{10,... | collective-permute-start | bytes 196616 | tf_op jit(solution)/shard_map/ppermute | solution.py:141
  56.5 0.9 %collective-permute-start.24 = (f32[128,128]{1,0:T(8,128)S(1)}, f32[128,128]{1,0:T(8,128)S(1)}, u32[]{:S(2)}, u32[]{:S(2)}) collective-permute-start(f32[128,128]{1,0:T(8,128)S(1)} %collective-permute-done.23.rest_4_), channel_id=1, source_target_pairs={{0,2},{1,3},{2,0},{3,1},{4,6},{5,7},{6,4},{7,5},{8,10},{9,11},{10,... | collective-permute-start | bytes 196616 | tf_op jit(solution)/shard_map/ppermute | solution.py:141
  57.4 0.8 %collective-permute-start.22 = (f32[128,128]{1,0:T(8,128)S(1)}, f32[128,128]{1,0:T(8,128)S(1)}, u32[]{:S(2)}, u32[]{:S(2)}) collective-permute-start(f32[128,128]{1,0:T(8,128)S(1)} %collective-permute-done.21.rest_2_), channel_id=1, source_target_pairs={{0,2},{1,3},{2,0},{3,1},{4,6},{5,7},{6,4},{7,5},{8,10},{9,11},{10,... | collective-permute-start | bytes 196616 | tf_op jit(solution)/shard_map/ppermute | solution.py:141
  58.3 0.9 %collective-permute-done.22.rest_3_ = f32[128,128]{1,0:T(8,128)S(1)} collective-permute-done((f32[128,128]{1,0:T(8,128)S(1)}, f32[128,128]{1,0:T(8,128)S(1)}, u32[]{:S(2)}, u32[]{:S(2)}) %collective-permute-start.22) | collective-permute-done | bytes 65568 | tf_op jit(solution)/shard_map/ppermute | solution.py:141
  59.1 0.7 next_step.5
  59.9 3.9 %collective-permute-start.28 = (f32[128,128]{1,0:T(8,128)S(1)}, f32[128,128]{1,0:T(8,128)S(1)}, u32[]{:S(2)}, u32[]{:S(2)}) collective-permute-start(f32[128,128]{1,0:T(8,128)S(1)} %get-tuple-element.28), channel_id=1, source_target_pairs={{1,16},{3,18},{5,20},{7,22},{9,24},{11,26},{13,28},{15,30},{16,1},... | collective-permute-start | bytes 196616 | tf_op jit(solution)/shard_map/ppermute | solution.py:141
  63.8 4.9 %collective-permute-done.28 = f32[128,128]{1,0:T(8,128)S(1)} collective-permute-done((f32[128,128]{1,0:T(8,128)S(1)}, f32[128,128]{1,0:T(8,128)S(1)}, u32[]{:S(2)}, u32[]{:S(2)}) %collective-permute-start.28) | collective-permute-done | bytes 65568 | tf_op jit(solution)/shard_map/ppermute | solution.py:141
  68.8 1.0 %collective-permute-done.27 = f32[128,128]{1,0:T(8,128)S(1)} collective-permute-done((f32[128,128]{1,0:T(8,128)S(1)}, f32[128,128]{1,0:T(8,128)S(1)}, u32[]{:S(2)}, u32[]{:S(2)}) %collective-permute-start.27) | collective-permute-done | bytes 65568 | tf_op jit(solution)/shard_map/ppermute | solution.py:141
  69.8 0.1 collective-permute-start.34
  69.9 0.3 collective-permute-start.32
  70.2 2.3 %collective-permute-start.30 = (f32[128,128]{1,0:T(8,128)S(1)}, f32[128,128]{1,0:T(8,128)S(1)}, u32[]{:S(2)}, u32[]{:S(2)}) collective-permute-start(f32[128,128]{1,0:T(8,128)S(1)} %add.15.rest_0_), channel_id=1, source_target_pairs={{0,4},{1,5},{2,6},{3,7},{4,0},{5,1},{6,2},{7,3},{8,12},{9,13},{10,... | collective-permute-start | bytes 196616 | tf_op jit(solution)/shard_map/ppermute | solution.py:141
  72.5 1.7 %collective-permute-start.29 = (f32[128,128]{1,0:T(8,128)S(1)}, f32[128,128]{1,0:T(8,128)S(1)}, u32[]{:S(2)}, u32[]{:S(2)}) collective-permute-start(f32[128,128]{1,0:T(8,128)S(1)} %add.15.rest_0_), channel_id=1, source_target_pairs={{0,2},{1,3},{2,0},{3,1},{4,6},{5,7},{6,4},{7,5},{8,10},{9,11},{10,... | collective-permute-start | bytes 196616 | tf_op jit(solution)/shard_map/ppermute | solution.py:141
  74.2 1.8 %collective-permute-start.35 = (f32[128,128]{1,0:T(8,128)S(1)}, f32[128,128]{1,0:T(8,128)S(1)}, u32[]{:S(2)}, u32[]{:S(2)}) collective-permute-start(f32[128,128]{1,0:T(8,128)S(1)} %collective-permute-done.34.rest_6_), channel_id=1, source_target_pairs={{0,2},{1,3},{2,0},{3,1},{4,6},{5,7},{6,4},{7,5},{8,10},{9,11},{10,... | collective-permute-start | bytes 196616 | tf_op jit(solution)/shard_map/ppermute | solution.py:141
  76.0 0.9 %collective-permute-start.31 = (f32[128,128]{1,0:T(8,128)S(1)}, f32[128,128]{1,0:T(8,128)S(1)}, u32[]{:S(2)}, u32[]{:S(2)}) collective-permute-start(f32[128,128]{1,0:T(8,128)S(1)} %collective-permute-done.30.rest_2_), channel_id=1, source_target_pairs={{0,2},{1,3},{2,0},{3,1},{4,6},{5,7},{6,4},{7,5},{8,10},{9,11},{10,... | collective-permute-start | bytes 196616 | tf_op jit(solution)/shard_map/ppermute | solution.py:141
  76.9 0.4 collective-permute-done.33.rest_5_
  77.2 0.5 collective-permute-done.31.rest_3_
  77.8 0.9 %last_step.1 = f32[1024,128]{1,0:T(8,128)} custom-call(f32[8,128,128]{2,1,0:T(8,128)S(1)} %get-tuple-element.27.prev_ref, f32[128,128]{1,0:T(8,128)S(1)} %add.15.rest_0_, f32[128,128]{1,0:T(8,128)S(1)} %collective-permute-done.29.rest_1_, f32[128,128]{1,0:T(8,128)S(1)} %collective-permute-done.30.rest_2_, f32[128,128]{1,0:T(8,128)S(1)} %collective-permute-done.31.rest_3_, ...), custom_call_target="tpu_custom_call" | custom-call | tf_op jit(solution)/shard_map/last_step/pallas_call | solution.py:206
  (35 shorter events, 0.4 us)
Async XLA Ops:
  0.0 21.9 %copy-start = (f32[4,128,8,128]{3,2,1,0:T(8,128)S(1)}, f32[4,128,8,128]{3,2,1,0:T(8,128)}, u32[]{:S(2)}) copy-start(f32[4,128,8,128]{3,2,1,0:T(8,128)} %param.11) | copy-start | bytes 6291460
  4.0 8.6 %collective-permute-start.1 = (f32[128,128]{1,0:T(8,128)S(1)}, f32[128,128]{1,0:T(8,128)S(1)}, u32[]{:S(2)}, u32[]{:S(2)}) collective-permute-start(f32[128,128]{1,0:T(8,128)S(1)} %get-tuple-element.22), channel_id=1, source_target_pairs={{1,16},{3,18},{5,20},{7,22},{9,24},{11,26},{13,28},{15,30},{16,1},... | collective-permute-start | bytes 196616 | tf_op jit(solution)/shard_map/ppermute | solution.py:141
  6.9 5.7 %collective-permute-start = (f32[128,128]{1,0:T(8,128)S(1)}, f32[128,128]{1,0:T(8,128)S(1)}, u32[]{:S(2)}, u32[]{:S(2)}) collective-permute-start(f32[128,128]{1,0:T(8,128)S(1)} %get-tuple-element.22), channel_id=1, source_target_pairs={{1,0},{3,2},{5,4},{7,6},{9,8},{11,10},{13,12},{15,14},{16,17},{18,... | collective-permute-start | bytes 196616 | tf_op jit(solution)/shard_map/ppermute | solution.py:141
  12.7 4.6 %collective-permute-start.7 = (f32[128,128]{1,0:T(8,128)S(1)}, f32[128,128]{1,0:T(8,128)S(1)}, u32[]{:S(2)}, u32[]{:S(2)}) collective-permute-start(f32[128,128]{1,0:T(8,128)S(1)} %add.12.rest_0_), channel_id=1, source_target_pairs={{0,12},{1,13},{2,14},{3,15},{4,8},{5,9},{6,10},{7,11},{8,4},{9,5},... | collective-permute-start | bytes 196616 | tf_op jit(solution)/shard_map/ppermute | solution.py:141
  12.8 6.2 %collective-permute-start.5 = (f32[128,128]{1,0:T(8,128)S(1)}, f32[128,128]{1,0:T(8,128)S(1)}, u32[]{:S(2)}, u32[]{:S(2)}) collective-permute-start(f32[128,128]{1,0:T(8,128)S(1)} %add.12.rest_0_), channel_id=1, source_target_pairs={{0,8},{1,9},{2,10},{3,11},{4,12},{5,13},{6,14},{7,15},{8,0},{9,1},... | collective-permute-start | bytes 196616 | tf_op jit(solution)/shard_map/ppermute | solution.py:141
  15.2 4.5 %collective-permute-start.3 = (f32[128,128]{1,0:T(8,128)S(1)}, f32[128,128]{1,0:T(8,128)S(1)}, u32[]{:S(2)}, u32[]{:S(2)}) collective-permute-start(f32[128,128]{1,0:T(8,128)S(1)} %add.12.rest_0_), channel_id=1, source_target_pairs={{0,4},{1,5},{2,6},{3,7},{4,0},{5,1},{6,2},{7,3},{8,12},{9,13},{10,... | collective-permute-start | bytes 196616 | tf_op jit(solution)/shard_map/ppermute | solution.py:141
  15.4 5.6 %collective-permute-start.2 = (f32[128,128]{1,0:T(8,128)S(1)}, f32[128,128]{1,0:T(8,128)S(1)}, u32[]{:S(2)}, u32[]{:S(2)}) collective-permute-start(f32[128,128]{1,0:T(8,128)S(1)} %add.12.rest_0_), channel_id=1, source_target_pairs={{0,2},{1,3},{2,0},{3,1},{4,6},{5,7},{6,4},{7,5},{8,10},{9,11},{10,... | collective-permute-start | bytes 196616 | tf_op jit(solution)/shard_map/ppermute | solution.py:141
  17.2 3.8 %collective-permute-start.8 = (f32[128,128]{1,0:T(8,128)S(1)}, f32[128,128]{1,0:T(8,128)S(1)}, u32[]{:S(2)}, u32[]{:S(2)}) collective-permute-start(f32[128,128]{1,0:T(8,128)S(1)} %collective-permute-done.7.rest_6_), channel_id=1, source_target_pairs={{0,2},{1,3},{2,0},{3,1},{4,6},{5,7},{6,4},{7,5},{8,10},{9,11},{10,... | collective-permute-start | bytes 196616 | tf_op jit(solution)/shard_map/ppermute | solution.py:141
  19.0 2.0 %collective-permute-start.6 = (f32[128,128]{1,0:T(8,128)S(1)}, f32[128,128]{1,0:T(8,128)S(1)}, u32[]{:S(2)}, u32[]{:S(2)}) collective-permute-start(f32[128,128]{1,0:T(8,128)S(1)} %collective-permute-done.5.rest_4_), channel_id=1, source_target_pairs={{0,2},{1,3},{2,0},{3,1},{4,6},{5,7},{6,4},{7,5},{8,10},{9,11},{10,... | collective-permute-start | bytes 196616 | tf_op jit(solution)/shard_map/ppermute | solution.py:141
  19.7 2.2 %collective-permute-start.4 = (f32[128,128]{1,0:T(8,128)S(1)}, f32[128,128]{1,0:T(8,128)S(1)}, u32[]{:S(2)}, u32[]{:S(2)}) collective-permute-start(f32[128,128]{1,0:T(8,128)S(1)} %collective-permute-done.3.rest_2_), channel_id=1, source_target_pairs={{0,2},{1,3},{2,0},{3,1},{4,6},{5,7},{6,4},{7,5},{8,10},{9,11},{10,... | collective-permute-start | bytes 196616 | tf_op jit(solution)/shard_map/ppermute | solution.py:141
  22.7 8.9 %collective-permute-start.10 = (f32[128,128]{1,0:T(8,128)S(1)}, f32[128,128]{1,0:T(8,128)S(1)}, u32[]{:S(2)}, u32[]{:S(2)}) collective-permute-start(f32[128,128]{1,0:T(8,128)S(1)} %get-tuple-element.24), channel_id=1, source_target_pairs={{1,16},{3,18},{5,20},{7,22},{9,24},{11,26},{13,28},{15,30},{16,1},... | collective-permute-start | bytes 196616 | tf_op jit(solution)/shard_map/ppermute | solution.py:141
  26.9 6.1 %collective-permute-start.9 = (f32[128,128]{1,0:T(8,128)S(1)}, f32[128,128]{1,0:T(8,128)S(1)}, u32[]{:S(2)}, u32[]{:S(2)}) collective-permute-start(f32[128,128]{1,0:T(8,128)S(1)} %get-tuple-element.24), channel_id=1, source_target_pairs={{1,0},{3,2},{5,4},{7,6},{9,8},{11,10},{13,12},{15,14},{16,17},{18,... | collective-permute-start | bytes 196616 | tf_op jit(solution)/shard_map/ppermute | solution.py:141
  32.9 4.2 %collective-permute-start.16 = (f32[128,128]{1,0:T(8,128)S(1)}, f32[128,128]{1,0:T(8,128)S(1)}, u32[]{:S(2)}, u32[]{:S(2)}) collective-permute-start(f32[128,128]{1,0:T(8,128)S(1)} %add.13.rest_0_), channel_id=1, source_target_pairs={{0,12},{1,13},{2,14},{3,15},{4,8},{5,9},{6,10},{7,11},{8,4},{9,5},... | collective-permute-start | bytes 196616 | tf_op jit(solution)/shard_map/ppermute | solution.py:141
  33.0 6.1 %collective-permute-start.14 = (f32[128,128]{1,0:T(8,128)S(1)}, f32[128,128]{1,0:T(8,128)S(1)}, u32[]{:S(2)}, u32[]{:S(2)}) collective-permute-start(f32[128,128]{1,0:T(8,128)S(1)} %add.13.rest_0_), channel_id=1, source_target_pairs={{0,8},{1,9},{2,10},{3,11},{4,12},{5,13},{6,14},{7,15},{8,0},{9,1},... | collective-permute-start | bytes 196616 | tf_op jit(solution)/shard_map/ppermute | solution.py:141
  34.0 5.1 %collective-permute-start.12 = (f32[128,128]{1,0:T(8,128)S(1)}, f32[128,128]{1,0:T(8,128)S(1)}, u32[]{:S(2)}, u32[]{:S(2)}) collective-permute-start(f32[128,128]{1,0:T(8,128)S(1)} %add.13.rest_0_), channel_id=1, source_target_pairs={{0,4},{1,5},{2,6},{3,7},{4,0},{5,1},{6,2},{7,3},{8,12},{9,13},{10,... | collective-permute-start | bytes 196616 | tf_op jit(solution)/shard_map/ppermute | solution.py:141
  35.6 4.2 %collective-permute-start.11 = (f32[128,128]{1,0:T(8,128)S(1)}, f32[128,128]{1,0:T(8,128)S(1)}, u32[]{:S(2)}, u32[]{:S(2)}) collective-permute-start(f32[128,128]{1,0:T(8,128)S(1)} %add.13.rest_0_), channel_id=1, source_target_pairs={{0,2},{1,3},{2,0},{3,1},{4,6},{5,7},{6,4},{7,5},{8,10},{9,11},{10,... | collective-permute-start | bytes 196616 | tf_op jit(solution)/shard_map/ppermute | solution.py:141
  37.1 2.9 %collective-permute-start.17 = (f32[128,128]{1,0:T(8,128)S(1)}, f32[128,128]{1,0:T(8,128)S(1)}, u32[]{:S(2)}, u32[]{:S(2)}) collective-permute-start(f32[128,128]{1,0:T(8,128)S(1)} %collective-permute-done.16.rest_6_), channel_id=1, source_target_pairs={{0,2},{1,3},{2,0},{3,1},{4,6},{5,7},{6,4},{7,5},{8,10},{9,11},{10,... | collective-permute-start | bytes 196616 | tf_op jit(solution)/shard_map/ppermute | solution.py:141
  39.1 1.3 %collective-permute-start.15 = (f32[128,128]{1,0:T(8,128)S(1)}, f32[128,128]{1,0:T(8,128)S(1)}, u32[]{:S(2)}, u32[]{:S(2)}) collective-permute-start(f32[128,128]{1,0:T(8,128)S(1)} %collective-permute-done.14.rest_4_), channel_id=1, source_target_pairs={{0,2},{1,3},{2,0},{3,1},{4,6},{5,7},{6,4},{7,5},{8,10},{9,11},{10,... | collective-permute-start | bytes 196616 | tf_op jit(solution)/shard_map/ppermute | solution.py:141
  39.1 1.6 %collective-permute-start.13 = (f32[128,128]{1,0:T(8,128)S(1)}, f32[128,128]{1,0:T(8,128)S(1)}, u32[]{:S(2)}, u32[]{:S(2)}) collective-permute-start(f32[128,128]{1,0:T(8,128)S(1)} %collective-permute-done.12.rest_2_), channel_id=1, source_target_pairs={{0,2},{1,3},{2,0},{3,1},{4,6},{5,7},{6,4},{7,5},{8,10},{9,11},{10,... | collective-permute-start | bytes 196616 | tf_op jit(solution)/shard_map/ppermute | solution.py:141
  41.5 8.7 %collective-permute-start.19 = (f32[128,128]{1,0:T(8,128)S(1)}, f32[128,128]{1,0:T(8,128)S(1)}, u32[]{:S(2)}, u32[]{:S(2)}) collective-permute-start(f32[128,128]{1,0:T(8,128)S(1)} %get-tuple-element.26), channel_id=1, source_target_pairs={{1,16},{3,18},{5,20},{7,22},{9,24},{11,26},{13,28},{15,30},{16,1},... | collective-permute-start | bytes 196616 | tf_op jit(solution)/shard_map/ppermute | solution.py:141
  43.6 6.6 %collective-permute-start.18 = (f32[128,128]{1,0:T(8,128)S(1)}, f32[128,128]{1,0:T(8,128)S(1)}, u32[]{:S(2)}, u32[]{:S(2)}) collective-permute-start(f32[128,128]{1,0:T(8,128)S(1)} %get-tuple-element.26), channel_id=1, source_target_pairs={{1,0},{3,2},{5,4},{7,6},{9,8},{11,10},{13,12},{15,14},{16,17},{18,... | collective-permute-start | bytes 196616 | tf_op jit(solution)/shard_map/ppermute | solution.py:141
  50.2 4.1 %collective-permute-start.25 = (f32[128,128]{1,0:T(8,128)S(1)}, f32[128,128]{1,0:T(8,128)S(1)}, u32[]{:S(2)}, u32[]{:S(2)}) collective-permute-start(f32[128,128]{1,0:T(8,128)S(1)} %add.14.rest_0_), channel_id=1, source_target_pairs={{0,12},{1,13},{2,14},{3,15},{4,8},{5,9},{6,10},{7,11},{8,4},{9,5},... | collective-permute-start | bytes 196616 | tf_op jit(solution)/shard_map/ppermute | solution.py:141
  50.3 6.2 %collective-permute-start.23 = (f32[128,128]{1,0:T(8,128)S(1)}, f32[128,128]{1,0:T(8,128)S(1)}, u32[]{:S(2)}, u32[]{:S(2)}) collective-permute-start(f32[128,128]{1,0:T(8,128)S(1)} %add.14.rest_0_), channel_id=1, source_target_pairs={{0,8},{1,9},{2,10},{3,11},{4,12},{5,13},{6,14},{7,15},{8,0},{9,1},... | collective-permute-start | bytes 196616 | tf_op jit(solution)/shard_map/ppermute | solution.py:141
  52.9 4.4 %collective-permute-start.21 = (f32[128,128]{1,0:T(8,128)S(1)}, f32[128,128]{1,0:T(8,128)S(1)}, u32[]{:S(2)}, u32[]{:S(2)}) collective-permute-start(f32[128,128]{1,0:T(8,128)S(1)} %add.14.rest_0_), channel_id=1, source_target_pairs={{0,4},{1,5},{2,6},{3,7},{4,0},{5,1},{6,2},{7,3},{8,12},{9,13},{10,... | collective-permute-start | bytes 196616 | tf_op jit(solution)/shard_map/ppermute | solution.py:141
  52.9 5.3 %collective-permute-start.20 = (f32[128,128]{1,0:T(8,128)S(1)}, f32[128,128]{1,0:T(8,128)S(1)}, u32[]{:S(2)}, u32[]{:S(2)}) collective-permute-start(f32[128,128]{1,0:T(8,128)S(1)} %add.14.rest_0_), channel_id=1, source_target_pairs={{0,2},{1,3},{2,0},{3,1},{4,6},{5,7},{6,4},{7,5},{8,10},{9,11},{10,... | collective-permute-start | bytes 196616 | tf_op jit(solution)/shard_map/ppermute | solution.py:141
  54.3 3.9 %collective-permute-start.26 = (f32[128,128]{1,0:T(8,128)S(1)}, f32[128,128]{1,0:T(8,128)S(1)}, u32[]{:S(2)}, u32[]{:S(2)}) collective-permute-start(f32[128,128]{1,0:T(8,128)S(1)} %collective-permute-done.25.rest_6_), channel_id=1, source_target_pairs={{0,2},{1,3},{2,0},{3,1},{4,6},{5,7},{6,4},{7,5},{8,10},{9,11},{10,... | collective-permute-start | bytes 196616 | tf_op jit(solution)/shard_map/ppermute | solution.py:141
  56.5 1.8 %collective-permute-start.24 = (f32[128,128]{1,0:T(8,128)S(1)}, f32[128,128]{1,0:T(8,128)S(1)}, u32[]{:S(2)}, u32[]{:S(2)}) collective-permute-start(f32[128,128]{1,0:T(8,128)S(1)} %collective-permute-done.23.rest_4_), channel_id=1, source_target_pairs={{0,2},{1,3},{2,0},{3,1},{4,6},{5,7},{6,4},{7,5},{8,10},{9,11},{10,... | collective-permute-start | bytes 196616 | tf_op jit(solution)/shard_map/ppermute | solution.py:141
  57.4 1.8 %collective-permute-start.22 = (f32[128,128]{1,0:T(8,128)S(1)}, f32[128,128]{1,0:T(8,128)S(1)}, u32[]{:S(2)}, u32[]{:S(2)}) collective-permute-start(f32[128,128]{1,0:T(8,128)S(1)} %collective-permute-done.21.rest_2_), channel_id=1, source_target_pairs={{0,2},{1,3},{2,0},{3,1},{4,6},{5,7},{6,4},{7,5},{8,10},{9,11},{10,... | collective-permute-start | bytes 196616 | tf_op jit(solution)/shard_map/ppermute | solution.py:141
  59.9 8.9 %collective-permute-start.28 = (f32[128,128]{1,0:T(8,128)S(1)}, f32[128,128]{1,0:T(8,128)S(1)}, u32[]{:S(2)}, u32[]{:S(2)}) collective-permute-start(f32[128,128]{1,0:T(8,128)S(1)} %get-tuple-element.28), channel_id=1, source_target_pairs={{1,16},{3,18},{5,20},{7,22},{9,24},{11,26},{13,28},{15,30},{16,1},... | collective-permute-start | bytes 196616 | tf_op jit(solution)/shard_map/ppermute | solution.py:141
  63.8 6.0 %collective-permute-start.27 = (f32[128,128]{1,0:T(8,128)S(1)}, f32[128,128]{1,0:T(8,128)S(1)}, u32[]{:S(2)}, u32[]{:S(2)}) collective-permute-start(f32[128,128]{1,0:T(8,128)S(1)} %get-tuple-element.28), channel_id=1, source_target_pairs={{1,0},{3,2},{5,4},{7,6},{9,8},{11,10},{13,12},{15,14},{16,17},{18,... | collective-permute-start | bytes 196616 | tf_op jit(solution)/shard_map/ppermute | solution.py:141
  69.8 4.4 %collective-permute-start.34 = (f32[128,128]{1,0:T(8,128)S(1)}, f32[128,128]{1,0:T(8,128)S(1)}, u32[]{:S(2)}, u32[]{:S(2)}) collective-permute-start(f32[128,128]{1,0:T(8,128)S(1)} %add.15.rest_0_), channel_id=1, source_target_pairs={{0,12},{1,13},{2,14},{3,15},{4,8},{5,9},{6,10},{7,11},{8,4},{9,5},... | collective-permute-start | bytes 196616 | tf_op jit(solution)/shard_map/ppermute | solution.py:141
  69.9 6.1 %collective-permute-start.32 = (f32[128,128]{1,0:T(8,128)S(1)}, f32[128,128]{1,0:T(8,128)S(1)}, u32[]{:S(2)}, u32[]{:S(2)}) collective-permute-start(f32[128,128]{1,0:T(8,128)S(1)} %add.15.rest_0_), channel_id=1, source_target_pairs={{0,8},{1,9},{2,10},{3,11},{4,12},{5,13},{6,14},{7,15},{8,0},{9,1},... | collective-permute-start | bytes 196616 | tf_op jit(solution)/shard_map/ppermute | solution.py:141
  70.2 5.8 %collective-permute-start.30 = (f32[128,128]{1,0:T(8,128)S(1)}, f32[128,128]{1,0:T(8,128)S(1)}, u32[]{:S(2)}, u32[]{:S(2)}) collective-permute-start(f32[128,128]{1,0:T(8,128)S(1)} %add.15.rest_0_), channel_id=1, source_target_pairs={{0,4},{1,5},{2,6},{3,7},{4,0},{5,1},{6,2},{7,3},{8,12},{9,13},{10,... | collective-permute-start | bytes 196616 | tf_op jit(solution)/shard_map/ppermute | solution.py:141
  72.5 4.3 %collective-permute-start.29 = (f32[128,128]{1,0:T(8,128)S(1)}, f32[128,128]{1,0:T(8,128)S(1)}, u32[]{:S(2)}, u32[]{:S(2)}) collective-permute-start(f32[128,128]{1,0:T(8,128)S(1)} %add.15.rest_0_), channel_id=1, source_target_pairs={{0,2},{1,3},{2,0},{3,1},{4,6},{5,7},{6,4},{7,5},{8,10},{9,11},{10,... | collective-permute-start | bytes 196616 | tf_op jit(solution)/shard_map/ppermute | solution.py:141
  74.2 2.7 %collective-permute-start.35 = (f32[128,128]{1,0:T(8,128)S(1)}, f32[128,128]{1,0:T(8,128)S(1)}, u32[]{:S(2)}, u32[]{:S(2)}) collective-permute-start(f32[128,128]{1,0:T(8,128)S(1)} %collective-permute-done.34.rest_6_), channel_id=1, source_target_pairs={{0,2},{1,3},{2,0},{3,1},{4,6},{5,7},{6,4},{7,5},{8,10},{9,11},{10,... | collective-permute-start | bytes 196616 | tf_op jit(solution)/shard_map/ppermute | solution.py:141
  76.0 1.3 %collective-permute-start.33 = (f32[128,128]{1,0:T(8,128)S(1)}, f32[128,128]{1,0:T(8,128)S(1)}, u32[]{:S(2)}, u32[]{:S(2)}) collective-permute-start(f32[128,128]{1,0:T(8,128)S(1)} %collective-permute-done.32.rest_4_), channel_id=1, source_target_pairs={{0,2},{1,3},{2,0},{3,1},{4,6},{5,7},{6,4},{7,5},{8,10},{9,11},{10,... | collective-permute-start | bytes 196616 | tf_op jit(solution)/shard_map/ppermute | solution.py:141
  76.0 1.8 %collective-permute-start.31 = (f32[128,128]{1,0:T(8,128)S(1)}, f32[128,128]{1,0:T(8,128)S(1)}, u32[]{:S(2)}, u32[]{:S(2)}) collective-permute-start(f32[128,128]{1,0:T(8,128)S(1)} %collective-permute-done.30.rest_2_), channel_id=1, source_target_pairs={{0,2},{1,3},{2,0},{3,1},{4,6},{5,7},{6,4},{7,5},{8,10},{9,11},{10,... | collective-permute-start | bytes 196616 | tf_op jit(solution)/shard_map/ppermute | solution.py:141

commit v4 on v3

--- a/solution.py
+++ b/solution.py
@@ -150,7 +150,7 @@
     cycle += [(at(h, block(h)), at(h ^ rows_dev, block(h))) for h in range(hist)]
     across = [(at(h, 1 - block(h)), at(h ^ rows_dev, block(h))) for h in range(hist)]
     across += [(at(h, block(h)), at(h, block(h))) for h in range(hist)]
-    own = moved(part, cycle) + moved(part, across)
+    own = moved(part, across) + moved(part, cycle)
     pieces = [own] + [None] * (rows_dev - 1)
     for bits in range(2, rows_dev, 2):
         pieces[bits] = flip(own, bits)

time: 79.5 us -> 77.9 us (0.980)
  starting transfers between devices: 43.5 us -> 40.1 us
  waiting for transfers between devices: 27.8 us -> 30.2 us
    ppermute x36, starting transfers between devices: 43.5 us -> 40.1 us  [moved(): return lax.ppermute(x, ('hist', 'col'), pairs)]
    ppermute x36, waiting for transfers between devices: 27.8 us -> 30.2 us  [moved(): return lax.ppermute(x, ('hist', 'col'), pairs)]
  transfers between devices with their start and end apart: 36 -> 36, of which waited for: 13 -> 16; matrix products, arithmetic and copies ran while one was open for 0% -> 0% of each run, Pallas kernels for 0% -> 0%
where the time goes in v4:
time: 77.9 us; the launch traced here: 77.6 us
  starting transfers between devices  40.1 us (51%)
  waiting for transfers between devices  30.2 us (39%)
  Pallas kernels  5.66 us (7%)
  between operations  1.6 us (2%)
    ppermute x36, starting transfers between devices, moved(): return lax.ppermute(x, ('hist', 'col'), pairs)  40.1 us
    ppermute x36, waiting for transfers between devices, moved(): return lax.ppermute(x, ('hist', 'col'), pairs)  30.2 us
    pallas_call x1, Pallas kernels, on_device(): call(functools.partial(first_kernel, rows_dev, n, steps), [hbm] * 8, [cur...  2.55 us
    pallas_call x3, Pallas kernels, on_device(): call(functools.partial(next_kernel, section, rows_dev, n, order), [vmem]...  2.23 us
  transfers between devices with their start and end apart: 36, of which 16 were waited for; matrix products, arithmetic and copies ran while one was open for 0% of the time, Pallas kernels for 0%

profile of v4, /device:TPU:25, one launch (start us, length us, event | category | flops | bytes accessed | tf_op | source)
XLA Modules:
  0.0 77.6 jit_solution(2505158678431047713)
XLA Ops:
  1.4 2.6 %first_step.1 = (f32[8,128,128]{2,1,0:T(8,128)S(1)}, bf16[2048,256]{1,0:T(8,128)(2,1)S(1)}, f32[32,128]{1,0:T(8,128)S(1)}, f32[128,128]{1,0:T(8,128)S(1)}, bf16[...) custom-call(s32[1]{0:T(128)S(6)} %copy.10.step_hbm, s32[1]{0:T(128)S(6)} %copy.9.cutoff_hbm, f32[1024,128]{1,0:T(8,128)} %bitcast.9, ...), custom_call_target="tpu_custom_call" | custom-call | tf_op jit(solution)/shard_map/first_step/pallas_call | solution.py:188
  4.0 1.3 %collective-permute-start.1 = (f32[128,128]{1,0:T(8,128)S(1)}, f32[128,128]{1,0:T(8,128)S(1)}, u32[]{:S(2)}, u32[]{:S(2)}) collective-permute-start(f32[128,128]{1,0:T(8,128)S(1)} %get-tuple-element.22), channel_id=1, source_target_pairs={{1,0},{3,2},{5,4},{7,6},{9,8},{11,10},{13,12},{15,14},{16,17},{18,... | collective-permute-start | bytes 196616 | tf_op jit(solution)/shard_map/ppermute | solution.py:141
  5.3 1.9 %collective-permute-start = (f32[128,128]{1,0:T(8,128)S(1)}, f32[128,128]{1,0:T(8,128)S(1)}, u32[]{:S(2)}, u32[]{:S(2)}) collective-permute-start(f32[128,128]{1,0:T(8,128)S(1)} %get-tuple-element.22), channel_id=1, source_target_pairs={{1,16},{3,18},{5,20},{7,22},{9,24},{11,26},{13,28},{15,30},{16,1},... | collective-permute-start | bytes 196616 | tf_op jit(solution)/shard_map/ppermute | solution.py:141
  7.2 2.7 %collective-permute-done.1 = f32[128,128]{1,0:T(8,128)S(1)} collective-permute-done((f32[128,128]{1,0:T(8,128)S(1)}, f32[128,128]{1,0:T(8,128)S(1)}, u32[]{:S(2)}, u32[]{:S(2)}) %collective-permute-start.1) | collective-permute-done | bytes 65568 | tf_op jit(solution)/shard_map/ppermute | solution.py:141
  9.9 2.8 %collective-permute-done = f32[128,128]{1,0:T(8,128)S(1)} collective-permute-done((f32[128,128]{1,0:T(8,128)S(1)}, f32[128,128]{1,0:T(8,128)S(1)}, u32[]{:S(2)}, u32[]{:S(2)}) %collective-permute-start) | collective-permute-done | bytes 65568 | tf_op jit(solution)/shard_map/ppermute | solution.py:141
  12.8 0.6 collective-permute-start.7
  13.3 1.8 %collective-permute-start.5 = (f32[128,128]{1,0:T(8,128)S(1)}, f32[128,128]{1,0:T(8,128)S(1)}, u32[]{:S(2)}, u32[]{:S(2)}) collective-permute-start(f32[128,128]{1,0:T(8,128)S(1)} %add.12.rest_0_), channel_id=1, source_target_pairs={{0,8},{1,9},{2,10},{3,11},{4,12},{5,13},{6,14},{7,15},{8,0},{9,1},... | collective-permute-start | bytes 196616 | tf_op jit(solution)/shard_map/ppermute | solution.py:141
  15.2 0.3 collective-permute-start.3
  15.5 2.9 %collective-permute-start.2 = (f32[128,128]{1,0:T(8,128)S(1)}, f32[128,128]{1,0:T(8,128)S(1)}, u32[]{:S(2)}, u32[]{:S(2)}) collective-permute-start(f32[128,128]{1,0:T(8,128)S(1)} %add.12.rest_0_), channel_id=1, source_target_pairs={{0,2},{1,3},{2,0},{3,1},{4,6},{5,7},{6,4},{7,5},{8,10},{9,11},{10,... | collective-permute-start | bytes 196616 | tf_op jit(solution)/shard_map/ppermute | solution.py:141
  18.4 1.7 %collective-permute-start.8 = (f32[128,128]{1,0:T(8,128)S(1)}, f32[128,128]{1,0:T(8,128)S(1)}, u32[]{:S(2)}, u32[]{:S(2)}) collective-permute-start(f32[128,128]{1,0:T(8,128)S(1)} %collective-permute-done.7.rest_6_), channel_id=1, source_target_pairs={{0,2},{1,3},{2,0},{3,1},{4,6},{5,7},{6,4},{7,5},{8,10},{9,11},{10,... | collective-permute-start | bytes 196616 | tf_op jit(solution)/shard_map/ppermute | solution.py:141
  20.1 0.8 %collective-permute-start.6 = (f32[128,128]{1,0:T(8,128)S(1)}, f32[128,128]{1,0:T(8,128)S(1)}, u32[]{:S(2)}, u32[]{:S(2)}) collective-permute-start(f32[128,128]{1,0:T(8,128)S(1)} %collective-permute-done.5.rest_4_), channel_id=1, source_target_pairs={{0,2},{1,3},{2,0},{3,1},{4,6},{5,7},{6,4},{7,5},{8,10},{9,11},{10,... | collective-permute-start | bytes 196616 | tf_op jit(solution)/shard_map/ppermute | solution.py:141
  20.9 1.3 %collective-permute-start.4 = (f32[128,128]{1,0:T(8,128)S(1)}, f32[128,128]{1,0:T(8,128)S(1)}, u32[]{:S(2)}, u32[]{:S(2)}) collective-permute-start(f32[128,128]{1,0:T(8,128)S(1)} %collective-permute-done.3.rest_2_), channel_id=1, source_target_pairs={{0,2},{1,3},{2,0},{3,1},{4,6},{5,7},{6,4},{7,5},{8,10},{9,11},{10,... | collective-permute-start | bytes 196616 | tf_op jit(solution)/shard_map/ppermute | solution.py:141
  22.2 0.9 %collective-permute-done.4.rest_3_ = f32[128,128]{1,0:T(8,128)S(1)} collective-permute-done((f32[128,128]{1,0:T(8,128)S(1)}, f32[128,128]{1,0:T(8,128)S(1)}, u32[]{:S(2)}, u32[]{:S(2)}) %collective-permute-start.4) | collective-permute-done | bytes 65568 | tf_op jit(solution)/shard_map/ppermute | solution.py:141
  23.1 0.7 next_step.3
  23.9 1.9 %collective-permute-start.9 = (f32[128,128]{1,0:T(8,128)S(1)}, f32[128,128]{1,0:T(8,128)S(1)}, u32[]{:S(2)}, u32[]{:S(2)}) collective-permute-start(f32[128,128]{1,0:T(8,128)S(1)} %get-tuple-element.24), channel_id=1, source_target_pairs={{1,16},{3,18},{5,20},{7,22},{9,24},{11,26},{13,28},{15,30},{16,1},... | collective-permute-start | bytes 196616 | tf_op jit(solution)/shard_map/ppermute | solution.py:141
  25.8 4.2 %collective-permute-done.10 = f32[128,128]{1,0:T(8,128)S(1)} collective-permute-done((f32[128,128]{1,0:T(8,128)S(1)}, f32[128,128]{1,0:T(8,128)S(1)}, u32[]{:S(2)}, u32[]{:S(2)}) %collective-permute-start.10) | collective-permute-done | bytes 65568 | tf_op jit(solution)/shard_map/ppermute | solution.py:141
  30.0 2.9 %collective-permute-done.9 = f32[128,128]{1,0:T(8,128)S(1)} collective-permute-done((f32[128,128]{1,0:T(8,128)S(1)}, f32[128,128]{1,0:T(8,128)S(1)}, u32[]{:S(2)}, u32[]{:S(2)}) %collective-permute-start.9) | collective-permute-done | bytes 65568 | tf_op jit(solution)/shard_map/ppermute | solution.py:141
  33.0 1.3 %collective-permute-start.14 = (f32[128,128]{1,0:T(8,128)S(1)}, f32[128,128]{1,0:T(8,128)S(1)}, u32[]{:S(2)}, u32[]{:S(2)}) collective-permute-start(f32[128,128]{1,0:T(8,128)S(1)} %add.13.rest_0_), channel_id=1, source_target_pairs={{0,8},{1,9},{2,10},{3,11},{4,12},{5,13},{6,14},{7,15},{8,0},{9,1},... | collective-permute-start | bytes 196616 | tf_op jit(solution)/shard_map/ppermute | solution.py:141
  34.3 1.3 %collective-permute-start.12 = (f32[128,128]{1,0:T(8,128)S(1)}, f32[128,128]{1,0:T(8,128)S(1)}, u32[]{:S(2)}, u32[]{:S(2)}) collective-permute-start(f32[128,128]{1,0:T(8,128)S(1)} %add.13.rest_0_), channel_id=1, source_target_pairs={{0,4},{1,5},{2,6},{3,7},{4,0},{5,1},{6,2},{7,3},{8,12},{9,13},{10,... | collective-permute-start | bytes 196616 | tf_op jit(solution)/shard_map/ppermute | solution.py:141
  35.6 1.4 %collective-permute-start.11 = (f32[128,128]{1,0:T(8,128)S(1)}, f32[128,128]{1,0:T(8,128)S(1)}, u32[]{:S(2)}, u32[]{:S(2)}) collective-permute-start(f32[128,128]{1,0:T(8,128)S(1)} %add.13.rest_0_), channel_id=1, source_target_pairs={{0,2},{1,3},{2,0},{3,1},{4,6},{5,7},{6,4},{7,5},{8,10},{9,11},{10,... | collective-permute-start | bytes 196616 | tf_op jit(solution)/shard_map/ppermute | solution.py:141
  37.0 2.1 %collective-permute-start.17 = (f32[128,128]{1,0:T(8,128)S(1)}, f32[128,128]{1,0:T(8,128)S(1)}, u32[]{:S(2)}, u32[]{:S(2)}) collective-permute-start(f32[128,128]{1,0:T(8,128)S(1)} %collective-permute-done.16.rest_6_), channel_id=1, source_target_pairs={{0,2},{1,3},{2,0},{3,1},{4,6},{5,7},{6,4},{7,5},{8,10},{9,11},{10,... | collective-permute-start | bytes 196616 | tf_op jit(solution)/shard_map/ppermute | solution.py:141
  39.1 0.7 collective-permute-start.13
  39.8 0.2 collective-permute-done.17.rest_7_
  40.0 0.4 collective-permute-done.15.rest_5_
  40.3 0.3 collective-permute-done.13.rest_3_
  40.7 0.7 next_step.4
  41.5 1.9 %collective-permute-start.18 = (f32[128,128]{1,0:T(8,128)S(1)}, f32[128,128]{1,0:T(8,128)S(1)}, u32[]{:S(2)}, u32[]{:S(2)}) collective-permute-start(f32[128,128]{1,0:T(8,128)S(1)} %get-tuple-element.26), channel_id=1, source_target_pairs={{1,16},{3,18},{5,20},{7,22},{9,24},{11,26},{13,28},{15,30},{16,1},... | collective-permute-start | bytes 196616 | tf_op jit(solution)/shard_map/ppermute | solution.py:141
  43.4 4.1 %collective-permute-done.19 = f32[128,128]{1,0:T(8,128)S(1)} collective-permute-done((f32[128,128]{1,0:T(8,128)S(1)}, f32[128,128]{1,0:T(8,128)S(1)}, u32[]{:S(2)}, u32[]{:S(2)}) %collective-permute-start.19) | collective-permute-done | bytes 65568 | tf_op jit(solution)/shard_map/ppermute | solution.py:141
  47.5 2.9 %collective-permute-done.18 = f32[128,128]{1,0:T(8,128)S(1)} collective-permute-done((f32[128,128]{1,0:T(8,128)S(1)}, f32[128,128]{1,0:T(8,128)S(1)}, u32[]{:S(2)}, u32[]{:S(2)}) %collective-permute-start.18) | collective-permute-done | bytes 65568 | tf_op jit(solution)/shard_map/ppermute | solution.py:141
  50.4 2.5 %collective-permute-start.23 = (f32[128,128]{1,0:T(8,128)S(1)}, f32[128,128]{1,0:T(8,128)S(1)}, u32[]{:S(2)}, u32[]{:S(2)}) collective-permute-start(f32[128,128]{1,0:T(8,128)S(1)} %add.14.rest_0_), channel_id=1, source_target_pairs={{0,8},{1,9},{2,10},{3,11},{4,12},{5,13},{6,14},{7,15},{8,0},{9,1},... | collective-permute-start | bytes 196616 | tf_op jit(solution)/shard_map/ppermute | solution.py:141
  53.1 1.4 %collective-permute-start.20 = (f32[128,128]{1,0:T(8,128)S(1)}, f32[128,128]{1,0:T(8,128)S(1)}, u32[]{:S(2)}, u32[]{:S(2)}) collective-permute-start(f32[128,128]{1,0:T(8,128)S(1)} %add.14.rest_0_), channel_id=1, source_target_pairs={{0,2},{1,3},{2,0},{3,1},{4,6},{5,7},{6,4},{7,5},{8,10},{9,11},{10,... | collective-permute-start | bytes 196616 | tf_op jit(solution)/shard_map/ppermute | solution.py:141
  54.5 2.2 %collective-permute-start.26 = (f32[128,128]{1,0:T(8,128)S(1)}, f32[128,128]{1,0:T(8,128)S(1)}, u32[]{:S(2)}, u32[]{:S(2)}) collective-permute-start(f32[128,128]{1,0:T(8,128)S(1)} %collective-permute-done.25.rest_6_), channel_id=1, source_target_pairs={{0,2},{1,3},{2,0},{3,1},{4,6},{5,7},{6,4},{7,5},{8,10},{9,11},{10,... | collective-permute-start | bytes 196616 | tf_op jit(solution)/shard_map/ppermute | solution.py:141
  56.7 0.7 collective-permute-start.24
  57.4 0.9 %collective-permute-start.22 = (f32[128,128]{1,0:T(8,128)S(1)}, f32[128,128]{1,0:T(8,128)S(1)}, u32[]{:S(2)}, u32[]{:S(2)}) collective-permute-start(f32[128,128]{1,0:T(8,128)S(1)} %collective-permute-done.21.rest_2_), channel_id=1, source_target_pairs={{0,2},{1,3},{2,0},{3,1},{4,6},{5,7},{6,4},{7,5},{8,10},{9,11},{10,... | collective-permute-start | bytes 196616 | tf_op jit(solution)/shard_map/ppermute | solution.py:141
  58.3 0.9 %collective-permute-done.22.rest_3_ = f32[128,128]{1,0:T(8,128)S(1)} collective-permute-done((f32[128,128]{1,0:T(8,128)S(1)}, f32[128,128]{1,0:T(8,128)S(1)}, u32[]{:S(2)}, u32[]{:S(2)}) %collective-permute-start.22) | collective-permute-done | bytes 65568 | tf_op jit(solution)/shard_map/ppermute | solution.py:141
  59.2 0.7 next_step.5
  60.0 1.9 %collective-permute-start.27 = (f32[128,128]{1,0:T(8,128)S(1)}, f32[128,128]{1,0:T(8,128)S(1)}, u32[]{:S(2)}, u32[]{:S(2)}) collective-permute-start(f32[128,128]{1,0:T(8,128)S(1)} %get-tuple-element.28), channel_id=1, source_target_pairs={{1,16},{3,18},{5,20},{7,22},{9,24},{11,26},{13,28},{15,30},{16,1},... | collective-permute-start | bytes 196616 | tf_op jit(solution)/shard_map/ppermute | solution.py:141
  61.9 4.2 %collective-permute-done.28 = f32[128,128]{1,0:T(8,128)S(1)} collective-permute-done((f32[128,128]{1,0:T(8,128)S(1)}, f32[128,128]{1,0:T(8,128)S(1)}, u32[]{:S(2)}, u32[]{:S(2)}) %collective-permute-start.28) | collective-permute-done | bytes 65568 | tf_op jit(solution)/shard_map/ppermute | solution.py:141
  66.1 2.9 %collective-permute-done.27 = f32[128,128]{1,0:T(8,128)S(1)} collective-permute-done((f32[128,128]{1,0:T(8,128)S(1)}, f32[128,128]{1,0:T(8,128)S(1)}, u32[]{:S(2)}, u32[]{:S(2)}) %collective-permute-start.27) | collective-permute-done | bytes 65568 | tf_op jit(solution)/shard_map/ppermute | solution.py:141
  69.1 1.3 %collective-permute-start.32 = (f32[128,128]{1,0:T(8,128)S(1)}, f32[128,128]{1,0:T(8,128)S(1)}, u32[]{:S(2)}, u32[]{:S(2)}) collective-permute-start(f32[128,128]{1,0:T(8,128)S(1)} %add.15.rest_0_), channel_id=1, source_target_pairs={{0,8},{1,9},{2,10},{3,11},{4,12},{5,13},{6,14},{7,15},{8,0},{9,1},... | collective-permute-start | bytes 196616 | tf_op jit(solution)/shard_map/ppermute | solution.py:141
  70.4 1.3 %collective-permute-start.30 = (f32[128,128]{1,0:T(8,128)S(1)}, f32[128,128]{1,0:T(8,128)S(1)}, u32[]{:S(2)}, u32[]{:S(2)}) collective-permute-start(f32[128,128]{1,0:T(8,128)S(1)} %add.15.rest_0_), channel_id=1, source_target_pairs={{0,4},{1,5},{2,6},{3,7},{4,0},{5,1},{6,2},{7,3},{8,12},{9,13},{10,... | collective-permute-start | bytes 196616 | tf_op jit(solution)/shard_map/ppermute | solution.py:141
  71.7 1.4 %collective-permute-start.29 = (f32[128,128]{1,0:T(8,128)S(1)}, f32[128,128]{1,0:T(8,128)S(1)}, u32[]{:S(2)}, u32[]{:S(2)}) collective-permute-start(f32[128,128]{1,0:T(8,128)S(1)} %add.15.rest_0_), channel_id=1, source_target_pairs={{0,2},{1,3},{2,0},{3,1},{4,6},{5,7},{6,4},{7,5},{8,10},{9,11},{10,... | collective-permute-start | bytes 196616 | tf_op jit(solution)/shard_map/ppermute | solution.py:141
  73.1 2.1 %collective-permute-start.35 = (f32[128,128]{1,0:T(8,128)S(1)}, f32[128,128]{1,0:T(8,128)S(1)}, u32[]{:S(2)}, u32[]{:S(2)}) collective-permute-start(f32[128,128]{1,0:T(8,128)S(1)} %collective-permute-done.34.rest_6_), channel_id=1, source_target_pairs={{0,2},{1,3},{2,0},{3,1},{4,6},{5,7},{6,4},{7,5},{8,10},{9,11},{10,... | collective-permute-start | bytes 196616 | tf_op jit(solution)/shard_map/ppermute | solution.py:141
  75.2 0.7 collective-permute-start.31
  75.9 0.2 collective-permute-done.35.rest_7_
  76.1 0.4 collective-permute-done.33.rest_5_
  76.4 0.3 collective-permute-done.31.rest_3_
  76.8 0.9 %last_step.1 = f32[1024,128]{1,0:T(8,128)} custom-call(f32[8,128,128]{2,1,0:T(8,128)S(1)} %get-tuple-element.27.prev_ref, f32[128,128]{1,0:T(8,128)S(1)} %add.15.rest_0_, f32[128,128]{1,0:T(8,128)S(1)} %collective-permute-done.29.rest_1_, f32[128,128]{1,0:T(8,128)S(1)} %collective-permute-done.30.rest_2_, f32[128,128]{1,0:T(8,128)S(1)} %collective-permute-done.31.rest_3_, ...), custom_call_target="tpu_custom_call" | custom-call | tf_op jit(solution)/shard_map/last_step/pallas_call | solution.py:206
  (35 shorter events, 0.7 us)
Async XLA Ops:
  0.0 23.1 %copy-start = (f32[4,128,8,128]{3,2,1,0:T(8,128)S(1)}, f32[4,128,8,128]{3,2,1,0:T(8,128)}, u32[]{:S(2)}) copy-start(f32[4,128,8,128]{3,2,1,0:T(8,128)} %param.11) | copy-start | bytes 6291460
  4.0 5.9 %collective-permute-start.1 = (f32[128,128]{1,0:T(8,128)S(1)}, f32[128,128]{1,0:T(8,128)S(1)}, u32[]{:S(2)}, u32[]{:S(2)}) collective-permute-start(f32[128,128]{1,0:T(8,128)S(1)} %get-tuple-element.22), channel_id=1, source_target_pairs={{1,0},{3,2},{5,4},{7,6},{9,8},{11,10},{13,12},{15,14},{16,17},{18,... | collective-permute-start | bytes 196616 | tf_op jit(solution)/shard_map/ppermute | solution.py:141
  5.3 7.5 %collective-permute-start = (f32[128,128]{1,0:T(8,128)S(1)}, f32[128,128]{1,0:T(8,128)S(1)}, u32[]{:S(2)}, u32[]{:S(2)}) collective-permute-start(f32[128,128]{1,0:T(8,128)S(1)} %get-tuple-element.22), channel_id=1, source_target_pairs={{1,16},{3,18},{5,20},{7,22},{9,24},{11,26},{13,28},{15,30},{16,1},... | collective-permute-start | bytes 196616 | tf_op jit(solution)/shard_map/ppermute | solution.py:141
  12.8 5.6 %collective-permute-start.7 = (f32[128,128]{1,0:T(8,128)S(1)}, f32[128,128]{1,0:T(8,128)S(1)}, u32[]{:S(2)}, u32[]{:S(2)}) collective-permute-start(f32[128,128]{1,0:T(8,128)S(1)} %add.12.rest_0_), channel_id=1, source_target_pairs={{0,12},{1,13},{2,14},{3,15},{4,8},{5,9},{6,10},{7,11},{8,4},{9,5},... | collective-permute-start | bytes 196616 | tf_op jit(solution)/shard_map/ppermute | solution.py:141
  13.3 6.7 %collective-permute-start.5 = (f32[128,128]{1,0:T(8,128)S(1)}, f32[128,128]{1,0:T(8,128)S(1)}, u32[]{:S(2)}, u32[]{:S(2)}) collective-permute-start(f32[128,128]{1,0:T(8,128)S(1)} %add.12.rest_0_), channel_id=1, source_target_pairs={{0,8},{1,9},{2,10},{3,11},{4,12},{5,13},{6,14},{7,15},{8,0},{9,1},... | collective-permute-start | bytes 196616 | tf_op jit(solution)/shard_map/ppermute | solution.py:141
  15.2 5.7 %collective-permute-start.3 = (f32[128,128]{1,0:T(8,128)S(1)}, f32[128,128]{1,0:T(8,128)S(1)}, u32[]{:S(2)}, u32[]{:S(2)}) collective-permute-start(f32[128,128]{1,0:T(8,128)S(1)} %add.12.rest_0_), channel_id=1, source_target_pairs={{0,4},{1,5},{2,6},{3,7},{4,0},{5,1},{6,2},{7,3},{8,12},{9,13},{10,... | collective-permute-start | bytes 196616 | tf_op jit(solution)/shard_map/ppermute | solution.py:141
  15.5 6.7 %collective-permute-start.2 = (f32[128,128]{1,0:T(8,128)S(1)}, f32[128,128]{1,0:T(8,128)S(1)}, u32[]{:S(2)}, u32[]{:S(2)}) collective-permute-start(f32[128,128]{1,0:T(8,128)S(1)} %add.12.rest_0_), channel_id=1, source_target_pairs={{0,2},{1,3},{2,0},{3,1},{4,6},{5,7},{6,4},{7,5},{8,10},{9,11},{10,... | collective-permute-start | bytes 196616 | tf_op jit(solution)/shard_map/ppermute | solution.py:141
  18.4 3.8 %collective-permute-start.8 = (f32[128,128]{1,0:T(8,128)S(1)}, f32[128,128]{1,0:T(8,128)S(1)}, u32[]{:S(2)}, u32[]{:S(2)}) collective-permute-start(f32[128,128]{1,0:T(8,128)S(1)} %collective-permute-done.7.rest_6_), channel_id=1, source_target_pairs={{0,2},{1,3},{2,0},{3,1},{4,6},{5,7},{6,4},{7,5},{8,10},{9,11},{10,... | collective-permute-start | bytes 196616 | tf_op jit(solution)/shard_map/ppermute | solution.py:141
  20.1 2.1 %collective-permute-start.6 = (f32[128,128]{1,0:T(8,128)S(1)}, f32[128,128]{1,0:T(8,128)S(1)}, u32[]{:S(2)}, u32[]{:S(2)}) collective-permute-start(f32[128,128]{1,0:T(8,128)S(1)} %collective-permute-done.5.rest_4_), channel_id=1, source_target_pairs={{0,2},{1,3},{2,0},{3,1},{4,6},{5,7},{6,4},{7,5},{8,10},{9,11},{10,... | collective-permute-start | bytes 196616 | tf_op jit(solution)/shard_map/ppermute | solution.py:141
  20.9 2.2 %collective-permute-start.4 = (f32[128,128]{1,0:T(8,128)S(1)}, f32[128,128]{1,0:T(8,128)S(1)}, u32[]{:S(2)}, u32[]{:S(2)}) collective-permute-start(f32[128,128]{1,0:T(8,128)S(1)} %collective-permute-done.3.rest_2_), channel_id=1, source_target_pairs={{0,2},{1,3},{2,0},{3,1},{4,6},{5,7},{6,4},{7,5},{8,10},{9,11},{10,... | collective-permute-start | bytes 196616 | tf_op jit(solution)/shard_map/ppermute | solution.py:141
  23.8 6.2 %collective-permute-start.10 = (f32[128,128]{1,0:T(8,128)S(1)}, f32[128,128]{1,0:T(8,128)S(1)}, u32[]{:S(2)}, u32[]{:S(2)}) collective-permute-start(f32[128,128]{1,0:T(8,128)S(1)} %get-tuple-element.24), channel_id=1, source_target_pairs={{1,0},{3,2},{5,4},{7,6},{9,8},{11,10},{13,12},{15,14},{16,17},{18,... | collective-permute-start | bytes 196616 | tf_op jit(solution)/shard_map/ppermute | solution.py:141
  23.9 9.0 %collective-permute-start.9 = (f32[128,128]{1,0:T(8,128)S(1)}, f32[128,128]{1,0:T(8,128)S(1)}, u32[]{:S(2)}, u32[]{:S(2)}) collective-permute-start(f32[128,128]{1,0:T(8,128)S(1)} %get-tuple-element.24), channel_id=1, source_target_pairs={{1,16},{3,18},{5,20},{7,22},{9,24},{11,26},{13,28},{15,30},{16,1},... | collective-permute-start | bytes 196616 | tf_op jit(solution)/shard_map/ppermute | solution.py:141
  32.9 4.1 %collective-permute-start.16 = (f32[128,128]{1,0:T(8,128)S(1)}, f32[128,128]{1,0:T(8,128)S(1)}, u32[]{:S(2)}, u32[]{:S(2)}) collective-permute-start(f32[128,128]{1,0:T(8,128)S(1)} %add.13.rest_0_), channel_id=1, source_target_pairs={{0,12},{1,13},{2,14},{3,15},{4,8},{5,9},{6,10},{7,11},{8,4},{9,5},... | collective-permute-start | bytes 196616 | tf_op jit(solution)/shard_map/ppermute | solution.py:141
  33.0 6.1 %collective-permute-start.14 = (f32[128,128]{1,0:T(8,128)S(1)}, f32[128,128]{1,0:T(8,128)S(1)}, u32[]{:S(2)}, u32[]{:S(2)}) collective-permute-start(f32[128,128]{1,0:T(8,128)S(1)} %add.13.rest_0_), channel_id=1, source_target_pairs={{0,8},{1,9},{2,10},{3,11},{4,12},{5,13},{6,14},{7,15},{8,0},{9,1},... | collective-permute-start | bytes 196616 | tf_op jit(solution)/shard_map/ppermute | solution.py:141
  34.3 4.8 %collective-permute-start.12 = (f32[128,128]{1,0:T(8,128)S(1)}, f32[128,128]{1,0:T(8,128)S(1)}, u32[]{:S(2)}, u32[]{:S(2)}) collective-permute-start(f32[128,128]{1,0:T(8,128)S(1)} %add.13.rest_0_), channel_id=1, source_target_pairs={{0,4},{1,5},{2,6},{3,7},{4,0},{5,1},{6,2},{7,3},{8,12},{9,13},{10,... | collective-permute-start | bytes 196616 | tf_op jit(solution)/shard_map/ppermute | solution.py:141
  35.6 4.2 %collective-permute-start.11 = (f32[128,128]{1,0:T(8,128)S(1)}, f32[128,128]{1,0:T(8,128)S(1)}, u32[]{:S(2)}, u32[]{:S(2)}) collective-permute-start(f32[128,128]{1,0:T(8,128)S(1)} %add.13.rest_0_), channel_id=1, source_target_pairs={{0,2},{1,3},{2,0},{3,1},{4,6},{5,7},{6,4},{7,5},{8,10},{9,11},{10,... | collective-permute-start | bytes 196616 | tf_op jit(solution)/shard_map/ppermute | solution.py:141
  37.0 3.0 %collective-permute-start.17 = (f32[128,128]{1,0:T(8,128)S(1)}, f32[128,128]{1,0:T(8,128)S(1)}, u32[]{:S(2)}, u32[]{:S(2)}) collective-permute-start(f32[128,128]{1,0:T(8,128)S(1)} %collective-permute-done.16.rest_6_), channel_id=1, source_target_pairs={{0,2},{1,3},{2,0},{3,1},{4,6},{5,7},{6,4},{7,5},{8,10},{9,11},{10,... | collective-permute-start | bytes 196616 | tf_op jit(solution)/shard_map/ppermute | solution.py:141
  39.1 1.3 %collective-permute-start.15 = (f32[128,128]{1,0:T(8,128)S(1)}, f32[128,128]{1,0:T(8,128)S(1)}, u32[]{:S(2)}, u32[]{:S(2)}) collective-permute-start(f32[128,128]{1,0:T(8,128)S(1)} %collective-permute-done.14.rest_4_), channel_id=1, source_target_pairs={{0,2},{1,3},{2,0},{3,1},{4,6},{5,7},{6,4},{7,5},{8,10},{9,11},{10,... | collective-permute-start | bytes 196616 | tf_op jit(solution)/shard_map/ppermute | solution.py:141
  39.1 1.6 %collective-permute-start.13 = (f32[128,128]{1,0:T(8,128)S(1)}, f32[128,128]{1,0:T(8,128)S(1)}, u32[]{:S(2)}, u32[]{:S(2)}) collective-permute-start(f32[128,128]{1,0:T(8,128)S(1)} %collective-permute-done.12.rest_2_), channel_id=1, source_target_pairs={{0,2},{1,3},{2,0},{3,1},{4,6},{5,7},{6,4},{7,5},{8,10},{9,11},{10,... | collective-permute-start | bytes 196616 | tf_op jit(solution)/shard_map/ppermute | solution.py:141
  41.4 6.1 %collective-permute-start.19 = (f32[128,128]{1,0:T(8,128)S(1)}, f32[128,128]{1,0:T(8,128)S(1)}, u32[]{:S(2)}, u32[]{:S(2)}) collective-permute-start(f32[128,128]{1,0:T(8,128)S(1)} %get-tuple-element.26), channel_id=1, source_target_pairs={{1,0},{3,2},{5,4},{7,6},{9,8},{11,10},{13,12},{15,14},{16,17},{18,... | collective-permute-start | bytes 196616 | tf_op jit(solution)/shard_map/ppermute | solution.py:141
  41.5 8.9 %collective-permute-start.18 = (f32[128,128]{1,0:T(8,128)S(1)}, f32[128,128]{1,0:T(8,128)S(1)}, u32[]{:S(2)}, u32[]{:S(2)}) collective-permute-start(f32[128,128]{1,0:T(8,128)S(1)} %get-tuple-element.26), channel_id=1, source_target_pairs={{1,16},{3,18},{5,20},{7,22},{9,24},{11,26},{13,28},{15,30},{16,1},... | collective-permute-start | bytes 196616 | tf_op jit(solution)/shard_map/ppermute | solution.py:141
  50.4 4.1 %collective-permute-start.25 = (f32[128,128]{1,0:T(8,128)S(1)}, f32[128,128]{1,0:T(8,128)S(1)}, u32[]{:S(2)}, u32[]{:S(2)}) collective-permute-start(f32[128,128]{1,0:T(8,128)S(1)} %add.14.rest_0_), channel_id=1, source_target_pairs={{0,12},{1,13},{2,14},{3,15},{4,8},{5,9},{6,10},{7,11},{8,4},{9,5},... | collective-permute-start | bytes 196616 | tf_op jit(solution)/shard_map/ppermute | solution.py:141
  50.4 6.2 %collective-permute-start.23 = (f32[128,128]{1,0:T(8,128)S(1)}, f32[128,128]{1,0:T(8,128)S(1)}, u32[]{:S(2)}, u32[]{:S(2)}) collective-permute-start(f32[128,128]{1,0:T(8,128)S(1)} %add.14.rest_0_), channel_id=1, source_target_pairs={{0,8},{1,9},{2,10},{3,11},{4,12},{5,13},{6,14},{7,15},{8,0},{9,1},... | collective-permute-start | bytes 196616 | tf_op jit(solution)/shard_map/ppermute | solution.py:141
  52.9 4.4 %collective-permute-start.21 = (f32[128,128]{1,0:T(8,128)S(1)}, f32[128,128]{1,0:T(8,128)S(1)}, u32[]{:S(2)}, u32[]{:S(2)}) collective-permute-start(f32[128,128]{1,0:T(8,128)S(1)} %add.14.rest_0_), channel_id=1, source_target_pairs={{0,4},{1,5},{2,6},{3,7},{4,0},{5,1},{6,2},{7,3},{8,12},{9,13},{10,... | collective-permute-start | bytes 196616 | tf_op jit(solution)/shard_map/ppermute | solution.py:141
  53.1 5.2 %collective-permute-start.20 = (f32[128,128]{1,0:T(8,128)S(1)}, f32[128,128]{1,0:T(8,128)S(1)}, u32[]{:S(2)}, u32[]{:S(2)}) collective-permute-start(f32[128,128]{1,0:T(8,128)S(1)} %add.14.rest_0_), channel_id=1, source_target_pairs={{0,2},{1,3},{2,0},{3,1},{4,6},{5,7},{6,4},{7,5},{8,10},{9,11},{10,... | collective-permute-start | bytes 196616 | tf_op jit(solution)/shard_map/ppermute | solution.py:141
  54.5 3.8 %collective-permute-start.26 = (f32[128,128]{1,0:T(8,128)S(1)}, f32[128,128]{1,0:T(8,128)S(1)}, u32[]{:S(2)}, u32[]{:S(2)}) collective-permute-start(f32[128,128]{1,0:T(8,128)S(1)} %collective-permute-done.25.rest_6_), channel_id=1, source_target_pairs={{0,2},{1,3},{2,0},{3,1},{4,6},{5,7},{6,4},{7,5},{8,10},{9,11},{10,... | collective-permute-start | bytes 196616 | tf_op jit(solution)/shard_map/ppermute | solution.py:141
  56.7 1.6 %collective-permute-start.24 = (f32[128,128]{1,0:T(8,128)S(1)}, f32[128,128]{1,0:T(8,128)S(1)}, u32[]{:S(2)}, u32[]{:S(2)}) collective-permute-start(f32[128,128]{1,0:T(8,128)S(1)} %collective-permute-done.23.rest_4_), channel_id=1, source_target_pairs={{0,2},{1,3},{2,0},{3,1},{4,6},{5,7},{6,4},{7,5},{8,10},{9,11},{10,... | collective-permute-start | bytes 196616 | tf_op jit(solution)/shard_map/ppermute | solution.py:141
  57.4 1.8 %collective-permute-start.22 = (f32[128,128]{1,0:T(8,128)S(1)}, f32[128,128]{1,0:T(8,128)S(1)}, u32[]{:S(2)}, u32[]{:S(2)}) collective-permute-start(f32[128,128]{1,0:T(8,128)S(1)} %collective-permute-done.21.rest_2_), channel_id=1, source_target_pairs={{0,2},{1,3},{2,0},{3,1},{4,6},{5,7},{6,4},{7,5},{8,10},{9,11},{10,... | collective-permute-start | bytes 196616 | tf_op jit(solution)/shard_map/ppermute | solution.py:141
  59.9 6.2 %collective-permute-start.28 = (f32[128,128]{1,0:T(8,128)S(1)}, f32[128,128]{1,0:T(8,128)S(1)}, u32[]{:S(2)}, u32[]{:S(2)}) collective-permute-start(f32[128,128]{1,0:T(8,128)S(1)} %get-tuple-element.28), channel_id=1, source_target_pairs={{1,0},{3,2},{5,4},{7,6},{9,8},{11,10},{13,12},{15,14},{16,17},{18,... | collective-permute-start | bytes 196616 | tf_op jit(solution)/shard_map/ppermute | solution.py:141
  60.0 9.0 %collective-permute-start.27 = (f32[128,128]{1,0:T(8,128)S(1)}, f32[128,128]{1,0:T(8,128)S(1)}, u32[]{:S(2)}, u32[]{:S(2)}) collective-permute-start(f32[128,128]{1,0:T(8,128)S(1)} %get-tuple-element.28), channel_id=1, source_target_pairs={{1,16},{3,18},{5,20},{7,22},{9,24},{11,26},{13,28},{15,30},{16,1},... | collective-permute-start | bytes 196616 | tf_op jit(solution)/shard_map/ppermute | solution.py:141
  69.0 4.1 %collective-permute-start.34 = (f32[128,128]{1,0:T(8,128)S(1)}, f32[128,128]{1,0:T(8,128)S(1)}, u32[]{:S(2)}, u32[]{:S(2)}) collective-permute-start(f32[128,128]{1,0:T(8,128)S(1)} %add.15.rest_0_), channel_id=1, source_target_pairs={{0,12},{1,13},{2,14},{3,15},{4,8},{5,9},{6,10},{7,11},{8,4},{9,5},... | collective-permute-start | bytes 196616 | tf_op jit(solution)/shard_map/ppermute | solution.py:141
  69.1 6.1 %collective-permute-start.32 = (f32[128,128]{1,0:T(8,128)S(1)}, f32[128,128]{1,0:T(8,128)S(1)}, u32[]{:S(2)}, u32[]{:S(2)}) collective-permute-start(f32[128,128]{1,0:T(8,128)S(1)} %add.15.rest_0_), channel_id=1, source_target_pairs={{0,8},{1,9},{2,10},{3,11},{4,12},{5,13},{6,14},{7,15},{8,0},{9,1},... | collective-permute-start | bytes 196616 | tf_op jit(solution)/shard_map/ppermute | solution.py:141
  70.4 4.8 %collective-permute-start.30 = (f32[128,128]{1,0:T(8,128)S(1)}, f32[128,128]{1,0:T(8,128)S(1)}, u32[]{:S(2)}, u32[]{:S(2)}) collective-permute-start(f32[128,128]{1,0:T(8,128)S(1)} %add.15.rest_0_), channel_id=1, source_target_pairs={{0,4},{1,5},{2,6},{3,7},{4,0},{5,1},{6,2},{7,3},{8,12},{9,13},{10,... | collective-permute-start | bytes 196616 | tf_op jit(solution)/shard_map/ppermute | solution.py:141
  71.7 4.2 %collective-permute-start.29 = (f32[128,128]{1,0:T(8,128)S(1)}, f32[128,128]{1,0:T(8,128)S(1)}, u32[]{:S(2)}, u32[]{:S(2)}) collective-permute-start(f32[128,128]{1,0:T(8,128)S(1)} %add.15.rest_0_), channel_id=1, source_target_pairs={{0,2},{1,3},{2,0},{3,1},{4,6},{5,7},{6,4},{7,5},{8,10},{9,11},{10,... | collective-permute-start | bytes 196616 | tf_op jit(solution)/shard_map/ppermute | solution.py:141
  73.1 3.0 %collective-permute-start.35 = (f32[128,128]{1,0:T(8,128)S(1)}, f32[128,128]{1,0:T(8,128)S(1)}, u32[]{:S(2)}, u32[]{:S(2)}) collective-permute-start(f32[128,128]{1,0:T(8,128)S(1)} %collective-permute-done.34.rest_6_), channel_id=1, source_target_pairs={{0,2},{1,3},{2,0},{3,1},{4,6},{5,7},{6,4},{7,5},{8,10},{9,11},{10,... | collective-permute-start | bytes 196616 | tf_op jit(solution)/shard_map/ppermute | solution.py:141
  75.2 1.3 %collective-permute-start.33 = (f32[128,128]{1,0:T(8,128)S(1)}, f32[128,128]{1,0:T(8,128)S(1)}, u32[]{:S(2)}, u32[]{:S(2)}) collective-permute-start(f32[128,128]{1,0:T(8,128)S(1)} %collective-permute-done.32.rest_4_), channel_id=1, source_target_pairs={{0,2},{1,3},{2,0},{3,1},{4,6},{5,7},{6,4},{7,5},{8,10},{9,11},{10,... | collective-permute-start | bytes 196616 | tf_op jit(solution)/shard_map/ppermute | solution.py:141
  75.2 1.6 %collective-permute-start.31 = (f32[128,128]{1,0:T(8,128)S(1)}, f32[128,128]{1,0:T(8,128)S(1)}, u32[]{:S(2)}, u32[]{:S(2)}) collective-permute-start(f32[128,128]{1,0:T(8,128)S(1)} %collective-permute-done.30.rest_2_), channel_id=1, source_target_pairs={{0,2},{1,3},{2,0},{3,1},{4,6},{5,7},{6,4},{7,5},{8,10},{9,11},{10,... | collective-permute-start | bytes 196616 | tf_op jit(solution)/shard_map/ppermute | solution.py:141

commit v5 on v0

v5 whole, which is shorter than its diff:
```python
import functools

import jax
import jax.numpy as jnp
from jax import lax
from jax.experimental import pallas as pl
from jax.experimental.pallas import tpu as pltpu
from jax.sharding import PartitionSpec as P

STEP_SIZE = 0.2
PRECISE = lax.Precision.HIGHEST
BF16 = jnp.bfloat16
F32 = jnp.float32
VMEM_BYTES = 12 * 2**20


def split(x):
    high = x.astype(BF16)
    return high, (x - high.astype(F32)).astype(BF16)


def tall(x):
    return jnp.concatenate(split(x), axis=0)


def wide(x):
    return jnp.concatenate(split(x), axis=1)


def product(rows, columns):
    m, n = rows.shape[0] // 2, columns.shape[1] // 2
    both = jnp.dot(rows, columns, preferred_element_type=F32)
    return both[:m, :n] + (both[:m, n:] + both[m:, :n])


def places(rows_dev):
    hist_pos = lax.axis_index("hist")
    return lax.rem(hist_pos, rows_dev), lax.rem(hist_pos, 2), lax.axis_index("col")


def every(first, s, half, rows_dev):
    return pl.ds(first * rows_dev + s, half, stride=rows_dev)


def sigmas(section, rows_dev, half, core, cur, g_ref, g_first, active_ref, strength_ref, sigma_ref):
    n = 2 * half
    strength = strength_ref[...]
    for s in range(rows_dev):
        x = cur[s]
        g = g_ref[every(g_first + core * half, s, half, rows_dev), :]
        u = strength * x * g
        less = -(u * x)
        ret = (u * x - u * g) * active_ref[pl.ds(section * rows_dev + s, 1), :]
        for where, value in ((s, ret), (rows_dev + s, less)):
            sigma_ref[:, where * n : (where + 1) * n] = tall(value)


def split_tables(rows_dev, n, col_pos, cutoff, lesser_ref, adv_ref, wide_ref):
    for s in range(rows_dev):
        inside = jnp.where(col_pos * rows_dev + s < cutoff, 1.0, 0.0).astype(F32)
        wide_ref[s * n : (s + 1) * n, :] = wide(lesser_ref[s * n : (s + 1) * n, :])
        wide_ref[(rows_dev + s) * n : (rows_dev + s + 1) * n, :] = wide(adv_ref[s * n : (s + 1) * n, :] * inside)


def first_kernel(rows_dev, half, steps, limits_ref, lesser_hbm, adv_hbm, first_hbm, greater_hbm, coup_hbm, ham_hbm,
                 cur_ref, wide_ref, active_ref, strength_ref, ham_ref, turned_ref, sigma_ref, own_ref,
                 lesser_ref, adv_ref, first_ref, g_ref, h_ref, sems):
    n = 2 * half
    own_row, core, col_pos = places(rows_dev)
    mine, other = core * half, (1 - core) * half
    rows = pl.ds(pl.multiple_of(mine, half), half)
    copies = [
        pltpu.make_async_copy(source, target, sems.at[k])
        for k, (source, target) in enumerate((
            (coup_hbm.at[rows], strength_ref),
            (ham_hbm.at[rows], h_ref),
            (first_hbm, first_ref),
            (greater_hbm.at[pl.ds(0, rows_dev * n)], g_ref),
            (lesser_hbm, lesser_ref),
            (adv_hbm, adv_ref),
        ))
    ]
    for copy in copies:
        copy.start()
    start, cutoff = limits_ref[0:1, :], limits_ref[1:2, :]
    for q in range(steps):
        for s in range(rows_dev):
            active_ref[q * rows_dev + s : q * rows_dev + s + 1, :] = jnp.where(
                col_pos * rows_dev + s < start + q, 1.0, 0.0
            ).astype(F32)
    for copy in copies[:4]:
        copy.wait()
    strength_ref[...] = strength_ref[...] * strength_ref[...]
    ham = h_ref[...]
    ham = tall(jnp.where(core == 0, ham, pltpu.roll(ham, half, 1)))
    ham_ref[...] = ham
    for s in range(rows_dev):
        cur_ref[s] = first_ref[every(mine, s, half, rows_dev), :]
    sigmas(0, rows_dev, half, core, cur_ref, g_ref, 0, active_ref, strength_ref, sigma_ref)
    for j in range(2):
        s = jnp.bitwise_xor(own_row, j)
        whole = jnp.concatenate(
            [first_ref[every(mine, s, half, rows_dev), :], first_ref[every(other, s, half, rows_dev), :]], axis=0
        )
        turned_ref[j * half : (j + 1) * half, :] = product(ham, wide(whole))
    for copy in copies[4:]:
        copy.wait()
    split_tables(rows_dev, n, col_pos, cutoff, lesser_ref, adv_ref, wide_ref)
    own_ref[...] = product(sigma_ref[...], wide_ref[...])


def second_kernel(rows_dev, half, limits_ref, lesser_ref, adv_ref, sigma_ref, own_ref, wide_ref, part_ref):
    col_pos = lax.axis_index("col")
    split_tables(rows_dev, 2 * half, col_pos, limits_ref[1:2, :], lesser_ref, adv_ref, wide_ref)
    part_ref[:half, :] = own_ref[...]
    part_ref[half:, :] = product(sigma_ref[...], wide_ref[...])


def next_kernel(section, rows_dev, half, prev_ref, greater_ref, active_ref, strength_ref, own_wide_ref, other_wide_ref, *rest):
    pieces, (cur_ref, mine_ref, part_ref, sigma_ref) = rest[: rows_dev // 2], rest[rows_dev // 2 :]
    own_row, core, _ = places(rows_dev)
    for k, piece in enumerate(pieces):
        for j in range(2):
            s = jnp.bitwise_xor(own_row, 2 * k + j)
            new = prev_ref[s] - STEP_SIZE * piece[j * half : (j + 1) * half, :]
            cur_ref[s] = new
            if k == 0:
                mine_ref[j * half : (j + 1) * half, :] = new
    sigmas(section, rows_dev, half, core, cur_ref, greater_ref, section * 2 * half, active_ref, strength_ref, sigma_ref)
    part_ref[:half, :] = product(sigma_ref[...], own_wide_ref[...])
    part_ref[half:, :] = product(sigma_ref[...], other_wide_ref[...])


def turn_kernel(half, ham_ref, mine_ref, other_ref, turned_ref):
    ham = ham_ref[...]
    for j in range(2):
        whole = jnp.concatenate(
            [mine_ref[j * half : (j + 1) * half, :], other_ref[(1 - j) * half : (2 - j) * half, :]], axis=0
        )
        turned_ref[j * half : (j + 1) * half, :] = product(ham, wide(whole))


def last_kernel(rows_dev, half, *refs):
    count = rows_dev // 2
    own_row, core, _ = places(rows_dev)
    out_hbm, out_ref, sems = refs[-3:]
    copies = []
    for away in range(2):
        prev_ref, pieces = refs[away], refs[2 + away * count : 2 + (away + 1) * count]
        side = jnp.bitwise_xor(core, away) * half
        for k, piece in enumerate(pieces):
            for j in range(2):
                s = jnp.bitwise_xor(own_row, (2 * k + j) ^ away)
                new = prev_ref[s] - STEP_SIZE * piece[j * half : (j + 1) * half, :]
                out_ref[every(side, s, half, rows_dev), :] = new
        flat = pl.ds(pl.multiple_of(side * rows_dev, half * rows_dev), half * rows_dev)
        copies.append(pltpu.make_async_copy(out_ref.at[flat], out_hbm.at[flat], sems.at[away]))
        copies[-1].start()
    for copy in copies:
        copy.wait()


def call(kernel, ins, outs, scratch, name):
    return pl.pallas_call(
        kernel,
        out_shape=[shape for shape, _ in outs],
        in_specs=[pl.BlockSpec(memory_space=space) for space in ins],
        out_specs=[pl.BlockSpec(memory_space=space) for _, space in outs],
        scratch_shapes=scratch,
        compiler_params=pltpu.CompilerParams(vmem_limit_bytes=VMEM_BYTES),
        name=name,
    )


def in_pairs(hist, lesser, advanced, first_row, greater_rows, hamiltonian, coupling, cutoff, step_index):
    rows_dev, n = lesser.shape[:2]
    steps, half = greater_rows.shape[0], n // 2
    flat = (rows_dev * n, n)
    shape, vmem, hbm = jax.ShapeDtypeStruct, pltpu.VMEM, pltpu.HBM

    def at(h, c):
        return h * 2 + c

    def block(h):
        return h // rows_dev

    def moved(x, pairs):
        return lax.ppermute(x, ("hist", "col"), pairs)

    def flip(x, bits):
        return moved(x, [(at(h, c), at(h ^ bits, c)) for h in range(hist) for c in range(2)])

    cycle = [(at(h, 1 - block(h)), at(h, block(h))) for h in range(hist)]
    cycle += [(at(h, block(h)), at(h ^ rows_dev, block(h))) for h in range(hist)]
    across = [(at(h, 1 - block(h)), at(h ^ rows_dev, block(h))) for h in range(hist)]
    across += [(at(h, block(h)), at(h, block(h))) for h in range(hist)]

    def exchange(part, turned):
        own = moved(part, across) + moved(part, cycle) + turned
        return [own] + [flip(own, bits) for bits in range(2, rows_dev, 2)]

    def out(dims, kind=F32):
        return shape(dims, kind), vmem

    greater = greater_rows.reshape(steps * rows_dev * n, n)
    tables = lesser.reshape(flat), advanced.reshape(flat)
    limits = jnp.broadcast_to(jnp.concatenate([step_index, cutoff])[:, None], (2, n))
    cur_out, pair_out, wide_out = out((rows_dev, half, n)), out((n, n)), out((2 * rows_dev * n, 2 * n), BF16)
    sigma = (n, 2 * rows_dev * n)
    current, own_wide, active, strength, ham, turned, first_sigma, own_part = call(
        functools.partial(first_kernel, rows_dev, half, steps),
        [vmem] + [hbm] * 6,
        [cur_out, wide_out, out((steps * rows_dev, n)), out((half, n)), out((n, n), BF16), pair_out, out(sigma, BF16), out((half, n))],
        [vmem(flat, F32)] * 4 + [vmem((half, n), F32), pltpu.SemaphoreType.DMA((6,))],
        "first_step",
    )(limits, *[
        pltpu.with_memory_space_constraint(x, hbm)
        for x in (*tables, first_row.reshape(flat), greater, coupling, hamiltonian)
    ])
    other_wide, part = call(
        functools.partial(second_kernel, rows_dev, half),
        [vmem] * 5, [wide_out, pair_out], [], "first_step_other",
    )(flip(limits, 1), *[flip(x, 1) for x in tables], first_sigma, own_part)
    for section in range(1, steps):
        pieces = exchange(part, turned)
        current, mine, part = call(
            functools.partial(next_kernel, section, rows_dev, half),
            [vmem] * (6 + rows_dev // 2), [cur_out, pair_out, pair_out], [vmem(sigma, BF16)], "next_step",
        )(current, greater, active, strength, own_wide, other_wide, *pieces)
        turned = call(functools.partial(turn_kernel, half), [vmem] * 3, [pair_out], [], "turn")(ham, mine, flip(mine, 1))[0]
    pieces = exchange(part, turned)
    final = call(
        functools.partial(last_kernel, rows_dev, half),
        [vmem] * (2 + rows_dev), [(shape(flat, F32), hbm)], [vmem(flat, F32), pltpu.SemaphoreType.DMA((2,))], "last_step",
    )(current, flip(current, 1), *pieces, *[flip(x, 1) for x in pieces])[0]
    return final.reshape(first_row.shape)


def in_general(lesser, advanced, first_row, greater_rows, hamiltonian, coupling, cutoff, step_index):
    rows_dev, orbitals, cols_dev, _ = lesser.shape
    row_times = lax.axis_index("col") * rows_dev + jnp.arange(rows_dev, dtype=jnp.int32)
    inside = (row_times[:, None] < cutoff[None, :]).astype(F32)
    adv_flat = (advanced * inside[:, None, :, None]).reshape(rows_dev * orbitals, cols_dev * orbitals)
    hist_flat = lesser.reshape(rows_dev * orbitals, cols_dev * orbitals)
    propagator = jnp.eye(orbitals, dtype=F32) - STEP_SIZE * hamiltonian
    strength = (coupling * coupling)[:, None, :]
    current = first_row
    for section in range(greater_rows.shape[0]):
        greater = greater_rows[section]
        sigma_less = -strength * current * current * greater
        sigma_ret = -strength * greater * greater * current - sigma_less
        active = (row_times < step_index[0] + section).astype(F32)
        ret_flat = (sigma_ret * active[None, :, None]).reshape(orbitals, rows_dev * orbitals)
        less_flat = sigma_less.reshape(orbitals, rows_dev * orbitals)
        memory = jnp.dot(ret_flat, hist_flat, precision=PRECISE, preferred_element_type=F32)
        memory = memory + jnp.dot(less_flat, adv_flat, precision=PRECISE, preferred_element_type=F32)
        share = lax.psum_scatter(memory.reshape(orbitals, cols_dev, orbitals), "col", scatter_dimension=0, tiled=True)
        spread = lax.all_gather(share, "hist", axis=1, tiled=True)
        memory_block = lax.all_to_all(spread, "col", split_axis=1, concat_axis=0, tiled=True)
        moved = jnp.einsum("ik,ksj->isj", propagator, current, precision=PRECISE)
        current = moved - STEP_SIZE * memory_block
    return current


def solution(mesh):
    hist, cols = mesh.shape["hist"], mesh.shape["col"]

    def on_device(lesser, *rest):
        rows_dev, _, cols_dev, _ = lesser.shape
        if cols == 2 and cols_dev == 1 and hist == 2 * rows_dev and hist & (hist - 1) == 0 and rows_dev > 1:
            return in_pairs(hist, lesser, *rest)
        return in_general(lesser, *rest)

    in_specs = (
        P("col", None, "hist", None),
        P("col", None, "hist", None),
        P(None, "col", None),
        P(None, None, "col", None),
        P(),
        P(),
        P("hist"),
        P(),
    )
    return jax.shard_map(on_device, mesh=mesh, in_specs=in_specs, out_specs=P(None, "col", None), check_vma=False)
```

time: 212 us -> 75.5 us (0.36)
  the two profiles are of different devices: /device:TPU:0 before, /device:TPU:25 now
where the time goes in v5:
time: 75.5 us; the launch traced here: 74.7 us
  waiting for transfers between devices  37.5 us (50%)
  starting transfers between devices  29.8 us (39%)
  Pallas kernels  5.71 us (8%)
  between operations  1.5 us (2%)
    ppermute x31, waiting for transfers between devices, moved(): return lax.ppermute(x, ('hist', 'col'), pairs)  37.5 us
    ppermute x31, starting transfers between devices, moved(): return lax.ppermute(x, ('hist', 'col'), pairs)  29.8 us
    pallas_call x1, Pallas kernels, in_pairs(): call(functools.partial(first_kernel, rows_dev, half, steps), [vmem] + [hb...  2.27 us
    pallas_call x3, Pallas kernels, in_pairs(): call(functools.partial(next_kernel, section, rows_dev, half), [vmem] * (6...  1.63 us
  transfers between devices with their start and end apart: 31, of which 20 were waited for; matrix products, arithmetic and copies ran while one was open for 0% of the time, Pallas kernels for 4%

profile of v5, /device:TPU:25, one launch (start us, length us, event | category | flops | bytes accessed | tf_op | source)
XLA Modules:
  0.0 74.7 jit_solution(11902473809987161150)
XLA Ops:
  0.0 0.7 collective-permute-start.1
  2.1 0.5 collective-permute-start
  2.6 2.3 %first_step.1 = (f32[8,64,128]{2,1,0:T(8,128)S(1)}, bf16[2048,256]{1,0:T(8,128)(2,1)S(1)}, f32[32,128]{1,0:T(8,128)S(1)}, f32[64,128]{1,0:T(8,128)S(1)}, bf16[12...) custom-call(s32[2,128]{1,0:T(2,128)S(1)} %broadcast_in_dim.2.limits_ref, ...), custom_call_target="tpu_custom_call" | custom-call | tf_op jit(solution)/shard_map/first_step/pallas_call | solution.py:210
  4.9 0.3 first_step_other.1
  5.3 1.3 %collective-permute-start.4 = (f32[128,128]{1,0:T(8,128)S(1)}, f32[128,128]{1,0:T(8,128)S(1)}, u32[]{:S(2)}, u32[]{:S(2)}) collective-permute-start(f32[128,128]{1,0:T(8,128)S(1)} %get-tuple-element.31), channel_id=1, source_target_pairs={{1,0},{3,2},{5,4},{7,6},{9,8},{11,10},{13,12},{15,14},{16,17},{18,... | collective-permute-start | bytes 196616 | tf_op jit(solution)/shard_map/ppermute | solution.py:188
  6.6 1.9 %collective-permute-start.3 = (f32[128,128]{1,0:T(8,128)S(1)}, f32[128,128]{1,0:T(8,128)S(1)}, u32[]{:S(2)}, u32[]{:S(2)}) collective-permute-start(f32[128,128]{1,0:T(8,128)S(1)} %get-tuple-element.31), channel_id=1, source_target_pairs={{1,16},{3,18},{5,20},{7,22},{9,24},{11,26},{13,28},{15,30},{16,1},... | collective-permute-start | bytes 196616 | tf_op jit(solution)/shard_map/ppermute | solution.py:188
  8.5 3.1 %collective-permute-done.4 = f32[128,128]{1,0:T(8,128)S(1)} collective-permute-done((f32[128,128]{1,0:T(8,128)S(1)}, f32[128,128]{1,0:T(8,128)S(1)}, u32[]{:S(2)}, u32[]{:S(2)}) %collective-permute-start.4) | collective-permute-done | bytes 65568 | tf_op jit(solution)/shard_map/ppermute | solution.py:188
  11.6 4.0 %collective-permute-done.3 = f32[128,128]{1,0:T(8,128)S(1)} collective-permute-done((f32[128,128]{1,0:T(8,128)S(1)}, f32[128,128]{1,0:T(8,128)S(1)}, u32[]{:S(2)}, u32[]{:S(2)}) %collective-permute-start.3) | collective-permute-done | bytes 65568 | tf_op jit(solution)/shard_map/ppermute | solution.py:188
  15.7 2.4 %collective-permute-start.6 = (f32[128,128]{1,0:T(8,128)S(1)}, f32[128,128]{1,0:T(8,128)S(1)}, u32[]{:S(2)}, u32[]{:S(2)}) collective-permute-start(f32[128,128]{1,0:T(8,128)S(1)} %add_add_fusion.3.rest_0_), channel_id=1, source_target_pairs={{0,8},{1,9},{2,10},{3,11},{4,12},{5,13},{6,14},{7,15},{8,0},{9,1},... | collective-permute-start | bytes 196616 | tf_op jit(solution)/shard_map/ppermute | solution.py:188
  18.1 0.2 collective-permute-start.5
  18.4 1.4 %collective-permute-done.7.rest_3_ = f32[128,128]{1,0:T(8,128)S(1)} collective-permute-done((f32[128,128]{1,0:T(8,128)S(1)}, f32[128,128]{1,0:T(8,128)S(1)}, u32[]{:S(2)}, u32[]{:S(2)}) %collective-permute-start.7) | collective-permute-done | bytes 65568 | tf_op jit(solution)/shard_map/ppermute | solution.py:188
  19.7 1.5 %collective-permute-done.6.rest_2_ = f32[128,128]{1,0:T(8,128)S(1)} collective-permute-done((f32[128,128]{1,0:T(8,128)S(1)}, f32[128,128]{1,0:T(8,128)S(1)}, u32[]{:S(2)}, u32[]{:S(2)}) %collective-permute-start.6) | collective-permute-done | bytes 65568 | tf_op jit(solution)/shard_map/ppermute | solution.py:188
  21.2 0.8 %collective-permute-done.5.rest_1_ = f32[128,128]{1,0:T(8,128)S(1)} collective-permute-done((f32[128,128]{1,0:T(8,128)S(1)}, f32[128,128]{1,0:T(8,128)S(1)}, u32[]{:S(2)}, u32[]{:S(2)}) %collective-permute-start.5) | collective-permute-done | bytes 65568 | tf_op jit(solution)/shard_map/ppermute | solution.py:188
  22.0 0.5 next_step.3
  22.5 1.6 %collective-permute-start.10 = (f32[128,128]{1,0:T(8,128)S(1)}, f32[128,128]{1,0:T(8,128)S(1)}, u32[]{:S(2)}, u32[]{:S(2)}) collective-permute-start(f32[128,128]{1,0:T(8,128)S(1)} %get-tuple-element.36.mine_ref), channel_id=1, source_target_pairs={{0,2},{1,3},{2,0},{3,1},{4,6},{5,7},{6,4},{7,5},{8,10},{9,11},{10,... | collective-permute-start | bytes 196616 | tf_op jit(solution)/shard_map/ppermute | solution.py:188
  24.1 1.9 %collective-permute-start.8 = (f32[128,128]{1,0:T(8,128)S(1)}, f32[128,128]{1,0:T(8,128)S(1)}, u32[]{:S(2)}, u32[]{:S(2)}) collective-permute-start(f32[128,128]{1,0:T(8,128)S(1)} %get-tuple-element.34), channel_id=1, source_target_pairs={{1,16},{3,18},{5,20},{7,22},{9,24},{11,26},{13,28},{15,30},{16,1},... | collective-permute-start | bytes 196616 | tf_op jit(solution)/shard_map/ppermute | solution.py:188
  26.0 0.2 turn.3
  26.2 3.7 %collective-permute-done.9 = f32[128,128]{1,0:T(8,128)S(1)} collective-permute-done((f32[128,128]{1,0:T(8,128)S(1)}, f32[128,128]{1,0:T(8,128)S(1)}, u32[]{:S(2)}, u32[]{:S(2)}) %collective-permute-start.9) | collective-permute-done | bytes 65568 | tf_op jit(solution)/shard_map/ppermute | solution.py:188
  29.9 2.8 %collective-permute-done.8 = f32[128,128]{1,0:T(8,128)S(1)} collective-permute-done((f32[128,128]{1,0:T(8,128)S(1)}, f32[128,128]{1,0:T(8,128)S(1)}, u32[]{:S(2)}, u32[]{:S(2)}) %collective-permute-start.8) | collective-permute-done | bytes 65568 | tf_op jit(solution)/shard_map/ppermute | solution.py:188
  32.8 1.5 %collective-permute-start.12 = (f32[128,128]{1,0:T(8,128)S(1)}, f32[128,128]{1,0:T(8,128)S(1)}, u32[]{:S(2)}, u32[]{:S(2)}) collective-permute-start(f32[128,128]{1,0:T(8,128)S(1)} %add_add_fusion.2.rest_0_), channel_id=1, source_target_pairs={{0,8},{1,9},{2,10},{3,11},{4,12},{5,13},{6,14},{7,15},{8,0},{9,1},... | collective-permute-start | bytes 196616 | tf_op jit(solution)/shard_map/ppermute | solution.py:188
  34.4 1.1 %collective-permute-start.11 = (f32[128,128]{1,0:T(8,128)S(1)}, f32[128,128]{1,0:T(8,128)S(1)}, u32[]{:S(2)}, u32[]{:S(2)}) collective-permute-start(f32[128,128]{1,0:T(8,128)S(1)} %add_add_fusion.2.rest_0_), channel_id=1, source_target_pairs={{0,4},{1,5},{2,6},{3,7},{4,0},{5,1},{6,2},{7,3},{8,12},{9,13},{10,... | collective-permute-start | bytes 196616 | tf_op jit(solution)/shard_map/ppermute | solution.py:188
  35.5 1.4 %collective-permute-done.13.rest_3_ = f32[128,128]{1,0:T(8,128)S(1)} collective-permute-done((f32[128,128]{1,0:T(8,128)S(1)}, f32[128,128]{1,0:T(8,128)S(1)}, u32[]{:S(2)}, u32[]{:S(2)}) %collective-permute-start.13) | collective-permute-done | bytes 65568 | tf_op jit(solution)/shard_map/ppermute | solution.py:188
  36.9 0.6 collective-permute-done.12.rest_2_
  37.5 0.8 %collective-permute-done.11.rest_1_ = f32[128,128]{1,0:T(8,128)S(1)} collective-permute-done((f32[128,128]{1,0:T(8,128)S(1)}, f32[128,128]{1,0:T(8,128)S(1)}, u32[]{:S(2)}, u32[]{:S(2)}) %collective-permute-start.11) | collective-permute-done | bytes 65568 | tf_op jit(solution)/shard_map/ppermute | solution.py:188
  38.3 0.5 next_step.4
  38.8 1.5 %collective-permute-start.16 = (f32[128,128]{1,0:T(8,128)S(1)}, f32[128,128]{1,0:T(8,128)S(1)}, u32[]{:S(2)}, u32[]{:S(2)}) collective-permute-start(f32[128,128]{1,0:T(8,128)S(1)} %get-tuple-element.39.mine_ref), channel_id=1, source_target_pairs={{0,2},{1,3},{2,0},{3,1},{4,6},{5,7},{6,4},{7,5},{8,10},{9,11},{10,... | collective-permute-start | bytes 196616 | tf_op jit(solution)/shard_map/ppermute | solution.py:188
  40.3 1.9 %collective-permute-start.14 = (f32[128,128]{1,0:T(8,128)S(1)}, f32[128,128]{1,0:T(8,128)S(1)}, u32[]{:S(2)}, u32[]{:S(2)}) collective-permute-start(f32[128,128]{1,0:T(8,128)S(1)} %get-tuple-element.38), channel_id=1, source_target_pairs={{1,16},{3,18},{5,20},{7,22},{9,24},{11,26},{13,28},{15,30},{16,1},... | collective-permute-start | bytes 196616 | tf_op jit(solution)/shard_map/ppermute | solution.py:188
  42.4 3.7 %collective-permute-done.15 = f32[128,128]{1,0:T(8,128)S(1)} collective-permute-done((f32[128,128]{1,0:T(8,128)S(1)}, f32[128,128]{1,0:T(8,128)S(1)}, u32[]{:S(2)}, u32[]{:S(2)}) %collective-permute-start.15) | collective-permute-done | bytes 65568 | tf_op jit(solution)/shard_map/ppermute | solution.py:188
  46.1 2.8 %collective-permute-done.14 = f32[128,128]{1,0:T(8,128)S(1)} collective-permute-done((f32[128,128]{1,0:T(8,128)S(1)}, f32[128,128]{1,0:T(8,128)S(1)}, u32[]{:S(2)}, u32[]{:S(2)}) %collective-permute-start.14) | collective-permute-done | bytes 65568 | tf_op jit(solution)/shard_map/ppermute | solution.py:188
  49.1 2.3 %collective-permute-start.18 = (f32[128,128]{1,0:T(8,128)S(1)}, f32[128,128]{1,0:T(8,128)S(1)}, u32[]{:S(2)}, u32[]{:S(2)}) collective-permute-start(f32[128,128]{1,0:T(8,128)S(1)} %add_add_fusion.1.rest_0_), channel_id=1, source_target_pairs={{0,8},{1,9},{2,10},{3,11},{4,12},{5,13},{6,14},{7,15},{8,0},{9,1},... | collective-permute-start | bytes 196616 | tf_op jit(solution)/shard_map/ppermute | solution.py:188
  51.3 0.4 collective-permute-start.17
  51.7 1.4 %collective-permute-done.19.rest_3_ = f32[128,128]{1,0:T(8,128)S(1)} collective-permute-done((f32[128,128]{1,0:T(8,128)S(1)}, f32[128,128]{1,0:T(8,128)S(1)}, u32[]{:S(2)}, u32[]{:S(2)}) %collective-permute-start.19) | collective-permute-done | bytes 65568 | tf_op jit(solution)/shard_map/ppermute | solution.py:188
  53.1 1.4 %collective-permute-done.18.rest_2_ = f32[128,128]{1,0:T(8,128)S(1)} collective-permute-done((f32[128,128]{1,0:T(8,128)S(1)}, f32[128,128]{1,0:T(8,128)S(1)}, u32[]{:S(2)}, u32[]{:S(2)}) %collective-permute-start.18) | collective-permute-done | bytes 65568 | tf_op jit(solution)/shard_map/ppermute | solution.py:188
  54.4 0.8 %collective-permute-done.17.rest_1_ = f32[128,128]{1,0:T(8,128)S(1)} collective-permute-done((f32[128,128]{1,0:T(8,128)S(1)}, f32[128,128]{1,0:T(8,128)S(1)}, u32[]{:S(2)}, u32[]{:S(2)}) %collective-permute-start.17) | collective-permute-done | bytes 65568 | tf_op jit(solution)/shard_map/ppermute | solution.py:188
  55.2 0.5 next_step.5
  55.8 1.5 %collective-permute-start.23 = (f32[128,128]{1,0:T(8,128)S(1)}, f32[128,128]{1,0:T(8,128)S(1)}, u32[]{:S(2)}, u32[]{:S(2)}) collective-permute-start(f32[128,128]{1,0:T(8,128)S(1)} %get-tuple-element.42.mine_ref), channel_id=1, source_target_pairs={{0,2},{1,3},{2,0},{3,1},{4,6},{5,7},{6,4},{7,5},{8,10},{9,11},{10,... | collective-permute-start | bytes 196616 | tf_op jit(solution)/shard_map/ppermute | solution.py:188
  57.3 1.9 %collective-permute-start.21 = (f32[128,128]{1,0:T(8,128)S(1)}, f32[128,128]{1,0:T(8,128)S(1)}, u32[]{:S(2)}, u32[]{:S(2)}) collective-permute-start(f32[128,128]{1,0:T(8,128)S(1)} %get-tuple-element.41), channel_id=1, source_target_pairs={{1,16},{3,18},{5,20},{7,22},{9,24},{11,26},{13,28},{15,30},{16,1},... | collective-permute-start | bytes 196616 | tf_op jit(solution)/shard_map/ppermute | solution.py:188
  59.4 0.2 turn.5
  59.5 3.5 %collective-permute-done.22 = f32[128,128]{1,0:T(8,128)S(1)} collective-permute-done((f32[128,128]{1,0:T(8,128)S(1)}, f32[128,128]{1,0:T(8,128)S(1)}, u32[]{:S(2)}, u32[]{:S(2)}) %collective-permute-start.22) | collective-permute-done | bytes 65568 | tf_op jit(solution)/shard_map/ppermute | solution.py:188
  63.1 2.8 %collective-permute-done.21 = f32[128,128]{1,0:T(8,128)S(1)} collective-permute-done((f32[128,128]{1,0:T(8,128)S(1)}, f32[128,128]{1,0:T(8,128)S(1)}, u32[]{:S(2)}, u32[]{:S(2)}) %collective-permute-start.21) | collective-permute-done | bytes 65568 | tf_op jit(solution)/shard_map/ppermute | solution.py:188
  66.0 1.5 %collective-permute-start.25 = (f32[128,128]{1,0:T(8,128)S(1)}, f32[128,128]{1,0:T(8,128)S(1)}, u32[]{:S(2)}, u32[]{:S(2)}) collective-permute-start(f32[128,128]{1,0:T(8,128)S(1)} %add_add_fusion.refs_2_), channel_id=1, source_target_pairs={{0,8},{1,9},{2,10},{3,11},{4,12},{5,13},{6,14},{7,15},{8,0},{9,1},... | collective-permute-start | bytes 196616 | tf_op jit(solution)/shard_map/ppermute | solution.py:188
  67.6 1.1 %collective-permute-start.24 = (f32[128,128]{1,0:T(8,128)S(1)}, f32[128,128]{1,0:T(8,128)S(1)}, u32[]{:S(2)}, u32[]{:S(2)}) collective-permute-start(f32[128,128]{1,0:T(8,128)S(1)} %add_add_fusion.refs_2_), channel_id=1, source_target_pairs={{0,4},{1,5},{2,6},{3,7},{4,0},{5,1},{6,2},{7,3},{8,12},{9,13},{10,... | collective-permute-start | bytes 196616 | tf_op jit(solution)/shard_map/ppermute | solution.py:188
  68.7 1.3 %collective-permute-start.27 = (f32[128,128]{1,0:T(8,128)S(1)}, f32[128,128]{1,0:T(8,128)S(1)}, u32[]{:S(2)}, u32[]{:S(2)}) collective-permute-start(f32[128,128]{1,0:T(8,128)S(1)} %add_add_fusion.refs_2_), channel_id=1, source_target_pairs={{0,2},{1,3},{2,0},{3,1},{4,6},{5,7},{6,4},{7,5},{8,10},{9,11},{10,... | collective-permute-start | bytes 196616 | tf_op jit(solution)/shard_map/ppermute | solution.py:188
  70.0 2.1 %collective-permute-start.30 = (f32[128,128]{1,0:T(8,128)S(1)}, f32[128,128]{1,0:T(8,128)S(1)}, u32[]{:S(2)}, u32[]{:S(2)}) collective-permute-start(f32[128,128]{1,0:T(8,128)S(1)} %collective-permute-done.26.refs_5_), channel_id=1, source_target_pairs={{0,2},{1,3},{2,0},{3,1},{4,6},{5,7},{6,4},{7,5},{8,10},{9,11},{10,... | collective-permute-start | bytes 196616 | tf_op jit(solution)/shard_map/ppermute | solution.py:188
  72.1 0.8 %collective-permute-start.28 = (f32[128,128]{1,0:T(8,128)S(1)}, f32[128,128]{1,0:T(8,128)S(1)}, u32[]{:S(2)}, u32[]{:S(2)}) collective-permute-start(f32[128,128]{1,0:T(8,128)S(1)} %collective-permute-done.24.refs_3_), channel_id=1, source_target_pairs={{0,2},{1,3},{2,0},{3,1},{4,6},{5,7},{6,4},{7,5},{8,10},{9,11},{10,... | collective-permute-start | bytes 196616 | tf_op jit(solution)/shard_map/ppermute | solution.py:188
  73.0 0.4 collective-permute-done.29.refs_8_
  73.4 0.4 collective-permute-done.28.refs_7_
  73.8 0.9 %last_step.1 = f32[1024,128]{1,0:T(8,128)} custom-call(f32[8,64,128]{2,1,0:T(8,128)S(1)} %get-tuple-element.40.refs_0_, f32[8,64,128]{2,1,0:T(8,128)S(1)} %collective-permute-done.20.refs_1_, f32[128,128]{1,0:T(8,128)S(1)} %add_add_fusion.refs_2_, f32[128,128]{1,0:T(8,128)S(1)} %collective-permute-done.24.refs_3_, ...), custom_call_target="tpu_custom_call" | custom-call | tf_op jit(solution)/shard_map/last_step/pallas_call | solution.py:232
  (31 shorter events, 1.0 us)
Async XLA Ops:
  0.0 4.9 %collective-permute-start.1 = (f32[1024,128]{1,0:T(8,128)}, f32[1024,128]{1,0:T(8,128)S(1)}, u32[]{:S(2)}, u32[]{:S(2)}) collective-permute-start(f32[1024,128]{1,0:T(8,128)} %bitcast.10), channel_id=1, source_target_pairs={{0,2},{1,3},{2,0},{3,1},{4,6},{5,7},{6,4},{7,5},{8,10},{9,11},{10,... | collective-permute-start | bytes 1572872 | tf_op jit(solution)/shard_map/ppermute | solution.py:188
  0.7 4.3 %collective-permute-start.2 = (f32[1024,128]{1,0:T(8,128)}, f32[1024,128]{1,0:T(8,128)S(1)}, u32[]{:S(2)}, u32[]{:S(2)}) collective-permute-start(f32[1024,128]{1,0:T(8,128)} %bitcast.12), channel_id=1, source_target_pairs={{0,2},{1,3},{2,0},{3,1},{4,6},{5,7},{6,4},{7,5},{8,10},{9,11},{10,... | collective-permute-start | bytes 1572872 | tf_op jit(solution)/shard_map/ppermute | solution.py:188
  2.1 2.8 %collective-permute-start = (s32[2,128]{1,0:T(2,128)S(1)}, s32[2,128]{1,0:T(2,128)S(1)}, u32[]{:S(2)}, u32[]{:S(2)}) collective-permute-start(s32[2,128]{1,0:T(2,128)S(1)} %broadcast_in_dim.2.limits_ref), channel_id=1, source_target_pairs={{0,2},{1,3},{2,0},{3,1},{4,6},{5,7},{6,4},{7,5},{8,10},{9,11},{10,... | collective-permute-start | bytes 3080 | tf_op jit(solution)/shard_map/ppermute | solution.py:188
  2.6 19.3 %copy-start = (f32[4,128,8,128]{3,2,1,0:T(8,128)S(1)}, f32[4,128,8,128]{3,2,1,0:T(8,128)}, u32[]{:S(2)}) copy-start(f32[4,128,8,128]{3,2,1,0:T(8,128)} %param.11) | copy-start | bytes 6291460
  5.3 6.3 %collective-permute-start.4 = (f32[128,128]{1,0:T(8,128)S(1)}, f32[128,128]{1,0:T(8,128)S(1)}, u32[]{:S(2)}, u32[]{:S(2)}) collective-permute-start(f32[128,128]{1,0:T(8,128)S(1)} %get-tuple-element.31), channel_id=1, source_target_pairs={{1,0},{3,2},{5,4},{7,6},{9,8},{11,10},{13,12},{15,14},{16,17},{18,... | collective-permute-start | bytes 196616 | tf_op jit(solution)/shard_map/ppermute | solution.py:188
  6.6 9.1 %collective-permute-start.3 = (f32[128,128]{1,0:T(8,128)S(1)}, f32[128,128]{1,0:T(8,128)S(1)}, u32[]{:S(2)}, u32[]{:S(2)}) collective-permute-start(f32[128,128]{1,0:T(8,128)S(1)} %get-tuple-element.31), channel_id=1, source_target_pairs={{1,16},{3,18},{5,20},{7,22},{9,24},{11,26},{13,28},{15,30},{16,1},... | collective-permute-start | bytes 196616 | tf_op jit(solution)/shard_map/ppermute | solution.py:188
  15.6 4.1 %collective-permute-start.7 = (f32[128,128]{1,0:T(8,128)S(1)}, f32[128,128]{1,0:T(8,128)S(1)}, u32[]{:S(2)}, u32[]{:S(2)}) collective-permute-start(f32[128,128]{1,0:T(8,128)S(1)} %add_add_fusion.3.rest_0_), channel_id=1, source_target_pairs={{0,12},{1,13},{2,14},{3,15},{4,8},{5,9},{6,10},{7,11},{8,4},{9,5},... | collective-permute-start | bytes 196616 | tf_op jit(solution)/shard_map/ppermute | solution.py:188
  15.7 5.5 %collective-permute-start.6 = (f32[128,128]{1,0:T(8,128)S(1)}, f32[128,128]{1,0:T(8,128)S(1)}, u32[]{:S(2)}, u32[]{:S(2)}) collective-permute-start(f32[128,128]{1,0:T(8,128)S(1)} %add_add_fusion.3.rest_0_), channel_id=1, source_target_pairs={{0,8},{1,9},{2,10},{3,11},{4,12},{5,13},{6,14},{7,15},{8,0},{9,1},... | collective-permute-start | bytes 196616 | tf_op jit(solution)/shard_map/ppermute | solution.py:188
  18.1 3.8 %collective-permute-start.5 = (f32[128,128]{1,0:T(8,128)S(1)}, f32[128,128]{1,0:T(8,128)S(1)}, u32[]{:S(2)}, u32[]{:S(2)}) collective-permute-start(f32[128,128]{1,0:T(8,128)S(1)} %add_add_fusion.3.rest_0_), channel_id=1, source_target_pairs={{0,4},{1,5},{2,6},{3,7},{4,0},{5,1},{6,2},{7,3},{8,12},{9,13},{10,... | collective-permute-start | bytes 196616 | tf_op jit(solution)/shard_map/ppermute | solution.py:188
  22.5 3.5 %collective-permute-start.10 = (f32[128,128]{1,0:T(8,128)S(1)}, f32[128,128]{1,0:T(8,128)S(1)}, u32[]{:S(2)}, u32[]{:S(2)}) collective-permute-start(f32[128,128]{1,0:T(8,128)S(1)} %get-tuple-element.36.mine_ref), channel_id=1, source_target_pairs={{0,2},{1,3},{2,0},{3,1},{4,6},{5,7},{6,4},{7,5},{8,10},{9,11},{10,... | collective-permute-start | bytes 196616 | tf_op jit(solution)/shard_map/ppermute | solution.py:188
  24.1 5.8 %collective-permute-start.9 = (f32[128,128]{1,0:T(8,128)S(1)}, f32[128,128]{1,0:T(8,128)S(1)}, u32[]{:S(2)}, u32[]{:S(2)}) collective-permute-start(f32[128,128]{1,0:T(8,128)S(1)} %get-tuple-element.34), channel_id=1, source_target_pairs={{1,0},{3,2},{5,4},{7,6},{9,8},{11,10},{13,12},{15,14},{16,17},{18,... | collective-permute-start | bytes 196616 | tf_op jit(solution)/shard_map/ppermute | solution.py:188
  24.1 8.6 %collective-permute-start.8 = (f32[128,128]{1,0:T(8,128)S(1)}, f32[128,128]{1,0:T(8,128)S(1)}, u32[]{:S(2)}, u32[]{:S(2)}) collective-permute-start(f32[128,128]{1,0:T(8,128)S(1)} %get-tuple-element.34), channel_id=1, source_target_pairs={{1,16},{3,18},{5,20},{7,22},{9,24},{11,26},{13,28},{15,30},{16,1},... | collective-permute-start | bytes 196616 | tf_op jit(solution)/shard_map/ppermute | solution.py:188
  32.8 4.1 %collective-permute-start.13 = (f32[128,128]{1,0:T(8,128)S(1)}, f32[128,128]{1,0:T(8,128)S(1)}, u32[]{:S(2)}, u32[]{:S(2)}) collective-permute-start(f32[128,128]{1,0:T(8,128)S(1)} %add_add_fusion.2.rest_0_), channel_id=1, source_target_pairs={{0,12},{1,13},{2,14},{3,15},{4,8},{5,9},{6,10},{7,11},{8,4},{9,5},... | collective-permute-start | bytes 196616 | tf_op jit(solution)/shard_map/ppermute | solution.py:188
  32.8 4.6 %collective-permute-start.12 = (f32[128,128]{1,0:T(8,128)S(1)}, f32[128,128]{1,0:T(8,128)S(1)}, u32[]{:S(2)}, u32[]{:S(2)}) collective-permute-start(f32[128,128]{1,0:T(8,128)S(1)} %add_add_fusion.2.rest_0_), channel_id=1, source_target_pairs={{0,8},{1,9},{2,10},{3,11},{4,12},{5,13},{6,14},{7,15},{8,0},{9,1},... | collective-permute-start | bytes 196616 | tf_op jit(solution)/shard_map/ppermute | solution.py:188
  34.4 3.9 %collective-permute-start.11 = (f32[128,128]{1,0:T(8,128)S(1)}, f32[128,128]{1,0:T(8,128)S(1)}, u32[]{:S(2)}, u32[]{:S(2)}) collective-permute-start(f32[128,128]{1,0:T(8,128)S(1)} %add_add_fusion.2.rest_0_), channel_id=1, source_target_pairs={{0,4},{1,5},{2,6},{3,7},{4,0},{5,1},{6,2},{7,3},{8,12},{9,13},{10,... | collective-permute-start | bytes 196616 | tf_op jit(solution)/shard_map/ppermute | solution.py:188
  38.8 3.4 %collective-permute-start.16 = (f32[128,128]{1,0:T(8,128)S(1)}, f32[128,128]{1,0:T(8,128)S(1)}, u32[]{:S(2)}, u32[]{:S(2)}) collective-permute-start(f32[128,128]{1,0:T(8,128)S(1)} %get-tuple-element.39.mine_ref), channel_id=1, source_target_pairs={{0,2},{1,3},{2,0},{3,1},{4,6},{5,7},{6,4},{7,5},{8,10},{9,11},{10,... | collective-permute-start | bytes 196616 | tf_op jit(solution)/shard_map/ppermute | solution.py:188
  40.3 5.8 %collective-permute-start.15 = (f32[128,128]{1,0:T(8,128)S(1)}, f32[128,128]{1,0:T(8,128)S(1)}, u32[]{:S(2)}, u32[]{:S(2)}) collective-permute-start(f32[128,128]{1,0:T(8,128)S(1)} %get-tuple-element.38), channel_id=1, source_target_pairs={{1,0},{3,2},{5,4},{7,6},{9,8},{11,10},{13,12},{15,14},{16,17},{18,... | collective-permute-start | bytes 196616 | tf_op jit(solution)/shard_map/ppermute | solution.py:188
  40.3 8.7 %collective-permute-start.14 = (f32[128,128]{1,0:T(8,128)S(1)}, f32[128,128]{1,0:T(8,128)S(1)}, u32[]{:S(2)}, u32[]{:S(2)}) collective-permute-start(f32[128,128]{1,0:T(8,128)S(1)} %get-tuple-element.38), channel_id=1, source_target_pairs={{1,16},{3,18},{5,20},{7,22},{9,24},{11,26},{13,28},{15,30},{16,1},... | collective-permute-start | bytes 196616 | tf_op jit(solution)/shard_map/ppermute | solution.py:188
  49.0 4.1 %collective-permute-start.19 = (f32[128,128]{1,0:T(8,128)S(1)}, f32[128,128]{1,0:T(8,128)S(1)}, u32[]{:S(2)}, u32[]{:S(2)}) collective-permute-start(f32[128,128]{1,0:T(8,128)S(1)} %add_add_fusion.1.rest_0_), channel_id=1, source_target_pairs={{0,12},{1,13},{2,14},{3,15},{4,8},{5,9},{6,10},{7,11},{8,4},{9,5},... | collective-permute-start | bytes 196616 | tf_op jit(solution)/shard_map/ppermute | solution.py:188
  49.1 5.4 %collective-permute-start.18 = (f32[128,128]{1,0:T(8,128)S(1)}, f32[128,128]{1,0:T(8,128)S(1)}, u32[]{:S(2)}, u32[]{:S(2)}) collective-permute-start(f32[128,128]{1,0:T(8,128)S(1)} %add_add_fusion.1.rest_0_), channel_id=1, source_target_pairs={{0,8},{1,9},{2,10},{3,11},{4,12},{5,13},{6,14},{7,15},{8,0},{9,1},... | collective-permute-start | bytes 196616 | tf_op jit(solution)/shard_map/ppermute | solution.py:188
  51.3 3.9 %collective-permute-start.17 = (f32[128,128]{1,0:T(8,128)S(1)}, f32[128,128]{1,0:T(8,128)S(1)}, u32[]{:S(2)}, u32[]{:S(2)}) collective-permute-start(f32[128,128]{1,0:T(8,128)S(1)} %add_add_fusion.1.rest_0_), channel_id=1, source_target_pairs={{0,4},{1,5},{2,6},{3,7},{4,0},{5,1},{6,2},{7,3},{8,12},{9,13},{10,... | collective-permute-start | bytes 196616 | tf_op jit(solution)/shard_map/ppermute | solution.py:188
  55.8 3.6 %collective-permute-start.23 = (f32[128,128]{1,0:T(8,128)S(1)}, f32[128,128]{1,0:T(8,128)S(1)}, u32[]{:S(2)}, u32[]{:S(2)}) collective-permute-start(f32[128,128]{1,0:T(8,128)S(1)} %get-tuple-element.42.mine_ref), channel_id=1, source_target_pairs={{0,2},{1,3},{2,0},{3,1},{4,6},{5,7},{6,4},{7,5},{8,10},{9,11},{10,... | collective-permute-start | bytes 196616 | tf_op jit(solution)/shard_map/ppermute | solution.py:188
  57.3 5.8 %collective-permute-start.22 = (f32[128,128]{1,0:T(8,128)S(1)}, f32[128,128]{1,0:T(8,128)S(1)}, u32[]{:S(2)}, u32[]{:S(2)}) collective-permute-start(f32[128,128]{1,0:T(8,128)S(1)} %get-tuple-element.41), channel_id=1, source_target_pairs={{1,0},{3,2},{5,4},{7,6},{9,8},{11,10},{13,12},{15,14},{16,17},{18,... | collective-permute-start | bytes 196616 | tf_op jit(solution)/shard_map/ppermute | solution.py:188
  57.3 8.6 %collective-permute-start.21 = (f32[128,128]{1,0:T(8,128)S(1)}, f32[128,128]{1,0:T(8,128)S(1)}, u32[]{:S(2)}, u32[]{:S(2)}) collective-permute-start(f32[128,128]{1,0:T(8,128)S(1)} %get-tuple-element.41), channel_id=1, source_target_pairs={{1,16},{3,18},{5,20},{7,22},{9,24},{11,26},{13,28},{15,30},{16,1},... | collective-permute-start | bytes 196616 | tf_op jit(solution)/shard_map/ppermute | solution.py:188
  59.2 14.6 %collective-permute-start.20 = (f32[8,64,128]{2,1,0:T(8,128)S(1)}, f32[8,64,128]{2,1,0:T(8,128)S(1)}, u32[]{:S(2)}, u32[]{:S(2)}) collective-permute-start(f32[8,64,128]{2,1,0:T(8,128)S(1)} %get-tuple-element.40.refs_0_), channel_id=1, source_target_pairs={{0,2},{1,3},{2,0},{3,1},{4,6},{5,7},{6,4},{7,5},{8,10},{9,11},{10,... | collective-permute-start | bytes 786440 | tf_op jit(solution)/shard_map/ppermute | solution.py:188
  66.0 4.1 %collective-permute-start.26 = (f32[128,128]{1,0:T(8,128)S(1)}, f32[128,128]{1,0:T(8,128)S(1)}, u32[]{:S(2)}, u32[]{:S(2)}) collective-permute-start(f32[128,128]{1,0:T(8,128)S(1)} %add_add_fusion.refs_2_), channel_id=1, source_target_pairs={{0,12},{1,13},{2,14},{3,15},{4,8},{5,9},{6,10},{7,11},{8,4},{9,5},... | collective-permute-start | bytes 196616 | tf_op jit(solution)/shard_map/ppermute | solution.py:188
  66.0 6.1 %collective-permute-start.25 = (f32[128,128]{1,0:T(8,128)S(1)}, f32[128,128]{1,0:T(8,128)S(1)}, u32[]{:S(2)}, u32[]{:S(2)}) collective-permute-start(f32[128,128]{1,0:T(8,128)S(1)} %add_add_fusion.refs_2_), channel_id=1, source_target_pairs={{0,8},{1,9},{2,10},{3,11},{4,12},{5,13},{6,14},{7,15},{8,0},{9,1},... | collective-permute-start | bytes 196616 | tf_op jit(solution)/shard_map/ppermute | solution.py:188
  67.6 4.6 %collective-permute-start.24 = (f32[128,128]{1,0:T(8,128)S(1)}, f32[128,128]{1,0:T(8,128)S(1)}, u32[]{:S(2)}, u32[]{:S(2)}) collective-permute-start(f32[128,128]{1,0:T(8,128)S(1)} %add_add_fusion.refs_2_), channel_id=1, source_target_pairs={{0,4},{1,5},{2,6},{3,7},{4,0},{5,1},{6,2},{7,3},{8,12},{9,13},{10,... | collective-permute-start | bytes 196616 | tf_op jit(solution)/shard_map/ppermute | solution.py:188
  68.7 4.2 %collective-permute-start.27 = (f32[128,128]{1,0:T(8,128)S(1)}, f32[128,128]{1,0:T(8,128)S(1)}, u32[]{:S(2)}, u32[]{:S(2)}) collective-permute-start(f32[128,128]{1,0:T(8,128)S(1)} %add_add_fusion.refs_2_), channel_id=1, source_target_pairs={{0,2},{1,3},{2,0},{3,1},{4,6},{5,7},{6,4},{7,5},{8,10},{9,11},{10,... | collective-permute-start | bytes 196616 | tf_op jit(solution)/shard_map/ppermute | solution.py:188
  70.0 3.0 %collective-permute-start.30 = (f32[128,128]{1,0:T(8,128)S(1)}, f32[128,128]{1,0:T(8,128)S(1)}, u32[]{:S(2)}, u32[]{:S(2)}) collective-permute-start(f32[128,128]{1,0:T(8,128)S(1)} %collective-permute-done.26.refs_5_), channel_id=1, source_target_pairs={{0,2},{1,3},{2,0},{3,1},{4,6},{5,7},{6,4},{7,5},{8,10},{9,11},{10,... | collective-permute-start | bytes 196616 | tf_op jit(solution)/shard_map/ppermute | solution.py:188
  72.1 1.3 %collective-permute-start.29 = (f32[128,128]{1,0:T(8,128)S(1)}, f32[128,128]{1,0:T(8,128)S(1)}, u32[]{:S(2)}, u32[]{:S(2)}) collective-permute-start(f32[128,128]{1,0:T(8,128)S(1)} %collective-permute-done.25.refs_4_), channel_id=1, source_target_pairs={{0,2},{1,3},{2,0},{3,1},{4,6},{5,7},{6,4},{7,5},{8,10},{9,11},{10,... | collective-permute-start | bytes 196616 | tf_op jit(solution)/shard_map/ppermute | solution.py:188
  72.1 1.7 %collective-permute-start.28 = (f32[128,128]{1,0:T(8,128)S(1)}, f32[128,128]{1,0:T(8,128)S(1)}, u32[]{:S(2)}, u32[]{:S(2)}) collective-permute-start(f32[128,128]{1,0:T(8,128)S(1)} %collective-permute-done.24.refs_3_), channel_id=1, source_target_pairs={{0,2},{1,3},{2,0},{3,1},{4,6},{5,7},{6,4},{7,5},{8,10},{9,11},{10,... | collective-permute-start | bytes 196616 | tf_op jit(solution)/shard_map/ppermute | solution.py:188

commit v6 on v5

--- a/solution.py
+++ b/solution.py
@@ -62,8 +62,13 @@
         wide_ref[(rows_dev + s) * n : (rows_dev + s + 1) * n, :] = wide(adv_ref[s * n : (s + 1) * n, :] * inside)
 
 
+def turn(half, ham_ref, near_ref, turned_ref):
+    for j in range(2):
+        turned_ref[j * half : (j + 1) * half, :] = product(ham_ref[...], wide(near_ref[j]))
+
+
 def first_kernel(rows_dev, half, steps, limits_ref, lesser_hbm, adv_hbm, first_hbm, greater_hbm, coup_hbm, ham_hbm,
-                 cur_ref, wide_ref, active_ref, strength_ref, ham_ref, turned_ref, sigma_ref, own_ref,
+                 cur_ref, wide_ref, active_ref, strength_ref, ham_ref, near_ref, turned_ref, sigma_ref, own_ref,
                  lesser_ref, adv_ref, first_ref, g_ref, h_ref, sems):
     n = 2 * half
     own_row, core, col_pos = places(rows_dev)
@@ -99,10 +104,9 @@
     sigmas(0, rows_dev, half, core, cur_ref, g_ref, 0, active_ref, strength_ref, sigma_ref)
     for j in range(2):
         s = jnp.bitwise_xor(own_row, j)
-        whole = jnp.concatenate(
-            [first_ref[every(mine, s, half, rows_dev), :], first_ref[every(other, s, half, rows_dev), :]], axis=0
-        )
-        turned_ref[j * half : (j + 1) * half, :] = product(ham, wide(whole))
+        near_ref[j, :half, :] = first_ref[every(mine, s, half, rows_dev), :]
+        near_ref[j, half:, :] = first_ref[every(other, s, half, rows_dev), :]
+    turn(half, ham_ref, near_ref, turned_ref)
     for copy in copies[4:]:
         copy.wait()
     split_tables(rows_dev, n, col_pos, cutoff, lesser_ref, adv_ref, wide_ref)
@@ -116,28 +120,20 @@
     part_ref[half:, :] = product(sigma_ref[...], wide_ref[...])
 
 
-def next_kernel(section, rows_dev, half, prev_ref, greater_ref, active_ref, strength_ref, own_wide_ref, other_wide_ref, *rest):
-    pieces, (cur_ref, mine_ref, part_ref, sigma_ref) = rest[: rows_dev // 2], rest[rows_dev // 2 :]
+def next_kernel(section, rows_dev, half, prev_ref, prev_near_ref, greater_ref, active_ref, strength_ref, own_wide_ref, other_wide_ref, *rest):
+    own_ref, swapped_ref, *others = rest[: rows_dev // 2 + 1]
+    cur_ref, near_ref, part_ref, sigma_ref = rest[rows_dev // 2 + 1 :]
     own_row, core, _ = places(rows_dev)
-    for k, piece in enumerate(pieces):
+    for k, piece in enumerate([own_ref] + others):
         for j in range(2):
             s = jnp.bitwise_xor(own_row, 2 * k + j)
-            new = prev_ref[s] - STEP_SIZE * piece[j * half : (j + 1) * half, :]
-            cur_ref[s] = new
-            if k == 0:
-                mine_ref[j * half : (j + 1) * half, :] = new
+            cur_ref[s] = prev_ref[s] - STEP_SIZE * piece[j * half : (j + 1) * half, :]
+    for j in range(2):
+        near_ref[j, :half, :] = prev_near_ref[j, :half, :] - STEP_SIZE * own_ref[j * half : (j + 1) * half, :]
+        near_ref[j, half:, :] = prev_near_ref[j, half:, :] - STEP_SIZE * swapped_ref[(1 - j) * half : (2 - j) * half, :]
     sigmas(section, rows_dev, half, core, cur_ref, greater_ref, section * 2 * half, active_ref, strength_ref, sigma_ref)
     part_ref[:half, :] = product(sigma_ref[...], own_wide_ref[...])
     part_ref[half:, :] = product(sigma_ref[...], other_wide_ref[...])
-
-
-def turn_kernel(half, ham_ref, mine_ref, other_ref, turned_ref):
-    ham = ham_ref[...]
-    for j in range(2):
-        whole = jnp.concatenate(
-            [mine_ref[j * half : (j + 1) * half, :], other_ref[(1 - j) * half : (2 - j) * half, :]], axis=0
-        )
-        turned_ref[j * half : (j + 1) * half, :] = product(ham, wide(whole))
 
 
 def last_kernel(rows_dev, half, *refs):
@@ -197,7 +193,7 @@
 
     def exchange(part, turned):
         own = moved(part, across) + moved(part, cycle) + turned
-        return [own] + [flip(own, bits) for bits in range(2, rows_dev, 2)]
+        return [own, flip(own, 1)] + [flip(own, bits) for bits in range(2, rows_dev, 2)]
 
     def out(dims, kind=F32):
         return shape(dims, kind), vmem
@@ -205,12 +201,13 @@
     greater = greater_rows.reshape(steps * rows_dev * n, n)
     tables = lesser.reshape(flat), advanced.reshape(flat)
     limits = jnp.broadcast_to(jnp.concatenate([step_index, cutoff])[:, None], (2, n))
+    near_out = out((2, n, n))
     cur_out, pair_out, wide_out = out((rows_dev, half, n)), out((n, n)), out((2 * rows_dev * n, 2 * n), BF16)
     sigma = (n, 2 * rows_dev * n)
-    current, own_wide, active, strength, ham, turned, first_sigma, own_part = call(
+    current, own_wide, active, strength, ham, near, turned, first_sigma, own_part = call(
         functools.partial(first_kernel, rows_dev, half, steps),
         [vmem] + [hbm] * 6,
-        [cur_out, wide_out, out((steps * rows_dev, n)), out((half, n)), out((n, n), BF16), pair_out, out(sigma, BF16), out((half, n))],
+        [cur_out, wide_out, out((steps * rows_dev, n)), out((half, n)), out((n, n), BF16), near_out, pair_out, out(sigma, BF16), out((half, n))],
         [vmem(flat, F32)] * 4 + [vmem((half, n), F32), pltpu.SemaphoreType.DMA((6,))],
         "first_step",
     )(limits, *[
@@ -223,16 +220,17 @@
     )(flip(limits, 1), *[flip(x, 1) for x in tables], first_sigma, own_part)
     for section in range(1, steps):
         pieces = exchange(part, turned)
-        current, mine, part = call(
+        current, near, part = call(
             functools.partial(next_kernel, section, rows_dev, half),
-            [vmem] * (6 + rows_dev // 2), [cur_out, pair_out, pair_out], [vmem(sigma, BF16)], "next_step",
-        )(current, greater, active, strength, own_wide, other_wide, *pieces)
-        turned = call(functools.partial(turn_kernel, half), [vmem] * 3, [pair_out], [], "turn")(ham, mine, flip(mine, 1))[0]
+            [vmem] * (8 + rows_dev // 2), [cur_out, near_out, pair_out], [vmem(sigma, BF16)], "next_step",
+        )(current, near, greater, active, strength, own_wide, other_wide, *pieces)
+        turned = call(functools.partial(turn, half), [vmem] * 2, [pair_out], [], "turn")(ham, near)[0]
     pieces = exchange(part, turned)
+    own, swapped = [pieces[0]] + pieces[2:], pieces[1]
     final = call(
         functools.partial(last_kernel, rows_dev, half),
         [vmem] * (2 + rows_dev), [(shape(flat, F32), hbm)], [vmem(flat, F32), pltpu.SemaphoreType.DMA((2,))], "last_step",
-    )(current, flip(current, 1), *pieces, *[flip(x, 1) for x in pieces])[0]
+    )(current, flip(current, 1), *own, swapped, *[flip(x, 1) for x in own[1:]])[0]
     return final.reshape(first_row.shape)
 
 

time: 75.5 us -> 72.4 us (0.959)
  waiting for transfers between devices: 37.5 us -> 23.9 us
  starting transfers between devices: 29.8 us -> 40.5 us
    ppermute x31, waiting for transfers between devices: 37.5 us -> 23.9 us  [moved(): return lax.ppermute(x, ('hist', 'col'), pairs)]
    ppermute x31, starting transfers between devices: 29.8 us -> 40.5 us  [moved(): return lax.ppermute(x, ('hist', 'col'), pairs)]
  transfers between devices with their start and end apart: 31 -> 31, of which waited for: 20 -> 13; matrix products, arithmetic and copies ran while one was open for 0% -> 0% of each run, Pallas kernels for 4% -> 4%
where the time goes in v6:
time: 72.4 us; the launch traced here: 71.8 us
  starting transfers between devices  40.5 us (56%)
  waiting for transfers between devices  23.9 us (33%)
  Pallas kernels  5.75 us (8%)
  between operations  1.51 us (2%)
    ppermute x31, starting transfers between devices, moved(): return lax.ppermute(x, ('hist', 'col'), pairs)  40.5 us
    ppermute x31, waiting for transfers between devices, moved(): return lax.ppermute(x, ('hist', 'col'), pairs)  23.9 us
    pallas_call x1, Pallas kernels, in_pairs(): call(functools.partial(first_kernel, rows_dev, half, steps), [vmem] + [hb...  2.24 us
    pallas_call x3, Pallas kernels, in_pairs(): call(functools.partial(next_kernel, section, rows_dev, half), [vmem] * (8...  1.71 us
  transfers between devices with their start and end apart: 31, of which 13 were waited for; matrix products, arithmetic and copies ran while one was open for 0% of the time, Pallas kernels for 4%

profile of v6, /device:TPU:25, one launch (start us, length us, event | category | flops | bytes accessed | tf_op | source)
XLA Modules:
  0.0 71.8 jit_solution(13708918527513317627)
XLA Ops:
  0.0 0.7 collective-permute-start.1
  2.0 0.1 pad_add_fusion
  2.1 0.1 broadcast_in_dim.2.limits_ref
  2.1 0.5 collective-permute-start
  2.6 2.2 %first_step.1 = (f32[8,64,128]{2,1,0:T(8,128)S(1)}, bf16[2048,256]{1,0:T(8,128)(2,1)S(1)}, f32[32,128]{1,0:T(8,128)S(1)}, f32[64,128]{1,0:T(8,128)S(1)}, bf16[12...) custom-call(s32[2,128]{1,0:T(2,128)S(1)} %broadcast_in_dim.2.limits_, ...), custom_call_target="tpu_custom_call" | custom-call | tf_op jit(solution)/shard_map/first_step/pallas_call | solution.py:207
  4.9 0.4 first_step_other.1
  5.3 1.3 %collective-permute-start.4 = (f32[128,128]{1,0:T(8,128)S(1)}, f32[128,128]{1,0:T(8,128)S(1)}, u32[]{:S(2)}, u32[]{:S(2)}) collective-permute-start(f32[128,128]{1,0:T(8,128)S(1)} %get-tuple-element.33), channel_id=1, source_target_pairs={{1,0},{3,2},{5,4},{7,6},{9,8},{11,10},{13,12},{15,14},{16,17},{18,... | collective-permute-start | bytes 196616 | tf_op jit(solution)/shard_map/ppermute | solution.py:184
  6.5 1.9 %collective-permute-start.3 = (f32[128,128]{1,0:T(8,128)S(1)}, f32[128,128]{1,0:T(8,128)S(1)}, u32[]{:S(2)}, u32[]{:S(2)}) collective-permute-start(f32[128,128]{1,0:T(8,128)S(1)} %get-tuple-element.33), channel_id=1, source_target_pairs={{1,16},{3,18},{5,20},{7,22},{9,24},{11,26},{13,28},{15,30},{16,1},... | collective-permute-start | bytes 196616 | tf_op jit(solution)/shard_map/ppermute | solution.py:184
  8.5 3.1 %collective-permute-done.4 = f32[128,128]{1,0:T(8,128)S(1)} collective-permute-done((f32[128,128]{1,0:T(8,128)S(1)}, f32[128,128]{1,0:T(8,128)S(1)}, u32[]{:S(2)}, u32[]{:S(2)}) %collective-permute-start.4) | collective-permute-done | bytes 65568 | tf_op jit(solution)/shard_map/ppermute | solution.py:184
  11.6 4.0 %collective-permute-done.3 = f32[128,128]{1,0:T(8,128)S(1)} collective-permute-done((f32[128,128]{1,0:T(8,128)S(1)}, f32[128,128]{1,0:T(8,128)S(1)}, u32[]{:S(2)}, u32[]{:S(2)}) %collective-permute-start.3) | collective-permute-done | bytes 65568 | tf_op jit(solution)/shard_map/ppermute | solution.py:184
  15.7 2.4 %collective-permute-start.7 = (f32[128,128]{1,0:T(8,128)S(1)}, f32[128,128]{1,0:T(8,128)S(1)}, u32[]{:S(2)}, u32[]{:S(2)}) collective-permute-start(f32[128,128]{1,0:T(8,128)S(1)} %add_add_fusion.3.rest_0_), channel_id=1, source_target_pairs={{0,8},{1,9},{2,10},{3,11},{4,12},{5,13},{6,14},{7,15},{8,0},{9,1},... | collective-permute-start | bytes 196616 | tf_op jit(solution)/shard_map/ppermute | solution.py:184
  18.1 0.2 collective-permute-start.6
  18.3 1.4 %collective-permute-start.5 = (f32[128,128]{1,0:T(8,128)S(1)}, f32[128,128]{1,0:T(8,128)S(1)}, u32[]{:S(2)}, u32[]{:S(2)}) collective-permute-start(f32[128,128]{1,0:T(8,128)S(1)} %add_add_fusion.3.rest_0_), channel_id=1, source_target_pairs={{0,2},{1,3},{2,0},{3,1},{4,6},{5,7},{6,4},{7,5},{8,10},{9,11},{10,... | collective-permute-start | bytes 196616 | tf_op jit(solution)/shard_map/ppermute | solution.py:184
  19.7 1.5 %collective-permute-done.7.rest_3_ = f32[128,128]{1,0:T(8,128)S(1)} collective-permute-done((f32[128,128]{1,0:T(8,128)S(1)}, f32[128,128]{1,0:T(8,128)S(1)}, u32[]{:S(2)}, u32[]{:S(2)}) %collective-permute-start.7) | collective-permute-done | bytes 65568 | tf_op jit(solution)/shard_map/ppermute | solution.py:184
  21.2 0.8 %collective-permute-done.6.rest_2_ = f32[128,128]{1,0:T(8,128)S(1)} collective-permute-done((f32[128,128]{1,0:T(8,128)S(1)}, f32[128,128]{1,0:T(8,128)S(1)}, u32[]{:S(2)}, u32[]{:S(2)}) %collective-permute-start.6) | collective-permute-done | bytes 65568 | tf_op jit(solution)/shard_map/ppermute | solution.py:184
  21.9 0.6 next_step.3
  22.6 1.9 %collective-permute-start.9 = (f32[128,128]{1,0:T(8,128)S(1)}, f32[128,128]{1,0:T(8,128)S(1)}, u32[]{:S(2)}, u32[]{:S(2)}) collective-permute-start(f32[128,128]{1,0:T(8,128)S(1)} %get-tuple-element.37), channel_id=1, source_target_pairs={{1,16},{3,18},{5,20},{7,22},{9,24},{11,26},{13,28},{15,30},{16,1},... | collective-permute-start | bytes 196616 | tf_op jit(solution)/shard_map/ppermute | solution.py:184
  24.5 0.2 turn.3
  24.7 1.9 %collective-permute-done.10 = f32[128,128]{1,0:T(8,128)S(1)} collective-permute-done((f32[128,128]{1,0:T(8,128)S(1)}, f32[128,128]{1,0:T(8,128)S(1)}, u32[]{:S(2)}, u32[]{:S(2)}) %collective-permute-start.10) | collective-permute-done | bytes 65568 | tf_op jit(solution)/shard_map/ppermute | solution.py:184
  26.6 2.9 %collective-permute-done.9 = f32[128,128]{1,0:T(8,128)S(1)} collective-permute-done((f32[128,128]{1,0:T(8,128)S(1)}, f32[128,128]{1,0:T(8,128)S(1)}, u32[]{:S(2)}, u32[]{:S(2)}) %collective-permute-start.9) | collective-permute-done | bytes 65568 | tf_op jit(solution)/shard_map/ppermute | solution.py:184
  29.6 1.6 %collective-permute-start.13 = (f32[128,128]{1,0:T(8,128)S(1)}, f32[128,128]{1,0:T(8,128)S(1)}, u32[]{:S(2)}, u32[]{:S(2)}) collective-permute-start(f32[128,128]{1,0:T(8,128)S(1)} %add_add_fusion.2.rest_0_), channel_id=1, source_target_pairs={{0,8},{1,9},{2,10},{3,11},{4,12},{5,13},{6,14},{7,15},{8,0},{9,1},... | collective-permute-start | bytes 196616 | tf_op jit(solution)/shard_map/ppermute | solution.py:184
  31.2 1.1 %collective-permute-start.12 = (f32[128,128]{1,0:T(8,128)S(1)}, f32[128,128]{1,0:T(8,128)S(1)}, u32[]{:S(2)}, u32[]{:S(2)}) collective-permute-start(f32[128,128]{1,0:T(8,128)S(1)} %add_add_fusion.2.rest_0_), channel_id=1, source_target_pairs={{0,4},{1,5},{2,6},{3,7},{4,0},{5,1},{6,2},{7,3},{8,12},{9,13},{10,... | collective-permute-start | bytes 196616 | tf_op jit(solution)/shard_map/ppermute | solution.py:184
  32.2 3.6 %collective-permute-start.11 = (f32[128,128]{1,0:T(8,128)S(1)}, f32[128,128]{1,0:T(8,128)S(1)}, u32[]{:S(2)}, u32[]{:S(2)}) collective-permute-start(f32[128,128]{1,0:T(8,128)S(1)} %add_add_fusion.2.rest_0_), channel_id=1, source_target_pairs={{0,2},{1,3},{2,0},{3,1},{4,6},{5,7},{6,4},{7,5},{8,10},{9,11},{10,... | collective-permute-start | bytes 196616 | tf_op jit(solution)/shard_map/ppermute | solution.py:184
  35.9 0.9 %collective-permute-done.11.rest_1_ = f32[128,128]{1,0:T(8,128)S(1)} collective-permute-done((f32[128,128]{1,0:T(8,128)S(1)}, f32[128,128]{1,0:T(8,128)S(1)}, u32[]{:S(2)}, u32[]{:S(2)}) %collective-permute-start.11) | collective-permute-done | bytes 65568 | tf_op jit(solution)/shard_map/ppermute | solution.py:184
  36.8 0.6 next_step.4
  37.4 1.9 %collective-permute-start.15 = (f32[128,128]{1,0:T(8,128)S(1)}, f32[128,128]{1,0:T(8,128)S(1)}, u32[]{:S(2)}, u32[]{:S(2)}) collective-permute-start(f32[128,128]{1,0:T(8,128)S(1)} %get-tuple-element.41), channel_id=1, source_target_pairs={{1,16},{3,18},{5,20},{7,22},{9,24},{11,26},{13,28},{15,30},{16,1},... | collective-permute-start | bytes 196616 | tf_op jit(solution)/shard_map/ppermute | solution.py:184
  39.3 0.2 turn.4
  39.5 2.0 %collective-permute-done.16 = f32[128,128]{1,0:T(8,128)S(1)} collective-permute-done((f32[128,128]{1,0:T(8,128)S(1)}, f32[128,128]{1,0:T(8,128)S(1)}, u32[]{:S(2)}, u32[]{:S(2)}) %collective-permute-start.16) | collective-permute-done | bytes 65568 | tf_op jit(solution)/shard_map/ppermute | solution.py:184
  41.5 2.9 %collective-permute-done.15 = f32[128,128]{1,0:T(8,128)S(1)} collective-permute-done((f32[128,128]{1,0:T(8,128)S(1)}, f32[128,128]{1,0:T(8,128)S(1)}, u32[]{:S(2)}, u32[]{:S(2)}) %collective-permute-start.15) | collective-permute-done | bytes 65568 | tf_op jit(solution)/shard_map/ppermute | solution.py:184
  44.5 0.1 collective-permute-start.20
  44.5 1.5 %collective-permute-start.19 = (f32[128,128]{1,0:T(8,128)S(1)}, f32[128,128]{1,0:T(8,128)S(1)}, u32[]{:S(2)}, u32[]{:S(2)}) collective-permute-start(f32[128,128]{1,0:T(8,128)S(1)} %add_add_fusion.1.rest_0_), channel_id=1, source_target_pairs={{0,8},{1,9},{2,10},{3,11},{4,12},{5,13},{6,14},{7,15},{8,0},{9,1},... | collective-permute-start | bytes 196616 | tf_op jit(solution)/shard_map/ppermute | solution.py:184
  46.1 1.1 %collective-permute-start.18 = (f32[128,128]{1,0:T(8,128)S(1)}, f32[128,128]{1,0:T(8,128)S(1)}, u32[]{:S(2)}, u32[]{:S(2)}) collective-permute-start(f32[128,128]{1,0:T(8,128)S(1)} %add_add_fusion.1.rest_0_), channel_id=1, source_target_pairs={{0,4},{1,5},{2,6},{3,7},{4,0},{5,1},{6,2},{7,3},{8,12},{9,13},{10,... | collective-permute-start | bytes 196616 | tf_op jit(solution)/shard_map/ppermute | solution.py:184
  47.2 3.9 %collective-permute-start.17 = (f32[128,128]{1,0:T(8,128)S(1)}, f32[128,128]{1,0:T(8,128)S(1)}, u32[]{:S(2)}, u32[]{:S(2)}) collective-permute-start(f32[128,128]{1,0:T(8,128)S(1)} %add_add_fusion.1.rest_0_), channel_id=1, source_target_pairs={{0,2},{1,3},{2,0},{3,1},{4,6},{5,7},{6,4},{7,5},{8,10},{9,11},{10,... | collective-permute-start | bytes 196616 | tf_op jit(solution)/shard_map/ppermute | solution.py:184
  51.1 0.9 %collective-permute-done.17.rest_1_ = f32[128,128]{1,0:T(8,128)S(1)} collective-permute-done((f32[128,128]{1,0:T(8,128)S(1)}, f32[128,128]{1,0:T(8,128)S(1)}, u32[]{:S(2)}, u32[]{:S(2)}) %collective-permute-start.17) | collective-permute-done | bytes 65568 | tf_op jit(solution)/shard_map/ppermute | solution.py:184
  52.0 0.6 next_step.5
  52.6 1.9 %collective-permute-start.22 = (f32[128,128]{1,0:T(8,128)S(1)}, f32[128,128]{1,0:T(8,128)S(1)}, u32[]{:S(2)}, u32[]{:S(2)}) collective-permute-start(f32[128,128]{1,0:T(8,128)S(1)} %get-tuple-element.43), channel_id=1, source_target_pairs={{1,16},{3,18},{5,20},{7,22},{9,24},{11,26},{13,28},{15,30},{16,1},... | collective-permute-start | bytes 196616 | tf_op jit(solution)/shard_map/ppermute | solution.py:184
  54.5 0.2 turn.5
  54.7 2.9 %collective-permute-start.21 = (f32[8,64,128]{2,1,0:T(8,128)S(1)}, f32[8,64,128]{2,1,0:T(8,128)S(1)}, u32[]{:S(2)}, u32[]{:S(2)}) collective-permute-start(f32[8,64,128]{2,1,0:T(8,128)S(1)} %get-tuple-element.42.refs_0_), channel_id=1, source_target_pairs={{0,2},{1,3},{2,0},{3,1},{4,6},{5,7},{6,4},{7,5},{8,10},{9,11},{10,... | collective-permute-start | bytes 786440 | tf_op jit(solution)/shard_map/ppermute | solution.py:184
  57.6 2.1 %collective-permute-done.22 = f32[128,128]{1,0:T(8,128)S(1)} collective-permute-done((f32[128,128]{1,0:T(8,128)S(1)}, f32[128,128]{1,0:T(8,128)S(1)}, u32[]{:S(2)}, u32[]{:S(2)}) %collective-permute-start.22) | collective-permute-done | bytes 65568 | tf_op jit(solution)/shard_map/ppermute | solution.py:184
  59.7 0.4 collective-permute-start.26
  60.2 2.0 %collective-permute-start.25 = (f32[128,128]{1,0:T(8,128)S(1)}, f32[128,128]{1,0:T(8,128)S(1)}, u32[]{:S(2)}, u32[]{:S(2)}) collective-permute-start(f32[128,128]{1,0:T(8,128)S(1)} %add_add_fusion.refs_2_), channel_id=1, source_target_pairs={{0,8},{1,9},{2,10},{3,11},{4,12},{5,13},{6,14},{7,15},{8,0},{9,1},... | collective-permute-start | bytes 196616 | tf_op jit(solution)/shard_map/ppermute | solution.py:184
  62.1 0.3 collective-permute-start.24
  62.5 4.8 %collective-permute-start.27 = (f32[128,128]{1,0:T(8,128)S(1)}, f32[128,128]{1,0:T(8,128)S(1)}, u32[]{:S(2)}, u32[]{:S(2)}) collective-permute-start(f32[128,128]{1,0:T(8,128)S(1)} %add_add_fusion.refs_2_), channel_id=1, source_target_pairs={{0,2},{1,3},{2,0},{3,1},{4,6},{5,7},{6,4},{7,5},{8,10},{9,11},{10,... | collective-permute-start | bytes 196616 | tf_op jit(solution)/shard_map/ppermute | solution.py:184
  67.2 1.7 %collective-permute-start.30 = (f32[128,128]{1,0:T(8,128)S(1)}, f32[128,128]{1,0:T(8,128)S(1)}, u32[]{:S(2)}, u32[]{:S(2)}) collective-permute-start(f32[128,128]{1,0:T(8,128)S(1)} %collective-permute-done.26.refs_5_), channel_id=1, source_target_pairs={{0,2},{1,3},{2,0},{3,1},{4,6},{5,7},{6,4},{7,5},{8,10},{9,11},{10,... | collective-permute-start | bytes 196616 | tf_op jit(solution)/shard_map/ppermute | solution.py:184
  68.9 1.1 %collective-permute-start.28 = (f32[128,128]{1,0:T(8,128)S(1)}, f32[128,128]{1,0:T(8,128)S(1)}, u32[]{:S(2)}, u32[]{:S(2)}) collective-permute-start(f32[128,128]{1,0:T(8,128)S(1)} %collective-permute-done.24.refs_3_), channel_id=1, source_target_pairs={{0,2},{1,3},{2,0},{3,1},{4,6},{5,7},{6,4},{7,5},{8,10},{9,11},{10,... | collective-permute-start | bytes 196616 | tf_op jit(solution)/shard_map/ppermute | solution.py:184
  70.0 0.2 collective-permute-done.29.refs_8_
  70.2 0.7 %collective-permute-done.28.refs_7_ = f32[128,128]{1,0:T(8,128)S(1)} collective-permute-done((f32[128,128]{1,0:T(8,128)S(1)}, f32[128,128]{1,0:T(8,128)S(1)}, u32[]{:S(2)}, u32[]{:S(2)}) %collective-permute-start.28) | collective-permute-done | bytes 65568 | tf_op jit(solution)/shard_map/ppermute | solution.py:184
  70.9 0.9 %last_step.1 = f32[1024,128]{1,0:T(8,128)} custom-call(f32[8,64,128]{2,1,0:T(8,128)S(1)} %get-tuple-element.42.refs_0_, f32[8,64,128]{2,1,0:T(8,128)S(1)} %collective-permute-done.21.refs_1_, f32[128,128]{1,0:T(8,128)S(1)} %add_add_fusion.refs_2_, f32[128,128]{1,0:T(8,128)S(1)} %collective-permute-done.24.refs_3_, ...), custom_call_target="tpu_custom_call" | custom-call | tf_op jit(solution)/shard_map/last_step/pallas_call | solution.py:230
  (31 shorter events, 0.4 us)
Async XLA Ops:
  0.0 4.9 %collective-permute-start.1 = (f32[1024,128]{1,0:T(8,128)}, f32[1024,128]{1,0:T(8,128)S(1)}, u32[]{:S(2)}, u32[]{:S(2)}) collective-permute-start(f32[1024,128]{1,0:T(8,128)} %bitcast.10), channel_id=1, source_target_pairs={{0,2},{1,3},{2,0},{3,1},{4,6},{5,7},{6,4},{7,5},{8,10},{9,11},{10,... | collective-permute-start | bytes 1572872 | tf_op jit(solution)/shard_map/ppermute | solution.py:184
  0.7 4.2 %collective-permute-start.2 = (f32[1024,128]{1,0:T(8,128)}, f32[1024,128]{1,0:T(8,128)S(1)}, u32[]{:S(2)}, u32[]{:S(2)}) collective-permute-start(f32[1024,128]{1,0:T(8,128)} %bitcast.12), channel_id=1, source_target_pairs={{0,2},{1,3},{2,0},{3,1},{4,6},{5,7},{6,4},{7,5},{8,10},{9,11},{10,... | collective-permute-start | bytes 1572872 | tf_op jit(solution)/shard_map/ppermute | solution.py:184
  2.1 2.8 %collective-permute-start = (s32[2,128]{1,0:T(2,128)S(1)}, s32[2,128]{1,0:T(2,128)S(1)}, u32[]{:S(2)}, u32[]{:S(2)}) collective-permute-start(s32[2,128]{1,0:T(2,128)S(1)} %broadcast_in_dim.2.limits_ref), channel_id=1, source_target_pairs={{0,2},{1,3},{2,0},{3,1},{4,6},{5,7},{6,4},{7,5},{8,10},{9,11},{10,... | collective-permute-start | bytes 3080 | tf_op jit(solution)/shard_map/ppermute | solution.py:184
  2.6 19.3 %copy-start = (f32[4,128,8,128]{3,2,1,0:T(8,128)S(1)}, f32[4,128,8,128]{3,2,1,0:T(8,128)}, u32[]{:S(2)}) copy-start(f32[4,128,8,128]{3,2,1,0:T(8,128)} %param.11) | copy-start | bytes 6291460
  5.3 6.3 %collective-permute-start.4 = (f32[128,128]{1,0:T(8,128)S(1)}, f32[128,128]{1,0:T(8,128)S(1)}, u32[]{:S(2)}, u32[]{:S(2)}) collective-permute-start(f32[128,128]{1,0:T(8,128)S(1)} %get-tuple-element.33), channel_id=1, source_target_pairs={{1,0},{3,2},{5,4},{7,6},{9,8},{11,10},{13,12},{15,14},{16,17},{18,... | collective-permute-start | bytes 196616 | tf_op jit(solution)/shard_map/ppermute | solution.py:184
  6.5 9.1 %collective-permute-start.3 = (f32[128,128]{1,0:T(8,128)S(1)}, f32[128,128]{1,0:T(8,128)S(1)}, u32[]{:S(2)}, u32[]{:S(2)}) collective-permute-start(f32[128,128]{1,0:T(8,128)S(1)} %get-tuple-element.33), channel_id=1, source_target_pairs={{1,16},{3,18},{5,20},{7,22},{9,24},{11,26},{13,28},{15,30},{16,1},... | collective-permute-start | bytes 196616 | tf_op jit(solution)/shard_map/ppermute | solution.py:184
  15.6 4.1 %collective-permute-start.8 = (f32[128,128]{1,0:T(8,128)S(1)}, f32[128,128]{1,0:T(8,128)S(1)}, u32[]{:S(2)}, u32[]{:S(2)}) collective-permute-start(f32[128,128]{1,0:T(8,128)S(1)} %add_add_fusion.3.rest_0_), channel_id=1, source_target_pairs={{0,12},{1,13},{2,14},{3,15},{4,8},{5,9},{6,10},{7,11},{8,4},{9,5},... | collective-permute-start | bytes 196616 | tf_op jit(solution)/shard_map/ppermute | solution.py:184
  15.7 5.5 %collective-permute-start.7 = (f32[128,128]{1,0:T(8,128)S(1)}, f32[128,128]{1,0:T(8,128)S(1)}, u32[]{:S(2)}, u32[]{:S(2)}) collective-permute-start(f32[128,128]{1,0:T(8,128)S(1)} %add_add_fusion.3.rest_0_), channel_id=1, source_target_pairs={{0,8},{1,9},{2,10},{3,11},{4,12},{5,13},{6,14},{7,15},{8,0},{9,1},... | collective-permute-start | bytes 196616 | tf_op jit(solution)/shard_map/ppermute | solution.py:184
  18.1 3.8 %collective-permute-start.6 = (f32[128,128]{1,0:T(8,128)S(1)}, f32[128,128]{1,0:T(8,128)S(1)}, u32[]{:S(2)}, u32[]{:S(2)}) collective-permute-start(f32[128,128]{1,0:T(8,128)S(1)} %add_add_fusion.3.rest_0_), channel_id=1, source_target_pairs={{0,4},{1,5},{2,6},{3,7},{4,0},{5,1},{6,2},{7,3},{8,12},{9,13},{10,... | collective-permute-start | bytes 196616 | tf_op jit(solution)/shard_map/ppermute | solution.py:184
  18.3 3.6 %collective-permute-start.5 = (f32[128,128]{1,0:T(8,128)S(1)}, f32[128,128]{1,0:T(8,128)S(1)}, u32[]{:S(2)}, u32[]{:S(2)}) collective-permute-start(f32[128,128]{1,0:T(8,128)S(1)} %add_add_fusion.3.rest_0_), channel_id=1, source_target_pairs={{0,2},{1,3},{2,0},{3,1},{4,6},{5,7},{6,4},{7,5},{8,10},{9,11},{10,... | collective-permute-start | bytes 196616 | tf_op jit(solution)/shard_map/ppermute | solution.py:184
  22.5 4.1 %collective-permute-start.10 = (f32[128,128]{1,0:T(8,128)S(1)}, f32[128,128]{1,0:T(8,128)S(1)}, u32[]{:S(2)}, u32[]{:S(2)}) collective-permute-start(f32[128,128]{1,0:T(8,128)S(1)} %get-tuple-element.37), channel_id=1, source_target_pairs={{1,0},{3,2},{5,4},{7,6},{9,8},{11,10},{13,12},{15,14},{16,17},{18,... | collective-permute-start | bytes 196616 | tf_op jit(solution)/shard_map/ppermute | solution.py:184
  22.6 6.9 %collective-permute-start.9 = (f32[128,128]{1,0:T(8,128)S(1)}, f32[128,128]{1,0:T(8,128)S(1)}, u32[]{:S(2)}, u32[]{:S(2)}) collective-permute-start(f32[128,128]{1,0:T(8,128)S(1)} %get-tuple-element.37), channel_id=1, source_target_pairs={{1,16},{3,18},{5,20},{7,22},{9,24},{11,26},{13,28},{15,30},{16,1},... | collective-permute-start | bytes 196616 | tf_op jit(solution)/shard_map/ppermute | solution.py:184
  29.5 6.4 %collective-permute-start.14 = (f32[128,128]{1,0:T(8,128)S(1)}, f32[128,128]{1,0:T(8,128)S(1)}, u32[]{:S(2)}, u32[]{:S(2)}) collective-permute-start(f32[128,128]{1,0:T(8,128)S(1)} %add_add_fusion.2.rest_0_), channel_id=1, source_target_pairs={{0,12},{1,13},{2,14},{3,15},{4,8},{5,9},{6,10},{7,11},{8,4},{9,5},... | collective-permute-start | bytes 196616 | tf_op jit(solution)/shard_map/ppermute | solution.py:184
  29.6 6.3 %collective-permute-start.13 = (f32[128,128]{1,0:T(8,128)S(1)}, f32[128,128]{1,0:T(8,128)S(1)}, u32[]{:S(2)}, u32[]{:S(2)}) collective-permute-start(f32[128,128]{1,0:T(8,128)S(1)} %add_add_fusion.2.rest_0_), channel_id=1, source_target_pairs={{0,8},{1,9},{2,10},{3,11},{4,12},{5,13},{6,14},{7,15},{8,0},{9,1},... | collective-permute-start | bytes 196616 | tf_op jit(solution)/shard_map/ppermute | solution.py:184
  31.2 4.7 %collective-permute-start.12 = (f32[128,128]{1,0:T(8,128)S(1)}, f32[128,128]{1,0:T(8,128)S(1)}, u32[]{:S(2)}, u32[]{:S(2)}) collective-permute-start(f32[128,128]{1,0:T(8,128)S(1)} %add_add_fusion.2.rest_0_), channel_id=1, source_target_pairs={{0,4},{1,5},{2,6},{3,7},{4,0},{5,1},{6,2},{7,3},{8,12},{9,13},{10,... | collective-permute-start | bytes 196616 | tf_op jit(solution)/shard_map/ppermute | solution.py:184
  32.2 4.5 %collective-permute-start.11 = (f32[128,128]{1,0:T(8,128)S(1)}, f32[128,128]{1,0:T(8,128)S(1)}, u32[]{:S(2)}, u32[]{:S(2)}) collective-permute-start(f32[128,128]{1,0:T(8,128)S(1)} %add_add_fusion.2.rest_0_), channel_id=1, source_target_pairs={{0,2},{1,3},{2,0},{3,1},{4,6},{5,7},{6,4},{7,5},{8,10},{9,11},{10,... | collective-permute-start | bytes 196616 | tf_op jit(solution)/shard_map/ppermute | solution.py:184
  37.3 4.2 %collective-permute-start.16 = (f32[128,128]{1,0:T(8,128)S(1)}, f32[128,128]{1,0:T(8,128)S(1)}, u32[]{:S(2)}, u32[]{:S(2)}) collective-permute-start(f32[128,128]{1,0:T(8,128)S(1)} %get-tuple-element.41), channel_id=1, source_target_pairs={{1,0},{3,2},{5,4},{7,6},{9,8},{11,10},{13,12},{15,14},{16,17},{18,... | collective-permute-start | bytes 196616 | tf_op jit(solution)/shard_map/ppermute | solution.py:184
  37.4 7.0 %collective-permute-start.15 = (f32[128,128]{1,0:T(8,128)S(1)}, f32[128,128]{1,0:T(8,128)S(1)}, u32[]{:S(2)}, u32[]{:S(2)}) collective-permute-start(f32[128,128]{1,0:T(8,128)S(1)} %get-tuple-element.41), channel_id=1, source_target_pairs={{1,16},{3,18},{5,20},{7,22},{9,24},{11,26},{13,28},{15,30},{16,1},... | collective-permute-start | bytes 196616 | tf_op jit(solution)/shard_map/ppermute | solution.py:184
  44.5 6.6 %collective-permute-start.20 = (f32[128,128]{1,0:T(8,128)S(1)}, f32[128,128]{1,0:T(8,128)S(1)}, u32[]{:S(2)}, u32[]{:S(2)}) collective-permute-start(f32[128,128]{1,0:T(8,128)S(1)} %add_add_fusion.1.rest_0_), channel_id=1, source_target_pairs={{0,12},{1,13},{2,14},{3,15},{4,8},{5,9},{6,10},{7,11},{8,4},{9,5},... | collective-permute-start | bytes 196616 | tf_op jit(solution)/shard_map/ppermute | solution.py:184
  44.5 6.5 %collective-permute-start.19 = (f32[128,128]{1,0:T(8,128)S(1)}, f32[128,128]{1,0:T(8,128)S(1)}, u32[]{:S(2)}, u32[]{:S(2)}) collective-permute-start(f32[128,128]{1,0:T(8,128)S(1)} %add_add_fusion.1.rest_0_), channel_id=1, source_target_pairs={{0,8},{1,9},{2,10},{3,11},{4,12},{5,13},{6,14},{7,15},{8,0},{9,1},... | collective-permute-start | bytes 196616 | tf_op jit(solution)/shard_map/ppermute | solution.py:184
  46.1 5.0 %collective-permute-start.18 = (f32[128,128]{1,0:T(8,128)S(1)}, f32[128,128]{1,0:T(8,128)S(1)}, u32[]{:S(2)}, u32[]{:S(2)}) collective-permute-start(f32[128,128]{1,0:T(8,128)S(1)} %add_add_fusion.1.rest_0_), channel_id=1, source_target_pairs={{0,4},{1,5},{2,6},{3,7},{4,0},{5,1},{6,2},{7,3},{8,12},{9,13},{10,... | collective-permute-start | bytes 196616 | tf_op jit(solution)/shard_map/ppermute | solution.py:184
  47.2 4.8 %collective-permute-start.17 = (f32[128,128]{1,0:T(8,128)S(1)}, f32[128,128]{1,0:T(8,128)S(1)}, u32[]{:S(2)}, u32[]{:S(2)}) collective-permute-start(f32[128,128]{1,0:T(8,128)S(1)} %add_add_fusion.1.rest_0_), channel_id=1, source_target_pairs={{0,2},{1,3},{2,0},{3,1},{4,6},{5,7},{6,4},{7,5},{8,10},{9,11},{10,... | collective-permute-start | bytes 196616 | tf_op jit(solution)/shard_map/ppermute | solution.py:184
  52.5 5.1 %collective-permute-start.23 = (f32[128,128]{1,0:T(8,128)S(1)}, f32[128,128]{1,0:T(8,128)S(1)}, u32[]{:S(2)}, u32[]{:S(2)}) collective-permute-start(f32[128,128]{1,0:T(8,128)S(1)} %get-tuple-element.43), channel_id=1, source_target_pairs={{1,0},{3,2},{5,4},{7,6},{9,8},{11,10},{13,12},{15,14},{16,17},{18,... | collective-permute-start | bytes 196616 | tf_op jit(solution)/shard_map/ppermute | solution.py:184
  52.6 7.1 %collective-permute-start.22 = (f32[128,128]{1,0:T(8,128)S(1)}, f32[128,128]{1,0:T(8,128)S(1)}, u32[]{:S(2)}, u32[]{:S(2)}) collective-permute-start(f32[128,128]{1,0:T(8,128)S(1)} %get-tuple-element.43), channel_id=1, source_target_pairs={{1,16},{3,18},{5,20},{7,22},{9,24},{11,26},{13,28},{15,30},{16,1},... | collective-permute-start | bytes 196616 | tf_op jit(solution)/shard_map/ppermute | solution.py:184
  54.7 16.2 %collective-permute-start.21 = (f32[8,64,128]{2,1,0:T(8,128)S(1)}, f32[8,64,128]{2,1,0:T(8,128)S(1)}, u32[]{:S(2)}, u32[]{:S(2)}) collective-permute-start(f32[8,64,128]{2,1,0:T(8,128)S(1)} %get-tuple-element.42.refs_0_), channel_id=1, source_target_pairs={{0,2},{1,3},{2,0},{3,1},{4,6},{5,7},{6,4},{7,5},{8,10},{9,11},{10,... | collective-permute-start | bytes 786440 | tf_op jit(solution)/shard_map/ppermute | solution.py:184
  59.7 7.5 %collective-permute-start.26 = (f32[128,128]{1,0:T(8,128)S(1)}, f32[128,128]{1,0:T(8,128)S(1)}, u32[]{:S(2)}, u32[]{:S(2)}) collective-permute-start(f32[128,128]{1,0:T(8,128)S(1)} %add_add_fusion.refs_2_), channel_id=1, source_target_pairs={{0,12},{1,13},{2,14},{3,15},{4,8},{5,9},{6,10},{7,11},{8,4},{9,5},... | collective-permute-start | bytes 196616 | tf_op jit(solution)/shard_map/ppermute | solution.py:184
  60.2 8.7 %collective-permute-start.25 = (f32[128,128]{1,0:T(8,128)S(1)}, f32[128,128]{1,0:T(8,128)S(1)}, u32[]{:S(2)}, u32[]{:S(2)}) collective-permute-start(f32[128,128]{1,0:T(8,128)S(1)} %add_add_fusion.refs_2_), channel_id=1, source_target_pairs={{0,8},{1,9},{2,10},{3,11},{4,12},{5,13},{6,14},{7,15},{8,0},{9,1},... | collective-permute-start | bytes 196616 | tf_op jit(solution)/shard_map/ppermute | solution.py:184
  62.1 6.8 %collective-permute-start.24 = (f32[128,128]{1,0:T(8,128)S(1)}, f32[128,128]{1,0:T(8,128)S(1)}, u32[]{:S(2)}, u32[]{:S(2)}) collective-permute-start(f32[128,128]{1,0:T(8,128)S(1)} %add_add_fusion.refs_2_), channel_id=1, source_target_pairs={{0,4},{1,5},{2,6},{3,7},{4,0},{5,1},{6,2},{7,3},{8,12},{9,13},{10,... | collective-permute-start | bytes 196616 | tf_op jit(solution)/shard_map/ppermute | solution.py:184
  62.5 7.5 %collective-permute-start.27 = (f32[128,128]{1,0:T(8,128)S(1)}, f32[128,128]{1,0:T(8,128)S(1)}, u32[]{:S(2)}, u32[]{:S(2)}) collective-permute-start(f32[128,128]{1,0:T(8,128)S(1)} %add_add_fusion.refs_2_), channel_id=1, source_target_pairs={{0,2},{1,3},{2,0},{3,1},{4,6},{5,7},{6,4},{7,5},{8,10},{9,11},{10,... | collective-permute-start | bytes 196616 | tf_op jit(solution)/shard_map/ppermute | solution.py:184
  67.2 2.8 %collective-permute-start.30 = (f32[128,128]{1,0:T(8,128)S(1)}, f32[128,128]{1,0:T(8,128)S(1)}, u32[]{:S(2)}, u32[]{:S(2)}) collective-permute-start(f32[128,128]{1,0:T(8,128)S(1)} %collective-permute-done.26.refs_5_), channel_id=1, source_target_pairs={{0,2},{1,3},{2,0},{3,1},{4,6},{5,7},{6,4},{7,5},{8,10},{9,11},{10,... | collective-permute-start | bytes 196616 | tf_op jit(solution)/shard_map/ppermute | solution.py:184
  68.9 1.3 %collective-permute-start.29 = (f32[128,128]{1,0:T(8,128)S(1)}, f32[128,128]{1,0:T(8,128)S(1)}, u32[]{:S(2)}, u32[]{:S(2)}) collective-permute-start(f32[128,128]{1,0:T(8,128)S(1)} %collective-permute-done.25.refs_4_), channel_id=1, source_target_pairs={{0,2},{1,3},{2,0},{3,1},{4,6},{5,7},{6,4},{7,5},{8,10},{9,11},{10,... | collective-permute-start | bytes 196616 | tf_op jit(solution)/shard_map/ppermute | solution.py:184
  68.9 2.0 %collective-permute-start.28 = (f32[128,128]{1,0:T(8,128)S(1)}, f32[128,128]{1,0:T(8,128)S(1)}, u32[]{:S(2)}, u32[]{:S(2)}) collective-permute-start(f32[128,128]{1,0:T(8,128)S(1)} %collective-permute-done.24.refs_3_), channel_id=1, source_target_pairs={{0,2},{1,3},{2,0},{3,1},{4,6},{5,7},{6,4},{7,5},{8,10},{9,11},{10,... | collective-permute-start | bytes 196616 | tf_op jit(solution)/shard_map/ppermute | solution.py:184

commit v7 on v6

--- a/solution.py
+++ b/solution.py
@@ -62,13 +62,21 @@
         wide_ref[(rows_dev + s) * n : (rows_dev + s + 1) * n, :] = wide(adv_ref[s * n : (s + 1) * n, :] * inside)
 
 
-def turn(half, ham_ref, near_ref, turned_ref):
+def turn(half, ham_ref, near_ref, part_ref, far_ref, turned_ref):
     for j in range(2):
-        turned_ref[j * half : (j + 1) * half, :] = product(ham_ref[...], wide(near_ref[j]))
+        rows = slice(j * half, (j + 1) * half)
+        turned_ref[rows, :] = product(ham_ref[...], wide(near_ref[j])) + (part_ref[rows, :] - far_ref[rows, :])
+
+
+def store(rows_dev, half, parts, part_ref, far_ref):
+    reads_own = lax.div(lax.axis_index("hist"), rows_dev) == lax.axis_index("col")
+    for j, part in enumerate(parts):
+        part_ref[j * half : (j + 1) * half, :] = part
+        far_ref[j * half : (j + 1) * half, :] = jnp.where(reads_own, 0.0, part)
 
 
 def first_kernel(rows_dev, half, steps, limits_ref, lesser_hbm, adv_hbm, first_hbm, greater_hbm, coup_hbm, ham_hbm,
-                 cur_ref, wide_ref, active_ref, strength_ref, ham_ref, near_ref, turned_ref, sigma_ref, own_ref,
+                 cur_ref, wide_ref, active_ref, strength_ref, ham_ref, near_ref, sigma_ref, own_ref,
                  lesser_ref, adv_ref, first_ref, g_ref, h_ref, sems):
     n = 2 * half
     own_row, core, col_pos = places(rows_dev)
@@ -106,23 +114,21 @@
         s = jnp.bitwise_xor(own_row, j)
         near_ref[j, :half, :] = first_ref[every(mine, s, half, rows_dev), :]
         near_ref[j, half:, :] = first_ref[every(other, s, half, rows_dev), :]
-    turn(half, ham_ref, near_ref, turned_ref)
     for copy in copies[4:]:
         copy.wait()
     split_tables(rows_dev, n, col_pos, cutoff, lesser_ref, adv_ref, wide_ref)
     own_ref[...] = product(sigma_ref[...], wide_ref[...])
 
 
-def second_kernel(rows_dev, half, limits_ref, lesser_ref, adv_ref, sigma_ref, own_ref, wide_ref, part_ref):
+def second_kernel(rows_dev, half, limits_ref, lesser_ref, adv_ref, sigma_ref, own_ref, wide_ref, part_ref, far_ref):
     col_pos = lax.axis_index("col")
     split_tables(rows_dev, 2 * half, col_pos, limits_ref[1:2, :], lesser_ref, adv_ref, wide_ref)
-    part_ref[:half, :] = own_ref[...]
-    part_ref[half:, :] = product(sigma_ref[...], wide_ref[...])
+    store(rows_dev, half, (own_ref[...], product(sigma_ref[...], wide_ref[...])), part_ref, far_ref)
 
 
 def next_kernel(section, rows_dev, half, prev_ref, prev_near_ref, greater_ref, active_ref, strength_ref, own_wide_ref, other_wide_ref, *rest):
     own_ref, swapped_ref, *others = rest[: rows_dev // 2 + 1]
-    cur_ref, near_ref, part_ref, sigma_ref = rest[rows_dev // 2 + 1 :]
+    cur_ref, near_ref, part_ref, far_ref, sigma_ref = rest[rows_dev // 2 + 1 :]
     own_row, core, _ = places(rows_dev)
     for k, piece in enumerate([own_ref] + others):
         for j in range(2):
@@ -132,8 +138,8 @@
         near_ref[j, :half, :] = prev_near_ref[j, :half, :] - STEP_SIZE * own_ref[j * half : (j + 1) * half, :]
         near_ref[j, half:, :] = prev_near_ref[j, half:, :] - STEP_SIZE * swapped_ref[(1 - j) * half : (2 - j) * half, :]
     sigmas(section, rows_dev, half, core, cur_ref, greater_ref, section * 2 * half, active_ref, strength_ref, sigma_ref)
-    part_ref[:half, :] = product(sigma_ref[...], own_wide_ref[...])
-    part_ref[half:, :] = product(sigma_ref[...], other_wide_ref[...])
+    parts = [product(sigma_ref[...], table[...]) for table in (own_wide_ref, other_wide_ref)]
+    store(rows_dev, half, parts, part_ref, far_ref)
 
 
 def last_kernel(rows_dev, half, *refs):
@@ -189,10 +195,10 @@
     cycle = [(at(h, 1 - block(h)), at(h, block(h))) for h in range(hist)]
     cycle += [(at(h, block(h)), at(h ^ rows_dev, block(h))) for h in range(hist)]
     across = [(at(h, 1 - block(h)), at(h ^ rows_dev, block(h))) for h in range(hist)]
-    across += [(at(h, block(h)), at(h, block(h))) for h in range(hist)]
-
-    def exchange(part, turned):
-        own = moved(part, across) + moved(part, cycle) + turned
+    across += [(at(h, block(h)), at(h ^ 1, block(h))) for h in range(hist)]
+
+    def exchange(part, far, turned):
+        own = moved(part, cycle) + moved(far, across) + turned
         return [own, flip(own, 1)] + [flip(own, bits) for bits in range(2, rows_dev, 2)]
 
     def out(dims, kind=F32):
@@ -204,28 +210,30 @@
     near_out = out((2, n, n))
     cur_out, pair_out, wide_out = out((rows_dev, half, n)), out((n, n)), out((2 * rows_dev * n, 2 * n), BF16)
     sigma = (n, 2 * rows_dev * n)
-    current, own_wide, active, strength, ham, near, turned, first_sigma, own_part = call(
+    current, own_wide, active, strength, ham, near, first_sigma, own_part = call(
         functools.partial(first_kernel, rows_dev, half, steps),
         [vmem] + [hbm] * 6,
-        [cur_out, wide_out, out((steps * rows_dev, n)), out((half, n)), out((n, n), BF16), near_out, pair_out, out(sigma, BF16), out((half, n))],
+        [cur_out, wide_out, out((steps * rows_dev, n)), out((half, n)), out((n, n), BF16), near_out, out(sigma, BF16), out((half, n))],
         [vmem(flat, F32)] * 4 + [vmem((half, n), F32), pltpu.SemaphoreType.DMA((6,))],
         "first_step",
     )(limits, *[
         pltpu.with_memory_space_constraint(x, hbm)
         for x in (*tables, first_row.reshape(flat), greater, coupling, hamiltonian)
     ])
-    other_wide, part = call(
+    other_wide, part, far = call(
         functools.partial(second_kernel, rows_dev, half),
-        [vmem] * 5, [wide_out, pair_out], [], "first_step_other",
+        [vmem] * 5, [wide_out, pair_out, pair_out], [], "first_step_other",
     )(flip(limits, 1), *[flip(x, 1) for x in tables], first_sigma, own_part)
+    def add_turned():
+        return call(functools.partial(turn, half), [vmem] * 4, [pair_out], [], "turn")(ham, near, part, far)[0]
+
     for section in range(1, steps):
-        pieces = exchange(part, turned)
-        current, near, part = call(
+        pieces = exchange(part, far, add_turned())
+        current, near, part, far = call(
             functools.partial(next_kernel, section, rows_dev, half),
-            [vmem] * (8 + rows_dev // 2), [cur_out, near_out, pair_out], [vmem(sigma, BF16)], "next_step",
+            [vmem] * (8 + rows_dev // 2), [cur_out, near_out, pair_out, pair_out], [vmem(sigma, BF16)], "next_step",
         )(current, near, greater, active, strength, own_wide, other_wide, *pieces)
-        turned = call(functools.partial(turn, half), [vmem] * 2, [pair_out], [], "turn")(ham, near)[0]
-    pieces = exchange(part, turned)
+    pieces = exchange(part, far, add_turned())
     own, swapped = [pieces[0]] + pieces[2:], pieces[1]
     final = call(
         functools.partial(last_kernel, rows_dev, half),

time: 72.4 us -> 64.7 us (0.89)
  starting transfers between devices: 40.5 us -> 33.3 us
    ppermute x31, starting transfers between devices: 40.5 us -> 33.3 us  [moved(): return lax.ppermute(x, ('hist', 'col'), pairs)]
  transfers between devices with their start and end apart: 31 -> 31, of which waited for: 13 -> 14; matrix products, arithmetic and copies ran while one was open for 0% -> 0% of each run, Pallas kernels for 4% -> 4%
where the time goes in v7:
time: 64.7 us; the launch traced here: 64.5 us
  starting transfers between devices  33.3 us (51%)
  waiting for transfers between devices  23.7 us (37%)
  Pallas kernels  5.86 us (9%)
  between operations  1.5 us (2%)
    ppermute x31, starting transfers between devices, moved(): return lax.ppermute(x, ('hist', 'col'), pairs)  33.3 us
    ppermute x31, waiting for transfers between devices, moved(): return lax.ppermute(x, ('hist', 'col'), pairs)  23.7 us
    pallas_call x1, Pallas kernels, in_pairs(): call(functools.partial(first_kernel, rows_dev, half, steps), [vmem] + [hb...  2.12 us
    pallas_call x3, Pallas kernels, in_pairs(): call(functools.partial(next_kernel, section, rows_dev, half), [vmem] * (8...  1.76 us
  transfers between devices with their start and end apart: 31, of which 14 were waited for; matrix products, arithmetic and copies ran while one was open for 0% of the time, Pallas kernels for 4%

profile of v7, /device:TPU:25, one launch (start us, length us, event | category | flops | bytes accessed | tf_op | source)
XLA Modules:
  0.0 64.5 jit_solution(492797265965176189)
XLA Ops:
  0.0 0.7 %collective-permute-start.1 = (f32[1024,128]{1,0:T(8,128)}, f32[1024,128]{1,0:T(8,128)S(1)}, u32[]{:S(2)}, u32[]{:S(2)}) collective-permute-start(f32[1024,128]{1,0:T(8,128)} %bitcast.10), channel_id=1, source_target_pairs={{0,2},{1,3},{2,0},{3,1},{4,6},{5,7},{6,4},{7,5},{8,10},{9,11},{10,... | collective-permute-start | bytes 1572872 | tf_op jit(solution)/shard_map/ppermute | solution.py:190
  2.0 0.1 pad_add_fusion
  2.1 0.1 broadcast_in_dim.2.limits_ref
  2.1 0.5 collective-permute-start
  2.6 2.1 %first_step.1 = (f32[8,64,128]{2,1,0:T(8,128)S(1)}, bf16[2048,256]{1,0:T(8,128)(2,1)S(1)}, f32[32,128]{1,0:T(8,128)S(1)}, f32[64,128]{1,0:T(8,128)S(1)}, bf16[12...) custom-call(s32[2,128]{1,0:T(2,128)S(1)} %broadcast_in_dim.2.limits_r, ...), custom_call_target="tpu_custom_call" | custom-call | tf_op jit(solution)/shard_map/first_step/pallas_call | solution.py:213
  4.8 0.4 first_step_other.1
  5.1 1.3 %collective-permute-start.3 = (f32[128,128]{1,0:T(8,128)S(1)}, f32[128,128]{1,0:T(8,128)S(1)}, u32[]{:S(2)}, u32[]{:S(2)}) collective-permute-start(f32[128,128]{1,0:T(8,128)S(1)} %get-tuple-element.36.part_ref), channel_id=1, source_target_pairs={{1,0},{3,2},{5,4},{7,6},{9,8},{11,10},{13,12},{15,14},{16,17},{18,... | collective-permute-start | bytes 196616 | tf_op jit(solution)/shard_map/ppermute | solution.py:190
  6.4 0.2 turn.4
  6.6 4.8 %collective-permute-done.3 = f32[128,128]{1,0:T(8,128)S(1)} collective-permute-done((f32[128,128]{1,0:T(8,128)S(1)}, f32[128,128]{1,0:T(8,128)S(1)}, u32[]{:S(2)}, u32[]{:S(2)}) %collective-permute-start.3) | collective-permute-done | bytes 65568 | tf_op jit(solution)/shard_map/ppermute | solution.py:190
  11.5 2.1 %collective-permute-done.4 = f32[128,128]{1,0:T(8,128)S(1)} collective-permute-done((f32[128,128]{1,0:T(8,128)S(1)}, f32[128,128]{1,0:T(8,128)S(1)}, u32[]{:S(2)}, u32[]{:S(2)}) %collective-permute-start.4) | collective-permute-done | bytes 65568 | tf_op jit(solution)/shard_map/ppermute | solution.py:190
  13.6 2.4 %collective-permute-start.7 = (f32[128,128]{1,0:T(8,128)S(1)}, f32[128,128]{1,0:T(8,128)S(1)}, u32[]{:S(2)}, u32[]{:S(2)}) collective-permute-start(f32[128,128]{1,0:T(8,128)S(1)} %add_add_fusion.3.rest_0_), channel_id=1, source_target_pairs={{0,8},{1,9},{2,10},{3,11},{4,12},{5,13},{6,14},{7,15},{8,0},{9,1},... | collective-permute-start | bytes 196616 | tf_op jit(solution)/shard_map/ppermute | solution.py:190
  16.0 0.2 collective-permute-start.6
  16.3 1.3 %collective-permute-start.5 = (f32[128,128]{1,0:T(8,128)S(1)}, f32[128,128]{1,0:T(8,128)S(1)}, u32[]{:S(2)}, u32[]{:S(2)}) collective-permute-start(f32[128,128]{1,0:T(8,128)S(1)} %add_add_fusion.3.rest_0_), channel_id=1, source_target_pairs={{0,2},{1,3},{2,0},{3,1},{4,6},{5,7},{6,4},{7,5},{8,10},{9,11},{10,... | collective-permute-start | bytes 196616 | tf_op jit(solution)/shard_map/ppermute | solution.py:190
  17.6 1.4 %collective-permute-done.7.rest_3_ = f32[128,128]{1,0:T(8,128)S(1)} collective-permute-done((f32[128,128]{1,0:T(8,128)S(1)}, f32[128,128]{1,0:T(8,128)S(1)}, u32[]{:S(2)}, u32[]{:S(2)}) %collective-permute-start.7) | collective-permute-done | bytes 65568 | tf_op jit(solution)/shard_map/ppermute | solution.py:190
  19.1 0.8 %collective-permute-done.6.rest_2_ = f32[128,128]{1,0:T(8,128)S(1)} collective-permute-done((f32[128,128]{1,0:T(8,128)S(1)}, f32[128,128]{1,0:T(8,128)S(1)}, u32[]{:S(2)}, u32[]{:S(2)}) %collective-permute-start.6) | collective-permute-done | bytes 65568 | tf_op jit(solution)/shard_map/ppermute | solution.py:190
  19.9 0.6 next_step.3
  20.6 0.2 turn.5
  20.8 3.7 %collective-permute-done.9 = f32[128,128]{1,0:T(8,128)S(1)} collective-permute-done((f32[128,128]{1,0:T(8,128)S(1)}, f32[128,128]{1,0:T(8,128)S(1)}, u32[]{:S(2)}, u32[]{:S(2)}) %collective-permute-start.9) | collective-permute-done | bytes 65568 | tf_op jit(solution)/shard_map/ppermute | solution.py:190
  24.5 1.0 %collective-permute-done.10 = f32[128,128]{1,0:T(8,128)S(1)} collective-permute-done((f32[128,128]{1,0:T(8,128)S(1)}, f32[128,128]{1,0:T(8,128)S(1)}, u32[]{:S(2)}, u32[]{:S(2)}) %collective-permute-start.10) | collective-permute-done | bytes 65568 | tf_op jit(solution)/shard_map/ppermute | solution.py:190
  25.5 0.1 collective-permute-start.14
  25.6 1.6 %collective-permute-start.13 = (f32[128,128]{1,0:T(8,128)S(1)}, f32[128,128]{1,0:T(8,128)S(1)}, u32[]{:S(2)}, u32[]{:S(2)}) collective-permute-start(f32[128,128]{1,0:T(8,128)S(1)} %add_add_fusion.2.rest_0_), channel_id=1, source_target_pairs={{0,8},{1,9},{2,10},{3,11},{4,12},{5,13},{6,14},{7,15},{8,0},{9,1},... | collective-permute-start | bytes 196616 | tf_op jit(solution)/shard_map/ppermute | solution.py:190
  27.2 1.1 %collective-permute-start.12 = (f32[128,128]{1,0:T(8,128)S(1)}, f32[128,128]{1,0:T(8,128)S(1)}, u32[]{:S(2)}, u32[]{:S(2)}) collective-permute-start(f32[128,128]{1,0:T(8,128)S(1)} %add_add_fusion.2.rest_0_), channel_id=1, source_target_pairs={{0,4},{1,5},{2,6},{3,7},{4,0},{5,1},{6,2},{7,3},{8,12},{9,13},{10,... | collective-permute-start | bytes 196616 | tf_op jit(solution)/shard_map/ppermute | solution.py:190
  28.2 3.8 %collective-permute-start.11 = (f32[128,128]{1,0:T(8,128)S(1)}, f32[128,128]{1,0:T(8,128)S(1)}, u32[]{:S(2)}, u32[]{:S(2)}) collective-permute-start(f32[128,128]{1,0:T(8,128)S(1)} %add_add_fusion.2.rest_0_), channel_id=1, source_target_pairs={{0,2},{1,3},{2,0},{3,1},{4,6},{5,7},{6,4},{7,5},{8,10},{9,11},{10,... | collective-permute-start | bytes 196616 | tf_op jit(solution)/shard_map/ppermute | solution.py:190
  32.1 0.9 %collective-permute-done.11.rest_1_ = f32[128,128]{1,0:T(8,128)S(1)} collective-permute-done((f32[128,128]{1,0:T(8,128)S(1)}, f32[128,128]{1,0:T(8,128)S(1)}, u32[]{:S(2)}, u32[]{:S(2)}) %collective-permute-start.11) | collective-permute-done | bytes 65568 | tf_op jit(solution)/shard_map/ppermute | solution.py:190
  33.0 0.6 next_step.4
  33.7 0.2 turn.6
  33.9 3.9 %collective-permute-done.15 = f32[128,128]{1,0:T(8,128)S(1)} collective-permute-done((f32[128,128]{1,0:T(8,128)S(1)}, f32[128,128]{1,0:T(8,128)S(1)}, u32[]{:S(2)}, u32[]{:S(2)}) %collective-permute-start.15) | collective-permute-done | bytes 65568 | tf_op jit(solution)/shard_map/ppermute | solution.py:190
  37.8 1.0 %collective-permute-done.16 = f32[128,128]{1,0:T(8,128)S(1)} collective-permute-done((f32[128,128]{1,0:T(8,128)S(1)}, f32[128,128]{1,0:T(8,128)S(1)}, u32[]{:S(2)}, u32[]{:S(2)}) %collective-permute-start.16) | collective-permute-done | bytes 65568 | tf_op jit(solution)/shard_map/ppermute | solution.py:190
  38.8 0.1 collective-permute-start.20
  38.8 1.5 %collective-permute-start.19 = (f32[128,128]{1,0:T(8,128)S(1)}, f32[128,128]{1,0:T(8,128)S(1)}, u32[]{:S(2)}, u32[]{:S(2)}) collective-permute-start(f32[128,128]{1,0:T(8,128)S(1)} %add_add_fusion.1.rest_0_), channel_id=1, source_target_pairs={{0,8},{1,9},{2,10},{3,11},{4,12},{5,13},{6,14},{7,15},{8,0},{9,1},... | collective-permute-start | bytes 196616 | tf_op jit(solution)/shard_map/ppermute | solution.py:190
  40.4 1.1 %collective-permute-start.18 = (f32[128,128]{1,0:T(8,128)S(1)}, f32[128,128]{1,0:T(8,128)S(1)}, u32[]{:S(2)}, u32[]{:S(2)}) collective-permute-start(f32[128,128]{1,0:T(8,128)S(1)} %add_add_fusion.1.rest_0_), channel_id=1, source_target_pairs={{0,4},{1,5},{2,6},{3,7},{4,0},{5,1},{6,2},{7,3},{8,12},{9,13},{10,... | collective-permute-start | bytes 196616 | tf_op jit(solution)/shard_map/ppermute | solution.py:190
  41.5 4.1 %collective-permute-start.17 = (f32[128,128]{1,0:T(8,128)S(1)}, f32[128,128]{1,0:T(8,128)S(1)}, u32[]{:S(2)}, u32[]{:S(2)}) collective-permute-start(f32[128,128]{1,0:T(8,128)S(1)} %add_add_fusion.1.rest_0_), channel_id=1, source_target_pairs={{0,2},{1,3},{2,0},{3,1},{4,6},{5,7},{6,4},{7,5},{8,10},{9,11},{10,... | collective-permute-start | bytes 196616 | tf_op jit(solution)/shard_map/ppermute | solution.py:190
  45.6 0.9 %collective-permute-done.17.rest_1_ = f32[128,128]{1,0:T(8,128)S(1)} collective-permute-done((f32[128,128]{1,0:T(8,128)S(1)}, f32[128,128]{1,0:T(8,128)S(1)}, u32[]{:S(2)}, u32[]{:S(2)}) %collective-permute-start.17) | collective-permute-done | bytes 65568 | tf_op jit(solution)/shard_map/ppermute | solution.py:190
  46.5 0.6 next_step.5
  47.1 0.3 collective-permute-start.23
  47.5 0.2 turn.7
  47.6 2.4 %collective-permute-start.21 = (f32[8,64,128]{2,1,0:T(8,128)S(1)}, f32[8,64,128]{2,1,0:T(8,128)S(1)}, u32[]{:S(2)}, u32[]{:S(2)}) collective-permute-start(f32[8,64,128]{2,1,0:T(8,128)S(1)} %get-tuple-element.47.refs_0_), channel_id=1, source_target_pairs={{0,2},{1,3},{2,0},{3,1},{4,6},{5,7},{6,4},{7,5},{8,10},{9,11},{10,... | collective-permute-start | bytes 786440 | tf_op jit(solution)/shard_map/ppermute | solution.py:190
  50.1 1.2 %collective-permute-done.22 = f32[128,128]{1,0:T(8,128)S(1)} collective-permute-done((f32[128,128]{1,0:T(8,128)S(1)}, f32[128,128]{1,0:T(8,128)S(1)}, u32[]{:S(2)}, u32[]{:S(2)}) %collective-permute-start.22) | collective-permute-done | bytes 65568 | tf_op jit(solution)/shard_map/ppermute | solution.py:190
  51.3 1.0 %collective-permute-done.23 = f32[128,128]{1,0:T(8,128)S(1)} collective-permute-done((f32[128,128]{1,0:T(8,128)S(1)}, f32[128,128]{1,0:T(8,128)S(1)}, u32[]{:S(2)}, u32[]{:S(2)}) %collective-permute-start.23) | collective-permute-done | bytes 65568 | tf_op jit(solution)/shard_map/ppermute | solution.py:190
  52.3 0.4 collective-permute-start.26
  52.6 1.9 %collective-permute-start.25 = (f32[128,128]{1,0:T(8,128)S(1)}, f32[128,128]{1,0:T(8,128)S(1)}, u32[]{:S(2)}, u32[]{:S(2)}) collective-permute-start(f32[128,128]{1,0:T(8,128)S(1)} %add_add_fusion.refs_2_), channel_id=1, source_target_pairs={{0,8},{1,9},{2,10},{3,11},{4,12},{5,13},{6,14},{7,15},{8,0},{9,1},... | collective-permute-start | bytes 196616 | tf_op jit(solution)/shard_map/ppermute | solution.py:190
  54.5 0.5 collective-permute-start.24
  55.0 4.6 %collective-permute-start.27 = (f32[128,128]{1,0:T(8,128)S(1)}, f32[128,128]{1,0:T(8,128)S(1)}, u32[]{:S(2)}, u32[]{:S(2)}) collective-permute-start(f32[128,128]{1,0:T(8,128)S(1)} %add_add_fusion.refs_2_), channel_id=1, source_target_pairs={{0,2},{1,3},{2,0},{3,1},{4,6},{5,7},{6,4},{7,5},{8,10},{9,11},{10,... | collective-permute-start | bytes 196616 | tf_op jit(solution)/shard_map/ppermute | solution.py:190
  59.6 1.7 %collective-permute-start.30 = (f32[128,128]{1,0:T(8,128)S(1)}, f32[128,128]{1,0:T(8,128)S(1)}, u32[]{:S(2)}, u32[]{:S(2)}) collective-permute-start(f32[128,128]{1,0:T(8,128)S(1)} %collective-permute-done.26.refs_5_), channel_id=1, source_target_pairs={{0,2},{1,3},{2,0},{3,1},{4,6},{5,7},{6,4},{7,5},{8,10},{9,11},{10,... | collective-permute-start | bytes 196616 | tf_op jit(solution)/shard_map/ppermute | solution.py:190
  61.2 0.1 collective-permute-start.29
  61.4 1.3 %collective-permute-start.28 = (f32[128,128]{1,0:T(8,128)S(1)}, f32[128,128]{1,0:T(8,128)S(1)}, u32[]{:S(2)}, u32[]{:S(2)}) collective-permute-start(f32[128,128]{1,0:T(8,128)S(1)} %collective-permute-done.24.refs_3_), channel_id=1, source_target_pairs={{0,2},{1,3},{2,0},{3,1},{4,6},{5,7},{6,4},{7,5},{8,10},{9,11},{10,... | collective-permute-start | bytes 196616 | tf_op jit(solution)/shard_map/ppermute | solution.py:190
  62.7 0.9 %collective-permute-done.28.refs_7_ = f32[128,128]{1,0:T(8,128)S(1)} collective-permute-done((f32[128,128]{1,0:T(8,128)S(1)}, f32[128,128]{1,0:T(8,128)S(1)}, u32[]{:S(2)}, u32[]{:S(2)}) %collective-permute-start.28) | collective-permute-done | bytes 65568 | tf_op jit(solution)/shard_map/ppermute | solution.py:190
  63.6 0.9 %last_step.1 = f32[1024,128]{1,0:T(8,128)} custom-call(f32[8,64,128]{2,1,0:T(8,128)S(1)} %get-tuple-element.47.refs_0_, f32[8,64,128]{2,1,0:T(8,128)S(1)} %collective-permute-done.21.refs_1_, f32[128,128]{1,0:T(8,128)S(1)} %add_add_fusion.refs_2_, f32[128,128]{1,0:T(8,128)S(1)} %collective-permute-done.24.refs_3_, ...), custom_call_target="tpu_custom_call" | custom-call | tf_op jit(solution)/shard_map/last_step/pallas_call | solution.py:238
  (32 shorter events, 0.6 us)
Async XLA Ops:
  0.0 4.8 %collective-permute-start.1 = (f32[1024,128]{1,0:T(8,128)}, f32[1024,128]{1,0:T(8,128)S(1)}, u32[]{:S(2)}, u32[]{:S(2)}) collective-permute-start(f32[1024,128]{1,0:T(8,128)} %bitcast.10), channel_id=1, source_target_pairs={{0,2},{1,3},{2,0},{3,1},{4,6},{5,7},{6,4},{7,5},{8,10},{9,11},{10,... | collective-permute-start | bytes 1572872 | tf_op jit(solution)/shard_map/ppermute | solution.py:190
  0.7 4.1 %collective-permute-start.2 = (f32[1024,128]{1,0:T(8,128)}, f32[1024,128]{1,0:T(8,128)S(1)}, u32[]{:S(2)}, u32[]{:S(2)}) collective-permute-start(f32[1024,128]{1,0:T(8,128)} %bitcast.12), channel_id=1, source_target_pairs={{0,2},{1,3},{2,0},{3,1},{4,6},{5,7},{6,4},{7,5},{8,10},{9,11},{10,... | collective-permute-start | bytes 1572872 | tf_op jit(solution)/shard_map/ppermute | solution.py:190
  2.1 2.6 %collective-permute-start = (s32[2,128]{1,0:T(2,128)S(1)}, s32[2,128]{1,0:T(2,128)S(1)}, u32[]{:S(2)}, u32[]{:S(2)}) collective-permute-start(s32[2,128]{1,0:T(2,128)S(1)} %broadcast_in_dim.2.limits_ref), channel_id=1, source_target_pairs={{0,2},{1,3},{2,0},{3,1},{4,6},{5,7},{6,4},{7,5},{8,10},{9,11},{10,... | collective-permute-start | bytes 3080 | tf_op jit(solution)/shard_map/ppermute | solution.py:190
  2.6 17.2 %copy-start = (f32[4,128,8,128]{3,2,1,0:T(8,128)S(1)}, f32[4,128,8,128]{3,2,1,0:T(8,128)}, u32[]{:S(2)}) copy-start(f32[4,128,8,128]{3,2,1,0:T(8,128)} %param.11) | copy-start | bytes 6291460
  5.1 6.3 %collective-permute-start.3 = (f32[128,128]{1,0:T(8,128)S(1)}, f32[128,128]{1,0:T(8,128)S(1)}, u32[]{:S(2)}, u32[]{:S(2)}) collective-permute-start(f32[128,128]{1,0:T(8,128)S(1)} %get-tuple-element.36.part_ref), channel_id=1, source_target_pairs={{1,0},{3,2},{5,4},{7,6},{9,8},{11,10},{13,12},{15,14},{16,17},{18,... | collective-permute-start | bytes 196616 | tf_op jit(solution)/shard_map/ppermute | solution.py:190
  6.4 7.1 %collective-permute-start.4 = (f32[128,128]{1,0:T(8,128)S(1)}, f32[128,128]{1,0:T(8,128)S(1)}, u32[]{:S(2)}, u32[]{:S(2)}) collective-permute-start(f32[128,128]{1,0:T(8,128)S(1)} %get-tuple-element.37.far_ref), channel_id=1, source_target_pairs={{1,16},{3,18},{5,20},{7,22},{9,24},{11,26},{13,28},{15,30},{16,1},... | collective-permute-start | bytes 196616 | tf_op jit(solution)/shard_map/ppermute | solution.py:190
  13.6 4.1 %collective-permute-start.8 = (f32[128,128]{1,0:T(8,128)S(1)}, f32[128,128]{1,0:T(8,128)S(1)}, u32[]{:S(2)}, u32[]{:S(2)}) collective-permute-start(f32[128,128]{1,0:T(8,128)S(1)} %add_add_fusion.3.rest_0_), channel_id=1, source_target_pairs={{0,12},{1,13},{2,14},{3,15},{4,8},{5,9},{6,10},{7,11},{8,4},{9,5},... | collective-permute-start | bytes 196616 | tf_op jit(solution)/shard_map/ppermute | solution.py:190
  13.6 5.4 %collective-permute-start.7 = (f32[128,128]{1,0:T(8,128)S(1)}, f32[128,128]{1,0:T(8,128)S(1)}, u32[]{:S(2)}, u32[]{:S(2)}) collective-permute-start(f32[128,128]{1,0:T(8,128)S(1)} %add_add_fusion.3.rest_0_), channel_id=1, source_target_pairs={{0,8},{1,9},{2,10},{3,11},{4,12},{5,13},{6,14},{7,15},{8,0},{9,1},... | collective-permute-start | bytes 196616 | tf_op jit(solution)/shard_map/ppermute | solution.py:190
  16.0 3.8 %collective-permute-start.6 = (f32[128,128]{1,0:T(8,128)S(1)}, f32[128,128]{1,0:T(8,128)S(1)}, u32[]{:S(2)}, u32[]{:S(2)}) collective-permute-start(f32[128,128]{1,0:T(8,128)S(1)} %add_add_fusion.3.rest_0_), channel_id=1, source_target_pairs={{0,4},{1,5},{2,6},{3,7},{4,0},{5,1},{6,2},{7,3},{8,12},{9,13},{10,... | collective-permute-start | bytes 196616 | tf_op jit(solution)/shard_map/ppermute | solution.py:190
  16.3 3.6 %collective-permute-start.5 = (f32[128,128]{1,0:T(8,128)S(1)}, f32[128,128]{1,0:T(8,128)S(1)}, u32[]{:S(2)}, u32[]{:S(2)}) collective-permute-start(f32[128,128]{1,0:T(8,128)S(1)} %add_add_fusion.3.rest_0_), channel_id=1, source_target_pairs={{0,2},{1,3},{2,0},{3,1},{4,6},{5,7},{6,4},{7,5},{8,10},{9,11},{10,... | collective-permute-start | bytes 196616 | tf_op jit(solution)/shard_map/ppermute | solution.py:190
  20.5 4.1 %collective-permute-start.9 = (f32[128,128]{1,0:T(8,128)S(1)}, f32[128,128]{1,0:T(8,128)S(1)}, u32[]{:S(2)}, u32[]{:S(2)}) collective-permute-start(f32[128,128]{1,0:T(8,128)S(1)} %get-tuple-element.41.part_ref), channel_id=1, source_target_pairs={{1,0},{3,2},{5,4},{7,6},{9,8},{11,10},{13,12},{15,14},{16,17},{18,... | collective-permute-start | bytes 196616 | tf_op jit(solution)/shard_map/ppermute | solution.py:190
  20.5 5.0 %collective-permute-start.10 = (f32[128,128]{1,0:T(8,128)S(1)}, f32[128,128]{1,0:T(8,128)S(1)}, u32[]{:S(2)}, u32[]{:S(2)}) collective-permute-start(f32[128,128]{1,0:T(8,128)S(1)} %get-tuple-element.42.far_ref), channel_id=1, source_target_pairs={{1,16},{3,18},{5,20},{7,22},{9,24},{11,26},{13,28},{15,30},{16,1},... | collective-permute-start | bytes 196616 | tf_op jit(solution)/shard_map/ppermute | solution.py:190
  25.5 6.5 %collective-permute-start.14 = (f32[128,128]{1,0:T(8,128)S(1)}, f32[128,128]{1,0:T(8,128)S(1)}, u32[]{:S(2)}, u32[]{:S(2)}) collective-permute-start(f32[128,128]{1,0:T(8,128)S(1)} %add_add_fusion.2.rest_0_), channel_id=1, source_target_pairs={{0,12},{1,13},{2,14},{3,15},{4,8},{5,9},{6,10},{7,11},{8,4},{9,5},... | collective-permute-start | bytes 196616 | tf_op jit(solution)/shard_map/ppermute | solution.py:190
  25.6 6.5 %collective-permute-start.13 = (f32[128,128]{1,0:T(8,128)S(1)}, f32[128,128]{1,0:T(8,128)S(1)}, u32[]{:S(2)}, u32[]{:S(2)}) collective-permute-start(f32[128,128]{1,0:T(8,128)S(1)} %add_add_fusion.2.rest_0_), channel_id=1, source_target_pairs={{0,8},{1,9},{2,10},{3,11},{4,12},{5,13},{6,14},{7,15},{8,0},{9,1},... | collective-permute-start | bytes 196616 | tf_op jit(solution)/shard_map/ppermute | solution.py:190
  27.2 4.9 %collective-permute-start.12 = (f32[128,128]{1,0:T(8,128)S(1)}, f32[128,128]{1,0:T(8,128)S(1)}, u32[]{:S(2)}, u32[]{:S(2)}) collective-permute-start(f32[128,128]{1,0:T(8,128)S(1)} %add_add_fusion.2.rest_0_), channel_id=1, source_target_pairs={{0,4},{1,5},{2,6},{3,7},{4,0},{5,1},{6,2},{7,3},{8,12},{9,13},{10,... | collective-permute-start | bytes 196616 | tf_op jit(solution)/shard_map/ppermute | solution.py:190
  28.2 4.7 %collective-permute-start.11 = (f32[128,128]{1,0:T(8,128)S(1)}, f32[128,128]{1,0:T(8,128)S(1)}, u32[]{:S(2)}, u32[]{:S(2)}) collective-permute-start(f32[128,128]{1,0:T(8,128)S(1)} %add_add_fusion.2.rest_0_), channel_id=1, source_target_pairs={{0,2},{1,3},{2,0},{3,1},{4,6},{5,7},{6,4},{7,5},{8,10},{9,11},{10,... | collective-permute-start | bytes 196616 | tf_op jit(solution)/shard_map/ppermute | solution.py:190
  33.6 4.2 %collective-permute-start.15 = (f32[128,128]{1,0:T(8,128)S(1)}, f32[128,128]{1,0:T(8,128)S(1)}, u32[]{:S(2)}, u32[]{:S(2)}) collective-permute-start(f32[128,128]{1,0:T(8,128)S(1)} %get-tuple-element.45.part_ref), channel_id=1, source_target_pairs={{1,0},{3,2},{5,4},{7,6},{9,8},{11,10},{13,12},{15,14},{16,17},{18,... | collective-permute-start | bytes 196616 | tf_op jit(solution)/shard_map/ppermute | solution.py:190
  33.6 5.1 %collective-permute-start.16 = (f32[128,128]{1,0:T(8,128)S(1)}, f32[128,128]{1,0:T(8,128)S(1)}, u32[]{:S(2)}, u32[]{:S(2)}) collective-permute-start(f32[128,128]{1,0:T(8,128)S(1)} %get-tuple-element.46.far_ref), channel_id=1, source_target_pairs={{1,16},{3,18},{5,20},{7,22},{9,24},{11,26},{13,28},{15,30},{16,1},... | collective-permute-start | bytes 196616 | tf_op jit(solution)/shard_map/ppermute | solution.py:190
  38.8 6.8 %collective-permute-start.20 = (f32[128,128]{1,0:T(8,128)S(1)}, f32[128,128]{1,0:T(8,128)S(1)}, u32[]{:S(2)}, u32[]{:S(2)}) collective-permute-start(f32[128,128]{1,0:T(8,128)S(1)} %add_add_fusion.1.rest_0_), channel_id=1, source_target_pairs={{0,12},{1,13},{2,14},{3,15},{4,8},{5,9},{6,10},{7,11},{8,4},{9,5},... | collective-permute-start | bytes 196616 | tf_op jit(solution)/shard_map/ppermute | solution.py:190
  38.8 6.7 %collective-permute-start.19 = (f32[128,128]{1,0:T(8,128)S(1)}, f32[128,128]{1,0:T(8,128)S(1)}, u32[]{:S(2)}, u32[]{:S(2)}) collective-permute-start(f32[128,128]{1,0:T(8,128)S(1)} %add_add_fusion.1.rest_0_), channel_id=1, source_target_pairs={{0,8},{1,9},{2,10},{3,11},{4,12},{5,13},{6,14},{7,15},{8,0},{9,1},... | collective-permute-start | bytes 196616 | tf_op jit(solution)/shard_map/ppermute | solution.py:190
  40.4 5.2 %collective-permute-start.18 = (f32[128,128]{1,0:T(8,128)S(1)}, f32[128,128]{1,0:T(8,128)S(1)}, u32[]{:S(2)}, u32[]{:S(2)}) collective-permute-start(f32[128,128]{1,0:T(8,128)S(1)} %add_add_fusion.1.rest_0_), channel_id=1, source_target_pairs={{0,4},{1,5},{2,6},{3,7},{4,0},{5,1},{6,2},{7,3},{8,12},{9,13},{10,... | collective-permute-start | bytes 196616 | tf_op jit(solution)/shard_map/ppermute | solution.py:190
  41.5 5.0 %collective-permute-start.17 = (f32[128,128]{1,0:T(8,128)S(1)}, f32[128,128]{1,0:T(8,128)S(1)}, u32[]{:S(2)}, u32[]{:S(2)}) collective-permute-start(f32[128,128]{1,0:T(8,128)S(1)} %add_add_fusion.1.rest_0_), channel_id=1, source_target_pairs={{0,2},{1,3},{2,0},{3,1},{4,6},{5,7},{6,4},{7,5},{8,10},{9,11},{10,... | collective-permute-start | bytes 196616 | tf_op jit(solution)/shard_map/ppermute | solution.py:190
  47.1 4.2 %collective-permute-start.22 = (f32[128,128]{1,0:T(8,128)S(1)}, f32[128,128]{1,0:T(8,128)S(1)}, u32[]{:S(2)}, u32[]{:S(2)}) collective-permute-start(f32[128,128]{1,0:T(8,128)S(1)} %get-tuple-element.48.part_ref), channel_id=1, source_target_pairs={{1,0},{3,2},{5,4},{7,6},{9,8},{11,10},{13,12},{15,14},{16,17},{18,... | collective-permute-start | bytes 196616 | tf_op jit(solution)/shard_map/ppermute | solution.py:190
  47.1 5.1 %collective-permute-start.23 = (f32[128,128]{1,0:T(8,128)S(1)}, f32[128,128]{1,0:T(8,128)S(1)}, u32[]{:S(2)}, u32[]{:S(2)}) collective-permute-start(f32[128,128]{1,0:T(8,128)S(1)} %get-tuple-element.49.far_ref), channel_id=1, source_target_pairs={{1,16},{3,18},{5,20},{7,22},{9,24},{11,26},{13,28},{15,30},{16,1},... | collective-permute-start | bytes 196616 | tf_op jit(solution)/shard_map/ppermute | solution.py:190
  47.6 15.9 %collective-permute-start.21 = (f32[8,64,128]{2,1,0:T(8,128)S(1)}, f32[8,64,128]{2,1,0:T(8,128)S(1)}, u32[]{:S(2)}, u32[]{:S(2)}) collective-permute-start(f32[8,64,128]{2,1,0:T(8,128)S(1)} %get-tuple-element.47.refs_0_), channel_id=1, source_target_pairs={{0,2},{1,3},{2,0},{3,1},{4,6},{5,7},{6,4},{7,5},{8,10},{9,11},{10,... | collective-permute-start | bytes 786440 | tf_op jit(solution)/shard_map/ppermute | solution.py:190
  52.3 7.3 %collective-permute-start.26 = (f32[128,128]{1,0:T(8,128)S(1)}, f32[128,128]{1,0:T(8,128)S(1)}, u32[]{:S(2)}, u32[]{:S(2)}) collective-permute-start(f32[128,128]{1,0:T(8,128)S(1)} %add_add_fusion.refs_2_), channel_id=1, source_target_pairs={{0,12},{1,13},{2,14},{3,15},{4,8},{5,9},{6,10},{7,11},{8,4},{9,5},... | collective-permute-start | bytes 196616 | tf_op jit(solution)/shard_map/ppermute | solution.py:190
  52.6 8.6 %collective-permute-start.25 = (f32[128,128]{1,0:T(8,128)S(1)}, f32[128,128]{1,0:T(8,128)S(1)}, u32[]{:S(2)}, u32[]{:S(2)}) collective-permute-start(f32[128,128]{1,0:T(8,128)S(1)} %add_add_fusion.refs_2_), channel_id=1, source_target_pairs={{0,8},{1,9},{2,10},{3,11},{4,12},{5,13},{6,14},{7,15},{8,0},{9,1},... | collective-permute-start | bytes 196616 | tf_op jit(solution)/shard_map/ppermute | solution.py:190
  54.5 6.9 %collective-permute-start.24 = (f32[128,128]{1,0:T(8,128)S(1)}, f32[128,128]{1,0:T(8,128)S(1)}, u32[]{:S(2)}, u32[]{:S(2)}) collective-permute-start(f32[128,128]{1,0:T(8,128)S(1)} %add_add_fusion.refs_2_), channel_id=1, source_target_pairs={{0,4},{1,5},{2,6},{3,7},{4,0},{5,1},{6,2},{7,3},{8,12},{9,13},{10,... | collective-permute-start | bytes 196616 | tf_op jit(solution)/shard_map/ppermute | solution.py:190
  55.0 7.7 %collective-permute-start.27 = (f32[128,128]{1,0:T(8,128)S(1)}, f32[128,128]{1,0:T(8,128)S(1)}, u32[]{:S(2)}, u32[]{:S(2)}) collective-permute-start(f32[128,128]{1,0:T(8,128)S(1)} %add_add_fusion.refs_2_), channel_id=1, source_target_pairs={{0,2},{1,3},{2,0},{3,1},{4,6},{5,7},{6,4},{7,5},{8,10},{9,11},{10,... | collective-permute-start | bytes 196616 | tf_op jit(solution)/shard_map/ppermute | solution.py:190
  59.6 3.1 %collective-permute-start.30 = (f32[128,128]{1,0:T(8,128)S(1)}, f32[128,128]{1,0:T(8,128)S(1)}, u32[]{:S(2)}, u32[]{:S(2)}) collective-permute-start(f32[128,128]{1,0:T(8,128)S(1)} %collective-permute-done.26.refs_5_), channel_id=1, source_target_pairs={{0,2},{1,3},{2,0},{3,1},{4,6},{5,7},{6,4},{7,5},{8,10},{9,11},{10,... | collective-permute-start | bytes 196616 | tf_op jit(solution)/shard_map/ppermute | solution.py:190
  61.2 1.4 %collective-permute-start.29 = (f32[128,128]{1,0:T(8,128)S(1)}, f32[128,128]{1,0:T(8,128)S(1)}, u32[]{:S(2)}, u32[]{:S(2)}) collective-permute-start(f32[128,128]{1,0:T(8,128)S(1)} %collective-permute-done.25.refs_4_), channel_id=1, source_target_pairs={{0,2},{1,3},{2,0},{3,1},{4,6},{5,7},{6,4},{7,5},{8,10},{9,11},{10,... | collective-permute-start | bytes 196616 | tf_op jit(solution)/shard_map/ppermute | solution.py:190
  61.4 2.2 %collective-permute-start.28 = (f32[128,128]{1,0:T(8,128)S(1)}, f32[128,128]{1,0:T(8,128)S(1)}, u32[]{:S(2)}, u32[]{:S(2)}) collective-permute-start(f32[128,128]{1,0:T(8,128)S(1)} %collective-permute-done.24.refs_3_), channel_id=1, source_target_pairs={{0,2},{1,3},{2,0},{3,1},{4,6},{5,7},{6,4},{7,5},{8,10},{9,11},{10,... | collective-permute-start | bytes 196616 | tf_op jit(solution)/shard_map/ppermute | solution.py:190

commit v8 on v7

--- a/solution.py
+++ b/solution.py
@@ -38,31 +38,52 @@
     return lax.rem(hist_pos, rows_dev), lax.rem(hist_pos, 2), lax.axis_index("col")
 
 
+def slots(rows_dev, late):
+    pairs = range(2, rows_dev - 2, 2) if late else (0, rows_dev - 2)
+    return [pair + j for pair in pairs for j in range(2)]
+
+
 def every(first, s, half, rows_dev):
     return pl.ds(first * rows_dev + s, half, stride=rows_dev)
 
 
-def sigmas(section, rows_dev, half, core, cur, g_ref, g_first, active_ref, strength_ref, sigma_ref):
+def sigmas(section, rows_dev, half, late, cur, g_ref, g_first, active_ref, strength_ref, sigma_ref):
     n = 2 * half
+    own_row, core, _ = places(rows_dev)
     strength = strength_ref[...]
-    for s in range(rows_dev):
-        x = cur[s]
+    near = slots(rows_dev, late)
+    for p, slot in enumerate(near):
+        s = jnp.bitwise_xor(own_row, slot)
+        x = cur[p]
         g = g_ref[every(g_first + core * half, s, half, rows_dev), :]
         u = strength * x * g
         less = -(u * x)
         ret = (u * x - u * g) * active_ref[pl.ds(section * rows_dev + s, 1), :]
-        for where, value in ((s, ret), (rows_dev + s, less)):
+        for where, value in ((p, ret), (len(near) + p, less)):
             sigma_ref[:, where * n : (where + 1) * n] = tall(value)
 
 
-def split_tables(rows_dev, n, col_pos, cutoff, lesser_ref, adv_ref, wide_ref):
-    for s in range(rows_dev):
-        inside = jnp.where(col_pos * rows_dev + s < cutoff, 1.0, 0.0).astype(F32)
-        wide_ref[s * n : (s + 1) * n, :] = wide(lesser_ref[s * n : (s + 1) * n, :])
-        wide_ref[(rows_dev + s) * n : (rows_dev + s + 1) * n, :] = wide(adv_ref[s * n : (s + 1) * n, :] * inside)
-
-
-def turn(half, ham_ref, near_ref, part_ref, far_ref, turned_ref):
+def split_tables(rows_dev, n, cutoff, lesser_ref, adv_ref, *wide_refs):
+    own_row, _, col_pos = places(rows_dev)
+    for late, wide_ref in enumerate(wide_refs):
+        near = slots(rows_dev, late)
+        for p, slot in enumerate(near):
+            s = jnp.bitwise_xor(own_row, slot)
+            inside = jnp.where(col_pos * rows_dev + s < cutoff, 1.0, 0.0).astype(F32)
+            rows = pl.ds(pl.multiple_of(s * n, n), n)
+            wide_ref[p * n : (p + 1) * n, :] = wide(lesser_ref[rows, :])
+            where = (len(near) + p) * n
+            wide_ref[where : where + n, :] = wide(adv_ref[rows, :] * inside)
+
+
+def turn(half, step, ham_ref, near_ref, part_ref, far_ref, *rest):
+    turned_ref = rest[-1]
+    if step:
+        own_ref, swapped_ref, new_ref = rest[:3]
+        for j in range(2):
+            new_ref[j, :half, :] = near_ref[j, :half, :] - STEP_SIZE * own_ref[j * half : (j + 1) * half, :]
+            new_ref[j, half:, :] = near_ref[j, half:, :] - STEP_SIZE * swapped_ref[(1 - j) * half : (2 - j) * half, :]
+        near_ref = new_ref
     for j in range(2):
         rows = slice(j * half, (j + 1) * half)
         turned_ref[rows, :] = product(ham_ref[...], wide(near_ref[j])) + (part_ref[rows, :] - far_ref[rows, :])
@@ -76,7 +97,7 @@
 
 
 def first_kernel(rows_dev, half, steps, limits_ref, lesser_hbm, adv_hbm, first_hbm, greater_hbm, coup_hbm, ham_hbm,
-                 cur_ref, wide_ref, active_ref, strength_ref, ham_ref, near_ref, sigma_ref, own_ref,
+                 cur_ref, late_cur_ref, wide_ref, late_wide_ref, active_ref, strength_ref, ham_ref, near_ref, sigma_ref, late_sigma_ref, own_ref,
                  lesser_ref, adv_ref, first_ref, g_ref, h_ref, sems):
     n = 2 * half
     own_row, core, col_pos = places(rows_dev)
@@ -107,38 +128,47 @@
     ham = h_ref[...]
     ham = tall(jnp.where(core == 0, ham, pltpu.roll(ham, half, 1)))
     ham_ref[...] = ham
-    for s in range(rows_dev):
-        cur_ref[s] = first_ref[every(mine, s, half, rows_dev), :]
-    sigmas(0, rows_dev, half, core, cur_ref, g_ref, 0, active_ref, strength_ref, sigma_ref)
+    for late, (c_ref, s_ref) in enumerate(((cur_ref, sigma_ref), (late_cur_ref, late_sigma_ref))):
+        for p, slot in enumerate(slots(rows_dev, late)):
+            c_ref[p] = first_ref[every(mine, jnp.bitwise_xor(own_row, slot), half, rows_dev), :]
+        sigmas(0, rows_dev, half, late, c_ref, g_ref, 0, active_ref, strength_ref, s_ref)
     for j in range(2):
         s = jnp.bitwise_xor(own_row, j)
         near_ref[j, :half, :] = first_ref[every(mine, s, half, rows_dev), :]
         near_ref[j, half:, :] = first_ref[every(other, s, half, rows_dev), :]
     for copy in copies[4:]:
         copy.wait()
-    split_tables(rows_dev, n, col_pos, cutoff, lesser_ref, adv_ref, wide_ref)
-    own_ref[...] = product(sigma_ref[...], wide_ref[...])
-
-
-def second_kernel(rows_dev, half, limits_ref, lesser_ref, adv_ref, sigma_ref, own_ref, wide_ref, part_ref, far_ref):
-    col_pos = lax.axis_index("col")
-    split_tables(rows_dev, 2 * half, col_pos, limits_ref[1:2, :], lesser_ref, adv_ref, wide_ref)
-    store(rows_dev, half, (own_ref[...], product(sigma_ref[...], wide_ref[...])), part_ref, far_ref)
-
-
-def next_kernel(section, rows_dev, half, prev_ref, prev_near_ref, greater_ref, active_ref, strength_ref, own_wide_ref, other_wide_ref, *rest):
-    own_ref, swapped_ref, *others = rest[: rows_dev // 2 + 1]
-    cur_ref, near_ref, part_ref, far_ref, sigma_ref = rest[rows_dev // 2 + 1 :]
-    own_row, core, _ = places(rows_dev)
-    for k, piece in enumerate([own_ref] + others):
+    split_tables(rows_dev, n, cutoff, lesser_ref, adv_ref, wide_ref, late_wide_ref)
+    own_ref[...] = product(sigma_ref[...], wide_ref[...]) + product(late_sigma_ref[...], late_wide_ref[...])
+
+
+def second_kernel(rows_dev, half, limits_ref, lesser_ref, adv_ref, sigma_ref, late_sigma_ref, own_ref, wide_ref, late_wide_ref, part_ref, far_ref):
+    split_tables(rows_dev, 2 * half, limits_ref[1:2, :], lesser_ref, adv_ref, wide_ref, late_wide_ref)
+    other = product(sigma_ref[...], wide_ref[...]) + product(late_sigma_ref[...], late_wide_ref[...])
+    store(rows_dev, half, (own_ref[...], other), part_ref, far_ref)
+
+
+def update(prev_ref, pieces, cur_ref, half):
+    for k, piece in enumerate(pieces):
         for j in range(2):
-            s = jnp.bitwise_xor(own_row, 2 * k + j)
-            cur_ref[s] = prev_ref[s] - STEP_SIZE * piece[j * half : (j + 1) * half, :]
-    for j in range(2):
-        near_ref[j, :half, :] = prev_near_ref[j, :half, :] - STEP_SIZE * own_ref[j * half : (j + 1) * half, :]
-        near_ref[j, half:, :] = prev_near_ref[j, half:, :] - STEP_SIZE * swapped_ref[(1 - j) * half : (2 - j) * half, :]
-    sigmas(section, rows_dev, half, core, cur_ref, greater_ref, section * 2 * half, active_ref, strength_ref, sigma_ref)
+            cur_ref[2 * k + j] = prev_ref[2 * k + j] - STEP_SIZE * piece[j * half : (j + 1) * half, :]
+
+
+def early_kernel(section, rows_dev, half, prev_ref, greater_ref, active_ref, strength_ref, own_wide_ref, other_wide_ref, *rest):
+    pieces, (cur_ref, part_ref, sigma_ref) = rest[:2], rest[2:]
+    update(prev_ref, pieces, cur_ref, half)
+    sigmas(section, rows_dev, half, 0, cur_ref, greater_ref, section * 2 * half, active_ref, strength_ref, sigma_ref)
+    part_ref[:half, :] = product(sigma_ref[...], own_wide_ref[...])
+    part_ref[half:, :] = product(sigma_ref[...], other_wide_ref[...])
+
+
+def late_kernel(section, rows_dev, half, prev_ref, greater_ref, active_ref, strength_ref, own_wide_ref, other_wide_ref, early_ref, *rest):
+    count = rows_dev // 2 - 2
+    pieces, (cur_ref, part_ref, far_ref, sigma_ref) = rest[:count], rest[count:]
+    update(prev_ref, pieces, cur_ref, half)
+    sigmas(section, rows_dev, half, 1, cur_ref, greater_ref, section * 2 * half, active_ref, strength_ref, sigma_ref)
     parts = [product(sigma_ref[...], table[...]) for table in (own_wide_ref, other_wide_ref)]
+    parts = [part + early_ref[j * half : (j + 1) * half, :] for j, part in enumerate(parts)]
     store(rows_dev, half, parts, part_ref, far_ref)
 
 
@@ -148,12 +178,13 @@
     out_hbm, out_ref, sems = refs[-3:]
     copies = []
     for away in range(2):
-        prev_ref, pieces = refs[away], refs[2 + away * count : 2 + (away + 1) * count]
+        prevs, pieces = refs[2 * away : 2 * away + 2], refs[4 + away * count : 4 + (away + 1) * count]
         side = jnp.bitwise_xor(core, away) * half
-        for k, piece in enumerate(pieces):
-            for j in range(2):
-                s = jnp.bitwise_xor(own_row, (2 * k + j) ^ away)
-                new = prev_ref[s] - STEP_SIZE * piece[j * half : (j + 1) * half, :]
+        for late, prev_ref in enumerate(prevs):
+            for p, slot in enumerate(slots(rows_dev, late)):
+                s = jnp.bitwise_xor(own_row, slot ^ away)
+                piece = pieces[slot // 2]
+                new = prev_ref[p] - STEP_SIZE * piece[slot % 2 * half : (slot % 2 + 1) * half, :]
                 out_ref[every(side, s, half, rows_dev), :] = new
         flat = pl.ds(pl.multiple_of(side * rows_dev, half * rows_dev), half * rows_dev)
         copies.append(pltpu.make_async_copy(out_ref.at[flat], out_hbm.at[flat], sems.at[away]))
@@ -208,37 +239,50 @@
     tables = lesser.reshape(flat), advanced.reshape(flat)
     limits = jnp.broadcast_to(jnp.concatenate([step_index, cutoff])[:, None], (2, n))
     near_out = out((2, n, n))
-    cur_out, pair_out, wide_out = out((rows_dev, half, n)), out((n, n)), out((2 * rows_dev * n, 2 * n), BF16)
-    sigma = (n, 2 * rows_dev * n)
-    current, own_wide, active, strength, ham, near, first_sigma, own_part = call(
+    few, rest = 4, rows_dev - 4
+    cur_outs = [out((count, half, n)) for count in (few, rest)]
+    wide_outs = [out((2 * count * n, 2 * n), BF16) for count in (few, rest)]
+    sigma_outs = [out((n, 2 * count * n), BF16) for count in (few, rest)]
+    pair_out = out((n, n))
+    *currents, own_wide, own_late_wide, active, strength, ham, near, sigma, late_sigma, own_part = call(
         functools.partial(first_kernel, rows_dev, half, steps),
         [vmem] + [hbm] * 6,
-        [cur_out, wide_out, out((steps * rows_dev, n)), out((half, n)), out((n, n), BF16), near_out, out(sigma, BF16), out((half, n))],
+        [*cur_outs, *wide_outs, out((steps * rows_dev, n)), out((half, n)), out((n, n), BF16), near_out, *sigma_outs, out((half, n))],
         [vmem(flat, F32)] * 4 + [vmem((half, n), F32), pltpu.SemaphoreType.DMA((6,))],
         "first_step",
     )(limits, *[
         pltpu.with_memory_space_constraint(x, hbm)
         for x in (*tables, first_row.reshape(flat), greater, coupling, hamiltonian)
     ])
-    other_wide, part, far = call(
+    other_wide, other_late_wide, part, far = call(
         functools.partial(second_kernel, rows_dev, half),
-        [vmem] * 5, [wide_out, pair_out, pair_out], [], "first_step_other",
-    )(flip(limits, 1), *[flip(x, 1) for x in tables], first_sigma, own_part)
-    def add_turned():
-        return call(functools.partial(turn, half), [vmem] * 4, [pair_out], [], "turn")(ham, near, part, far)[0]
-
-    for section in range(1, steps):
-        pieces = exchange(part, far, add_turned())
-        current, near, part, far = call(
-            functools.partial(next_kernel, section, rows_dev, half),
-            [vmem] * (8 + rows_dev // 2), [cur_out, near_out, pair_out, pair_out], [vmem(sigma, BF16)], "next_step",
-        )(current, near, greater, active, strength, own_wide, other_wide, *pieces)
-    pieces = exchange(part, far, add_turned())
-    own, swapped = [pieces[0]] + pieces[2:], pieces[1]
+        [vmem] * 6, [*wide_outs, pair_out, pair_out], [], "first_step_other",
+    )(flip(limits, 1), *[flip(x, 1) for x in tables], sigma, late_sigma, own_part)
+    swap = []
+    for section in range(1, steps + 1):
+        *new, turned = call(
+            functools.partial(turn, half, len(swap)), [vmem] * (4 + len(swap)), [near_out] * (len(swap) // 2) + [pair_out], [], "turn",
+        )(ham, near, part, far, *swap)
+        near = new[0] if new else near
+        own, swapped, *others = exchange(part, far, turned)
+        swap = [own, swapped]
+        if section == steps:
+            break
+        given = greater, active, strength
+        early, part = call(
+            functools.partial(early_kernel, section, rows_dev, half),
+            [vmem] * 8, [cur_outs[0], pair_out], [vmem(*x) for x in [((n, 2 * few * n), BF16)]], "next_step_early",
+        )(currents[0], *given, own_wide, other_wide, own, others[-1])
+        late, part, far = call(
+            functools.partial(late_kernel, section, rows_dev, half),
+            [vmem] * (7 + len(others) - 1), [cur_outs[1], pair_out, pair_out], [vmem((n, 2 * rest * n), BF16)], "next_step",
+        )(currents[1], *given, own_late_wide, other_late_wide, part, *others[:-1])
+        currents = [early, late]
+    pieces = [own] + others
     final = call(
         functools.partial(last_kernel, rows_dev, half),
-        [vmem] * (2 + rows_dev), [(shape(flat, F32), hbm)], [vmem(flat, F32), pltpu.SemaphoreType.DMA((2,))], "last_step",
-    )(current, flip(current, 1), *own, swapped, *[flip(x, 1) for x in own[1:]])[0]
+        [vmem] * (4 + rows_dev), [(shape(flat, F32), hbm)], [vmem(flat, F32), pltpu.SemaphoreType.DMA((2,))], "last_step",
+    )(*currents, *[flip(x, 1) for x in currents], *pieces, swapped, *[flip(x, 1) for x in others])[0]
     return final.reshape(first_row.shape)
 
 
@@ -273,7 +317,7 @@
 
     def on_device(lesser, *rest):
         rows_dev, _, cols_dev, _ = lesser.shape
-        if cols == 2 and cols_dev == 1 and hist == 2 * rows_dev and hist & (hist - 1) == 0 and rows_dev > 1:
+        if cols == 2 and cols_dev == 1 and hist == 2 * rows_dev and hist & (hist - 1) == 0 and rows_dev > 4:
             return in_pairs(hist, lesser, *rest)
         return in_general(lesser, *rest)
 

time: 64.7 us -> 64.2 us (level)
  waiting for transfers between devices: 23.7 us -> 20.8 us
  starting transfers between devices: 33.3 us -> 34.8 us
  Pallas kernels: 5.86 us -> 6.72 us
    ppermute x31 -> x32, waiting for transfers between devices: 23.7 us -> 20.8 us  [moved(): return lax.ppermute(x, ('hist', 'col'), pairs)]
    ppermute x31 -> x32, starting transfers between devices: 33.3 us -> 34.8 us  [moved(): return lax.ppermute(x, ('hist', 'col'), pairs)]
    pallas_call x9 -> x12, Pallas kernels: 3.74 us -> 4.59 us  [the longest x4 1.23 us: in_pairs(): call(functools.partial(turn, half, len(swap)), [vmem] * (4 + len(swap)),...]
  transfers between devices with their start and end apart: 31 -> 32, of which waited for: 14 -> 14; matrix products, arithmetic and copies ran while one was open for 0% -> 0% of each run, Pallas kernels for 4% -> 9%
where the time goes in v8:
time: 64.2 us; the launch traced here: 64.1 us
  starting transfers between devices  34.8 us (54%)
  waiting for transfers between devices  20.8 us (32%)
  Pallas kernels  6.72 us (10%)
  between operations  1.55 us (2%)
    ppermute x32, starting transfers between devices, moved(): return lax.ppermute(x, ('hist', 'col'), pairs)  34.8 us
    ppermute x32, waiting for transfers between devices, moved(): return lax.ppermute(x, ('hist', 'col'), pairs)  20.8 us
    pallas_call x1, Pallas kernels, in_pairs(): call(functools.partial(first_kernel, rows_dev, half, steps), [vmem] + [hb...  2.13 us
  transfers between devices with their start and end apart: 32, of which 14 were waited for; matrix products, arithmetic and copies ran while one was open for 0% of the time, Pallas kernels for 9%

profile of v8, /device:TPU:25, one launch (start us, length us, event | category | flops | bytes accessed | tf_op | source)
XLA Modules:
  0.0 64.1 jit_solution(6179309453372294352)
XLA Ops:
  0.0 0.7 %collective-permute-start.1 = (f32[1024,128]{1,0:T(8,128)}, f32[1024,128]{1,0:T(8,128)S(1)}, u32[]{:S(2)}, u32[]{:S(2)}) collective-permute-start(f32[1024,128]{1,0:T(8,128)} %bitcast.13), channel_id=1, source_target_pairs={{0,2},{1,3},{2,0},{3,1},{4,6},{5,7},{6,4},{7,5},{8,10},{9,11},{10,... | collective-permute-start | bytes 1572872 | tf_op jit(solution)/shard_map/ppermute | solution.py:221
  2.0 0.1 pad_add_fusion
  2.1 0.5 collective-permute-start
  2.6 2.1 %first_step.1 = (f32[4,64,128]{2,1,0:T(8,128)S(1)}, f32[4,64,128]{2,1,0:T(8,128)S(1)}, bf16[1024,256]{1,0:T(8,128)(2,1)S(1)}, bf16[1024,256]{1,0:T(8,128)(2,1)S(...) custom-call(s32[2,128]{1,0:T(2,128)S(1)} %broadcast_in_dim.2.limits_, ...), custom_call_target="tpu_custom_call" | custom-call | tf_op jit(solution)/shard_map/first_step/pallas_call | solution.py:247
  4.8 0.4 first_step_other.1
  5.2 1.3 %collective-permute-start.3 = (f32[128,128]{1,0:T(8,128)S(1)}, f32[128,128]{1,0:T(8,128)S(1)}, u32[]{:S(2)}, u32[]{:S(2)}) collective-permute-start(f32[128,128]{1,0:T(8,128)S(1)} %get-tuple-element.48.part_ref), channel_id=1, source_target_pairs={{1,0},{3,2},{5,4},{7,6},{9,8},{11,10},{13,12},{15,14},{16,17},{18,... | collective-permute-start | bytes 196616 | tf_op jit(solution)/shard_map/ppermute | solution.py:221
  6.5 0.2 turn.4
  6.7 4.8 %collective-permute-done.3 = f32[128,128]{1,0:T(8,128)S(1)} collective-permute-done((f32[128,128]{1,0:T(8,128)S(1)}, f32[128,128]{1,0:T(8,128)S(1)}, u32[]{:S(2)}, u32[]{:S(2)}) %collective-permute-start.3) | collective-permute-done | bytes 65568 | tf_op jit(solution)/shard_map/ppermute | solution.py:221
  11.5 2.1 %collective-permute-done.4 = f32[128,128]{1,0:T(8,128)S(1)} collective-permute-done((f32[128,128]{1,0:T(8,128)S(1)}, f32[128,128]{1,0:T(8,128)S(1)}, u32[]{:S(2)}, u32[]{:S(2)}) %collective-permute-start.4) | collective-permute-done | bytes 65568 | tf_op jit(solution)/shard_map/ppermute | solution.py:221
  13.7 2.4 %collective-permute-start.7 = (f32[128,128]{1,0:T(8,128)S(1)}, f32[128,128]{1,0:T(8,128)S(1)}, u32[]{:S(2)}, u32[]{:S(2)}) collective-permute-start(f32[128,128]{1,0:T(8,128)S(1)} %add_add_fusion.3.rest_0_), channel_id=1, source_target_pairs={{0,8},{1,9},{2,10},{3,11},{4,12},{5,13},{6,14},{7,15},{8,0},{9,1},... | collective-permute-start | bytes 196616 | tf_op jit(solution)/shard_map/ppermute | solution.py:221
  16.1 0.2 collective-permute-start.6
  16.3 1.3 %collective-permute-start.10 = (f32[128,128]{1,0:T(8,128)S(1)}, f32[128,128]{1,0:T(8,128)S(1)}, u32[]{:S(2)}, u32[]{:S(2)}) collective-permute-start(f32[128,128]{1,0:T(8,128)S(1)} %add_add_fusion.3.rest_0_), channel_id=1, source_target_pairs={{0,2},{1,3},{2,0},{3,1},{4,6},{5,7},{6,4},{7,5},{8,10},{9,11},{10,... | collective-permute-start | bytes 196616 | tf_op jit(solution)/shard_map/ppermute | solution.py:221
  17.7 0.4 next_step_early.3
  18.1 1.1 %collective-permute-done.7.rest_1_ = f32[128,128]{1,0:T(8,128)S(1)} collective-permute-done((f32[128,128]{1,0:T(8,128)S(1)}, f32[128,128]{1,0:T(8,128)S(1)}, u32[]{:S(2)}, u32[]{:S(2)}) %collective-permute-start.7) | collective-permute-done | bytes 65568 | tf_op jit(solution)/shard_map/ppermute | solution.py:221
  19.1 0.8 %collective-permute-done.6.rest_0_ = f32[128,128]{1,0:T(8,128)S(1)} collective-permute-done((f32[128,128]{1,0:T(8,128)S(1)}, f32[128,128]{1,0:T(8,128)S(1)}, u32[]{:S(2)}, u32[]{:S(2)}) %collective-permute-start.6) | collective-permute-done | bytes 65568 | tf_op jit(solution)/shard_map/ppermute | solution.py:221
  19.9 0.3 next_step.3
  20.4 0.2 turn.5
  20.6 3.7 %collective-permute-done.8 = f32[128,128]{1,0:T(8,128)S(1)} collective-permute-done((f32[128,128]{1,0:T(8,128)S(1)}, f32[128,128]{1,0:T(8,128)S(1)}, u32[]{:S(2)}, u32[]{:S(2)}) %collective-permute-start.8) | collective-permute-done | bytes 65568 | tf_op jit(solution)/shard_map/ppermute | solution.py:221
  24.3 1.0 %collective-permute-done.9 = f32[128,128]{1,0:T(8,128)S(1)} collective-permute-done((f32[128,128]{1,0:T(8,128)S(1)}, f32[128,128]{1,0:T(8,128)S(1)}, u32[]{:S(2)}, u32[]{:S(2)}) %collective-permute-start.9) | collective-permute-done | bytes 65568 | tf_op jit(solution)/shard_map/ppermute | solution.py:221
  25.4 1.6 %collective-permute-start.13 = (f32[128,128]{1,0:T(8,128)S(1)}, f32[128,128]{1,0:T(8,128)S(1)}, u32[]{:S(2)}, u32[]{:S(2)}) collective-permute-start(f32[128,128]{1,0:T(8,128)S(1)} %add_add_fusion.2.rest_0_), channel_id=1, source_target_pairs={{0,8},{1,9},{2,10},{3,11},{4,12},{5,13},{6,14},{7,15},{8,0},{9,1},... | collective-permute-start | bytes 196616 | tf_op jit(solution)/shard_map/ppermute | solution.py:221
  27.0 1.1 %collective-permute-start.12 = (f32[128,128]{1,0:T(8,128)S(1)}, f32[128,128]{1,0:T(8,128)S(1)}, u32[]{:S(2)}, u32[]{:S(2)}) collective-permute-start(f32[128,128]{1,0:T(8,128)S(1)} %add_add_fusion.2.rest_0_), channel_id=1, source_target_pairs={{0,4},{1,5},{2,6},{3,7},{4,0},{5,1},{6,2},{7,3},{8,12},{9,13},{10,... | collective-permute-start | bytes 196616 | tf_op jit(solution)/shard_map/ppermute | solution.py:221
  28.0 3.8 %collective-permute-start.16 = (f32[128,128]{1,0:T(8,128)S(1)}, f32[128,128]{1,0:T(8,128)S(1)}, u32[]{:S(2)}, u32[]{:S(2)}) collective-permute-start(f32[128,128]{1,0:T(8,128)S(1)} %add_add_fusion.2.rest_0_), channel_id=1, source_target_pairs={{0,2},{1,3},{2,0},{3,1},{4,6},{5,7},{6,4},{7,5},{8,10},{9,11},{10,... | collective-permute-start | bytes 196616 | tf_op jit(solution)/shard_map/ppermute | solution.py:221
  31.9 0.3 next_step_early.4
  32.2 0.4 next_step.4
  32.8 0.2 turn.6
  32.9 3.8 %collective-permute-done.14 = f32[128,128]{1,0:T(8,128)S(1)} collective-permute-done((f32[128,128]{1,0:T(8,128)S(1)}, f32[128,128]{1,0:T(8,128)S(1)}, u32[]{:S(2)}, u32[]{:S(2)}) %collective-permute-start.14) | collective-permute-done | bytes 65568 | tf_op jit(solution)/shard_map/ppermute | solution.py:221
  36.8 1.0 %collective-permute-done.15 = f32[128,128]{1,0:T(8,128)S(1)} collective-permute-done((f32[128,128]{1,0:T(8,128)S(1)}, f32[128,128]{1,0:T(8,128)S(1)}, u32[]{:S(2)}, u32[]{:S(2)}) %collective-permute-start.15) | collective-permute-done | bytes 65568 | tf_op jit(solution)/shard_map/ppermute | solution.py:221
  37.9 1.5 %collective-permute-start.19 = (f32[128,128]{1,0:T(8,128)S(1)}, f32[128,128]{1,0:T(8,128)S(1)}, u32[]{:S(2)}, u32[]{:S(2)}) collective-permute-start(f32[128,128]{1,0:T(8,128)S(1)} %add_add_fusion.1.rest_0_), channel_id=1, source_target_pairs={{0,8},{1,9},{2,10},{3,11},{4,12},{5,13},{6,14},{7,15},{8,0},{9,1},... | collective-permute-start | bytes 196616 | tf_op jit(solution)/shard_map/ppermute | solution.py:221
  39.4 1.1 %collective-permute-start.18 = (f32[128,128]{1,0:T(8,128)S(1)}, f32[128,128]{1,0:T(8,128)S(1)}, u32[]{:S(2)}, u32[]{:S(2)}) collective-permute-start(f32[128,128]{1,0:T(8,128)S(1)} %add_add_fusion.1.rest_0_), channel_id=1, source_target_pairs={{0,4},{1,5},{2,6},{3,7},{4,0},{5,1},{6,2},{7,3},{8,12},{9,13},{10,... | collective-permute-start | bytes 196616 | tf_op jit(solution)/shard_map/ppermute | solution.py:221
  40.5 4.6 %collective-permute-start.24 = (f32[128,128]{1,0:T(8,128)S(1)}, f32[128,128]{1,0:T(8,128)S(1)}, u32[]{:S(2)}, u32[]{:S(2)}) collective-permute-start(f32[128,128]{1,0:T(8,128)S(1)} %add_add_fusion.1.rest_0_), channel_id=1, source_target_pairs={{0,2},{1,3},{2,0},{3,1},{4,6},{5,7},{6,4},{7,5},{8,10},{9,11},{10,... | collective-permute-start | bytes 196616 | tf_op jit(solution)/shard_map/ppermute | solution.py:221
  45.1 0.3 next_step_early.5
  45.5 0.3 next_step.5
  45.9 0.9 %collective-permute-start.23 = (f32[128,128]{1,0:T(8,128)S(1)}, f32[128,128]{1,0:T(8,128)S(1)}, u32[]{:S(2)}, u32[]{:S(2)}) collective-permute-start(f32[128,128]{1,0:T(8,128)S(1)} %get-tuple-element.72.far_ref), channel_id=1, source_target_pairs={{1,16},{3,18},{5,20},{7,22},{9,24},{11,26},{13,28},{15,30},{16,1},... | collective-permute-start | bytes 196616 | tf_op jit(solution)/shard_map/ppermute | solution.py:221
  46.8 2.4 %collective-permute-start.21 = (f32[4,64,128]{2,1,0:T(8,128)S(1)}, f32[4,64,128]{2,1,0:T(8,128)S(1)}, u32[]{:S(2)}, u32[]{:S(2)}) collective-permute-start(f32[4,64,128]{2,1,0:T(8,128)S(1)} %get-tuple-element.70.refs_1_), channel_id=1, source_target_pairs={{0,2},{1,3},{2,0},{3,1},{4,6},{5,7},{6,4},{7,5},{8,10},{9,11},{10,... | collective-permute-start | bytes 393224 | tf_op jit(solution)/shard_map/ppermute | solution.py:221
  49.2 0.7 %turn.7 = (f32[2,128,128]{2,1,0:T(8,128)}, f32[128,128]{1,0:T(8,128)S(1)}) custom-call(bf16[128,128]{1,0:T(8,128)(2,1)S(1)} %get-tuple-element.50.ham_ref, f32[2,128,128]{2,1,0:T(8,128)S(1)} %get-tuple-element.73.near_ref, f32[128,128]{1,0:T(8,128)S(1)} %get-tuple-element.71.part_ref, f32[128,128]{1,0:T(8,128)S(1)} %get-tuple-element.72.far_ref, ...), custom_call_target="tpu_custom_call" | custom-call | tf_op jit(solution)/shard_map/turn/pallas_call | solution.py:263
  49.9 0.2 collective-permute-done.22
  50.1 1.0 %collective-permute-done.23 = f32[128,128]{1,0:T(8,128)S(1)} collective-permute-done((f32[128,128]{1,0:T(8,128)S(1)}, f32[128,128]{1,0:T(8,128)S(1)}, u32[]{:S(2)}, u32[]{:S(2)}) %collective-permute-start.23) | collective-permute-done | bytes 65568 | tf_op jit(solution)/shard_map/ppermute | solution.py:221
  51.1 0.4 collective-permute-start.27
  51.5 4.0 %collective-permute-start.20 = (f32[4,64,128]{2,1,0:T(8,128)S(1)}, f32[4,64,128]{2,1,0:T(8,128)S(1)}, u32[]{:S(2)}, u32[]{:S(2)}) collective-permute-start(f32[4,64,128]{2,1,0:T(8,128)S(1)} %get-tuple-element.67.refs_0_), channel_id=1, source_target_pairs={{0,2},{1,3},{2,0},{3,1},{4,6},{5,7},{6,4},{7,5},{8,10},{9,11},{10,... | collective-permute-start | bytes 393224 | tf_op jit(solution)/shard_map/ppermute | solution.py:221
  55.5 1.8 %collective-permute-start.26 = (f32[128,128]{1,0:T(8,128)S(1)}, f32[128,128]{1,0:T(8,128)S(1)}, u32[]{:S(2)}, u32[]{:S(2)}) collective-permute-start(f32[128,128]{1,0:T(8,128)S(1)} %add_add_fusion.refs_4_), channel_id=1, source_target_pairs={{0,8},{1,9},{2,10},{3,11},{4,12},{5,13},{6,14},{7,15},{8,0},{9,1},... | collective-permute-start | bytes 196616 | tf_op jit(solution)/shard_map/ppermute | solution.py:221
  57.3 1.0 %collective-permute-start.25 = (f32[128,128]{1,0:T(8,128)S(1)}, f32[128,128]{1,0:T(8,128)S(1)}, u32[]{:S(2)}, u32[]{:S(2)}) collective-permute-start(f32[128,128]{1,0:T(8,128)S(1)} %add_add_fusion.refs_4_), channel_id=1, source_target_pairs={{0,4},{1,5},{2,6},{3,7},{4,0},{5,1},{6,2},{7,3},{8,12},{9,13},{10,... | collective-permute-start | bytes 196616 | tf_op jit(solution)/shard_map/ppermute | solution.py:221
  58.4 0.6 collective-permute-start.28
  58.9 2.3 %collective-permute-start.31 = (f32[128,128]{1,0:T(8,128)S(1)}, f32[128,128]{1,0:T(8,128)S(1)}, u32[]{:S(2)}, u32[]{:S(2)}) collective-permute-start(f32[128,128]{1,0:T(8,128)S(1)} %collective-permute-done.27.refs_7_), channel_id=1, source_target_pairs={{0,2},{1,3},{2,0},{3,1},{4,6},{5,7},{6,4},{7,5},{8,10},{9,11},{10,... | collective-permute-start | bytes 196616 | tf_op jit(solution)/shard_map/ppermute | solution.py:221
  61.2 0.3 collective-permute-done.25.refs_5_
  61.5 0.7 %collective-permute-start.29 = (f32[128,128]{1,0:T(8,128)S(1)}, f32[128,128]{1,0:T(8,128)S(1)}, u32[]{:S(2)}, u32[]{:S(2)}) collective-permute-start(f32[128,128]{1,0:T(8,128)S(1)} %collective-permute-done.25.refs_5_), channel_id=1, source_target_pairs={{0,2},{1,3},{2,0},{3,1},{4,6},{5,7},{6,4},{7,5},{8,10},{9,11},{10,... | collective-permute-start | bytes 196616 | tf_op jit(solution)/shard_map/ppermute | solution.py:221
  62.3 0.2 collective-permute-done.30.refs_10_
  62.5 0.7 %collective-permute-done.29.refs_9_ = f32[128,128]{1,0:T(8,128)S(1)} collective-permute-done((f32[128,128]{1,0:T(8,128)S(1)}, f32[128,128]{1,0:T(8,128)S(1)}, u32[]{:S(2)}, u32[]{:S(2)}) %collective-permute-start.29) | collective-permute-done | bytes 65568 | tf_op jit(solution)/shard_map/ppermute | solution.py:221
  63.2 0.9 %last_step.1 = f32[1024,128]{1,0:T(8,128)} custom-call(f32[4,64,128]{2,1,0:T(8,128)S(1)} %get-tuple-element.67.refs_0_, f32[4,64,128]{2,1,0:T(8,128)S(1)} %get-tuple-element.70.refs_1_, f32[4,64,128]{2,1,0:T(8,128)S(1)} %collective-permute-done.20.refs_2_, f32[4,64,128]{2,1,0:T(8,128)S(1)} %collective-permute-done.21.refs_3_, ...), custom_call_target="tpu_custom_call" | custom-call | tf_op jit(solution)/shard_map/last_step/pallas_call | solution.py:282
  (37 shorter events, 0.8 us)
Async XLA Ops:
  0.0 4.8 %collective-permute-start.1 = (f32[1024,128]{1,0:T(8,128)}, f32[1024,128]{1,0:T(8,128)S(1)}, u32[]{:S(2)}, u32[]{:S(2)}) collective-permute-start(f32[1024,128]{1,0:T(8,128)} %bitcast.13), channel_id=1, source_target_pairs={{0,2},{1,3},{2,0},{3,1},{4,6},{5,7},{6,4},{7,5},{8,10},{9,11},{10,... | collective-permute-start | bytes 1572872 | tf_op jit(solution)/shard_map/ppermute | solution.py:221
  0.7 4.1 %collective-permute-start.2 = (f32[1024,128]{1,0:T(8,128)}, f32[1024,128]{1,0:T(8,128)S(1)}, u32[]{:S(2)}, u32[]{:S(2)}) collective-permute-start(f32[1024,128]{1,0:T(8,128)} %bitcast.15), channel_id=1, source_target_pairs={{0,2},{1,3},{2,0},{3,1},{4,6},{5,7},{6,4},{7,5},{8,10},{9,11},{10,... | collective-permute-start | bytes 1572872 | tf_op jit(solution)/shard_map/ppermute | solution.py:221
  2.1 2.6 %collective-permute-start = (s32[2,128]{1,0:T(2,128)S(1)}, s32[2,128]{1,0:T(2,128)S(1)}, u32[]{:S(2)}, u32[]{:S(2)}) collective-permute-start(s32[2,128]{1,0:T(2,128)S(1)} %broadcast_in_dim.2.limits_ref), channel_id=1, source_target_pairs={{0,2},{1,3},{2,0},{3,1},{4,6},{5,7},{6,4},{7,5},{8,10},{9,11},{10,... | collective-permute-start | bytes 3080 | tf_op jit(solution)/shard_map/ppermute | solution.py:221
  2.6 15.1 %copy-start = (f32[4,128,8,128]{3,2,1,0:T(8,128)S(1)}, f32[4,128,8,128]{3,2,1,0:T(8,128)}, u32[]{:S(2)}) copy-start(f32[4,128,8,128]{3,2,1,0:T(8,128)} %param.11) | copy-start | bytes 6291460
  5.2 6.3 %collective-permute-start.3 = (f32[128,128]{1,0:T(8,128)S(1)}, f32[128,128]{1,0:T(8,128)S(1)}, u32[]{:S(2)}, u32[]{:S(2)}) collective-permute-start(f32[128,128]{1,0:T(8,128)S(1)} %get-tuple-element.48.part_ref), channel_id=1, source_target_pairs={{1,0},{3,2},{5,4},{7,6},{9,8},{11,10},{13,12},{15,14},{16,17},{18,... | collective-permute-start | bytes 196616 | tf_op jit(solution)/shard_map/ppermute | solution.py:221
  6.5 7.1 %collective-permute-start.4 = (f32[128,128]{1,0:T(8,128)S(1)}, f32[128,128]{1,0:T(8,128)S(1)}, u32[]{:S(2)}, u32[]{:S(2)}) collective-permute-start(f32[128,128]{1,0:T(8,128)S(1)} %get-tuple-element.49.far_ref), channel_id=1, source_target_pairs={{1,16},{3,18},{5,20},{7,22},{9,24},{11,26},{13,28},{15,30},{16,1},... | collective-permute-start | bytes 196616 | tf_op jit(solution)/shard_map/ppermute | solution.py:221
  13.6 4.1 %collective-permute-start.5 = (f32[128,128]{1,0:T(8,128)S(1)}, f32[128,128]{1,0:T(8,128)S(1)}, u32[]{:S(2)}, u32[]{:S(2)}) collective-permute-start(f32[128,128]{1,0:T(8,128)S(1)} %add_add_fusion.3.rest_0_), channel_id=1, source_target_pairs={{0,12},{1,13},{2,14},{3,15},{4,8},{5,9},{6,10},{7,11},{8,4},{9,5},... | collective-permute-start | bytes 196616 | tf_op jit(solution)/shard_map/ppermute | solution.py:221
  13.7 5.4 %collective-permute-start.7 = (f32[128,128]{1,0:T(8,128)S(1)}, f32[128,128]{1,0:T(8,128)S(1)}, u32[]{:S(2)}, u32[]{:S(2)}) collective-permute-start(f32[128,128]{1,0:T(8,128)S(1)} %add_add_fusion.3.rest_0_), channel_id=1, source_target_pairs={{0,8},{1,9},{2,10},{3,11},{4,12},{5,13},{6,14},{7,15},{8,0},{9,1},... | collective-permute-start | bytes 196616 | tf_op jit(solution)/shard_map/ppermute | solution.py:221
  16.1 3.8 %collective-permute-start.6 = (f32[128,128]{1,0:T(8,128)S(1)}, f32[128,128]{1,0:T(8,128)S(1)}, u32[]{:S(2)}, u32[]{:S(2)}) collective-permute-start(f32[128,128]{1,0:T(8,128)S(1)} %add_add_fusion.3.rest_0_), channel_id=1, source_target_pairs={{0,4},{1,5},{2,6},{3,7},{4,0},{5,1},{6,2},{7,3},{8,12},{9,13},{10,... | collective-permute-start | bytes 196616 | tf_op jit(solution)/shard_map/ppermute | solution.py:221
  16.3 4.1 %collective-permute-start.10 = (f32[128,128]{1,0:T(8,128)S(1)}, f32[128,128]{1,0:T(8,128)S(1)}, u32[]{:S(2)}, u32[]{:S(2)}) collective-permute-start(f32[128,128]{1,0:T(8,128)S(1)} %add_add_fusion.3.rest_0_), channel_id=1, source_target_pairs={{0,2},{1,3},{2,0},{3,1},{4,6},{5,7},{6,4},{7,5},{8,10},{9,11},{10,... | collective-permute-start | bytes 196616 | tf_op jit(solution)/shard_map/ppermute | solution.py:221
  20.3 4.1 %collective-permute-start.8 = (f32[128,128]{1,0:T(8,128)S(1)}, f32[128,128]{1,0:T(8,128)S(1)}, u32[]{:S(2)}, u32[]{:S(2)}) collective-permute-start(f32[128,128]{1,0:T(8,128)S(1)} %get-tuple-element.57.part_ref), channel_id=1, source_target_pairs={{1,0},{3,2},{5,4},{7,6},{9,8},{11,10},{13,12},{15,14},{16,17},{18,... | collective-permute-start | bytes 196616 | tf_op jit(solution)/shard_map/ppermute | solution.py:221
  20.3 5.0 %collective-permute-start.9 = (f32[128,128]{1,0:T(8,128)S(1)}, f32[128,128]{1,0:T(8,128)S(1)}, u32[]{:S(2)}, u32[]{:S(2)}) collective-permute-start(f32[128,128]{1,0:T(8,128)S(1)} %get-tuple-element.58.far_ref), channel_id=1, source_target_pairs={{1,16},{3,18},{5,20},{7,22},{9,24},{11,26},{13,28},{15,30},{16,1},... | collective-permute-start | bytes 196616 | tf_op jit(solution)/shard_map/ppermute | solution.py:221
  25.3 6.5 %collective-permute-start.11 = (f32[128,128]{1,0:T(8,128)S(1)}, f32[128,128]{1,0:T(8,128)S(1)}, u32[]{:S(2)}, u32[]{:S(2)}) collective-permute-start(f32[128,128]{1,0:T(8,128)S(1)} %add_add_fusion.2.rest_0_), channel_id=1, source_target_pairs={{0,12},{1,13},{2,14},{3,15},{4,8},{5,9},{6,10},{7,11},{8,4},{9,5},... | collective-permute-start | bytes 196616 | tf_op jit(solution)/shard_map/ppermute | solution.py:221
  25.4 6.8 %collective-permute-start.13 = (f32[128,128]{1,0:T(8,128)S(1)}, f32[128,128]{1,0:T(8,128)S(1)}, u32[]{:S(2)}, u32[]{:S(2)}) collective-permute-start(f32[128,128]{1,0:T(8,128)S(1)} %add_add_fusion.2.rest_0_), channel_id=1, source_target_pairs={{0,8},{1,9},{2,10},{3,11},{4,12},{5,13},{6,14},{7,15},{8,0},{9,1},... | collective-permute-start | bytes 196616 | tf_op jit(solution)/shard_map/ppermute | solution.py:221
  27.0 5.3 %collective-permute-start.12 = (f32[128,128]{1,0:T(8,128)S(1)}, f32[128,128]{1,0:T(8,128)S(1)}, u32[]{:S(2)}, u32[]{:S(2)}) collective-permute-start(f32[128,128]{1,0:T(8,128)S(1)} %add_add_fusion.2.rest_0_), channel_id=1, source_target_pairs={{0,4},{1,5},{2,6},{3,7},{4,0},{5,1},{6,2},{7,3},{8,12},{9,13},{10,... | collective-permute-start | bytes 196616 | tf_op jit(solution)/shard_map/ppermute | solution.py:221
  28.0 4.7 %collective-permute-start.16 = (f32[128,128]{1,0:T(8,128)S(1)}, f32[128,128]{1,0:T(8,128)S(1)}, u32[]{:S(2)}, u32[]{:S(2)}) collective-permute-start(f32[128,128]{1,0:T(8,128)S(1)} %add_add_fusion.2.rest_0_), channel_id=1, source_target_pairs={{0,2},{1,3},{2,0},{3,1},{4,6},{5,7},{6,4},{7,5},{8,10},{9,11},{10,... | collective-permute-start | bytes 196616 | tf_op jit(solution)/shard_map/ppermute | solution.py:221
  32.6 4.2 %collective-permute-start.14 = (f32[128,128]{1,0:T(8,128)S(1)}, f32[128,128]{1,0:T(8,128)S(1)}, u32[]{:S(2)}, u32[]{:S(2)}) collective-permute-start(f32[128,128]{1,0:T(8,128)S(1)} %get-tuple-element.63.part_ref), channel_id=1, source_target_pairs={{1,0},{3,2},{5,4},{7,6},{9,8},{11,10},{13,12},{15,14},{16,17},{18,... | collective-permute-start | bytes 196616 | tf_op jit(solution)/shard_map/ppermute | solution.py:221
  32.7 5.1 %collective-permute-start.15 = (f32[128,128]{1,0:T(8,128)S(1)}, f32[128,128]{1,0:T(8,128)S(1)}, u32[]{:S(2)}, u32[]{:S(2)}) collective-permute-start(f32[128,128]{1,0:T(8,128)S(1)} %get-tuple-element.64.far_ref), channel_id=1, source_target_pairs={{1,16},{3,18},{5,20},{7,22},{9,24},{11,26},{13,28},{15,30},{16,1},... | collective-permute-start | bytes 196616 | tf_op jit(solution)/shard_map/ppermute | solution.py:221
  37.8 7.3 %collective-permute-start.17 = (f32[128,128]{1,0:T(8,128)S(1)}, f32[128,128]{1,0:T(8,128)S(1)}, u32[]{:S(2)}, u32[]{:S(2)}) collective-permute-start(f32[128,128]{1,0:T(8,128)S(1)} %add_add_fusion.1.rest_0_), channel_id=1, source_target_pairs={{0,12},{1,13},{2,14},{3,15},{4,8},{5,9},{6,10},{7,11},{8,4},{9,5},... | collective-permute-start | bytes 196616 | tf_op jit(solution)/shard_map/ppermute | solution.py:221
  37.9 7.6 %collective-permute-start.19 = (f32[128,128]{1,0:T(8,128)S(1)}, f32[128,128]{1,0:T(8,128)S(1)}, u32[]{:S(2)}, u32[]{:S(2)}) collective-permute-start(f32[128,128]{1,0:T(8,128)S(1)} %add_add_fusion.1.rest_0_), channel_id=1, source_target_pairs={{0,8},{1,9},{2,10},{3,11},{4,12},{5,13},{6,14},{7,15},{8,0},{9,1},... | collective-permute-start | bytes 196616 | tf_op jit(solution)/shard_map/ppermute | solution.py:221
  39.4 6.1 %collective-permute-start.18 = (f32[128,128]{1,0:T(8,128)S(1)}, f32[128,128]{1,0:T(8,128)S(1)}, u32[]{:S(2)}, u32[]{:S(2)}) collective-permute-start(f32[128,128]{1,0:T(8,128)S(1)} %add_add_fusion.1.rest_0_), channel_id=1, source_target_pairs={{0,4},{1,5},{2,6},{3,7},{4,0},{5,1},{6,2},{7,3},{8,12},{9,13},{10,... | collective-permute-start | bytes 196616 | tf_op jit(solution)/shard_map/ppermute | solution.py:221
  40.5 8.7 %collective-permute-start.24 = (f32[128,128]{1,0:T(8,128)S(1)}, f32[128,128]{1,0:T(8,128)S(1)}, u32[]{:S(2)}, u32[]{:S(2)}) collective-permute-start(f32[128,128]{1,0:T(8,128)S(1)} %add_add_fusion.1.rest_0_), channel_id=1, source_target_pairs={{0,2},{1,3},{2,0},{3,1},{4,6},{5,7},{6,4},{7,5},{8,10},{9,11},{10,... | collective-permute-start | bytes 196616 | tf_op jit(solution)/shard_map/ppermute | solution.py:221
  45.8 4.2 %collective-permute-start.22 = (f32[128,128]{1,0:T(8,128)S(1)}, f32[128,128]{1,0:T(8,128)S(1)}, u32[]{:S(2)}, u32[]{:S(2)}) collective-permute-start(f32[128,128]{1,0:T(8,128)S(1)} %get-tuple-element.71.part_ref), channel_id=1, source_target_pairs={{1,0},{3,2},{5,4},{7,6},{9,8},{11,10},{13,12},{15,14},{16,17},{18,... | collective-permute-start | bytes 196616 | tf_op jit(solution)/shard_map/ppermute | solution.py:221
  45.9 5.1 %collective-permute-start.23 = (f32[128,128]{1,0:T(8,128)S(1)}, f32[128,128]{1,0:T(8,128)S(1)}, u32[]{:S(2)}, u32[]{:S(2)}) collective-permute-start(f32[128,128]{1,0:T(8,128)S(1)} %get-tuple-element.72.far_ref), channel_id=1, source_target_pairs={{1,16},{3,18},{5,20},{7,22},{9,24},{11,26},{13,28},{15,30},{16,1},... | collective-permute-start | bytes 196616 | tf_op jit(solution)/shard_map/ppermute | solution.py:221
  46.8 11.6 %collective-permute-start.21 = (f32[4,64,128]{2,1,0:T(8,128)S(1)}, f32[4,64,128]{2,1,0:T(8,128)S(1)}, u32[]{:S(2)}, u32[]{:S(2)}) collective-permute-start(f32[4,64,128]{2,1,0:T(8,128)S(1)} %get-tuple-element.70.refs_1_), channel_id=1, source_target_pairs={{0,2},{1,3},{2,0},{3,1},{4,6},{5,7},{6,4},{7,5},{8,10},{9,11},{10,... | collective-permute-start | bytes 393224 | tf_op jit(solution)/shard_map/ppermute | solution.py:221
  51.1 7.9 %collective-permute-start.27 = (f32[128,128]{1,0:T(8,128)S(1)}, f32[128,128]{1,0:T(8,128)S(1)}, u32[]{:S(2)}, u32[]{:S(2)}) collective-permute-start(f32[128,128]{1,0:T(8,128)S(1)} %add_add_fusion.refs_4_), channel_id=1, source_target_pairs={{0,12},{1,13},{2,14},{3,15},{4,8},{5,9},{6,10},{7,11},{8,4},{9,5},... | collective-permute-start | bytes 196616 | tf_op jit(solution)/shard_map/ppermute | solution.py:221
  51.5 10.8 %collective-permute-start.20 = (f32[4,64,128]{2,1,0:T(8,128)S(1)}, f32[4,64,128]{2,1,0:T(8,128)S(1)}, u32[]{:S(2)}, u32[]{:S(2)}) collective-permute-start(f32[4,64,128]{2,1,0:T(8,128)S(1)} %get-tuple-element.67.refs_0_), channel_id=1, source_target_pairs={{0,2},{1,3},{2,0},{3,1},{4,6},{5,7},{6,4},{7,5},{8,10},{9,11},{10,... | collective-permute-start | bytes 393224 | tf_op jit(solution)/shard_map/ppermute | solution.py:221
  55.5 5.7 %collective-permute-start.26 = (f32[128,128]{1,0:T(8,128)S(1)}, f32[128,128]{1,0:T(8,128)S(1)}, u32[]{:S(2)}, u32[]{:S(2)}) collective-permute-start(f32[128,128]{1,0:T(8,128)S(1)} %add_add_fusion.refs_4_), channel_id=1, source_target_pairs={{0,8},{1,9},{2,10},{3,11},{4,12},{5,13},{6,14},{7,15},{8,0},{9,1},... | collective-permute-start | bytes 196616 | tf_op jit(solution)/shard_map/ppermute | solution.py:221
  57.3 4.2 %collective-permute-start.25 = (f32[128,128]{1,0:T(8,128)S(1)}, f32[128,128]{1,0:T(8,128)S(1)}, u32[]{:S(2)}, u32[]{:S(2)}) collective-permute-start(f32[128,128]{1,0:T(8,128)S(1)} %add_add_fusion.refs_4_), channel_id=1, source_target_pairs={{0,4},{1,5},{2,6},{3,7},{4,0},{5,1},{6,2},{7,3},{8,12},{9,13},{10,... | collective-permute-start | bytes 196616 | tf_op jit(solution)/shard_map/ppermute | solution.py:221
  58.4 3.9 %collective-permute-start.28 = (f32[128,128]{1,0:T(8,128)S(1)}, f32[128,128]{1,0:T(8,128)S(1)}, u32[]{:S(2)}, u32[]{:S(2)}) collective-permute-start(f32[128,128]{1,0:T(8,128)S(1)} %add_add_fusion.refs_4_), channel_id=1, source_target_pairs={{0,2},{1,3},{2,0},{3,1},{4,6},{5,7},{6,4},{7,5},{8,10},{9,11},{10,... | collective-permute-start | bytes 196616 | tf_op jit(solution)/shard_map/ppermute | solution.py:221
  58.9 3.4 %collective-permute-start.31 = (f32[128,128]{1,0:T(8,128)S(1)}, f32[128,128]{1,0:T(8,128)S(1)}, u32[]{:S(2)}, u32[]{:S(2)}) collective-permute-start(f32[128,128]{1,0:T(8,128)S(1)} %collective-permute-done.27.refs_7_), channel_id=1, source_target_pairs={{0,2},{1,3},{2,0},{3,1},{4,6},{5,7},{6,4},{7,5},{8,10},{9,11},{10,... | collective-permute-start | bytes 196616 | tf_op jit(solution)/shard_map/ppermute | solution.py:221
  61.2 1.3 %collective-permute-start.30 = (f32[128,128]{1,0:T(8,128)S(1)}, f32[128,128]{1,0:T(8,128)S(1)}, u32[]{:S(2)}, u32[]{:S(2)}) collective-permute-start(f32[128,128]{1,0:T(8,128)S(1)} %collective-permute-done.26.refs_6_), channel_id=1, source_target_pairs={{0,2},{1,3},{2,0},{3,1},{4,6},{5,7},{6,4},{7,5},{8,10},{9,11},{10,... | collective-permute-start | bytes 196616 | tf_op jit(solution)/shard_map/ppermute | solution.py:221
  61.5 1.6 %collective-permute-start.29 = (f32[128,128]{1,0:T(8,128)S(1)}, f32[128,128]{1,0:T(8,128)S(1)}, u32[]{:S(2)}, u32[]{:S(2)}) collective-permute-start(f32[128,128]{1,0:T(8,128)S(1)} %collective-permute-done.25.refs_5_), channel_id=1, source_target_pairs={{0,2},{1,3},{2,0},{3,1},{4,6},{5,7},{6,4},{7,5},{8,10},{9,11},{10,... | collective-permute-start | bytes 196616 | tf_op jit(solution)/shard_map/ppermute | solution.py:221

commit v9 on v8

--- a/solution.py
+++ b/solution.py
@@ -172,28 +172,24 @@
     store(rows_dev, half, parts, part_ref, far_ref)
 
 
-def last_kernel(rows_dev, half, *refs):
-    count = rows_dev // 2
+def last_kernel(rows_dev, half, away, *refs):
     own_row, core, _ = places(rows_dev)
-    out_hbm, out_ref, sems = refs[-3:]
-    copies = []
-    for away in range(2):
-        prevs, pieces = refs[2 * away : 2 * away + 2], refs[4 + away * count : 4 + (away + 1) * count]
-        side = jnp.bitwise_xor(core, away) * half
-        for late, prev_ref in enumerate(prevs):
-            for p, slot in enumerate(slots(rows_dev, late)):
-                s = jnp.bitwise_xor(own_row, slot ^ away)
-                piece = pieces[slot // 2]
-                new = prev_ref[p] - STEP_SIZE * piece[slot % 2 * half : (slot % 2 + 1) * half, :]
-                out_ref[every(side, s, half, rows_dev), :] = new
-        flat = pl.ds(pl.multiple_of(side * rows_dev, half * rows_dev), half * rows_dev)
-        copies.append(pltpu.make_async_copy(out_ref.at[flat], out_hbm.at[flat], sems.at[away]))
-        copies[-1].start()
-    for copy in copies:
-        copy.wait()
-
-
-def call(kernel, ins, outs, scratch, name):
+    out_hbm, out_ref, sem = refs[-3:]
+    prevs, pieces = refs[:2], refs[2 : 2 + rows_dev // 2]
+    side = jnp.bitwise_xor(core, away) * half
+    for late, prev_ref in enumerate(prevs):
+        for p, slot in enumerate(slots(rows_dev, late)):
+            s = jnp.bitwise_xor(own_row, slot ^ away)
+            piece = pieces[slot // 2]
+            new = prev_ref[p] - STEP_SIZE * piece[slot % 2 * half : (slot % 2 + 1) * half, :]
+            out_ref[pl.ds(s, half, stride=rows_dev), :] = new
+    flat = pl.ds(pl.multiple_of(side * rows_dev, half * rows_dev), half * rows_dev)
+    copy = pltpu.make_async_copy(out_ref, out_hbm.at[flat], sem)
+    copy.start()
+    copy.wait()
+
+
+def call(kernel, ins, outs, scratch, name, aliases={}):
     return pl.pallas_call(
         kernel,
         out_shape=[shape for shape, _ in outs],
@@ -202,6 +198,7 @@
         scratch_shapes=scratch,
         compiler_params=pltpu.CompilerParams(vmem_limit_bytes=VMEM_BYTES),
         name=name,
+        input_output_aliases=aliases,
     )
 
 
@@ -279,10 +276,14 @@
         )(currents[1], *given, own_late_wide, other_late_wide, part, *others[:-1])
         currents = [early, late]
     pieces = [own] + others
+    final_out, stage = [(shape(flat, F32), hbm)], [vmem((half * rows_dev, n), F32), pltpu.SemaphoreType.DMA]
     final = call(
-        functools.partial(last_kernel, rows_dev, half),
-        [vmem] * (4 + rows_dev), [(shape(flat, F32), hbm)], [vmem(flat, F32), pltpu.SemaphoreType.DMA((2,))], "last_step",
-    )(*currents, *[flip(x, 1) for x in currents], *pieces, swapped, *[flip(x, 1) for x in others])[0]
+        functools.partial(last_kernel, rows_dev, half, 0), [vmem] * (2 + rows_dev // 2), final_out, stage, "last_step",
+    )(*currents, *pieces)[0]
+    final = call(
+        functools.partial(last_kernel, rows_dev, half, 1),
+        [vmem] * (2 + rows_dev // 2) + [hbm], final_out, stage, "last_step_other", {2 + rows_dev // 2: 0},
+    )(*[flip(x, 1) for x in currents], swapped, *[flip(x, 1) for x in others], final)[0]
     return final.reshape(first_row.shape)
 
 

time: 64.2 us -> 64.1 us (level)
  waiting for transfers between devices: 20.8 us -> 20 us
  Pallas kernels: 6.72 us -> 7.41 us
    ppermute x32, waiting for transfers between devices: 20.8 us -> 20 us  [moved(): return lax.ppermute(x, ('hist', 'col'), pairs)]
    pallas_call x1 -> x2, Pallas kernels: 0.88 us -> 1.57 us  [the longest x1 0.79 us: in_pairs(): call(functools.partial(last_kernel, rows_dev, half, 0), [vmem] * (2 + row...]
  transfers between devices with their start and end apart: 32 -> 32, of which waited for: 14 -> 13; matrix products, arithmetic and copies ran while one was open for 0% -> 0% of each run, Pallas kernels for 9% -> 10%
where the time goes in v9:
time: 64.1 us; the launch traced here: 64 us
  starting transfers between devices  34.8 us (54%)
  waiting for transfers between devices  20 us (31%)
  Pallas kernels  7.41 us (12%)
  between operations  1.58 us (2%)
    ppermute x32, starting transfers between devices, moved(): return lax.ppermute(x, ('hist', 'col'), pairs)  34.8 us
    ppermute x32, waiting for transfers between devices, moved(): return lax.ppermute(x, ('hist', 'col'), pairs)  20 us
    pallas_call x1, Pallas kernels, in_pairs(): call(functools.partial(first_kernel, rows_dev, half, steps), [vmem] + [hb...  2.13 us
  transfers between devices with their start and end apart: 32, of which 13 were waited for; matrix products, arithmetic and copies ran while one was open for 0% of the time, Pallas kernels for 10%

profile of v9, /device:TPU:25, one launch (start us, length us, event | category | flops | bytes accessed | tf_op | source)
XLA Modules:
  0.0 64.0 jit_solution(14338268642920021993)
XLA Ops:
  0.0 0.7 %collective-permute-start.1 = (f32[1024,128]{1,0:T(8,128)}, f32[1024,128]{1,0:T(8,128)S(1)}, u32[]{:S(2)}, u32[]{:S(2)}) collective-permute-start(f32[1024,128]{1,0:T(8,128)} %bitcast.13), channel_id=1, source_target_pairs={{0,2},{1,3},{2,0},{3,1},{4,6},{5,7},{6,4},{7,5},{8,10},{9,11},{10,... | collective-permute-start | bytes 1572872 | tf_op jit(solution)/shard_map/ppermute | solution.py:218
  2.0 0.1 pad_add_fusion
  2.1 0.1 broadcast_in_dim.2.limits_ref
  2.1 0.5 collective-permute-start
  2.6 2.1 %first_step.1 = (f32[4,64,128]{2,1,0:T(8,128)S(1)}, f32[4,64,128]{2,1,0:T(8,128)S(1)}, bf16[1024,256]{1,0:T(8,128)(2,1)S(1)}, bf16[1024,256]{1,0:T(8,128)(2,1)S(...) custom-call(s32[2,128]{1,0:T(2,128)S(1)} %broadcast_in_dim.2.limits_, ...), custom_call_target="tpu_custom_call" | custom-call | tf_op jit(solution)/shard_map/first_step/pallas_call | solution.py:244
  4.8 0.4 first_step_other.1
  5.2 1.3 %collective-permute-start.3 = (f32[128,128]{1,0:T(8,128)S(1)}, f32[128,128]{1,0:T(8,128)S(1)}, u32[]{:S(2)}, u32[]{:S(2)}) collective-permute-start(f32[128,128]{1,0:T(8,128)S(1)} %get-tuple-element.48.part_ref), channel_id=1, source_target_pairs={{1,0},{3,2},{5,4},{7,6},{9,8},{11,10},{13,12},{15,14},{16,17},{18,... | collective-permute-start | bytes 196616 | tf_op jit(solution)/shard_map/ppermute | solution.py:218
  6.5 0.2 turn.4
  6.7 4.8 %collective-permute-done.3 = f32[128,128]{1,0:T(8,128)S(1)} collective-permute-done((f32[128,128]{1,0:T(8,128)S(1)}, f32[128,128]{1,0:T(8,128)S(1)}, u32[]{:S(2)}, u32[]{:S(2)}) %collective-permute-start.3) | collective-permute-done | bytes 65568 | tf_op jit(solution)/shard_map/ppermute | solution.py:218
  11.5 2.1 %collective-permute-done.4 = f32[128,128]{1,0:T(8,128)S(1)} collective-permute-done((f32[128,128]{1,0:T(8,128)S(1)}, f32[128,128]{1,0:T(8,128)S(1)}, u32[]{:S(2)}, u32[]{:S(2)}) %collective-permute-start.4) | collective-permute-done | bytes 65568 | tf_op jit(solution)/shard_map/ppermute | solution.py:218
  13.7 2.4 %collective-permute-start.7 = (f32[128,128]{1,0:T(8,128)S(1)}, f32[128,128]{1,0:T(8,128)S(1)}, u32[]{:S(2)}, u32[]{:S(2)}) collective-permute-start(f32[128,128]{1,0:T(8,128)S(1)} %add_add_fusion.3.rest_0_), channel_id=1, source_target_pairs={{0,8},{1,9},{2,10},{3,11},{4,12},{5,13},{6,14},{7,15},{8,0},{9,1},... | collective-permute-start | bytes 196616 | tf_op jit(solution)/shard_map/ppermute | solution.py:218
  16.1 0.2 collective-permute-start.6
  16.3 1.3 %collective-permute-start.10 = (f32[128,128]{1,0:T(8,128)S(1)}, f32[128,128]{1,0:T(8,128)S(1)}, u32[]{:S(2)}, u32[]{:S(2)}) collective-permute-start(f32[128,128]{1,0:T(8,128)S(1)} %add_add_fusion.3.rest_0_), channel_id=1, source_target_pairs={{0,2},{1,3},{2,0},{3,1},{4,6},{5,7},{6,4},{7,5},{8,10},{9,11},{10,... | collective-permute-start | bytes 196616 | tf_op jit(solution)/shard_map/ppermute | solution.py:218
  17.7 0.4 next_step_early.3
  18.1 1.1 %collective-permute-done.7.rest_1_ = f32[128,128]{1,0:T(8,128)S(1)} collective-permute-done((f32[128,128]{1,0:T(8,128)S(1)}, f32[128,128]{1,0:T(8,128)S(1)}, u32[]{:S(2)}, u32[]{:S(2)}) %collective-permute-start.7) | collective-permute-done | bytes 65568 | tf_op jit(solution)/shard_map/ppermute | solution.py:218
  19.1 0.8 %collective-permute-done.6.rest_0_ = f32[128,128]{1,0:T(8,128)S(1)} collective-permute-done((f32[128,128]{1,0:T(8,128)S(1)}, f32[128,128]{1,0:T(8,128)S(1)}, u32[]{:S(2)}, u32[]{:S(2)}) %collective-permute-start.6) | collective-permute-done | bytes 65568 | tf_op jit(solution)/shard_map/ppermute | solution.py:218
  19.9 0.3 next_step.3
  20.4 0.2 turn.5
  20.6 3.7 %collective-permute-done.8 = f32[128,128]{1,0:T(8,128)S(1)} collective-permute-done((f32[128,128]{1,0:T(8,128)S(1)}, f32[128,128]{1,0:T(8,128)S(1)}, u32[]{:S(2)}, u32[]{:S(2)}) %collective-permute-start.8) | collective-permute-done | bytes 65568 | tf_op jit(solution)/shard_map/ppermute | solution.py:218
  24.3 1.0 %collective-permute-done.9 = f32[128,128]{1,0:T(8,128)S(1)} collective-permute-done((f32[128,128]{1,0:T(8,128)S(1)}, f32[128,128]{1,0:T(8,128)S(1)}, u32[]{:S(2)}, u32[]{:S(2)}) %collective-permute-start.9) | collective-permute-done | bytes 65568 | tf_op jit(solution)/shard_map/ppermute | solution.py:218
  25.4 1.6 %collective-permute-start.13 = (f32[128,128]{1,0:T(8,128)S(1)}, f32[128,128]{1,0:T(8,128)S(1)}, u32[]{:S(2)}, u32[]{:S(2)}) collective-permute-start(f32[128,128]{1,0:T(8,128)S(1)} %add_add_fusion.2.rest_0_), channel_id=1, source_target_pairs={{0,8},{1,9},{2,10},{3,11},{4,12},{5,13},{6,14},{7,15},{8,0},{9,1},... | collective-permute-start | bytes 196616 | tf_op jit(solution)/shard_map/ppermute | solution.py:218
  27.0 1.1 %collective-permute-start.12 = (f32[128,128]{1,0:T(8,128)S(1)}, f32[128,128]{1,0:T(8,128)S(1)}, u32[]{:S(2)}, u32[]{:S(2)}) collective-permute-start(f32[128,128]{1,0:T(8,128)S(1)} %add_add_fusion.2.rest_0_), channel_id=1, source_target_pairs={{0,4},{1,5},{2,6},{3,7},{4,0},{5,1},{6,2},{7,3},{8,12},{9,13},{10,... | collective-permute-start | bytes 196616 | tf_op jit(solution)/shard_map/ppermute | solution.py:218
  28.0 3.8 %collective-permute-start.16 = (f32[128,128]{1,0:T(8,128)S(1)}, f32[128,128]{1,0:T(8,128)S(1)}, u32[]{:S(2)}, u32[]{:S(2)}) collective-permute-start(f32[128,128]{1,0:T(8,128)S(1)} %add_add_fusion.2.rest_0_), channel_id=1, source_target_pairs={{0,2},{1,3},{2,0},{3,1},{4,6},{5,7},{6,4},{7,5},{8,10},{9,11},{10,... | collective-permute-start | bytes 196616 | tf_op jit(solution)/shard_map/ppermute | solution.py:218
  31.9 0.3 next_step_early.4
  32.2 0.4 next_step.4
  32.8 0.2 turn.6
  32.9 3.8 %collective-permute-done.14 = f32[128,128]{1,0:T(8,128)S(1)} collective-permute-done((f32[128,128]{1,0:T(8,128)S(1)}, f32[128,128]{1,0:T(8,128)S(1)}, u32[]{:S(2)}, u32[]{:S(2)}) %collective-permute-start.14) | collective-permute-done | bytes 65568 | tf_op jit(solution)/shard_map/ppermute | solution.py:218
  36.8 1.0 %collective-permute-done.15 = f32[128,128]{1,0:T(8,128)S(1)} collective-permute-done((f32[128,128]{1,0:T(8,128)S(1)}, f32[128,128]{1,0:T(8,128)S(1)}, u32[]{:S(2)}, u32[]{:S(2)}) %collective-permute-start.15) | collective-permute-done | bytes 65568 | tf_op jit(solution)/shard_map/ppermute | solution.py:218
  37.9 1.5 %collective-permute-start.20 = (f32[128,128]{1,0:T(8,128)S(1)}, f32[128,128]{1,0:T(8,128)S(1)}, u32[]{:S(2)}, u32[]{:S(2)}) collective-permute-start(f32[128,128]{1,0:T(8,128)S(1)} %add_add_fusion.1.rest_0_), channel_id=1, source_target_pairs={{0,8},{1,9},{2,10},{3,11},{4,12},{5,13},{6,14},{7,15},{8,0},{9,1},... | collective-permute-start | bytes 196616 | tf_op jit(solution)/shard_map/ppermute | solution.py:218
  39.4 1.1 %collective-permute-start.19 = (f32[128,128]{1,0:T(8,128)S(1)}, f32[128,128]{1,0:T(8,128)S(1)}, u32[]{:S(2)}, u32[]{:S(2)}) collective-permute-start(f32[128,128]{1,0:T(8,128)S(1)} %add_add_fusion.1.rest_0_), channel_id=1, source_target_pairs={{0,4},{1,5},{2,6},{3,7},{4,0},{5,1},{6,2},{7,3},{8,12},{9,13},{10,... | collective-permute-start | bytes 196616 | tf_op jit(solution)/shard_map/ppermute | solution.py:218
  40.5 4.6 %collective-permute-start.24 = (f32[128,128]{1,0:T(8,128)S(1)}, f32[128,128]{1,0:T(8,128)S(1)}, u32[]{:S(2)}, u32[]{:S(2)}) collective-permute-start(f32[128,128]{1,0:T(8,128)S(1)} %add_add_fusion.1.rest_0_), channel_id=1, source_target_pairs={{0,2},{1,3},{2,0},{3,1},{4,6},{5,7},{6,4},{7,5},{8,10},{9,11},{10,... | collective-permute-start | bytes 196616 | tf_op jit(solution)/shard_map/ppermute | solution.py:218
  45.1 0.3 next_step_early.5
  45.5 0.3 next_step.5
  45.9 0.9 %collective-permute-start.23 = (f32[128,128]{1,0:T(8,128)S(1)}, f32[128,128]{1,0:T(8,128)S(1)}, u32[]{:S(2)}, u32[]{:S(2)}) collective-permute-start(f32[128,128]{1,0:T(8,128)S(1)} %get-tuple-element.72.far_ref), channel_id=1, source_target_pairs={{1,16},{3,18},{5,20},{7,22},{9,24},{11,26},{13,28},{15,30},{16,1},... | collective-permute-start | bytes 196616 | tf_op jit(solution)/shard_map/ppermute | solution.py:218
  46.8 2.4 %collective-permute-start.21 = (f32[4,64,128]{2,1,0:T(8,128)S(1)}, f32[4,64,128]{2,1,0:T(8,128)S(1)}, u32[]{:S(2)}, u32[]{:S(2)}) collective-permute-start(f32[4,64,128]{2,1,0:T(8,128)S(1)} %get-tuple-element.70.refs_1_), channel_id=1, source_target_pairs={{0,2},{1,3},{2,0},{3,1},{4,6},{5,7},{6,4},{7,5},{8,10},{9,11},{10,... | collective-permute-start | bytes 393224 | tf_op jit(solution)/shard_map/ppermute | solution.py:218
  49.2 0.7 %turn.7 = (f32[2,128,128]{2,1,0:T(8,128)}, f32[128,128]{1,0:T(8,128)S(1)}) custom-call(bf16[128,128]{1,0:T(8,128)(2,1)S(1)} %get-tuple-element.50.ham_ref, f32[2,128,128]{2,1,0:T(8,128)S(1)} %get-tuple-element.73.near_ref, f32[128,128]{1,0:T(8,128)S(1)} %get-tuple-element.71.part_ref, f32[128,128]{1,0:T(8,128)S(1)} %get-tuple-element.72.far_ref, ...), custom_call_target="tpu_custom_call" | custom-call | tf_op jit(solution)/shard_map/turn/pallas_call | solution.py:260
  49.9 0.2 collective-permute-done.22
  50.1 1.0 %collective-permute-done.23 = f32[128,128]{1,0:T(8,128)S(1)} collective-permute-done((f32[128,128]{1,0:T(8,128)S(1)}, f32[128,128]{1,0:T(8,128)S(1)}, u32[]{:S(2)}, u32[]{:S(2)}) %collective-permute-start.23) | collective-permute-done | bytes 65568 | tf_op jit(solution)/shard_map/ppermute | solution.py:218
  51.1 0.4 collective-permute-start.30
  51.5 4.0 %collective-permute-start.18 = (f32[4,64,128]{2,1,0:T(8,128)S(1)}, f32[4,64,128]{2,1,0:T(8,128)S(1)}, u32[]{:S(2)}, u32[]{:S(2)}) collective-permute-start(f32[4,64,128]{2,1,0:T(8,128)S(1)} %get-tuple-element.67.refs_0_), channel_id=1, source_target_pairs={{0,2},{1,3},{2,0},{3,1},{4,6},{5,7},{6,4},{7,5},{8,10},{9,11},{10,... | collective-permute-start | bytes 393224 | tf_op jit(solution)/shard_map/ppermute | solution.py:218
  55.5 1.8 %collective-permute-start.28 = (f32[128,128]{1,0:T(8,128)S(1)}, f32[128,128]{1,0:T(8,128)S(1)}, u32[]{:S(2)}, u32[]{:S(2)}) collective-permute-start(f32[128,128]{1,0:T(8,128)S(1)} %add_add_fusion.refs_2_), channel_id=1, source_target_pairs={{0,8},{1,9},{2,10},{3,11},{4,12},{5,13},{6,14},{7,15},{8,0},{9,1},... | collective-permute-start | bytes 196616 | tf_op jit(solution)/shard_map/ppermute | solution.py:218
  57.3 1.0 %collective-permute-start.26 = (f32[128,128]{1,0:T(8,128)S(1)}, f32[128,128]{1,0:T(8,128)S(1)}, u32[]{:S(2)}, u32[]{:S(2)}) collective-permute-start(f32[128,128]{1,0:T(8,128)S(1)} %add_add_fusion.refs_2_), channel_id=1, source_target_pairs={{0,4},{1,5},{2,6},{3,7},{4,0},{5,1},{6,2},{7,3},{8,12},{9,13},{10,... | collective-permute-start | bytes 196616 | tf_op jit(solution)/shard_map/ppermute | solution.py:218
  58.4 0.6 collective-permute-start.25
  58.9 2.3 %collective-permute-start.31 = (f32[128,128]{1,0:T(8,128)S(1)}, f32[128,128]{1,0:T(8,128)S(1)}, u32[]{:S(2)}, u32[]{:S(2)}) collective-permute-start(f32[128,128]{1,0:T(8,128)S(1)} %collective-permute-done.30.refs_5_), channel_id=1, source_target_pairs={{0,2},{1,3},{2,0},{3,1},{4,6},{5,7},{6,4},{7,5},{8,10},{9,11},{10,... | collective-permute-start | bytes 196616 | tf_op jit(solution)/shard_map/ppermute | solution.py:218
  61.2 0.3 collective-permute-done.26.refs_3_
  61.5 0.7 %collective-permute-start.27 = (f32[128,128]{1,0:T(8,128)S(1)}, f32[128,128]{1,0:T(8,128)S(1)}, u32[]{:S(2)}, u32[]{:S(2)}) collective-permute-start(f32[128,128]{1,0:T(8,128)S(1)} %collective-permute-done.26.refs_3_), channel_id=1, source_target_pairs={{0,2},{1,3},{2,0},{3,1},{4,6},{5,7},{6,4},{7,5},{8,10},{9,11},{10,... | collective-permute-start | bytes 196616 | tf_op jit(solution)/shard_map/ppermute | solution.py:218
  62.3 0.8 %last_step.1.refs_6_ = f32[1024,128]{1,0:T(8,128)} custom-call(f32[4,64,128]{2,1,0:T(8,128)S(1)} %get-tuple-element.67.refs_0_, f32[4,64,128]{2,1,0:T(8,128)S(1)} %get-tuple-element.70.refs_1_, f32[128,128]{1,0:T(8,128)S(1)} %add_add_fusion.refs_2_, f32[128,128]{1,0:T(8,128)S(1)} %collective-permute-done.26.refs_3_, ...), custom_call_target="tpu_custom_call" | custom-call | tf_op jit(solution)/shard_map/last_step/pallas_call | solution.py:280
  63.2 0.8 %last_step_other.1 = f32[1024,128]{1,0:T(8,128)} custom-call(f32[4,64,128]{2,1,0:T(8,128)S(1)} %collective-permute-done.18.refs_0_, f32[4,64,128]{2,1,0:T(8,128)S(1)} %collective-permute-done.21.refs_1_, f32[128,128]{1,0:T(8,128)S(1)} %collective-permute-done.25.refs_2_, ...), custom_call_target="tpu_custom_call", output_to_operand_aliasing={{}: (6, {})} | custom-call | tf_op jit(solution)/shard_map/last_step_other/pallas_call | solution.py:283
  (38 shorter events, 0.8 us)
Async XLA Ops:
  0.0 4.8 %collective-permute-start.1 = (f32[1024,128]{1,0:T(8,128)}, f32[1024,128]{1,0:T(8,128)S(1)}, u32[]{:S(2)}, u32[]{:S(2)}) collective-permute-start(f32[1024,128]{1,0:T(8,128)} %bitcast.13), channel_id=1, source_target_pairs={{0,2},{1,3},{2,0},{3,1},{4,6},{5,7},{6,4},{7,5},{8,10},{9,11},{10,... | collective-permute-start | bytes 1572872 | tf_op jit(solution)/shard_map/ppermute | solution.py:218
  0.7 4.1 %collective-permute-start.2 = (f32[1024,128]{1,0:T(8,128)}, f32[1024,128]{1,0:T(8,128)S(1)}, u32[]{:S(2)}, u32[]{:S(2)}) collective-permute-start(f32[1024,128]{1,0:T(8,128)} %bitcast.15), channel_id=1, source_target_pairs={{0,2},{1,3},{2,0},{3,1},{4,6},{5,7},{6,4},{7,5},{8,10},{9,11},{10,... | collective-permute-start | bytes 1572872 | tf_op jit(solution)/shard_map/ppermute | solution.py:218
  2.1 2.6 %collective-permute-start = (s32[2,128]{1,0:T(2,128)S(1)}, s32[2,128]{1,0:T(2,128)S(1)}, u32[]{:S(2)}, u32[]{:S(2)}) collective-permute-start(s32[2,128]{1,0:T(2,128)S(1)} %broadcast_in_dim.2.limits_ref), channel_id=1, source_target_pairs={{0,2},{1,3},{2,0},{3,1},{4,6},{5,7},{6,4},{7,5},{8,10},{9,11},{10,... | collective-permute-start | bytes 3080 | tf_op jit(solution)/shard_map/ppermute | solution.py:218
  2.6 15.1 %copy-start = (f32[4,128,8,128]{3,2,1,0:T(8,128)S(1)}, f32[4,128,8,128]{3,2,1,0:T(8,128)}, u32[]{:S(2)}) copy-start(f32[4,128,8,128]{3,2,1,0:T(8,128)} %param.11) | copy-start | bytes 6291460
  5.2 6.3 %collective-permute-start.3 = (f32[128,128]{1,0:T(8,128)S(1)}, f32[128,128]{1,0:T(8,128)S(1)}, u32[]{:S(2)}, u32[]{:S(2)}) collective-permute-start(f32[128,128]{1,0:T(8,128)S(1)} %get-tuple-element.48.part_ref), channel_id=1, source_target_pairs={{1,0},{3,2},{5,4},{7,6},{9,8},{11,10},{13,12},{15,14},{16,17},{18,... | collective-permute-start | bytes 196616 | tf_op jit(solution)/shard_map/ppermute | solution.py:218
  6.5 7.1 %collective-permute-start.4 = (f32[128,128]{1,0:T(8,128)S(1)}, f32[128,128]{1,0:T(8,128)S(1)}, u32[]{:S(2)}, u32[]{:S(2)}) collective-permute-start(f32[128,128]{1,0:T(8,128)S(1)} %get-tuple-element.49.far_ref), channel_id=1, source_target_pairs={{1,16},{3,18},{5,20},{7,22},{9,24},{11,26},{13,28},{15,30},{16,1},... | collective-permute-start | bytes 196616 | tf_op jit(solution)/shard_map/ppermute | solution.py:218
  13.6 4.1 %collective-permute-start.5 = (f32[128,128]{1,0:T(8,128)S(1)}, f32[128,128]{1,0:T(8,128)S(1)}, u32[]{:S(2)}, u32[]{:S(2)}) collective-permute-start(f32[128,128]{1,0:T(8,128)S(1)} %add_add_fusion.3.rest_0_), channel_id=1, source_target_pairs={{0,12},{1,13},{2,14},{3,15},{4,8},{5,9},{6,10},{7,11},{8,4},{9,5},... | collective-permute-start | bytes 196616 | tf_op jit(solution)/shard_map/ppermute | solution.py:218
  13.7 5.4 %collective-permute-start.7 = (f32[128,128]{1,0:T(8,128)S(1)}, f32[128,128]{1,0:T(8,128)S(1)}, u32[]{:S(2)}, u32[]{:S(2)}) collective-permute-start(f32[128,128]{1,0:T(8,128)S(1)} %add_add_fusion.3.rest_0_), channel_id=1, source_target_pairs={{0,8},{1,9},{2,10},{3,11},{4,12},{5,13},{6,14},{7,15},{8,0},{9,1},... | collective-permute-start | bytes 196616 | tf_op jit(solution)/shard_map/ppermute | solution.py:218
  16.1 3.8 %collective-permute-start.6 = (f32[128,128]{1,0:T(8,128)S(1)}, f32[128,128]{1,0:T(8,128)S(1)}, u32[]{:S(2)}, u32[]{:S(2)}) collective-permute-start(f32[128,128]{1,0:T(8,128)S(1)} %add_add_fusion.3.rest_0_), channel_id=1, source_target_pairs={{0,4},{1,5},{2,6},{3,7},{4,0},{5,1},{6,2},{7,3},{8,12},{9,13},{10,... | collective-permute-start | bytes 196616 | tf_op jit(solution)/shard_map/ppermute | solution.py:218
  16.3 4.1 %collective-permute-start.10 = (f32[128,128]{1,0:T(8,128)S(1)}, f32[128,128]{1,0:T(8,128)S(1)}, u32[]{:S(2)}, u32[]{:S(2)}) collective-permute-start(f32[128,128]{1,0:T(8,128)S(1)} %add_add_fusion.3.rest_0_), channel_id=1, source_target_pairs={{0,2},{1,3},{2,0},{3,1},{4,6},{5,7},{6,4},{7,5},{8,10},{9,11},{10,... | collective-permute-start | bytes 196616 | tf_op jit(solution)/shard_map/ppermute | solution.py:218
  20.3 4.1 %collective-permute-start.8 = (f32[128,128]{1,0:T(8,128)S(1)}, f32[128,128]{1,0:T(8,128)S(1)}, u32[]{:S(2)}, u32[]{:S(2)}) collective-permute-start(f32[128,128]{1,0:T(8,128)S(1)} %get-tuple-element.57.part_ref), channel_id=1, source_target_pairs={{1,0},{3,2},{5,4},{7,6},{9,8},{11,10},{13,12},{15,14},{16,17},{18,... | collective-permute-start | bytes 196616 | tf_op jit(solution)/shard_map/ppermute | solution.py:218
  20.3 5.0 %collective-permute-start.9 = (f32[128,128]{1,0:T(8,128)S(1)}, f32[128,128]{1,0:T(8,128)S(1)}, u32[]{:S(2)}, u32[]{:S(2)}) collective-permute-start(f32[128,128]{1,0:T(8,128)S(1)} %get-tuple-element.58.far_ref), channel_id=1, source_target_pairs={{1,16},{3,18},{5,20},{7,22},{9,24},{11,26},{13,28},{15,30},{16,1},... | collective-permute-start | bytes 196616 | tf_op jit(solution)/shard_map/ppermute | solution.py:218
  25.3 6.5 %collective-permute-start.11 = (f32[128,128]{1,0:T(8,128)S(1)}, f32[128,128]{1,0:T(8,128)S(1)}, u32[]{:S(2)}, u32[]{:S(2)}) collective-permute-start(f32[128,128]{1,0:T(8,128)S(1)} %add_add_fusion.2.rest_0_), channel_id=1, source_target_pairs={{0,12},{1,13},{2,14},{3,15},{4,8},{5,9},{6,10},{7,11},{8,4},{9,5},... | collective-permute-start | bytes 196616 | tf_op jit(solution)/shard_map/ppermute | solution.py:218
  25.4 6.8 %collective-permute-start.13 = (f32[128,128]{1,0:T(8,128)S(1)}, f32[128,128]{1,0:T(8,128)S(1)}, u32[]{:S(2)}, u32[]{:S(2)}) collective-permute-start(f32[128,128]{1,0:T(8,128)S(1)} %add_add_fusion.2.rest_0_), channel_id=1, source_target_pairs={{0,8},{1,9},{2,10},{3,11},{4,12},{5,13},{6,14},{7,15},{8,0},{9,1},... | collective-permute-start | bytes 196616 | tf_op jit(solution)/shard_map/ppermute | solution.py:218
  27.0 5.3 %collective-permute-start.12 = (f32[128,128]{1,0:T(8,128)S(1)}, f32[128,128]{1,0:T(8,128)S(1)}, u32[]{:S(2)}, u32[]{:S(2)}) collective-permute-start(f32[128,128]{1,0:T(8,128)S(1)} %add_add_fusion.2.rest_0_), channel_id=1, source_target_pairs={{0,4},{1,5},{2,6},{3,7},{4,0},{5,1},{6,2},{7,3},{8,12},{9,13},{10,... | collective-permute-start | bytes 196616 | tf_op jit(solution)/shard_map/ppermute | solution.py:218
  28.0 4.7 %collective-permute-start.16 = (f32[128,128]{1,0:T(8,128)S(1)}, f32[128,128]{1,0:T(8,128)S(1)}, u32[]{:S(2)}, u32[]{:S(2)}) collective-permute-start(f32[128,128]{1,0:T(8,128)S(1)} %add_add_fusion.2.rest_0_), channel_id=1, source_target_pairs={{0,2},{1,3},{2,0},{3,1},{4,6},{5,7},{6,4},{7,5},{8,10},{9,11},{10,... | collective-permute-start | bytes 196616 | tf_op jit(solution)/shard_map/ppermute | solution.py:218
  32.6 4.2 %collective-permute-start.14 = (f32[128,128]{1,0:T(8,128)S(1)}, f32[128,128]{1,0:T(8,128)S(1)}, u32[]{:S(2)}, u32[]{:S(2)}) collective-permute-start(f32[128,128]{1,0:T(8,128)S(1)} %get-tuple-element.63.part_ref), channel_id=1, source_target_pairs={{1,0},{3,2},{5,4},{7,6},{9,8},{11,10},{13,12},{15,14},{16,17},{18,... | collective-permute-start | bytes 196616 | tf_op jit(solution)/shard_map/ppermute | solution.py:218
  32.7 5.1 %collective-permute-start.15 = (f32[128,128]{1,0:T(8,128)S(1)}, f32[128,128]{1,0:T(8,128)S(1)}, u32[]{:S(2)}, u32[]{:S(2)}) collective-permute-start(f32[128,128]{1,0:T(8,128)S(1)} %get-tuple-element.64.far_ref), channel_id=1, source_target_pairs={{1,16},{3,18},{5,20},{7,22},{9,24},{11,26},{13,28},{15,30},{16,1},... | collective-permute-start | bytes 196616 | tf_op jit(solution)/shard_map/ppermute | solution.py:218
  37.8 7.3 %collective-permute-start.17 = (f32[128,128]{1,0:T(8,128)S(1)}, f32[128,128]{1,0:T(8,128)S(1)}, u32[]{:S(2)}, u32[]{:S(2)}) collective-permute-start(f32[128,128]{1,0:T(8,128)S(1)} %add_add_fusion.1.rest_0_), channel_id=1, source_target_pairs={{0,12},{1,13},{2,14},{3,15},{4,8},{5,9},{6,10},{7,11},{8,4},{9,5},... | collective-permute-start | bytes 196616 | tf_op jit(solution)/shard_map/ppermute | solution.py:218
  37.9 7.6 %collective-permute-start.20 = (f32[128,128]{1,0:T(8,128)S(1)}, f32[128,128]{1,0:T(8,128)S(1)}, u32[]{:S(2)}, u32[]{:S(2)}) collective-permute-start(f32[128,128]{1,0:T(8,128)S(1)} %add_add_fusion.1.rest_0_), channel_id=1, source_target_pairs={{0,8},{1,9},{2,10},{3,11},{4,12},{5,13},{6,14},{7,15},{8,0},{9,1},... | collective-permute-start | bytes 196616 | tf_op jit(solution)/shard_map/ppermute | solution.py:218
  39.4 6.1 %collective-permute-start.19 = (f32[128,128]{1,0:T(8,128)S(1)}, f32[128,128]{1,0:T(8,128)S(1)}, u32[]{:S(2)}, u32[]{:S(2)}) collective-permute-start(f32[128,128]{1,0:T(8,128)S(1)} %add_add_fusion.1.rest_0_), channel_id=1, source_target_pairs={{0,4},{1,5},{2,6},{3,7},{4,0},{5,1},{6,2},{7,3},{8,12},{9,13},{10,... | collective-permute-start | bytes 196616 | tf_op jit(solution)/shard_map/ppermute | solution.py:218
  40.5 8.7 %collective-permute-start.24 = (f32[128,128]{1,0:T(8,128)S(1)}, f32[128,128]{1,0:T(8,128)S(1)}, u32[]{:S(2)}, u32[]{:S(2)}) collective-permute-start(f32[128,128]{1,0:T(8,128)S(1)} %add_add_fusion.1.rest_0_), channel_id=1, source_target_pairs={{0,2},{1,3},{2,0},{3,1},{4,6},{5,7},{6,4},{7,5},{8,10},{9,11},{10,... | collective-permute-start | bytes 196616 | tf_op jit(solution)/shard_map/ppermute | solution.py:218
  45.8 4.2 %collective-permute-start.22 = (f32[128,128]{1,0:T(8,128)S(1)}, f32[128,128]{1,0:T(8,128)S(1)}, u32[]{:S(2)}, u32[]{:S(2)}) collective-permute-start(f32[128,128]{1,0:T(8,128)S(1)} %get-tuple-element.71.part_ref), channel_id=1, source_target_pairs={{1,0},{3,2},{5,4},{7,6},{9,8},{11,10},{13,12},{15,14},{16,17},{18,... | collective-permute-start | bytes 196616 | tf_op jit(solution)/shard_map/ppermute | solution.py:218
  45.9 5.1 %collective-permute-start.23 = (f32[128,128]{1,0:T(8,128)S(1)}, f32[128,128]{1,0:T(8,128)S(1)}, u32[]{:S(2)}, u32[]{:S(2)}) collective-permute-start(f32[128,128]{1,0:T(8,128)S(1)} %get-tuple-element.72.far_ref), channel_id=1, source_target_pairs={{1,16},{3,18},{5,20},{7,22},{9,24},{11,26},{13,28},{15,30},{16,1},... | collective-permute-start | bytes 196616 | tf_op jit(solution)/shard_map/ppermute | solution.py:218
  46.8 11.6 %collective-permute-start.21 = (f32[4,64,128]{2,1,0:T(8,128)S(1)}, f32[4,64,128]{2,1,0:T(8,128)S(1)}, u32[]{:S(2)}, u32[]{:S(2)}) collective-permute-start(f32[4,64,128]{2,1,0:T(8,128)S(1)} %get-tuple-element.70.refs_1_), channel_id=1, source_target_pairs={{0,2},{1,3},{2,0},{3,1},{4,6},{5,7},{6,4},{7,5},{8,10},{9,11},{10,... | collective-permute-start | bytes 393224 | tf_op jit(solution)/shard_map/ppermute | solution.py:218
  51.1 7.9 %collective-permute-start.30 = (f32[128,128]{1,0:T(8,128)S(1)}, f32[128,128]{1,0:T(8,128)S(1)}, u32[]{:S(2)}, u32[]{:S(2)}) collective-permute-start(f32[128,128]{1,0:T(8,128)S(1)} %add_add_fusion.refs_2_), channel_id=1, source_target_pairs={{0,12},{1,13},{2,14},{3,15},{4,8},{5,9},{6,10},{7,11},{8,4},{9,5},... | collective-permute-start | bytes 196616 | tf_op jit(solution)/shard_map/ppermute | solution.py:218
  51.5 11.6 %collective-permute-start.18 = (f32[4,64,128]{2,1,0:T(8,128)S(1)}, f32[4,64,128]{2,1,0:T(8,128)S(1)}, u32[]{:S(2)}, u32[]{:S(2)}) collective-permute-start(f32[4,64,128]{2,1,0:T(8,128)S(1)} %get-tuple-element.67.refs_0_), channel_id=1, source_target_pairs={{0,2},{1,3},{2,0},{3,1},{4,6},{5,7},{6,4},{7,5},{8,10},{9,11},{10,... | collective-permute-start | bytes 393224 | tf_op jit(solution)/shard_map/ppermute | solution.py:218
  55.5 5.7 %collective-permute-start.28 = (f32[128,128]{1,0:T(8,128)S(1)}, f32[128,128]{1,0:T(8,128)S(1)}, u32[]{:S(2)}, u32[]{:S(2)}) collective-permute-start(f32[128,128]{1,0:T(8,128)S(1)} %add_add_fusion.refs_2_), channel_id=1, source_target_pairs={{0,8},{1,9},{2,10},{3,11},{4,12},{5,13},{6,14},{7,15},{8,0},{9,1},... | collective-permute-start | bytes 196616 | tf_op jit(solution)/shard_map/ppermute | solution.py:218
  57.3 4.2 %collective-permute-start.26 = (f32[128,128]{1,0:T(8,128)S(1)}, f32[128,128]{1,0:T(8,128)S(1)}, u32[]{:S(2)}, u32[]{:S(2)}) collective-permute-start(f32[128,128]{1,0:T(8,128)S(1)} %add_add_fusion.refs_2_), channel_id=1, source_target_pairs={{0,4},{1,5},{2,6},{3,7},{4,0},{5,1},{6,2},{7,3},{8,12},{9,13},{10,... | collective-permute-start | bytes 196616 | tf_op jit(solution)/shard_map/ppermute | solution.py:218
  58.4 4.7 %collective-permute-start.25 = (f32[128,128]{1,0:T(8,128)S(1)}, f32[128,128]{1,0:T(8,128)S(1)}, u32[]{:S(2)}, u32[]{:S(2)}) collective-permute-start(f32[128,128]{1,0:T(8,128)S(1)} %add_add_fusion.refs_2_), channel_id=1, source_target_pairs={{0,2},{1,3},{2,0},{3,1},{4,6},{5,7},{6,4},{7,5},{8,10},{9,11},{10,... | collective-permute-start | bytes 196616 | tf_op jit(solution)/shard_map/ppermute | solution.py:218
  58.9 4.2 %collective-permute-start.31 = (f32[128,128]{1,0:T(8,128)S(1)}, f32[128,128]{1,0:T(8,128)S(1)}, u32[]{:S(2)}, u32[]{:S(2)}) collective-permute-start(f32[128,128]{1,0:T(8,128)S(1)} %collective-permute-done.30.refs_5_), channel_id=1, source_target_pairs={{0,2},{1,3},{2,0},{3,1},{4,6},{5,7},{6,4},{7,5},{8,10},{9,11},{10,... | collective-permute-start | bytes 196616 | tf_op jit(solution)/shard_map/ppermute | solution.py:218
  61.2 1.9 %collective-permute-start.29 = (f32[128,128]{1,0:T(8,128)S(1)}, f32[128,128]{1,0:T(8,128)S(1)}, u32[]{:S(2)}, u32[]{:S(2)}) collective-permute-start(f32[128,128]{1,0:T(8,128)S(1)} %collective-permute-done.28.refs_4_), channel_id=1, source_target_pairs={{0,2},{1,3},{2,0},{3,1},{4,6},{5,7},{6,4},{7,5},{8,10},{9,11},{10,... | collective-permute-start | bytes 196616 | tf_op jit(solution)/shard_map/ppermute | solution.py:218
  61.5 1.6 %collective-permute-start.27 = (f32[128,128]{1,0:T(8,128)S(1)}, f32[128,128]{1,0:T(8,128)S(1)}, u32[]{:S(2)}, u32[]{:S(2)}) collective-permute-start(f32[128,128]{1,0:T(8,128)S(1)} %collective-permute-done.26.refs_3_), channel_id=1, source_target_pairs={{0,2},{1,3},{2,0},{3,1},{4,6},{5,7},{6,4},{7,5},{8,10},{9,11},{10,... | collective-permute-start | bytes 196616 | tf_op jit(solution)/shard_map/ppermute | solution.py:218

commit v10 on v8

--- a/solution.py
+++ b/solution.py
@@ -257,7 +257,7 @@
     other_wide, other_late_wide, part, far = call(
         functools.partial(second_kernel, rows_dev, half),
         [vmem] * 6, [*wide_outs, pair_out, pair_out], [], "first_step_other",
-    )(flip(limits, 1), *[flip(x, 1) for x in tables], sigma, late_sigma, own_part)
+    )(flip(limits, 1), *[flip(x, 1) for x in lax.optimization_barrier((limits, *tables))[1:]], sigma, late_sigma, own_part)
     swap = []
     for section in range(1, steps + 1):
         *new, turned = call(

time: 64.2 us -> 64.5 us (level)
  transfers between devices with their start and end apart: 32 -> 32, of which waited for: 14 -> 13; matrix products, arithmetic and copies ran while one was open for 0% -> 0% of each run, Pallas kernels for 9% -> 9%
where the time goes in v10:
time: 64.5 us; the launch traced here: 64 us
  starting transfers between devices  35.1 us (54%)
  waiting for transfers between devices  20.5 us (32%)
  Pallas kernels  6.72 us (10%)
  between operations  1.55 us (2%)
    ppermute x32, starting transfers between devices, moved(): return lax.ppermute(x, ('hist', 'col'), pairs)  35.1 us
    ppermute x32, waiting for transfers between devices, moved(): return lax.ppermute(x, ('hist', 'col'), pairs)  20.5 us
    pallas_call x1, Pallas kernels, in_pairs(): call(functools.partial(first_kernel, rows_dev, half, steps), [vmem] + [hb...  2.13 us
  transfers between devices with their start and end apart: 32, of which 13 were waited for; matrix products, arithmetic and copies ran while one was open for 0% of the time, Pallas kernels for 9%

profile of v10, /device:TPU:25, one launch (start us, length us, event | category | flops | bytes accessed | tf_op | source)
XLA Modules:
  0.0 64.0 jit_solution(15196799288228494338)
XLA Ops:
  1.3 0.1 pad_add_fusion
  1.4 0.7 %collective-permute-start.1 = (f32[1024,128]{1,0:T(8,128)}, f32[1024,128]{1,0:T(8,128)S(1)}, u32[]{:S(2)}, u32[]{:S(2)}) collective-permute-start(f32[1024,128]{1,0:T(8,128)} %bitcast.13), channel_id=1, source_target_pairs={{0,2},{1,3},{2,0},{3,1},{4,6},{5,7},{6,4},{7,5},{8,10},{9,11},{10,... | collective-permute-start | bytes 1572872 | tf_op jit(solution)/shard_map/ppermute | solution.py:221
  2.1 0.5 collective-permute-start
  2.6 2.1 %first_step.1 = (f32[4,64,128]{2,1,0:T(8,128)S(1)}, f32[4,64,128]{2,1,0:T(8,128)S(1)}, bf16[1024,256]{1,0:T(8,128)(2,1)S(1)}, bf16[1024,256]{1,0:T(8,128)(2,1)S(...) custom-call(s32[2,128]{1,0:T(2,128)S(1)} %broadcast_in_dim.2.limits_, ...), custom_call_target="tpu_custom_call" | custom-call | tf_op jit(solution)/shard_map/first_step/pallas_call | solution.py:247
  4.8 0.4 first_step_other.1
  5.2 1.3 %collective-permute-start.3 = (f32[128,128]{1,0:T(8,128)S(1)}, f32[128,128]{1,0:T(8,128)S(1)}, u32[]{:S(2)}, u32[]{:S(2)}) collective-permute-start(f32[128,128]{1,0:T(8,128)S(1)} %get-tuple-element.52.part_ref), channel_id=1, source_target_pairs={{1,0},{3,2},{5,4},{7,6},{9,8},{11,10},{13,12},{15,14},{16,17},{18,... | collective-permute-start | bytes 196616 | tf_op jit(solution)/shard_map/ppermute | solution.py:221
  6.5 0.2 turn.4
  6.7 4.8 %collective-permute-done.3 = f32[128,128]{1,0:T(8,128)S(1)} collective-permute-done((f32[128,128]{1,0:T(8,128)S(1)}, f32[128,128]{1,0:T(8,128)S(1)}, u32[]{:S(2)}, u32[]{:S(2)}) %collective-permute-start.3) | collective-permute-done | bytes 65568 | tf_op jit(solution)/shard_map/ppermute | solution.py:221
  11.5 2.0 %collective-permute-done.4 = f32[128,128]{1,0:T(8,128)S(1)} collective-permute-done((f32[128,128]{1,0:T(8,128)S(1)}, f32[128,128]{1,0:T(8,128)S(1)}, u32[]{:S(2)}, u32[]{:S(2)}) %collective-permute-start.4) | collective-permute-done | bytes 65568 | tf_op jit(solution)/shard_map/ppermute | solution.py:221
  13.6 2.4 %collective-permute-start.7 = (f32[128,128]{1,0:T(8,128)S(1)}, f32[128,128]{1,0:T(8,128)S(1)}, u32[]{:S(2)}, u32[]{:S(2)}) collective-permute-start(f32[128,128]{1,0:T(8,128)S(1)} %add_add_fusion.3.rest_0_), channel_id=1, source_target_pairs={{0,8},{1,9},{2,10},{3,11},{4,12},{5,13},{6,14},{7,15},{8,0},{9,1},... | collective-permute-start | bytes 196616 | tf_op jit(solution)/shard_map/ppermute | solution.py:221
  16.0 0.2 collective-permute-start.6
  16.2 1.5 %collective-permute-start.10 = (f32[128,128]{1,0:T(8,128)S(1)}, f32[128,128]{1,0:T(8,128)S(1)}, u32[]{:S(2)}, u32[]{:S(2)}) collective-permute-start(f32[128,128]{1,0:T(8,128)S(1)} %add_add_fusion.3.rest_0_), channel_id=1, source_target_pairs={{0,2},{1,3},{2,0},{3,1},{4,6},{5,7},{6,4},{7,5},{8,10},{9,11},{10,... | collective-permute-start | bytes 196616 | tf_op jit(solution)/shard_map/ppermute | solution.py:221
  17.7 0.4 next_step_early.3
  18.0 0.9 %collective-permute-done.7.rest_1_ = f32[128,128]{1,0:T(8,128)S(1)} collective-permute-done((f32[128,128]{1,0:T(8,128)S(1)}, f32[128,128]{1,0:T(8,128)S(1)}, u32[]{:S(2)}, u32[]{:S(2)}) %collective-permute-start.7) | collective-permute-done | bytes 65568 | tf_op jit(solution)/shard_map/ppermute | solution.py:221
  18.9 1.0 %collective-permute-done.6.rest_0_ = f32[128,128]{1,0:T(8,128)S(1)} collective-permute-done((f32[128,128]{1,0:T(8,128)S(1)}, f32[128,128]{1,0:T(8,128)S(1)}, u32[]{:S(2)}, u32[]{:S(2)}) %collective-permute-start.6) | collective-permute-done | bytes 65568 | tf_op jit(solution)/shard_map/ppermute | solution.py:221
  19.9 0.4 next_step.3
  20.4 0.2 turn.5
  20.6 3.7 %collective-permute-done.8 = f32[128,128]{1,0:T(8,128)S(1)} collective-permute-done((f32[128,128]{1,0:T(8,128)S(1)}, f32[128,128]{1,0:T(8,128)S(1)}, u32[]{:S(2)}, u32[]{:S(2)}) %collective-permute-start.8) | collective-permute-done | bytes 65568 | tf_op jit(solution)/shard_map/ppermute | solution.py:221
  24.3 1.0 %collective-permute-done.9 = f32[128,128]{1,0:T(8,128)S(1)} collective-permute-done((f32[128,128]{1,0:T(8,128)S(1)}, f32[128,128]{1,0:T(8,128)S(1)}, u32[]{:S(2)}, u32[]{:S(2)}) %collective-permute-start.9) | collective-permute-done | bytes 65568 | tf_op jit(solution)/shard_map/ppermute | solution.py:221
  25.4 1.4 %collective-permute-start.13 = (f32[128,128]{1,0:T(8,128)S(1)}, f32[128,128]{1,0:T(8,128)S(1)}, u32[]{:S(2)}, u32[]{:S(2)}) collective-permute-start(f32[128,128]{1,0:T(8,128)S(1)} %add_add_fusion.2.rest_0_), channel_id=1, source_target_pairs={{0,8},{1,9},{2,10},{3,11},{4,12},{5,13},{6,14},{7,15},{8,0},{9,1},... | collective-permute-start | bytes 196616 | tf_op jit(solution)/shard_map/ppermute | solution.py:221
  26.8 1.3 %collective-permute-start.12 = (f32[128,128]{1,0:T(8,128)S(1)}, f32[128,128]{1,0:T(8,128)S(1)}, u32[]{:S(2)}, u32[]{:S(2)}) collective-permute-start(f32[128,128]{1,0:T(8,128)S(1)} %add_add_fusion.2.rest_0_), channel_id=1, source_target_pairs={{0,4},{1,5},{2,6},{3,7},{4,0},{5,1},{6,2},{7,3},{8,12},{9,13},{10,... | collective-permute-start | bytes 196616 | tf_op jit(solution)/shard_map/ppermute | solution.py:221
  28.0 3.8 %collective-permute-start.16 = (f32[128,128]{1,0:T(8,128)S(1)}, f32[128,128]{1,0:T(8,128)S(1)}, u32[]{:S(2)}, u32[]{:S(2)}) collective-permute-start(f32[128,128]{1,0:T(8,128)S(1)} %add_add_fusion.2.rest_0_), channel_id=1, source_target_pairs={{0,2},{1,3},{2,0},{3,1},{4,6},{5,7},{6,4},{7,5},{8,10},{9,11},{10,... | collective-permute-start | bytes 196616 | tf_op jit(solution)/shard_map/ppermute | solution.py:221
  31.9 0.3 next_step_early.4
  32.2 0.4 next_step.4
  32.8 0.2 turn.6
  33.0 3.8 %collective-permute-done.14 = f32[128,128]{1,0:T(8,128)S(1)} collective-permute-done((f32[128,128]{1,0:T(8,128)S(1)}, f32[128,128]{1,0:T(8,128)S(1)}, u32[]{:S(2)}, u32[]{:S(2)}) %collective-permute-start.14) | collective-permute-done | bytes 65568 | tf_op jit(solution)/shard_map/ppermute | solution.py:221
  36.8 1.0 %collective-permute-done.15 = f32[128,128]{1,0:T(8,128)S(1)} collective-permute-done((f32[128,128]{1,0:T(8,128)S(1)}, f32[128,128]{1,0:T(8,128)S(1)}, u32[]{:S(2)}, u32[]{:S(2)}) %collective-permute-start.15) | collective-permute-done | bytes 65568 | tf_op jit(solution)/shard_map/ppermute | solution.py:221
  37.9 1.5 %collective-permute-start.19 = (f32[128,128]{1,0:T(8,128)S(1)}, f32[128,128]{1,0:T(8,128)S(1)}, u32[]{:S(2)}, u32[]{:S(2)}) collective-permute-start(f32[128,128]{1,0:T(8,128)S(1)} %add_add_fusion.1.rest_0_), channel_id=1, source_target_pairs={{0,8},{1,9},{2,10},{3,11},{4,12},{5,13},{6,14},{7,15},{8,0},{9,1},... | collective-permute-start | bytes 196616 | tf_op jit(solution)/shard_map/ppermute | solution.py:221
  39.4 1.1 %collective-permute-start.18 = (f32[128,128]{1,0:T(8,128)S(1)}, f32[128,128]{1,0:T(8,128)S(1)}, u32[]{:S(2)}, u32[]{:S(2)}) collective-permute-start(f32[128,128]{1,0:T(8,128)S(1)} %add_add_fusion.1.rest_0_), channel_id=1, source_target_pairs={{0,4},{1,5},{2,6},{3,7},{4,0},{5,1},{6,2},{7,3},{8,12},{9,13},{10,... | collective-permute-start | bytes 196616 | tf_op jit(solution)/shard_map/ppermute | solution.py:221
  40.5 4.5 %collective-permute-start.24 = (f32[128,128]{1,0:T(8,128)S(1)}, f32[128,128]{1,0:T(8,128)S(1)}, u32[]{:S(2)}, u32[]{:S(2)}) collective-permute-start(f32[128,128]{1,0:T(8,128)S(1)} %add_add_fusion.1.rest_0_), channel_id=1, source_target_pairs={{0,2},{1,3},{2,0},{3,1},{4,6},{5,7},{6,4},{7,5},{8,10},{9,11},{10,... | collective-permute-start | bytes 196616 | tf_op jit(solution)/shard_map/ppermute | solution.py:221
  45.0 0.3 next_step_early.5
  45.4 0.4 next_step.5
  45.8 0.9 %collective-permute-start.23 = (f32[128,128]{1,0:T(8,128)S(1)}, f32[128,128]{1,0:T(8,128)S(1)}, u32[]{:S(2)}, u32[]{:S(2)}) collective-permute-start(f32[128,128]{1,0:T(8,128)S(1)} %get-tuple-element.76.far_ref), channel_id=1, source_target_pairs={{1,16},{3,18},{5,20},{7,22},{9,24},{11,26},{13,28},{15,30},{16,1},... | collective-permute-start | bytes 196616 | tf_op jit(solution)/shard_map/ppermute | solution.py:221
  46.8 2.4 %collective-permute-start.21 = (f32[4,64,128]{2,1,0:T(8,128)S(1)}, f32[4,64,128]{2,1,0:T(8,128)S(1)}, u32[]{:S(2)}, u32[]{:S(2)}) collective-permute-start(f32[4,64,128]{2,1,0:T(8,128)S(1)} %get-tuple-element.74.refs_1_), channel_id=1, source_target_pairs={{0,2},{1,3},{2,0},{3,1},{4,6},{5,7},{6,4},{7,5},{8,10},{9,11},{10,... | collective-permute-start | bytes 393224 | tf_op jit(solution)/shard_map/ppermute | solution.py:221
  49.2 0.7 %turn.7 = (f32[2,128,128]{2,1,0:T(8,128)}, f32[128,128]{1,0:T(8,128)S(1)}) custom-call(bf16[128,128]{1,0:T(8,128)(2,1)S(1)} %get-tuple-element.54.ham_ref, f32[2,128,128]{2,1,0:T(8,128)S(1)} %get-tuple-element.77.near_ref, f32[128,128]{1,0:T(8,128)S(1)} %get-tuple-element.75.part_ref, f32[128,128]{1,0:T(8,128)S(1)} %get-tuple-element.76.far_ref, ...), custom_call_target="tpu_custom_call" | custom-call | tf_op jit(solution)/shard_map/turn/pallas_call | solution.py:263
  49.9 0.1 collective-permute-done.22
  50.0 1.0 %collective-permute-done.23 = f32[128,128]{1,0:T(8,128)S(1)} collective-permute-done((f32[128,128]{1,0:T(8,128)S(1)}, f32[128,128]{1,0:T(8,128)S(1)}, u32[]{:S(2)}, u32[]{:S(2)}) %collective-permute-start.23) | collective-permute-done | bytes 65568 | tf_op jit(solution)/shard_map/ppermute | solution.py:221
  51.0 0.5 collective-permute-start.27
  51.4 4.1 %collective-permute-start.20 = (f32[4,64,128]{2,1,0:T(8,128)S(1)}, f32[4,64,128]{2,1,0:T(8,128)S(1)}, u32[]{:S(2)}, u32[]{:S(2)}) collective-permute-start(f32[4,64,128]{2,1,0:T(8,128)S(1)} %get-tuple-element.71.refs_0_), channel_id=1, source_target_pairs={{0,2},{1,3},{2,0},{3,1},{4,6},{5,7},{6,4},{7,5},{8,10},{9,11},{10,... | collective-permute-start | bytes 393224 | tf_op jit(solution)/shard_map/ppermute | solution.py:221
  55.5 1.8 %collective-permute-start.26 = (f32[128,128]{1,0:T(8,128)S(1)}, f32[128,128]{1,0:T(8,128)S(1)}, u32[]{:S(2)}, u32[]{:S(2)}) collective-permute-start(f32[128,128]{1,0:T(8,128)S(1)} %add_add_fusion.refs_4_), channel_id=1, source_target_pairs={{0,8},{1,9},{2,10},{3,11},{4,12},{5,13},{6,14},{7,15},{8,0},{9,1},... | collective-permute-start | bytes 196616 | tf_op jit(solution)/shard_map/ppermute | solution.py:221
  57.3 1.1 %collective-permute-start.25 = (f32[128,128]{1,0:T(8,128)S(1)}, f32[128,128]{1,0:T(8,128)S(1)}, u32[]{:S(2)}, u32[]{:S(2)}) collective-permute-start(f32[128,128]{1,0:T(8,128)S(1)} %add_add_fusion.refs_4_), channel_id=1, source_target_pairs={{0,4},{1,5},{2,6},{3,7},{4,0},{5,1},{6,2},{7,3},{8,12},{9,13},{10,... | collective-permute-start | bytes 196616 | tf_op jit(solution)/shard_map/ppermute | solution.py:221
  58.3 0.6 collective-permute-start.28
  58.9 2.3 %collective-permute-start.31 = (f32[128,128]{1,0:T(8,128)S(1)}, f32[128,128]{1,0:T(8,128)S(1)}, u32[]{:S(2)}, u32[]{:S(2)}) collective-permute-start(f32[128,128]{1,0:T(8,128)S(1)} %collective-permute-done.27.refs_7_), channel_id=1, source_target_pairs={{0,2},{1,3},{2,0},{3,1},{4,6},{5,7},{6,4},{7,5},{8,10},{9,11},{10,... | collective-permute-start | bytes 196616 | tf_op jit(solution)/shard_map/ppermute | solution.py:221
  61.2 0.3 collective-permute-done.25.refs_5_
  61.5 0.7 %collective-permute-start.29 = (f32[128,128]{1,0:T(8,128)S(1)}, f32[128,128]{1,0:T(8,128)S(1)}, u32[]{:S(2)}, u32[]{:S(2)}) collective-permute-start(f32[128,128]{1,0:T(8,128)S(1)} %collective-permute-done.25.refs_5_), channel_id=1, source_target_pairs={{0,2},{1,3},{2,0},{3,1},{4,6},{5,7},{6,4},{7,5},{8,10},{9,11},{10,... | collective-permute-start | bytes 196616 | tf_op jit(solution)/shard_map/ppermute | solution.py:221
  62.2 0.2 collective-permute-done.30.refs_10_
  62.5 0.7 %collective-permute-done.29.refs_9_ = f32[128,128]{1,0:T(8,128)S(1)} collective-permute-done((f32[128,128]{1,0:T(8,128)S(1)}, f32[128,128]{1,0:T(8,128)S(1)}, u32[]{:S(2)}, u32[]{:S(2)}) %collective-permute-start.29) | collective-permute-done | bytes 65568 | tf_op jit(solution)/shard_map/ppermute | solution.py:221
  63.1 0.9 %last_step.1 = f32[1024,128]{1,0:T(8,128)} custom-call(f32[4,64,128]{2,1,0:T(8,128)S(1)} %get-tuple-element.71.refs_0_, f32[4,64,128]{2,1,0:T(8,128)S(1)} %get-tuple-element.74.refs_1_, f32[4,64,128]{2,1,0:T(8,128)S(1)} %collective-permute-done.20.refs_2_, f32[4,64,128]{2,1,0:T(8,128)S(1)} %collective-permute-done.21.refs_3_, ...), custom_call_target="tpu_custom_call" | custom-call | tf_op jit(solution)/shard_map/last_step/pallas_call | solution.py:282
  (37 shorter events, 0.8 us)
Async XLA Ops:
  1.4 3.3 %collective-permute-start.1 = (f32[1024,128]{1,0:T(8,128)}, f32[1024,128]{1,0:T(8,128)S(1)}, u32[]{:S(2)}, u32[]{:S(2)}) collective-permute-start(f32[1024,128]{1,0:T(8,128)} %bitcast.13), channel_id=1, source_target_pairs={{0,2},{1,3},{2,0},{3,1},{4,6},{5,7},{6,4},{7,5},{8,10},{9,11},{10,... | collective-permute-start | bytes 1572872 | tf_op jit(solution)/shard_map/ppermute | solution.py:221
  2.1 2.7 %collective-permute-start.2 = (f32[1024,128]{1,0:T(8,128)}, f32[1024,128]{1,0:T(8,128)S(1)}, u32[]{:S(2)}, u32[]{:S(2)}) collective-permute-start(f32[1024,128]{1,0:T(8,128)} %bitcast.15), channel_id=1, source_target_pairs={{0,2},{1,3},{2,0},{3,1},{4,6},{5,7},{6,4},{7,5},{8,10},{9,11},{10,... | collective-permute-start | bytes 1572872 | tf_op jit(solution)/shard_map/ppermute | solution.py:221
  2.1 2.6 %collective-permute-start = (s32[2,128]{1,0:T(2,128)S(1)}, s32[2,128]{1,0:T(2,128)S(1)}, u32[]{:S(2)}, u32[]{:S(2)}) collective-permute-start(s32[2,128]{1,0:T(2,128)S(1)} %broadcast_in_dim.2.limits_ref), channel_id=1, source_target_pairs={{0,2},{1,3},{2,0},{3,1},{4,6},{5,7},{6,4},{7,5},{8,10},{9,11},{10,... | collective-permute-start | bytes 3080 | tf_op jit(solution)/shard_map/ppermute | solution.py:221
  2.6 15.0 %copy-start = (f32[4,128,8,128]{3,2,1,0:T(8,128)S(1)}, f32[4,128,8,128]{3,2,1,0:T(8,128)}, u32[]{:S(2)}) copy-start(f32[4,128,8,128]{3,2,1,0:T(8,128)} %param.11) | copy-start | bytes 6291460
  5.2 6.3 %collective-permute-start.3 = (f32[128,128]{1,0:T(8,128)S(1)}, f32[128,128]{1,0:T(8,128)S(1)}, u32[]{:S(2)}, u32[]{:S(2)}) collective-permute-start(f32[128,128]{1,0:T(8,128)S(1)} %get-tuple-element.52.part_ref), channel_id=1, source_target_pairs={{1,0},{3,2},{5,4},{7,6},{9,8},{11,10},{13,12},{15,14},{16,17},{18,... | collective-permute-start | bytes 196616 | tf_op jit(solution)/shard_map/ppermute | solution.py:221
  6.5 7.0 %collective-permute-start.4 = (f32[128,128]{1,0:T(8,128)S(1)}, f32[128,128]{1,0:T(8,128)S(1)}, u32[]{:S(2)}, u32[]{:S(2)}) collective-permute-start(f32[128,128]{1,0:T(8,128)S(1)} %get-tuple-element.53.far_ref), channel_id=1, source_target_pairs={{1,16},{3,18},{5,20},{7,22},{9,24},{11,26},{13,28},{15,30},{16,1},... | collective-permute-start | bytes 196616 | tf_op jit(solution)/shard_map/ppermute | solution.py:221
  13.5 4.2 %collective-permute-start.5 = (f32[128,128]{1,0:T(8,128)S(1)}, f32[128,128]{1,0:T(8,128)S(1)}, u32[]{:S(2)}, u32[]{:S(2)}) collective-permute-start(f32[128,128]{1,0:T(8,128)S(1)} %add_add_fusion.3.rest_0_), channel_id=1, source_target_pairs={{0,12},{1,13},{2,14},{3,15},{4,8},{5,9},{6,10},{7,11},{8,4},{9,5},... | collective-permute-start | bytes 196616 | tf_op jit(solution)/shard_map/ppermute | solution.py:221
  13.6 5.4 %collective-permute-start.7 = (f32[128,128]{1,0:T(8,128)S(1)}, f32[128,128]{1,0:T(8,128)S(1)}, u32[]{:S(2)}, u32[]{:S(2)}) collective-permute-start(f32[128,128]{1,0:T(8,128)S(1)} %add_add_fusion.3.rest_0_), channel_id=1, source_target_pairs={{0,8},{1,9},{2,10},{3,11},{4,12},{5,13},{6,14},{7,15},{8,0},{9,1},... | collective-permute-start | bytes 196616 | tf_op jit(solution)/shard_map/ppermute | solution.py:221
  16.0 3.9 %collective-permute-start.6 = (f32[128,128]{1,0:T(8,128)S(1)}, f32[128,128]{1,0:T(8,128)S(1)}, u32[]{:S(2)}, u32[]{:S(2)}) collective-permute-start(f32[128,128]{1,0:T(8,128)S(1)} %add_add_fusion.3.rest_0_), channel_id=1, source_target_pairs={{0,4},{1,5},{2,6},{3,7},{4,0},{5,1},{6,2},{7,3},{8,12},{9,13},{10,... | collective-permute-start | bytes 196616 | tf_op jit(solution)/shard_map/ppermute | solution.py:221
  16.2 4.2 %collective-permute-start.10 = (f32[128,128]{1,0:T(8,128)S(1)}, f32[128,128]{1,0:T(8,128)S(1)}, u32[]{:S(2)}, u32[]{:S(2)}) collective-permute-start(f32[128,128]{1,0:T(8,128)S(1)} %add_add_fusion.3.rest_0_), channel_id=1, source_target_pairs={{0,2},{1,3},{2,0},{3,1},{4,6},{5,7},{6,4},{7,5},{8,10},{9,11},{10,... | collective-permute-start | bytes 196616 | tf_op jit(solution)/shard_map/ppermute | solution.py:221
  20.2 4.1 %collective-permute-start.8 = (f32[128,128]{1,0:T(8,128)S(1)}, f32[128,128]{1,0:T(8,128)S(1)}, u32[]{:S(2)}, u32[]{:S(2)}) collective-permute-start(f32[128,128]{1,0:T(8,128)S(1)} %get-tuple-element.61.part_ref), channel_id=1, source_target_pairs={{1,0},{3,2},{5,4},{7,6},{9,8},{11,10},{13,12},{15,14},{16,17},{18,... | collective-permute-start | bytes 196616 | tf_op jit(solution)/shard_map/ppermute | solution.py:221
  20.3 5.0 %collective-permute-start.9 = (f32[128,128]{1,0:T(8,128)S(1)}, f32[128,128]{1,0:T(8,128)S(1)}, u32[]{:S(2)}, u32[]{:S(2)}) collective-permute-start(f32[128,128]{1,0:T(8,128)S(1)} %get-tuple-element.62.far_ref), channel_id=1, source_target_pairs={{1,16},{3,18},{5,20},{7,22},{9,24},{11,26},{13,28},{15,30},{16,1},... | collective-permute-start | bytes 196616 | tf_op jit(solution)/shard_map/ppermute | solution.py:221
  25.3 6.6 %collective-permute-start.11 = (f32[128,128]{1,0:T(8,128)S(1)}, f32[128,128]{1,0:T(8,128)S(1)}, u32[]{:S(2)}, u32[]{:S(2)}) collective-permute-start(f32[128,128]{1,0:T(8,128)S(1)} %add_add_fusion.2.rest_0_), channel_id=1, source_target_pairs={{0,12},{1,13},{2,14},{3,15},{4,8},{5,9},{6,10},{7,11},{8,4},{9,5},... | collective-permute-start | bytes 196616 | tf_op jit(solution)/shard_map/ppermute | solution.py:221
  25.4 6.8 %collective-permute-start.13 = (f32[128,128]{1,0:T(8,128)S(1)}, f32[128,128]{1,0:T(8,128)S(1)}, u32[]{:S(2)}, u32[]{:S(2)}) collective-permute-start(f32[128,128]{1,0:T(8,128)S(1)} %add_add_fusion.2.rest_0_), channel_id=1, source_target_pairs={{0,8},{1,9},{2,10},{3,11},{4,12},{5,13},{6,14},{7,15},{8,0},{9,1},... | collective-permute-start | bytes 196616 | tf_op jit(solution)/shard_map/ppermute | solution.py:221
  26.8 5.5 %collective-permute-start.12 = (f32[128,128]{1,0:T(8,128)S(1)}, f32[128,128]{1,0:T(8,128)S(1)}, u32[]{:S(2)}, u32[]{:S(2)}) collective-permute-start(f32[128,128]{1,0:T(8,128)S(1)} %add_add_fusion.2.rest_0_), channel_id=1, source_target_pairs={{0,4},{1,5},{2,6},{3,7},{4,0},{5,1},{6,2},{7,3},{8,12},{9,13},{10,... | collective-permute-start | bytes 196616 | tf_op jit(solution)/shard_map/ppermute | solution.py:221
  28.0 4.8 %collective-permute-start.16 = (f32[128,128]{1,0:T(8,128)S(1)}, f32[128,128]{1,0:T(8,128)S(1)}, u32[]{:S(2)}, u32[]{:S(2)}) collective-permute-start(f32[128,128]{1,0:T(8,128)S(1)} %add_add_fusion.2.rest_0_), channel_id=1, source_target_pairs={{0,2},{1,3},{2,0},{3,1},{4,6},{5,7},{6,4},{7,5},{8,10},{9,11},{10,... | collective-permute-start | bytes 196616 | tf_op jit(solution)/shard_map/ppermute | solution.py:221
  32.6 4.2 %collective-permute-start.14 = (f32[128,128]{1,0:T(8,128)S(1)}, f32[128,128]{1,0:T(8,128)S(1)}, u32[]{:S(2)}, u32[]{:S(2)}) collective-permute-start(f32[128,128]{1,0:T(8,128)S(1)} %get-tuple-element.67.part_ref), channel_id=1, source_target_pairs={{1,0},{3,2},{5,4},{7,6},{9,8},{11,10},{13,12},{15,14},{16,17},{18,... | collective-permute-start | bytes 196616 | tf_op jit(solution)/shard_map/ppermute | solution.py:221
  32.7 5.1 %collective-permute-start.15 = (f32[128,128]{1,0:T(8,128)S(1)}, f32[128,128]{1,0:T(8,128)S(1)}, u32[]{:S(2)}, u32[]{:S(2)}) collective-permute-start(f32[128,128]{1,0:T(8,128)S(1)} %get-tuple-element.68.far_ref), channel_id=1, source_target_pairs={{1,16},{3,18},{5,20},{7,22},{9,24},{11,26},{13,28},{15,30},{16,1},... | collective-permute-start | bytes 196616 | tf_op jit(solution)/shard_map/ppermute | solution.py:221
  37.8 7.2 %collective-permute-start.17 = (f32[128,128]{1,0:T(8,128)S(1)}, f32[128,128]{1,0:T(8,128)S(1)}, u32[]{:S(2)}, u32[]{:S(2)}) collective-permute-start(f32[128,128]{1,0:T(8,128)S(1)} %add_add_fusion.1.rest_0_), channel_id=1, source_target_pairs={{0,12},{1,13},{2,14},{3,15},{4,8},{5,9},{6,10},{7,11},{8,4},{9,5},... | collective-permute-start | bytes 196616 | tf_op jit(solution)/shard_map/ppermute | solution.py:221
  37.9 7.5 %collective-permute-start.19 = (f32[128,128]{1,0:T(8,128)S(1)}, f32[128,128]{1,0:T(8,128)S(1)}, u32[]{:S(2)}, u32[]{:S(2)}) collective-permute-start(f32[128,128]{1,0:T(8,128)S(1)} %add_add_fusion.1.rest_0_), channel_id=1, source_target_pairs={{0,8},{1,9},{2,10},{3,11},{4,12},{5,13},{6,14},{7,15},{8,0},{9,1},... | collective-permute-start | bytes 196616 | tf_op jit(solution)/shard_map/ppermute | solution.py:221
  39.4 6.0 %collective-permute-start.18 = (f32[128,128]{1,0:T(8,128)S(1)}, f32[128,128]{1,0:T(8,128)S(1)}, u32[]{:S(2)}, u32[]{:S(2)}) collective-permute-start(f32[128,128]{1,0:T(8,128)S(1)} %add_add_fusion.1.rest_0_), channel_id=1, source_target_pairs={{0,4},{1,5},{2,6},{3,7},{4,0},{5,1},{6,2},{7,3},{8,12},{9,13},{10,... | collective-permute-start | bytes 196616 | tf_op jit(solution)/shard_map/ppermute | solution.py:221
  40.5 8.7 %collective-permute-start.24 = (f32[128,128]{1,0:T(8,128)S(1)}, f32[128,128]{1,0:T(8,128)S(1)}, u32[]{:S(2)}, u32[]{:S(2)}) collective-permute-start(f32[128,128]{1,0:T(8,128)S(1)} %add_add_fusion.1.rest_0_), channel_id=1, source_target_pairs={{0,2},{1,3},{2,0},{3,1},{4,6},{5,7},{6,4},{7,5},{8,10},{9,11},{10,... | collective-permute-start | bytes 196616 | tf_op jit(solution)/shard_map/ppermute | solution.py:221
  45.8 4.2 %collective-permute-start.22 = (f32[128,128]{1,0:T(8,128)S(1)}, f32[128,128]{1,0:T(8,128)S(1)}, u32[]{:S(2)}, u32[]{:S(2)}) collective-permute-start(f32[128,128]{1,0:T(8,128)S(1)} %get-tuple-element.75.part_ref), channel_id=1, source_target_pairs={{1,0},{3,2},{5,4},{7,6},{9,8},{11,10},{13,12},{15,14},{16,17},{18,... | collective-permute-start | bytes 196616 | tf_op jit(solution)/shard_map/ppermute | solution.py:221
  45.8 5.1 %collective-permute-start.23 = (f32[128,128]{1,0:T(8,128)S(1)}, f32[128,128]{1,0:T(8,128)S(1)}, u32[]{:S(2)}, u32[]{:S(2)}) collective-permute-start(f32[128,128]{1,0:T(8,128)S(1)} %get-tuple-element.76.far_ref), channel_id=1, source_target_pairs={{1,16},{3,18},{5,20},{7,22},{9,24},{11,26},{13,28},{15,30},{16,1},... | collective-permute-start | bytes 196616 | tf_op jit(solution)/shard_map/ppermute | solution.py:221
  46.8 11.6 %collective-permute-start.21 = (f32[4,64,128]{2,1,0:T(8,128)S(1)}, f32[4,64,128]{2,1,0:T(8,128)S(1)}, u32[]{:S(2)}, u32[]{:S(2)}) collective-permute-start(f32[4,64,128]{2,1,0:T(8,128)S(1)} %get-tuple-element.74.refs_1_), channel_id=1, source_target_pairs={{0,2},{1,3},{2,0},{3,1},{4,6},{5,7},{6,4},{7,5},{8,10},{9,11},{10,... | collective-permute-start | bytes 393224 | tf_op jit(solution)/shard_map/ppermute | solution.py:221
  51.0 7.9 %collective-permute-start.27 = (f32[128,128]{1,0:T(8,128)S(1)}, f32[128,128]{1,0:T(8,128)S(1)}, u32[]{:S(2)}, u32[]{:S(2)}) collective-permute-start(f32[128,128]{1,0:T(8,128)S(1)} %add_add_fusion.refs_4_), channel_id=1, source_target_pairs={{0,12},{1,13},{2,14},{3,15},{4,8},{5,9},{6,10},{7,11},{8,4},{9,5},... | collective-permute-start | bytes 196616 | tf_op jit(solution)/shard_map/ppermute | solution.py:221
  51.4 10.8 %collective-permute-start.20 = (f32[4,64,128]{2,1,0:T(8,128)S(1)}, f32[4,64,128]{2,1,0:T(8,128)S(1)}, u32[]{:S(2)}, u32[]{:S(2)}) collective-permute-start(f32[4,64,128]{2,1,0:T(8,128)S(1)} %get-tuple-element.71.refs_0_), channel_id=1, source_target_pairs={{0,2},{1,3},{2,0},{3,1},{4,6},{5,7},{6,4},{7,5},{8,10},{9,11},{10,... | collective-permute-start | bytes 393224 | tf_op jit(solution)/shard_map/ppermute | solution.py:221
  55.5 5.7 %collective-permute-start.26 = (f32[128,128]{1,0:T(8,128)S(1)}, f32[128,128]{1,0:T(8,128)S(1)}, u32[]{:S(2)}, u32[]{:S(2)}) collective-permute-start(f32[128,128]{1,0:T(8,128)S(1)} %add_add_fusion.refs_4_), channel_id=1, source_target_pairs={{0,8},{1,9},{2,10},{3,11},{4,12},{5,13},{6,14},{7,15},{8,0},{9,1},... | collective-permute-start | bytes 196616 | tf_op jit(solution)/shard_map/ppermute | solution.py:221
  57.3 4.2 %collective-permute-start.25 = (f32[128,128]{1,0:T(8,128)S(1)}, f32[128,128]{1,0:T(8,128)S(1)}, u32[]{:S(2)}, u32[]{:S(2)}) collective-permute-start(f32[128,128]{1,0:T(8,128)S(1)} %add_add_fusion.refs_4_), channel_id=1, source_target_pairs={{0,4},{1,5},{2,6},{3,7},{4,0},{5,1},{6,2},{7,3},{8,12},{9,13},{10,... | collective-permute-start | bytes 196616 | tf_op jit(solution)/shard_map/ppermute | solution.py:221
  58.3 3.9 %collective-permute-start.28 = (f32[128,128]{1,0:T(8,128)S(1)}, f32[128,128]{1,0:T(8,128)S(1)}, u32[]{:S(2)}, u32[]{:S(2)}) collective-permute-start(f32[128,128]{1,0:T(8,128)S(1)} %add_add_fusion.refs_4_), channel_id=1, source_target_pairs={{0,2},{1,3},{2,0},{3,1},{4,6},{5,7},{6,4},{7,5},{8,10},{9,11},{10,... | collective-permute-start | bytes 196616 | tf_op jit(solution)/shard_map/ppermute | solution.py:221
  58.9 3.3 %collective-permute-start.31 = (f32[128,128]{1,0:T(8,128)S(1)}, f32[128,128]{1,0:T(8,128)S(1)}, u32[]{:S(2)}, u32[]{:S(2)}) collective-permute-start(f32[128,128]{1,0:T(8,128)S(1)} %collective-permute-done.27.refs_7_), channel_id=1, source_target_pairs={{0,2},{1,3},{2,0},{3,1},{4,6},{5,7},{6,4},{7,5},{8,10},{9,11},{10,... | collective-permute-start | bytes 196616 | tf_op jit(solution)/shard_map/ppermute | solution.py:221
  61.2 1.3 %collective-permute-start.30 = (f32[128,128]{1,0:T(8,128)S(1)}, f32[128,128]{1,0:T(8,128)S(1)}, u32[]{:S(2)}, u32[]{:S(2)}) collective-permute-start(f32[128,128]{1,0:T(8,128)S(1)} %collective-permute-done.26.refs_6_), channel_id=1, source_target_pairs={{0,2},{1,3},{2,0},{3,1},{4,6},{5,7},{6,4},{7,5},{8,10},{9,11},{10,... | collective-permute-start | bytes 196616 | tf_op jit(solution)/shard_map/ppermute | solution.py:221
  61.5 1.6 %collective-permute-start.29 = (f32[128,128]{1,0:T(8,128)S(1)}, f32[128,128]{1,0:T(8,128)S(1)}, u32[]{:S(2)}, u32[]{:S(2)}) collective-permute-start(f32[128,128]{1,0:T(8,128)S(1)} %collective-permute-done.25.refs_5_), channel_id=1, source_target_pairs={{0,2},{1,3},{2,0},{3,1},{4,6},{5,7},{6,4},{7,5},{8,10},{9,11},{10,... | collective-permute-start | bytes 196616 | tf_op jit(solution)/shard_map/ppermute | solution.py:221

commit v11 on v8

--- a/solution.py
+++ b/solution.py
@@ -87,6 +87,10 @@
     for j in range(2):
         rows = slice(j * half, (j + 1) * half)
         turned_ref[rows, :] = product(ham_ref[...], wide(near_ref[j])) + (part_ref[rows, :] - far_ref[rows, :])
+
+
+def turn_last(half, *refs):
+    turn(half, 2, *refs[:6], refs[7], refs[6])
 
 
 def store(rows_dev, half, parts, part_ref, far_ref):
@@ -260,8 +264,13 @@
     )(flip(limits, 1), *[flip(x, 1) for x in tables], sigma, late_sigma, own_part)
     swap = []
     for section in range(1, steps + 1):
+        last = section == steps and len(swap) == 2
         *new, turned = call(
-            functools.partial(turn, half, len(swap)), [vmem] * (4 + len(swap)), [near_out] * (len(swap) // 2) + [pair_out], [], "turn",
+            functools.partial(turn_last, half) if last else functools.partial(turn, half, len(swap)),
+            [vmem] * (4 + len(swap)),
+            [near_out] * (0 if last else len(swap) // 2) + [pair_out],
+            [vmem((2, n, n), F32)] if last else [],
+            "turn",
         )(ham, near, part, far, *swap)
         near = new[0] if new else near
         own, swapped, *others = exchange(part, far, turned)

time: 64.2 us -> 64.2 us (level)
  transfers between devices with their start and end apart: 32 -> 32, of which waited for: 14 -> 14; matrix products, arithmetic and copies ran while one was open for 0% -> 0% of each run, Pallas kernels for 9% -> 8%
where the time goes in v11:
time: 64.2 us; the launch traced here: 64.1 us
  starting transfers between devices  34.8 us (54%)
  waiting for transfers between devices  21.3 us (33%)
  Pallas kernels  6.22 us (10%)
  between operations  1.56 us (2%)
    ppermute x32, starting transfers between devices, moved(): return lax.ppermute(x, ('hist', 'col'), pairs)  34.8 us
    ppermute x32, waiting for transfers between devices, moved(): return lax.ppermute(x, ('hist', 'col'), pairs)  21.3 us
    pallas_call x1, Pallas kernels, in_pairs(): call(functools.partial(first_kernel, rows_dev, half, steps), [vmem] + [hb...  2.13 us
  transfers between devices with their start and end apart: 32, of which 14 were waited for; matrix products, arithmetic and copies ran while one was open for 0% of the time, Pallas kernels for 8%

profile of v11, /device:TPU:25, one launch (start us, length us, event | category | flops | bytes accessed | tf_op | source)
XLA Modules:
  0.0 64.1 jit_solution(3972016853104207904)
XLA Ops:
  0.0 0.7 %collective-permute-start.1 = (f32[1024,128]{1,0:T(8,128)}, f32[1024,128]{1,0:T(8,128)S(1)}, u32[]{:S(2)}, u32[]{:S(2)}) collective-permute-start(f32[1024,128]{1,0:T(8,128)} %bitcast.13), channel_id=1, source_target_pairs={{0,2},{1,3},{2,0},{3,1},{4,6},{5,7},{6,4},{7,5},{8,10},{9,11},{10,... | collective-permute-start | bytes 1572872 | tf_op jit(solution)/shard_map/ppermute | solution.py:225
  2.0 0.1 pad_add_fusion
  2.1 0.5 collective-permute-start
  2.6 2.1 %first_step.1 = (f32[4,64,128]{2,1,0:T(8,128)S(1)}, f32[4,64,128]{2,1,0:T(8,128)S(1)}, bf16[1024,256]{1,0:T(8,128)(2,1)S(1)}, bf16[1024,256]{1,0:T(8,128)(2,1)S(...) custom-call(s32[2,128]{1,0:T(2,128)S(1)} %broadcast_in_dim.2.limits_, ...), custom_call_target="tpu_custom_call" | custom-call | tf_op jit(solution)/shard_map/first_step/pallas_call | solution.py:251
  4.8 0.4 first_step_other.1
  5.2 1.3 %collective-permute-start.3 = (f32[128,128]{1,0:T(8,128)S(1)}, f32[128,128]{1,0:T(8,128)S(1)}, u32[]{:S(2)}, u32[]{:S(2)}) collective-permute-start(f32[128,128]{1,0:T(8,128)S(1)} %get-tuple-element.47.part_ref), channel_id=1, source_target_pairs={{1,0},{3,2},{5,4},{7,6},{9,8},{11,10},{13,12},{15,14},{16,17},{18,... | collective-permute-start | bytes 196616 | tf_op jit(solution)/shard_map/ppermute | solution.py:225
  6.5 0.2 turn.4
  6.7 4.8 %collective-permute-done.3 = f32[128,128]{1,0:T(8,128)S(1)} collective-permute-done((f32[128,128]{1,0:T(8,128)S(1)}, f32[128,128]{1,0:T(8,128)S(1)}, u32[]{:S(2)}, u32[]{:S(2)}) %collective-permute-start.3) | collective-permute-done | bytes 65568 | tf_op jit(solution)/shard_map/ppermute | solution.py:225
  11.5 2.1 %collective-permute-done.4 = f32[128,128]{1,0:T(8,128)S(1)} collective-permute-done((f32[128,128]{1,0:T(8,128)S(1)}, f32[128,128]{1,0:T(8,128)S(1)}, u32[]{:S(2)}, u32[]{:S(2)}) %collective-permute-start.4) | collective-permute-done | bytes 65568 | tf_op jit(solution)/shard_map/ppermute | solution.py:225
  13.7 2.4 %collective-permute-start.7 = (f32[128,128]{1,0:T(8,128)S(1)}, f32[128,128]{1,0:T(8,128)S(1)}, u32[]{:S(2)}, u32[]{:S(2)}) collective-permute-start(f32[128,128]{1,0:T(8,128)S(1)} %add_add_fusion.3.rest_0_), channel_id=1, source_target_pairs={{0,8},{1,9},{2,10},{3,11},{4,12},{5,13},{6,14},{7,15},{8,0},{9,1},... | collective-permute-start | bytes 196616 | tf_op jit(solution)/shard_map/ppermute | solution.py:225
  16.1 0.2 collective-permute-start.6
  16.3 1.3 %collective-permute-start.10 = (f32[128,128]{1,0:T(8,128)S(1)}, f32[128,128]{1,0:T(8,128)S(1)}, u32[]{:S(2)}, u32[]{:S(2)}) collective-permute-start(f32[128,128]{1,0:T(8,128)S(1)} %add_add_fusion.3.rest_0_), channel_id=1, source_target_pairs={{0,2},{1,3},{2,0},{3,1},{4,6},{5,7},{6,4},{7,5},{8,10},{9,11},{10,... | collective-permute-start | bytes 196616 | tf_op jit(solution)/shard_map/ppermute | solution.py:225
  17.7 0.4 next_step_early.3
  18.1 1.1 %collective-permute-done.7.rest_1_ = f32[128,128]{1,0:T(8,128)S(1)} collective-permute-done((f32[128,128]{1,0:T(8,128)S(1)}, f32[128,128]{1,0:T(8,128)S(1)}, u32[]{:S(2)}, u32[]{:S(2)}) %collective-permute-start.7) | collective-permute-done | bytes 65568 | tf_op jit(solution)/shard_map/ppermute | solution.py:225
  19.1 0.8 %collective-permute-done.6.rest_0_ = f32[128,128]{1,0:T(8,128)S(1)} collective-permute-done((f32[128,128]{1,0:T(8,128)S(1)}, f32[128,128]{1,0:T(8,128)S(1)}, u32[]{:S(2)}, u32[]{:S(2)}) %collective-permute-start.6) | collective-permute-done | bytes 65568 | tf_op jit(solution)/shard_map/ppermute | solution.py:225
  19.9 0.3 next_step.3
  20.4 0.2 turn.5
  20.6 3.7 %collective-permute-done.8 = f32[128,128]{1,0:T(8,128)S(1)} collective-permute-done((f32[128,128]{1,0:T(8,128)S(1)}, f32[128,128]{1,0:T(8,128)S(1)}, u32[]{:S(2)}, u32[]{:S(2)}) %collective-permute-start.8) | collective-permute-done | bytes 65568 | tf_op jit(solution)/shard_map/ppermute | solution.py:225
  24.3 1.0 %collective-permute-done.9 = f32[128,128]{1,0:T(8,128)S(1)} collective-permute-done((f32[128,128]{1,0:T(8,128)S(1)}, f32[128,128]{1,0:T(8,128)S(1)}, u32[]{:S(2)}, u32[]{:S(2)}) %collective-permute-start.9) | collective-permute-done | bytes 65568 | tf_op jit(solution)/shard_map/ppermute | solution.py:225
  25.4 1.6 %collective-permute-start.13 = (f32[128,128]{1,0:T(8,128)S(1)}, f32[128,128]{1,0:T(8,128)S(1)}, u32[]{:S(2)}, u32[]{:S(2)}) collective-permute-start(f32[128,128]{1,0:T(8,128)S(1)} %add_add_fusion.2.rest_0_), channel_id=1, source_target_pairs={{0,8},{1,9},{2,10},{3,11},{4,12},{5,13},{6,14},{7,15},{8,0},{9,1},... | collective-permute-start | bytes 196616 | tf_op jit(solution)/shard_map/ppermute | solution.py:225
  27.0 1.1 %collective-permute-start.12 = (f32[128,128]{1,0:T(8,128)S(1)}, f32[128,128]{1,0:T(8,128)S(1)}, u32[]{:S(2)}, u32[]{:S(2)}) collective-permute-start(f32[128,128]{1,0:T(8,128)S(1)} %add_add_fusion.2.rest_0_), channel_id=1, source_target_pairs={{0,4},{1,5},{2,6},{3,7},{4,0},{5,1},{6,2},{7,3},{8,12},{9,13},{10,... | collective-permute-start | bytes 196616 | tf_op jit(solution)/shard_map/ppermute | solution.py:225
  28.0 3.8 %collective-permute-start.16 = (f32[128,128]{1,0:T(8,128)S(1)}, f32[128,128]{1,0:T(8,128)S(1)}, u32[]{:S(2)}, u32[]{:S(2)}) collective-permute-start(f32[128,128]{1,0:T(8,128)S(1)} %add_add_fusion.2.rest_0_), channel_id=1, source_target_pairs={{0,2},{1,3},{2,0},{3,1},{4,6},{5,7},{6,4},{7,5},{8,10},{9,11},{10,... | collective-permute-start | bytes 196616 | tf_op jit(solution)/shard_map/ppermute | solution.py:225
  31.9 0.3 next_step_early.4
  32.2 0.4 next_step.4
  32.8 0.2 turn.6
  32.9 3.8 %collective-permute-done.14 = f32[128,128]{1,0:T(8,128)S(1)} collective-permute-done((f32[128,128]{1,0:T(8,128)S(1)}, f32[128,128]{1,0:T(8,128)S(1)}, u32[]{:S(2)}, u32[]{:S(2)}) %collective-permute-start.14) | collective-permute-done | bytes 65568 | tf_op jit(solution)/shard_map/ppermute | solution.py:225
  36.8 1.0 %collective-permute-done.15 = f32[128,128]{1,0:T(8,128)S(1)} collective-permute-done((f32[128,128]{1,0:T(8,128)S(1)}, f32[128,128]{1,0:T(8,128)S(1)}, u32[]{:S(2)}, u32[]{:S(2)}) %collective-permute-start.15) | collective-permute-done | bytes 65568 | tf_op jit(solution)/shard_map/ppermute | solution.py:225
  37.9 1.5 %collective-permute-start.19 = (f32[128,128]{1,0:T(8,128)S(1)}, f32[128,128]{1,0:T(8,128)S(1)}, u32[]{:S(2)}, u32[]{:S(2)}) collective-permute-start(f32[128,128]{1,0:T(8,128)S(1)} %add_add_fusion.1.rest_0_.refs_4_), channel_id=1, source_target_pairs={{0,8},{1,9},{2,10},{3,11},{4,12},{5,13},{6,14},{7,15},{8,0},{9,1},... | collective-permute-start | bytes 196616 | tf_op jit(solution)/shard_map/ppermute | solution.py:225
  39.4 1.1 %collective-permute-start.18 = (f32[128,128]{1,0:T(8,128)S(1)}, f32[128,128]{1,0:T(8,128)S(1)}, u32[]{:S(2)}, u32[]{:S(2)}) collective-permute-start(f32[128,128]{1,0:T(8,128)S(1)} %add_add_fusion.1.rest_0_.refs_4_), channel_id=1, source_target_pairs={{0,4},{1,5},{2,6},{3,7},{4,0},{5,1},{6,2},{7,3},{8,12},{9,13},{10,... | collective-permute-start | bytes 196616 | tf_op jit(solution)/shard_map/ppermute | solution.py:225
  40.5 4.6 %collective-permute-start.24 = (f32[128,128]{1,0:T(8,128)S(1)}, f32[128,128]{1,0:T(8,128)S(1)}, u32[]{:S(2)}, u32[]{:S(2)}) collective-permute-start(f32[128,128]{1,0:T(8,128)S(1)} %add_add_fusion.1.rest_0_.refs_4_), channel_id=1, source_target_pairs={{0,2},{1,3},{2,0},{3,1},{4,6},{5,7},{6,4},{7,5},{8,10},{9,11},{10,... | collective-permute-start | bytes 196616 | tf_op jit(solution)/shard_map/ppermute | solution.py:225
  45.1 0.3 next_step_early.5
  45.5 0.3 next_step.5
  45.9 0.9 %collective-permute-start.23 = (f32[128,128]{1,0:T(8,128)S(1)}, f32[128,128]{1,0:T(8,128)S(1)}, u32[]{:S(2)}, u32[]{:S(2)}) collective-permute-start(f32[128,128]{1,0:T(8,128)S(1)} %get-tuple-element.71.refs_3_), channel_id=1, source_target_pairs={{1,16},{3,18},{5,20},{7,22},{9,24},{11,26},{13,28},{15,30},{16,1},... | collective-permute-start | bytes 196616 | tf_op jit(solution)/shard_map/ppermute | solution.py:225
  46.8 2.4 %collective-permute-start.21 = (f32[4,64,128]{2,1,0:T(8,128)S(1)}, f32[4,64,128]{2,1,0:T(8,128)S(1)}, u32[]{:S(2)}, u32[]{:S(2)}) collective-permute-start(f32[4,64,128]{2,1,0:T(8,128)S(1)} %get-tuple-element.69.refs_1_), channel_id=1, source_target_pairs={{0,2},{1,3},{2,0},{3,1},{4,6},{5,7},{6,4},{7,5},{8,10},{9,11},{10,... | collective-permute-start | bytes 393224 | tf_op jit(solution)/shard_map/ppermute | solution.py:225
  49.2 0.2 turn.7
  49.4 0.7 %collective-permute-done.22 = f32[128,128]{1,0:T(8,128)S(1)} collective-permute-done((f32[128,128]{1,0:T(8,128)S(1)}, f32[128,128]{1,0:T(8,128)S(1)}, u32[]{:S(2)}, u32[]{:S(2)}) %collective-permute-start.22) | collective-permute-done | bytes 65568 | tf_op jit(solution)/shard_map/ppermute | solution.py:225
  50.1 1.0 %collective-permute-done.23 = f32[128,128]{1,0:T(8,128)S(1)} collective-permute-done((f32[128,128]{1,0:T(8,128)S(1)}, f32[128,128]{1,0:T(8,128)S(1)}, u32[]{:S(2)}, u32[]{:S(2)}) %collective-permute-start.23) | collective-permute-done | bytes 65568 | tf_op jit(solution)/shard_map/ppermute | solution.py:225
  51.1 0.4 collective-permute-start.27
  51.5 4.0 %collective-permute-start.20 = (f32[4,64,128]{2,1,0:T(8,128)S(1)}, f32[4,64,128]{2,1,0:T(8,128)S(1)}, u32[]{:S(2)}, u32[]{:S(2)}) collective-permute-start(f32[4,64,128]{2,1,0:T(8,128)S(1)} %get-tuple-element.66.refs_0_), channel_id=1, source_target_pairs={{0,2},{1,3},{2,0},{3,1},{4,6},{5,7},{6,4},{7,5},{8,10},{9,11},{10,... | collective-permute-start | bytes 393224 | tf_op jit(solution)/shard_map/ppermute | solution.py:225
  55.5 1.8 %collective-permute-start.26 = (f32[128,128]{1,0:T(8,128)S(1)}, f32[128,128]{1,0:T(8,128)S(1)}, u32[]{:S(2)}, u32[]{:S(2)}) collective-permute-start(f32[128,128]{1,0:T(8,128)S(1)} %add_add_fusion.refs_4_), channel_id=1, source_target_pairs={{0,8},{1,9},{2,10},{3,11},{4,12},{5,13},{6,14},{7,15},{8,0},{9,1},... | collective-permute-start | bytes 196616 | tf_op jit(solution)/shard_map/ppermute | solution.py:225
  57.3 1.0 %collective-permute-start.25 = (f32[128,128]{1,0:T(8,128)S(1)}, f32[128,128]{1,0:T(8,128)S(1)}, u32[]{:S(2)}, u32[]{:S(2)}) collective-permute-start(f32[128,128]{1,0:T(8,128)S(1)} %add_add_fusion.refs_4_), channel_id=1, source_target_pairs={{0,4},{1,5},{2,6},{3,7},{4,0},{5,1},{6,2},{7,3},{8,12},{9,13},{10,... | collective-permute-start | bytes 196616 | tf_op jit(solution)/shard_map/ppermute | solution.py:225
  58.4 0.6 collective-permute-start.28
  58.9 2.3 %collective-permute-start.31 = (f32[128,128]{1,0:T(8,128)S(1)}, f32[128,128]{1,0:T(8,128)S(1)}, u32[]{:S(2)}, u32[]{:S(2)}) collective-permute-start(f32[128,128]{1,0:T(8,128)S(1)} %collective-permute-done.27.refs_7_), channel_id=1, source_target_pairs={{0,2},{1,3},{2,0},{3,1},{4,6},{5,7},{6,4},{7,5},{8,10},{9,11},{10,... | collective-permute-start | bytes 196616 | tf_op jit(solution)/shard_map/ppermute | solution.py:225
  61.2 0.3 collective-permute-done.25.refs_5_
  61.5 0.7 %collective-permute-start.29 = (f32[128,128]{1,0:T(8,128)S(1)}, f32[128,128]{1,0:T(8,128)S(1)}, u32[]{:S(2)}, u32[]{:S(2)}) collective-permute-start(f32[128,128]{1,0:T(8,128)S(1)} %collective-permute-done.25.refs_5_), channel_id=1, source_target_pairs={{0,2},{1,3},{2,0},{3,1},{4,6},{5,7},{6,4},{7,5},{8,10},{9,11},{10,... | collective-permute-start | bytes 196616 | tf_op jit(solution)/shard_map/ppermute | solution.py:225
  62.3 0.2 collective-permute-done.30.refs_10_
  62.5 0.7 %collective-permute-done.29.refs_9_ = f32[128,128]{1,0:T(8,128)S(1)} collective-permute-done((f32[128,128]{1,0:T(8,128)S(1)}, f32[128,128]{1,0:T(8,128)S(1)}, u32[]{:S(2)}, u32[]{:S(2)}) %collective-permute-start.29) | collective-permute-done | bytes 65568 | tf_op jit(solution)/shard_map/ppermute | solution.py:225
  63.2 0.9 %last_step.1 = f32[1024,128]{1,0:T(8,128)} custom-call(f32[4,64,128]{2,1,0:T(8,128)S(1)} %get-tuple-element.66.refs_0_, f32[4,64,128]{2,1,0:T(8,128)S(1)} %get-tuple-element.69.refs_1_, f32[4,64,128]{2,1,0:T(8,128)S(1)} %collective-permute-done.20.refs_2_, f32[4,64,128]{2,1,0:T(8,128)S(1)} %collective-permute-done.21.refs_3_, ...), custom_call_target="tpu_custom_call" | custom-call | tf_op jit(solution)/shard_map/last_step/pallas_call | solution.py:291
  (37 shorter events, 0.8 us)
Async XLA Ops:
  0.0 4.8 %collective-permute-start.1 = (f32[1024,128]{1,0:T(8,128)}, f32[1024,128]{1,0:T(8,128)S(1)}, u32[]{:S(2)}, u32[]{:S(2)}) collective-permute-start(f32[1024,128]{1,0:T(8,128)} %bitcast.13), channel_id=1, source_target_pairs={{0,2},{1,3},{2,0},{3,1},{4,6},{5,7},{6,4},{7,5},{8,10},{9,11},{10,... | collective-permute-start | bytes 1572872 | tf_op jit(solution)/shard_map/ppermute | solution.py:225
  0.7 4.1 %collective-permute-start.2 = (f32[1024,128]{1,0:T(8,128)}, f32[1024,128]{1,0:T(8,128)S(1)}, u32[]{:S(2)}, u32[]{:S(2)}) collective-permute-start(f32[1024,128]{1,0:T(8,128)} %bitcast.15), channel_id=1, source_target_pairs={{0,2},{1,3},{2,0},{3,1},{4,6},{5,7},{6,4},{7,5},{8,10},{9,11},{10,... | collective-permute-start | bytes 1572872 | tf_op jit(solution)/shard_map/ppermute | solution.py:225
  2.1 2.6 %collective-permute-start = (s32[2,128]{1,0:T(2,128)S(1)}, s32[2,128]{1,0:T(2,128)S(1)}, u32[]{:S(2)}, u32[]{:S(2)}) collective-permute-start(s32[2,128]{1,0:T(2,128)S(1)} %broadcast_in_dim.2.limits_ref), channel_id=1, source_target_pairs={{0,2},{1,3},{2,0},{3,1},{4,6},{5,7},{6,4},{7,5},{8,10},{9,11},{10,... | collective-permute-start | bytes 3080 | tf_op jit(solution)/shard_map/ppermute | solution.py:225
  2.6 15.1 %copy-start = (f32[4,128,8,128]{3,2,1,0:T(8,128)S(1)}, f32[4,128,8,128]{3,2,1,0:T(8,128)}, u32[]{:S(2)}) copy-start(f32[4,128,8,128]{3,2,1,0:T(8,128)} %param.11) | copy-start | bytes 6291460
  5.2 6.3 %collective-permute-start.3 = (f32[128,128]{1,0:T(8,128)S(1)}, f32[128,128]{1,0:T(8,128)S(1)}, u32[]{:S(2)}, u32[]{:S(2)}) collective-permute-start(f32[128,128]{1,0:T(8,128)S(1)} %get-tuple-element.47.part_ref), channel_id=1, source_target_pairs={{1,0},{3,2},{5,4},{7,6},{9,8},{11,10},{13,12},{15,14},{16,17},{18,... | collective-permute-start | bytes 196616 | tf_op jit(solution)/shard_map/ppermute | solution.py:225
  6.5 7.1 %collective-permute-start.4 = (f32[128,128]{1,0:T(8,128)S(1)}, f32[128,128]{1,0:T(8,128)S(1)}, u32[]{:S(2)}, u32[]{:S(2)}) collective-permute-start(f32[128,128]{1,0:T(8,128)S(1)} %get-tuple-element.48.far_ref), channel_id=1, source_target_pairs={{1,16},{3,18},{5,20},{7,22},{9,24},{11,26},{13,28},{15,30},{16,1},... | collective-permute-start | bytes 196616 | tf_op jit(solution)/shard_map/ppermute | solution.py:225
  13.6 4.1 %collective-permute-start.5 = (f32[128,128]{1,0:T(8,128)S(1)}, f32[128,128]{1,0:T(8,128)S(1)}, u32[]{:S(2)}, u32[]{:S(2)}) collective-permute-start(f32[128,128]{1,0:T(8,128)S(1)} %add_add_fusion.3.rest_0_), channel_id=1, source_target_pairs={{0,12},{1,13},{2,14},{3,15},{4,8},{5,9},{6,10},{7,11},{8,4},{9,5},... | collective-permute-start | bytes 196616 | tf_op jit(solution)/shard_map/ppermute | solution.py:225
  13.7 5.4 %collective-permute-start.7 = (f32[128,128]{1,0:T(8,128)S(1)}, f32[128,128]{1,0:T(8,128)S(1)}, u32[]{:S(2)}, u32[]{:S(2)}) collective-permute-start(f32[128,128]{1,0:T(8,128)S(1)} %add_add_fusion.3.rest_0_), channel_id=1, source_target_pairs={{0,8},{1,9},{2,10},{3,11},{4,12},{5,13},{6,14},{7,15},{8,0},{9,1},... | collective-permute-start | bytes 196616 | tf_op jit(solution)/shard_map/ppermute | solution.py:225
  16.1 3.8 %collective-permute-start.6 = (f32[128,128]{1,0:T(8,128)S(1)}, f32[128,128]{1,0:T(8,128)S(1)}, u32[]{:S(2)}, u32[]{:S(2)}) collective-permute-start(f32[128,128]{1,0:T(8,128)S(1)} %add_add_fusion.3.rest_0_), channel_id=1, source_target_pairs={{0,4},{1,5},{2,6},{3,7},{4,0},{5,1},{6,2},{7,3},{8,12},{9,13},{10,... | collective-permute-start | bytes 196616 | tf_op jit(solution)/shard_map/ppermute | solution.py:225
  16.3 4.1 %collective-permute-start.10 = (f32[128,128]{1,0:T(8,128)S(1)}, f32[128,128]{1,0:T(8,128)S(1)}, u32[]{:S(2)}, u32[]{:S(2)}) collective-permute-start(f32[128,128]{1,0:T(8,128)S(1)} %add_add_fusion.3.rest_0_), channel_id=1, source_target_pairs={{0,2},{1,3},{2,0},{3,1},{4,6},{5,7},{6,4},{7,5},{8,10},{9,11},{10,... | collective-permute-start | bytes 196616 | tf_op jit(solution)/shard_map/ppermute | solution.py:225
  20.3 4.1 %collective-permute-start.8 = (f32[128,128]{1,0:T(8,128)S(1)}, f32[128,128]{1,0:T(8,128)S(1)}, u32[]{:S(2)}, u32[]{:S(2)}) collective-permute-start(f32[128,128]{1,0:T(8,128)S(1)} %get-tuple-element.56.part_ref), channel_id=1, source_target_pairs={{1,0},{3,2},{5,4},{7,6},{9,8},{11,10},{13,12},{15,14},{16,17},{18,... | collective-permute-start | bytes 196616 | tf_op jit(solution)/shard_map/ppermute | solution.py:225
  20.3 5.0 %collective-permute-start.9 = (f32[128,128]{1,0:T(8,128)S(1)}, f32[128,128]{1,0:T(8,128)S(1)}, u32[]{:S(2)}, u32[]{:S(2)}) collective-permute-start(f32[128,128]{1,0:T(8,128)S(1)} %get-tuple-element.57.far_ref), channel_id=1, source_target_pairs={{1,16},{3,18},{5,20},{7,22},{9,24},{11,26},{13,28},{15,30},{16,1},... | collective-permute-start | bytes 196616 | tf_op jit(solution)/shard_map/ppermute | solution.py:225
  25.3 6.5 %collective-permute-start.11 = (f32[128,128]{1,0:T(8,128)S(1)}, f32[128,128]{1,0:T(8,128)S(1)}, u32[]{:S(2)}, u32[]{:S(2)}) collective-permute-start(f32[128,128]{1,0:T(8,128)S(1)} %add_add_fusion.2.rest_0_), channel_id=1, source_target_pairs={{0,12},{1,13},{2,14},{3,15},{4,8},{5,9},{6,10},{7,11},{8,4},{9,5},... | collective-permute-start | bytes 196616 | tf_op jit(solution)/shard_map/ppermute | solution.py:225
  25.4 6.8 %collective-permute-start.13 = (f32[128,128]{1,0:T(8,128)S(1)}, f32[128,128]{1,0:T(8,128)S(1)}, u32[]{:S(2)}, u32[]{:S(2)}) collective-permute-start(f32[128,128]{1,0:T(8,128)S(1)} %add_add_fusion.2.rest_0_), channel_id=1, source_target_pairs={{0,8},{1,9},{2,10},{3,11},{4,12},{5,13},{6,14},{7,15},{8,0},{9,1},... | collective-permute-start | bytes 196616 | tf_op jit(solution)/shard_map/ppermute | solution.py:225
  27.0 5.3 %collective-permute-start.12 = (f32[128,128]{1,0:T(8,128)S(1)}, f32[128,128]{1,0:T(8,128)S(1)}, u32[]{:S(2)}, u32[]{:S(2)}) collective-permute-start(f32[128,128]{1,0:T(8,128)S(1)} %add_add_fusion.2.rest_0_), channel_id=1, source_target_pairs={{0,4},{1,5},{2,6},{3,7},{4,0},{5,1},{6,2},{7,3},{8,12},{9,13},{10,... | collective-permute-start | bytes 196616 | tf_op jit(solution)/shard_map/ppermute | solution.py:225
  28.0 4.7 %collective-permute-start.16 = (f32[128,128]{1,0:T(8,128)S(1)}, f32[128,128]{1,0:T(8,128)S(1)}, u32[]{:S(2)}, u32[]{:S(2)}) collective-permute-start(f32[128,128]{1,0:T(8,128)S(1)} %add_add_fusion.2.rest_0_), channel_id=1, source_target_pairs={{0,2},{1,3},{2,0},{3,1},{4,6},{5,7},{6,4},{7,5},{8,10},{9,11},{10,... | collective-permute-start | bytes 196616 | tf_op jit(solution)/shard_map/ppermute | solution.py:225
  32.6 4.2 %collective-permute-start.14 = (f32[128,128]{1,0:T(8,128)S(1)}, f32[128,128]{1,0:T(8,128)S(1)}, u32[]{:S(2)}, u32[]{:S(2)}) collective-permute-start(f32[128,128]{1,0:T(8,128)S(1)} %get-tuple-element.62.part_ref), channel_id=1, source_target_pairs={{1,0},{3,2},{5,4},{7,6},{9,8},{11,10},{13,12},{15,14},{16,17},{18,... | collective-permute-start | bytes 196616 | tf_op jit(solution)/shard_map/ppermute | solution.py:225
  32.7 5.1 %collective-permute-start.15 = (f32[128,128]{1,0:T(8,128)S(1)}, f32[128,128]{1,0:T(8,128)S(1)}, u32[]{:S(2)}, u32[]{:S(2)}) collective-permute-start(f32[128,128]{1,0:T(8,128)S(1)} %get-tuple-element.63.far_ref), channel_id=1, source_target_pairs={{1,16},{3,18},{5,20},{7,22},{9,24},{11,26},{13,28},{15,30},{16,1},... | collective-permute-start | bytes 196616 | tf_op jit(solution)/shard_map/ppermute | solution.py:225
  37.8 7.3 %collective-permute-start.17 = (f32[128,128]{1,0:T(8,128)S(1)}, f32[128,128]{1,0:T(8,128)S(1)}, u32[]{:S(2)}, u32[]{:S(2)}) collective-permute-start(f32[128,128]{1,0:T(8,128)S(1)} %add_add_fusion.1.rest_0_.refs_4_), channel_id=1, source_target_pairs={{0,12},{1,13},{2,14},{3,15},{4,8},{5,9},{6,10},{7,11},{8,4},{9,5},... | collective-permute-start | bytes 196616 | tf_op jit(solution)/shard_map/ppermute | solution.py:225
  37.9 7.6 %collective-permute-start.19 = (f32[128,128]{1,0:T(8,128)S(1)}, f32[128,128]{1,0:T(8,128)S(1)}, u32[]{:S(2)}, u32[]{:S(2)}) collective-permute-start(f32[128,128]{1,0:T(8,128)S(1)} %add_add_fusion.1.rest_0_.refs_4_), channel_id=1, source_target_pairs={{0,8},{1,9},{2,10},{3,11},{4,12},{5,13},{6,14},{7,15},{8,0},{9,1},... | collective-permute-start | bytes 196616 | tf_op jit(solution)/shard_map/ppermute | solution.py:225
  39.4 6.1 %collective-permute-start.18 = (f32[128,128]{1,0:T(8,128)S(1)}, f32[128,128]{1,0:T(8,128)S(1)}, u32[]{:S(2)}, u32[]{:S(2)}) collective-permute-start(f32[128,128]{1,0:T(8,128)S(1)} %add_add_fusion.1.rest_0_.refs_4_), channel_id=1, source_target_pairs={{0,4},{1,5},{2,6},{3,7},{4,0},{5,1},{6,2},{7,3},{8,12},{9,13},{10,... | collective-permute-start | bytes 196616 | tf_op jit(solution)/shard_map/ppermute | solution.py:225
  40.5 8.7 %collective-permute-start.24 = (f32[128,128]{1,0:T(8,128)S(1)}, f32[128,128]{1,0:T(8,128)S(1)}, u32[]{:S(2)}, u32[]{:S(2)}) collective-permute-start(f32[128,128]{1,0:T(8,128)S(1)} %add_add_fusion.1.rest_0_.refs_4_), channel_id=1, source_target_pairs={{0,2},{1,3},{2,0},{3,1},{4,6},{5,7},{6,4},{7,5},{8,10},{9,11},{10,... | collective-permute-start | bytes 196616 | tf_op jit(solution)/shard_map/ppermute | solution.py:225
  45.8 4.2 %collective-permute-start.22 = (f32[128,128]{1,0:T(8,128)S(1)}, f32[128,128]{1,0:T(8,128)S(1)}, u32[]{:S(2)}, u32[]{:S(2)}) collective-permute-start(f32[128,128]{1,0:T(8,128)S(1)} %get-tuple-element.70.refs_2_), channel_id=1, source_target_pairs={{1,0},{3,2},{5,4},{7,6},{9,8},{11,10},{13,12},{15,14},{16,17},{18,... | collective-permute-start | bytes 196616 | tf_op jit(solution)/shard_map/ppermute | solution.py:225
  45.9 5.1 %collective-permute-start.23 = (f32[128,128]{1,0:T(8,128)S(1)}, f32[128,128]{1,0:T(8,128)S(1)}, u32[]{:S(2)}, u32[]{:S(2)}) collective-permute-start(f32[128,128]{1,0:T(8,128)S(1)} %get-tuple-element.71.refs_3_), channel_id=1, source_target_pairs={{1,16},{3,18},{5,20},{7,22},{9,24},{11,26},{13,28},{15,30},{16,1},... | collective-permute-start | bytes 196616 | tf_op jit(solution)/shard_map/ppermute | solution.py:225
  46.8 11.6 %collective-permute-start.21 = (f32[4,64,128]{2,1,0:T(8,128)S(1)}, f32[4,64,128]{2,1,0:T(8,128)S(1)}, u32[]{:S(2)}, u32[]{:S(2)}) collective-permute-start(f32[4,64,128]{2,1,0:T(8,128)S(1)} %get-tuple-element.69.refs_1_), channel_id=1, source_target_pairs={{0,2},{1,3},{2,0},{3,1},{4,6},{5,7},{6,4},{7,5},{8,10},{9,11},{10,... | collective-permute-start | bytes 393224 | tf_op jit(solution)/shard_map/ppermute | solution.py:225
  51.1 7.9 %collective-permute-start.27 = (f32[128,128]{1,0:T(8,128)S(1)}, f32[128,128]{1,0:T(8,128)S(1)}, u32[]{:S(2)}, u32[]{:S(2)}) collective-permute-start(f32[128,128]{1,0:T(8,128)S(1)} %add_add_fusion.refs_4_), channel_id=1, source_target_pairs={{0,12},{1,13},{2,14},{3,15},{4,8},{5,9},{6,10},{7,11},{8,4},{9,5},... | collective-permute-start | bytes 196616 | tf_op jit(solution)/shard_map/ppermute | solution.py:225
  51.5 10.8 %collective-permute-start.20 = (f32[4,64,128]{2,1,0:T(8,128)S(1)}, f32[4,64,128]{2,1,0:T(8,128)S(1)}, u32[]{:S(2)}, u32[]{:S(2)}) collective-permute-start(f32[4,64,128]{2,1,0:T(8,128)S(1)} %get-tuple-element.66.refs_0_), channel_id=1, source_target_pairs={{0,2},{1,3},{2,0},{3,1},{4,6},{5,7},{6,4},{7,5},{8,10},{9,11},{10,... | collective-permute-start | bytes 393224 | tf_op jit(solution)/shard_map/ppermute | solution.py:225
  55.5 5.7 %collective-permute-start.26 = (f32[128,128]{1,0:T(8,128)S(1)}, f32[128,128]{1,0:T(8,128)S(1)}, u32[]{:S(2)}, u32[]{:S(2)}) collective-permute-start(f32[128,128]{1,0:T(8,128)S(1)} %add_add_fusion.refs_4_), channel_id=1, source_target_pairs={{0,8},{1,9},{2,10},{3,11},{4,12},{5,13},{6,14},{7,15},{8,0},{9,1},... | collective-permute-start | bytes 196616 | tf_op jit(solution)/shard_map/ppermute | solution.py:225
  57.3 4.2 %collective-permute-start.25 = (f32[128,128]{1,0:T(8,128)S(1)}, f32[128,128]{1,0:T(8,128)S(1)}, u32[]{:S(2)}, u32[]{:S(2)}) collective-permute-start(f32[128,128]{1,0:T(8,128)S(1)} %add_add_fusion.refs_4_), channel_id=1, source_target_pairs={{0,4},{1,5},{2,6},{3,7},{4,0},{5,1},{6,2},{7,3},{8,12},{9,13},{10,... | collective-permute-start | bytes 196616 | tf_op jit(solution)/shard_map/ppermute | solution.py:225
  58.4 3.9 %collective-permute-start.28 = (f32[128,128]{1,0:T(8,128)S(1)}, f32[128,128]{1,0:T(8,128)S(1)}, u32[]{:S(2)}, u32[]{:S(2)}) collective-permute-start(f32[128,128]{1,0:T(8,128)S(1)} %add_add_fusion.refs_4_), channel_id=1, source_target_pairs={{0,2},{1,3},{2,0},{3,1},{4,6},{5,7},{6,4},{7,5},{8,10},{9,11},{10,... | collective-permute-start | bytes 196616 | tf_op jit(solution)/shard_map/ppermute | solution.py:225
  58.9 3.4 %collective-permute-start.31 = (f32[128,128]{1,0:T(8,128)S(1)}, f32[128,128]{1,0:T(8,128)S(1)}, u32[]{:S(2)}, u32[]{:S(2)}) collective-permute-start(f32[128,128]{1,0:T(8,128)S(1)} %collective-permute-done.27.refs_7_), channel_id=1, source_target_pairs={{0,2},{1,3},{2,0},{3,1},{4,6},{5,7},{6,4},{7,5},{8,10},{9,11},{10,... | collective-permute-start | bytes 196616 | tf_op jit(solution)/shard_map/ppermute | solution.py:225
  61.2 1.3 %collective-permute-start.30 = (f32[128,128]{1,0:T(8,128)S(1)}, f32[128,128]{1,0:T(8,128)S(1)}, u32[]{:S(2)}, u32[]{:S(2)}) collective-permute-start(f32[128,128]{1,0:T(8,128)S(1)} %collective-permute-done.26.refs_6_), channel_id=1, source_target_pairs={{0,2},{1,3},{2,0},{3,1},{4,6},{5,7},{6,4},{7,5},{8,10},{9,11},{10,... | collective-permute-start | bytes 196616 | tf_op jit(solution)/shard_map/ppermute | solution.py:225
  61.5 1.6 %collective-permute-start.29 = (f32[128,128]{1,0:T(8,128)S(1)}, f32[128,128]{1,0:T(8,128)S(1)}, u32[]{:S(2)}, u32[]{:S(2)}) collective-permute-start(f32[128,128]{1,0:T(8,128)S(1)} %collective-permute-done.25.refs_5_), channel_id=1, source_target_pairs={{0,2},{1,3},{2,0},{3,1},{4,6},{5,7},{6,4},{7,5},{8,10},{9,11},{10,... | collective-permute-start | bytes 196616 | tf_op jit(solution)/shard_map/ppermute | solution.py:225
